TPU v7x, 32 devices: a whole 2x2x4 slice. The times are simulated.
32 devices in a mesh: parts: 1, rows: 32 (over z, y, x, core), cls: 1.
Axes of the slice: x: 2, y: 2, z: 4, core: 2. Of those that a mesh axis runs over, the one named last changes fastest.
Arguments:
- seeds: bfloat16 [16384, 1024], P(('parts', 'rows'), 'cls'), may hold values from -6 to 6
- neighbor_pos: int32 [16384, 50], P(('parts', 'rows')), may hold values from 0 to 1023, as said below
- edge_weight: int32 [16384, 50], P(('parts', 'rows')), may hold values from 1 to 192
- tile_blocks: int32 [128, 8], P(('parts', 'rows')), may hold values from 0 to 7, as said below
- wanted: int32 [32, 32, 16], P(('parts', 'rows')), may hold values from 0 to 511
Outputs:
- labels: bfloat16 [16384, 1024], P(('parts', 'rows'), 'cls')
Inputs may be any that keep to these rules, and one draw needn't show every extreme that they name: `neighbor_pos`: the 50 positions of a row are distinct; position q names column q % 128 of the row block's tile q // 128. `tile_blocks`: the 8 numbers of a row block are distinct; a number below 4 is a row block of the same index of rows, a larger one e a block of 128 received rows, row r = (e - 4) * 128 + c standing for wanted[d, r // 16, r % 16]. wanted[d, p, c] is a row number local to index p of rows.
All inputs are finite; a program needn't handle non-finite values.
Results may differ from a plain program's by a relative error of at most 0.0034.
Values may be sent and summed in bfloat16 or wider, within the bound.
No kernel may reach another device: no remote copies, remote signals or barrier semaphores. Data moves between devices by JAX's collectives and lax.ppermute only.
A program may use at most 64 MiB of HBM per device.

v0:
```python
import jax
import jax.numpy as jnp
from jax import lax
from jax.sharding import PartitionSpec as P

BLK = 128
ITERS = 2


def build_tiles(neighbor_pos, share, block_count, columns):
    neighbours = neighbor_pos.shape[1]
    pos_blocks = neighbor_pos.reshape(block_count, -1, neighbours)
    share_blocks = share.reshape(block_count, -1, neighbours)
    column_ids = jnp.arange(columns, dtype=jnp.int32)[None, None, :]

    def build_one_block(pair):
        positions, weights = pair
        total = jnp.zeros((positions.shape[0], columns), jnp.float32)
        for first in range(0, neighbours, 10):
            last = min(first + 10, neighbours)
            hits = positions[:, first:last, None] == column_ids
            total = total + jnp.sum(jnp.where(hits, weights[:, first:last, None], 0.0), axis=1)
        return total.astype(jnp.bfloat16)

    return lax.map(build_one_block, (pos_blocks, share_blocks))


def on_device(seeds, neighbor_pos, edge_weight, tile_blocks, wanted):
    rows_dev, width = seeds.shape
    block_count, tile_count = tile_blocks.shape
    peer_count = wanted.shape[1]
    slot_count = wanted.shape[2]
    asked = lax.all_to_all(wanted[0], "rows", split_axis=0, concat_axis=0, tiled=True)
    asked_flat = asked.reshape(peer_count * slot_count)
    weights = edge_weight.astype(jnp.float32)
    share = weights / jnp.sum(weights, axis=1, keepdims=True)
    tiles = build_tiles(neighbor_pos, share, block_count, tile_count * BLK)
    seeds_float = seeds.astype(jnp.float32)
    current = seeds
    for step in range(ITERS):
        outgoing = current[asked_flat].reshape(peer_count, slot_count, width)
        received = lax.all_to_all(outgoing, "rows", split_axis=0, concat_axis=0, tiled=True)
        extended = jnp.concatenate(
            [current, received.reshape(peer_count * slot_count, width)], axis=0
        )
        ext_blocks = extended.reshape(-1, BLK, width)

        def body_one_block(pair):
            tile_row, block_list = pair
            operand = ext_blocks[block_list].reshape(tile_count * BLK, width)
            return jnp.dot(tile_row, operand, preferred_element_type=jnp.float32)

        summed = lax.map(body_one_block, (tiles, tile_blocks))
        current = (0.85 * summed.reshape(rows_dev, width) + 0.15 * seeds_float).astype(jnp.bfloat16)
    return current


def solution(mesh):
    in_specs = (
        P(("parts", "rows"), "cls"),
        P(("parts", "rows"), None),
        P(("parts", "rows"), None),
        P(("parts", "rows"), None),
        P(("parts", "rows"), None, None),
    )
    out_specs = P(("parts", "rows"), "cls")
    return jax.shard_map(
        on_device, mesh=mesh, in_specs=in_specs, out_specs=out_specs, check_vma=False
    )
```

profile of v0, /device:TPU:0, one launch (start us, length us, event | category | flops | bytes accessed | tf_op | source)
XLA Modules:
  0.0 130.3 jit_solution(7909842866963089829)
XLA Ops:
  0.0 1.4 %copy.17 = s32[1,32,16]{2,1,0:T(8,128)} copy(s32[1,32,16]{1,2,0:T(8,128)} %param.15) | data formatting | bytes 4096 | tf_op args[4]
  1.4 7.3 %all-to-all-start = ((s32[32,1,16]{2,1,0:T(1,128)}), s32[32,1,16]{2,1,0:T(1,128)S(1)}, u32[]{:S(2)}, u32[]{:S(2)}) async-start(s32[32,1,16]{2,1,0:T(1,128)} %bitcast.10), calls=%async_computation | async-start | bytes 32768 | tf_op jit(solution)/shard_map/all_to_all | solution.py:33
  8.7 0.9 convert_reduce_fusion
  9.6 0.9 convert_divide_fusion
  10.6 0.9 reshape.178
  11.5 4.3 %all-to-all-done = s32[32,1,16]{2,1,0:T(1,128)S(1)} async-done(((s32[32,1,16]{2,1,0:T(1,128)}), s32[32,1,16]{2,1,0:T(1,128)S(1)}, u32[]{:S(2)}, u32[]{:S(2)}) %all-to-all-start) | async-done | bytes 2080 | tf_op jit(solution)/shard_map/all_to_all | solution.py:33
  15.8 0.6 broadcast.115
  16.4 0.7 reduce.3
  17.1 0.1 reshape.180
  17.2 4.8 %gather_fusion.2 = bf16[512,1024]{1,0:T(8,128)(2,1)} fusion(bf16[512,1024]{1,0:T(8,128)(2,1)} %param.11, s32[1024]{0:T(1024)S(1)} %pad_clamp_fusion.2), kind=kCustom, calls=%fused_computation.2 | custom fusion | bytes 2099200 | tf_op jit(solution)/shard_map/gather | solution.py:41
  22.1 2.6 %all-to-all-start.1 = ((bf16[32,16,1024]{2,1,0:T(8,128)(2,1)}), bf16[32,16,1024]{2,1,0:T(8,128)(2,1)S(1)}, u32[]{:S(2)}, u32[]{:S(2)}) async-start(bf16[32,16,1024]{2,1,0:T(8,128)(2,1)} %bitcast.12), calls=%async_computation.1 | async-start | bytes 2097152 | tf_op jit(solution)/shard_map/all_to_all | solution.py:42
  24.7 0.0 copy-start
  24.8 19.7 %while.34 = (s32[]{:T(128)}, bf16[4,128,1024]{2,1,0:T(8,128)(2,1)}, s32[4,128,50]{1,0,2:T(4,128)S(1)}, f32[4,128,50]{1,0,2:T(4,128)S(1)}, s32[]{:T(128)}) while((s32[]{:T(128)}, bf16[4,128,1024]{2,1,0:T(8,128)(2,1)}, s32[4,128,50]{1,0,2:T(4,128)S(1)}, f32[4,128,50]{1,0,2:T(4,128)S(1)}, s32[]{:T(128)}) %tuple.69), condition=%wide.region_7.8_spmd.clone.clone, body=%wide.region_1.7_spmd.clone.clone.sunk | while | flops 19660800 | bytes 5864005 | solution.py:25
  24.9 1.5 %select_reduce_fusion.9 = (f32[128,1024]{1,0:T(8,128)S(1)}, f32[128,1024]{1,0:T(8,128)S(1)}) fusion(f32[128,10]{0,1:T(8,128)S(1)} %get-tuple-element.281, s32[128,10]{0,1:T(8,128)S(1)} %get-tuple-element.282, f32[128,10]{0,1:T(8,128)S(1)} %get-tuple-element.283, s32[128,10]{0,1:T(8,128)S(1)} %get-tuple-element.284), kind=kLoop, calls=%fused_computation.32.clone.1 | loop fusion | flops 7602176 | bytes 1069056 | tf_op jit(solution)/shard_map/while/body/eval_jaxpr/reduce_sum | solution.py:22
  26.4 1.5 %select_reduce_fusion.8 = (f32[128,1024]{1,0:T(8,128)S(1)}, f32[128,1024]{1,0:T(8,128)S(1)}) fusion(f32[128,10]{0,1:T(8,128)S(1)} %get-tuple-element.275, s32[128,10]{0,1:T(8,128)S(1)} %get-tuple-element.276, f32[128,10]{0,1:T(8,128)S(1)} %get-tuple-element.277, s32[128,10]{0,1:T(8,128)S(1)} %get-tuple-element.278), kind=kLoop, calls=%fused_computation.30.clone.1 | loop fusion | flops 7602176 | bytes 1069056 | tf_op jit(solution)/shard_map/while/body/eval_jaxpr/reduce_sum | solution.py:22
  28.0 0.8 select_reduce_fusion.10
  28.8 0.9 fusion.43
  29.8 1.5 %select_reduce_fusion.9 = (f32[128,1024]{1,0:T(8,128)S(1)}, f32[128,1024]{1,0:T(8,128)S(1)}) fusion(f32[128,10]{0,1:T(8,128)S(1)} %get-tuple-element.281, s32[128,10]{0,1:T(8,128)S(1)} %get-tuple-element.282, f32[128,10]{0,1:T(8,128)S(1)} %get-tuple-element.283, s32[128,10]{0,1:T(8,128)S(1)} %get-tuple-element.284), kind=kLoop, calls=%fused_computation.32.clone.1 | loop fusion | flops 7602176 | bytes 1069056 | tf_op jit(solution)/shard_map/while/body/eval_jaxpr/reduce_sum | solution.py:22
  31.4 1.5 %select_reduce_fusion.8 = (f32[128,1024]{1,0:T(8,128)S(1)}, f32[128,1024]{1,0:T(8,128)S(1)}) fusion(f32[128,10]{0,1:T(8,128)S(1)} %get-tuple-element.275, s32[128,10]{0,1:T(8,128)S(1)} %get-tuple-element.276, f32[128,10]{0,1:T(8,128)S(1)} %get-tuple-element.277, s32[128,10]{0,1:T(8,128)S(1)} %get-tuple-element.278), kind=kLoop, calls=%fused_computation.30.clone.1 | loop fusion | flops 7602176 | bytes 1069056 | tf_op jit(solution)/shard_map/while/body/eval_jaxpr/reduce_sum | solution.py:22
  32.9 0.8 select_reduce_fusion.10
  33.7 0.9 fusion.43
  34.7 1.5 %select_reduce_fusion.9 = (f32[128,1024]{1,0:T(8,128)S(1)}, f32[128,1024]{1,0:T(8,128)S(1)}) fusion(f32[128,10]{0,1:T(8,128)S(1)} %get-tuple-element.281, s32[128,10]{0,1:T(8,128)S(1)} %get-tuple-element.282, f32[128,10]{0,1:T(8,128)S(1)} %get-tuple-element.283, s32[128,10]{0,1:T(8,128)S(1)} %get-tuple-element.284), kind=kLoop, calls=%fused_computation.32.clone.1 | loop fusion | flops 7602176 | bytes 1069056 | tf_op jit(solution)/shard_map/while/body/eval_jaxpr/reduce_sum | solution.py:22
  36.3 1.5 %select_reduce_fusion.8 = (f32[128,1024]{1,0:T(8,128)S(1)}, f32[128,1024]{1,0:T(8,128)S(1)}) fusion(f32[128,10]{0,1:T(8,128)S(1)} %get-tuple-element.275, s32[128,10]{0,1:T(8,128)S(1)} %get-tuple-element.276, f32[128,10]{0,1:T(8,128)S(1)} %get-tuple-element.277, s32[128,10]{0,1:T(8,128)S(1)} %get-tuple-element.278), kind=kLoop, calls=%fused_computation.30.clone.1 | loop fusion | flops 7602176 | bytes 1069056 | tf_op jit(solution)/shard_map/while/body/eval_jaxpr/reduce_sum | solution.py:22
  37.8 0.8 select_reduce_fusion.10
  38.6 0.9 fusion.43
  39.6 1.5 %select_reduce_fusion.9 = (f32[128,1024]{1,0:T(8,128)S(1)}, f32[128,1024]{1,0:T(8,128)S(1)}) fusion(f32[128,10]{0,1:T(8,128)S(1)} %get-tuple-element.281, s32[128,10]{0,1:T(8,128)S(1)} %get-tuple-element.282, f32[128,10]{0,1:T(8,128)S(1)} %get-tuple-element.283, s32[128,10]{0,1:T(8,128)S(1)} %get-tuple-element.284), kind=kLoop, calls=%fused_computation.32.clone.1 | loop fusion | flops 7602176 | bytes 1069056 | tf_op jit(solution)/shard_map/while/body/eval_jaxpr/reduce_sum | solution.py:22
  41.2 1.5 %select_reduce_fusion.8 = (f32[128,1024]{1,0:T(8,128)S(1)}, f32[128,1024]{1,0:T(8,128)S(1)}) fusion(f32[128,10]{0,1:T(8,128)S(1)} %get-tuple-element.275, s32[128,10]{0,1:T(8,128)S(1)} %get-tuple-element.276, f32[128,10]{0,1:T(8,128)S(1)} %get-tuple-element.277, s32[128,10]{0,1:T(8,128)S(1)} %get-tuple-element.278), kind=kLoop, calls=%fused_computation.30.clone.1 | loop fusion | flops 7602176 | bytes 1069056 | tf_op jit(solution)/shard_map/while/body/eval_jaxpr/reduce_sum | solution.py:22
  42.7 0.8 select_reduce_fusion.10
  43.6 0.9 fusion.43
  44.4 6.5 %all-to-all-done.1 = bf16[32,16,1024]{2,1,0:T(8,128)(2,1)S(1)} async-done(((bf16[32,16,1024]{2,1,0:T(8,128)(2,1)}), bf16[32,16,1024]{2,1,0:T(8,128)(2,1)S(1)}, u32[]{:S(2)}, u32[]{:S(2)}) %all-to-all-start.1) | async-done | bytes 1048608 | tf_op jit(solution)/shard_map/all_to_all | solution.py:42
  51.0 0.0 copy-done
  51.0 1.5 %pad_maximum_fusion = bf16[1024,1024]{1,0:T(8,128)(2,1)} fusion(bf16[512,1024]{1,0:T(8,128)(2,1)S(1)} %bitcast.101, bf16[512,1024]{1,0:T(8,128)(2,1)S(1)} %copy-done), kind=kLoop, calls=%fused_computation.42 | loop fusion | flops 4194304 | bytes 4194304 | tf_op jit(solution)/shard_map/concatenate | solution.py:43
  52.5 0.0 copy-start.1
  52.5 1.6 %broadcast.83.clone = f32[4,128,1024]{2,1,0:T(8,128)} broadcast(f32[]{:T(128)} %constant.35.clone.1), dimensions={} | broadcast | bytes 2097156 | tf_op jit(solution)/shard_map/broadcast.15
  54.0 0.0 copy-done.1
  54.0 18.0 %while.32 = (s32[]{:T(128)}, f32[4,128,1024]{2,1,0:T(8,128)}, bf16[4,128,1024]{2,1,0:T(8,128)(2,1)}, s32[4,8]{1,0:T(4,128)S(1)}, bf16[8,128,1024]{2,1,0:T(8,128)(2,1)}, /*index=5*/s32[]{:T(128)}) while((s32[]{:T(128)}, f32[4,128,1024]{2,1,0:T(8,128)}, bf16[4,128,1024]{2,1,0:T(8,128)(2,1)}, s32[4,8]{1,0:T(4,128)S(1)}, ...), condition=%wide.region_9.10_spmd, body=%wide.region_8.9_spmd.sunk | while | flops 268436512 | bytes 7083209 | solution.py:53
  54.1 2.3 %gather_fusion = bf16[8,128,1024]{2,1,0:T(8,128)(2,1)S(1)} fusion(bf16[8,128,1024]{2,1,0:T(8,128)(2,1)} %get-tuple-element.320, s32[1024]{0:T(1024)S(1)} %pad_clamp_fusion.5), kind=kCustom, calls=%fused_computation.clone.1 | custom fusion | bytes 4194336 | tf_op jit(solution)/shard_map/while/body/eval_jaxpr/gather | solution.py:50
  56.3 2.2 %fusion.36 = f32[4,128,1024]{2,1,0:T(8,128)} fusion(f32[4,128,1024]{2,1,0:T(8,128)} %get-tuple-element.311, s32[]{:T(128)} %get-tuple-element.310, bf16[1024,1024]{1,0:T(8,128)(2,1)S(1)} %bitcast.94, bf16[4,128,1024]{2,1,0:T(8,128)(2,1)} %get-tuple-element.318), kind=kOutput, calls=%fused_computation.6.clone.1 | convolution fusion | flops 268435456 | bytes 2884608 | tf_op jit(solution)/shard_map/while/body/eval_jaxpr/dot_general | solution.py:51
  58.6 2.3 %gather_fusion = bf16[8,128,1024]{2,1,0:T(8,128)(2,1)S(1)} fusion(bf16[8,128,1024]{2,1,0:T(8,128)(2,1)} %get-tuple-element.320, s32[1024]{0:T(1024)S(1)} %pad_clamp_fusion.5), kind=kCustom, calls=%fused_computation.clone.1 | custom fusion | bytes 4194336 | tf_op jit(solution)/shard_map/while/body/eval_jaxpr/gather | solution.py:50
  60.8 2.2 %fusion.36 = f32[4,128,1024]{2,1,0:T(8,128)} fusion(f32[4,128,1024]{2,1,0:T(8,128)} %get-tuple-element.311, s32[]{:T(128)} %get-tuple-element.310, bf16[1024,1024]{1,0:T(8,128)(2,1)S(1)} %bitcast.94, bf16[4,128,1024]{2,1,0:T(8,128)(2,1)} %get-tuple-element.318), kind=kOutput, calls=%fused_computation.6.clone.1 | convolution fusion | flops 268435456 | bytes 2884608 | tf_op jit(solution)/shard_map/while/body/eval_jaxpr/dot_general | solution.py:51
  63.1 2.3 %gather_fusion = bf16[8,128,1024]{2,1,0:T(8,128)(2,1)S(1)} fusion(bf16[8,128,1024]{2,1,0:T(8,128)(2,1)} %get-tuple-element.320, s32[1024]{0:T(1024)S(1)} %pad_clamp_fusion.5), kind=kCustom, calls=%fused_computation.clone.1 | custom fusion | bytes 4194336 | tf_op jit(solution)/shard_map/while/body/eval_jaxpr/gather | solution.py:50
  65.4 2.2 %fusion.36 = f32[4,128,1024]{2,1,0:T(8,128)} fusion(f32[4,128,1024]{2,1,0:T(8,128)} %get-tuple-element.311, s32[]{:T(128)} %get-tuple-element.310, bf16[1024,1024]{1,0:T(8,128)(2,1)S(1)} %bitcast.94, bf16[4,128,1024]{2,1,0:T(8,128)(2,1)} %get-tuple-element.318), kind=kOutput, calls=%fused_computation.6.clone.1 | convolution fusion | flops 268435456 | bytes 2884608 | tf_op jit(solution)/shard_map/while/body/eval_jaxpr/dot_general | solution.py:51
  67.6 2.3 %gather_fusion = bf16[8,128,1024]{2,1,0:T(8,128)(2,1)S(1)} fusion(bf16[8,128,1024]{2,1,0:T(8,128)(2,1)} %get-tuple-element.320, s32[1024]{0:T(1024)S(1)} %pad_clamp_fusion.5), kind=kCustom, calls=%fused_computation.clone.1 | custom fusion | bytes 4194336 | tf_op jit(solution)/shard_map/while/body/eval_jaxpr/gather | solution.py:50
  69.8 2.2 %fusion.36 = f32[4,128,1024]{2,1,0:T(8,128)} fusion(f32[4,128,1024]{2,1,0:T(8,128)} %get-tuple-element.311, s32[]{:T(128)} %get-tuple-element.310, bf16[1024,1024]{1,0:T(8,128)(2,1)S(1)} %bitcast.94, bf16[4,128,1024]{2,1,0:T(8,128)(2,1)} %get-tuple-element.318), kind=kOutput, calls=%fused_computation.6.clone.1 | convolution fusion | flops 268435456 | bytes 2884608 | tf_op jit(solution)/shard_map/while/body/eval_jaxpr/dot_general | solution.py:51
  72.1 1.8 %broadcast_multiply_fusion.1 = f32[4,128,1024]{2,1,0:T(8,128)S(1)} fusion(f32[4,128,1024]{2,1,0:T(8,128)} %get-tuple-element.99), kind=kLoop, calls=%fused_computation.50 | loop fusion | flops 524288 | bytes 4194304 | tf_op jit(solution)/shard_map/mul | solution.py:54
  73.9 0.4 fusion.17
  74.3 2.1 %gather_fusion.3 = bf16[512,1024]{1,0:T(8,128)(2,1)S(1)} fusion(bf16[512,1024]{1,0:T(8,128)(2,1)S(1)} %fusion.17, s32[1024]{0:T(1024)S(1)} %pad_clamp_fusion.2), kind=kCustom, calls=%fused_computation.3 | custom fusion | bytes 2099200 | tf_op jit(solution)/shard_map/gather | solution.py:41
  76.3 29.6 %all_to_all.19 = bf16[32,16,1024]{2,1,0:T(8,128)(2,1)S(1)} all-to-all(bf16[32,16,1024]{2,1,0:T(8,128)(2,1)S(1)} %bitcast.100), channel_id=1, replica_groups=mesh['parts'=1,'rows'=32,'cls'=1] {'rows'}, dimensions={0} | all-to-all | bytes 2097152 | tf_op jit(solution)/shard_map/all_to_all | solution.py:42
  105.9 1.6 %pad_maximum_fusion.1 = bf16[1024,1024]{1,0:T(8,128)(2,1)} fusion(bf16[512,1024]{1,0:T(8,128)(2,1)S(1)} %bitcast.102, bf16[512,1024]{1,0:T(8,128)(2,1)S(1)} %fusion.17), kind=kLoop, calls=%fused_computation.43 | loop fusion | flops 4194304 | bytes 4194304 | tf_op jit(solution)/shard_map/concatenate | solution.py:43
  107.6 1.6 %broadcast.83 = f32[4,128,1024]{2,1,0:T(8,128)} broadcast(f32[]{:T(128)} %constant.35.clone.1), dimensions={} | broadcast | bytes 2097156 | tf_op jit(solution)/shard_map/broadcast.15
  109.1 18.0 %while.33 = (s32[]{:T(128)}, f32[4,128,1024]{2,1,0:T(8,128)}, bf16[4,128,1024]{2,1,0:T(8,128)(2,1)}, s32[4,8]{1,0:T(4,128)S(1)}, bf16[8,128,1024]{2,1,0:T(8,128)(2,1)}, /*index=5*/s32[]{:T(128)}) while((s32[]{:T(128)}, f32[4,128,1024]{2,1,0:T(8,128)}, bf16[4,128,1024]{2,1,0:T(8,128)(2,1)}, s32[4,8]{1,0:T(4,128)S(1)}, ...), condition=%wide.region_11.12_spmd, body=%wide.region_10.11_spmd.sunk | while | flops 268436512 | bytes 7083209 | solution.py:53
  109.1 2.3 %gather_fusion.1 = bf16[8,128,1024]{2,1,0:T(8,128)(2,1)S(1)} fusion(bf16[8,128,1024]{2,1,0:T(8,128)(2,1)} %get-tuple-element.338, s32[1024]{0:T(1024)S(1)} %pad_clamp_fusion.6), kind=kCustom, calls=%fused_computation.1.clone.1 | custom fusion | bytes 4194336 | tf_op jit(solution)/shard_map/while/body/eval_jaxpr/gather | solution.py:50
  111.4 2.2 %fusion.40 = f32[4,128,1024]{2,1,0:T(8,128)} fusion(f32[4,128,1024]{2,1,0:T(8,128)} %get-tuple-element.329, s32[]{:T(128)} %get-tuple-element.328, bf16[1024,1024]{1,0:T(8,128)(2,1)S(1)} %bitcast.95, bf16[4,128,1024]{2,1,0:T(8,128)(2,1)} %get-tuple-element.336), kind=kOutput, calls=%fused_computation.16.clone.1 | convolution fusion | flops 268435456 | bytes 2884608 | tf_op jit(solution)/shard_map/while/body/eval_jaxpr/dot_general | solution.py:51
  113.6 2.3 %gather_fusion.1 = bf16[8,128,1024]{2,1,0:T(8,128)(2,1)S(1)} fusion(bf16[8,128,1024]{2,1,0:T(8,128)(2,1)} %get-tuple-element.338, s32[1024]{0:T(1024)S(1)} %pad_clamp_fusion.6), kind=kCustom, calls=%fused_computation.1.clone.1 | custom fusion | bytes 4194336 | tf_op jit(solution)/shard_map/while/body/eval_jaxpr/gather | solution.py:50
  115.9 2.2 %fusion.40 = f32[4,128,1024]{2,1,0:T(8,128)} fusion(f32[4,128,1024]{2,1,0:T(8,128)} %get-tuple-element.329, s32[]{:T(128)} %get-tuple-element.328, bf16[1024,1024]{1,0:T(8,128)(2,1)S(1)} %bitcast.95, bf16[4,128,1024]{2,1,0:T(8,128)(2,1)} %get-tuple-element.336), kind=kOutput, calls=%fused_computation.16.clone.1 | convolution fusion | flops 268435456 | bytes 2884608 | tf_op jit(solution)/shard_map/while/body/eval_jaxpr/dot_general | solution.py:51
  118.1 2.3 %gather_fusion.1 = bf16[8,128,1024]{2,1,0:T(8,128)(2,1)S(1)} fusion(bf16[8,128,1024]{2,1,0:T(8,128)(2,1)} %get-tuple-element.338, s32[1024]{0:T(1024)S(1)} %pad_clamp_fusion.6), kind=kCustom, calls=%fused_computation.1.clone.1 | custom fusion | bytes 4194336 | tf_op jit(solution)/shard_map/while/body/eval_jaxpr/gather | solution.py:50
  120.4 2.2 %fusion.40 = f32[4,128,1024]{2,1,0:T(8,128)} fusion(f32[4,128,1024]{2,1,0:T(8,128)} %get-tuple-element.329, s32[]{:T(128)} %get-tuple-element.328, bf16[1024,1024]{1,0:T(8,128)(2,1)S(1)} %bitcast.95, bf16[4,128,1024]{2,1,0:T(8,128)(2,1)} %get-tuple-element.336), kind=kOutput, calls=%fused_computation.16.clone.1 | convolution fusion | flops 268435456 | bytes 2884608 | tf_op jit(solution)/shard_map/while/body/eval_jaxpr/dot_general | solution.py:51
  122.6 2.3 %gather_fusion.1 = bf16[8,128,1024]{2,1,0:T(8,128)(2,1)S(1)} fusion(bf16[8,128,1024]{2,1,0:T(8,128)(2,1)} %get-tuple-element.338, s32[1024]{0:T(1024)S(1)} %pad_clamp_fusion.6), kind=kCustom, calls=%fused_computation.1.clone.1 | custom fusion | bytes 4194336 | tf_op jit(solution)/shard_map/while/body/eval_jaxpr/gather | solution.py:50
  124.9 2.2 %fusion.40 = f32[4,128,1024]{2,1,0:T(8,128)} fusion(f32[4,128,1024]{2,1,0:T(8,128)} %get-tuple-element.329, s32[]{:T(128)} %get-tuple-element.328, bf16[1024,1024]{1,0:T(8,128)(2,1)S(1)} %bitcast.95, bf16[4,128,1024]{2,1,0:T(8,128)(2,1)} %get-tuple-element.336), kind=kOutput, calls=%fused_computation.16.clone.1 | convolution fusion | flops 268435456 | bytes 2884608 | tf_op jit(solution)/shard_map/while/body/eval_jaxpr/dot_general | solution.py:51
  127.1 1.8 %broadcast_multiply_fusion = f32[4,128,1024]{2,1,0:T(8,128)S(1)} fusion(f32[4,128,1024]{2,1,0:T(8,128)} %get-tuple-element.100), kind=kLoop, calls=%fused_computation.49 | loop fusion | flops 524288 | bytes 4194304 | tf_op jit(solution)/shard_map/mul | solution.py:54
  128.9 1.4 %fusion.16 = bf16[512,1024]{1,0:T(8,128)(2,1)} fusion(f32[4,128,1024]{2,1,0:T(8,128)S(1)} %broadcast_multiply_fusion, bf16[512,1024]{1,0:T(8,128)(2,1)S(1)} %copy-done), kind=kLoop, calls=%fused_computation.45 | loop fusion | flops 2097152 | bytes 4194304 | tf_op jit(solution)/shard_map/convert_element_type | solution.py:54
  (44 shorter events, 0.5 us)
Async XLA Ops:
  1.4 14.4 %all-to-all-start = ((s32[32,1,16]{2,1,0:T(1,128)}), s32[32,1,16]{2,1,0:T(1,128)S(1)}, u32[]{:S(2)}, u32[]{:S(2)}) async-start(s32[32,1,16]{2,1,0:T(1,128)} %bitcast.10), calls=%async_computation | async-start | bytes 32768 | tf_op jit(solution)/shard_map/all_to_all | solution.py:33
  22.1 28.9 %all-to-all-start.1 = ((bf16[32,16,1024]{2,1,0:T(8,128)(2,1)}), bf16[32,16,1024]{2,1,0:T(8,128)(2,1)S(1)}, u32[]{:S(2)}, u32[]{:S(2)}) async-start(bf16[32,16,1024]{2,1,0:T(8,128)(2,1)} %bitcast.12), calls=%async_computation.1 | async-start | bytes 2097152 | tf_op jit(solution)/shard_map/all_to_all | solution.py:42
  24.7 26.2 %copy-start = (bf16[512,1024]{1,0:T(8,128)(2,1)S(1)}, bf16[512,1024]{1,0:T(8,128)(2,1)}, u32[]{:S(2)}) copy-start(bf16[512,1024]{1,0:T(8,128)(2,1)} %param.11) | copy-start | bytes 3145732
  52.5 1.6 %copy-start.1 = (s32[4,8]{1,0:T(4,128)S(1)}, s32[4,8]{1,0:T(4,128)}, u32[]{:S(2)}) copy-start(s32[4,8]{1,0:T(4,128)} %param.14) | copy-start | bytes 388
where the time goes:
time: 131 us; the launch traced here: 130 us
  local copies, waits for them, and re-layouts  31.5 us (24%)
  other arithmetic  30.4 us (23%)
  blocking collectives  29.6 us (23%)
  matrix products  17.6 us (13%)
  waiting for transfers between devices  10.8 us (8%)
  starting transfers between devices  9.94 us (8%)
    all_to_all x1, blocking collectives, on_device(): lax.all_to_all(outgoing, 'rows', split_axis=0, concat_axis=0, tiled=True)  29.6 us
    gather x8, local copies, waits for them, and re-layouts, body_one_block(): operand = ext_blocks[block_list].reshape(tile_count * BLK, width)  18.2 us
    dot_general x8, matrix products, body_one_block(): return jnp.dot(tile_row, operand, preferred_element_type=jnp.float32)  17.6 us
    reduce_sum x12, other arithmetic, build_one_block(): jnp.sum(jnp.where(hits, weights[:, first:last, None], 0.0), axis=1)  15.6 us
    all_to_all x1, starting transfers between devices, on_device(): lax.all_to_all(wanted[0], 'rows', split_axis=0, concat_axis=0, tiled=True)  7.3 us
    gather x2, local copies, waits for them, and re-layouts, on_device(): outgoing = current[asked_flat].reshape(peer_count, slot_count, width)  6.91 us
    all_to_all x1, waiting for transfers between devices, on_device(): lax.all_to_all(outgoing, 'rows', split_axis=0, concat_axis=0, tiled=True)  6.52 us
    all_to_all x1, waiting for transfers between devices, on_device(): lax.all_to_all(wanted[0], 'rows', split_axis=0, concat_axis=0, tiled=True)  4.31 us
  transfers between devices with their start and end apart: 2, of which 2 were waited for; matrix products, arithmetic and copies ran while one was open for 17% of the time, Pallas kernels for 0%

commit v1 on v0

v1 whole, which is shorter than its diff:
```python
import functools

import jax
import jax.numpy as jnp
from jax import lax
from jax.experimental import pallas as pl
from jax.experimental.pallas import tpu as pltpu
from jax.sharding import PartitionSpec as P

BLK = 128
COLS = 256
VMEM = 48 * 1024 * 1024


def tiles_kernel(blocks_ref, pos_ref, weight_ref, tiles_ref, column_ref, share_ref):
    block_count, tile_count = blocks_ref.shape
    neighbours = pos_ref.shape[0]
    weights = weight_ref[...].astype(jnp.float32)
    share = weights / jnp.sum(weights, axis=0, keepdims=True)
    share_ref[...] = share.astype(jnp.bfloat16).astype(jnp.float32)
    for block in range(block_count):
        lanes = slice(block * BLK, (block + 1) * BLK)
        pos = pos_ref[:, lanes]
        tile = pos // BLK
        base = jnp.full(pos.shape, blocks_ref[block, 0], jnp.int32)
        for j in range(1, tile_count):
            base = jnp.where(tile == j, blocks_ref[block, j], base)
        column_ref[:, lanes] = base * BLK + pos % BLK

    sub = lax.broadcasted_iota(jnp.int32, (BLK, BLK), 0)

    @pl.loop(0, block_count)
    def _(block):
        lanes = pl.ds(pl.multiple_of(block * BLK, BLK), BLK)

        @pl.loop(0, tiles_ref.shape[1] // BLK)
        def _(chunk):
            first = pl.multiple_of(chunk * BLK, BLK)
            total = jnp.zeros((BLK, BLK), jnp.float32)
            for k in range(neighbours):
                spot = column_ref[k : k + 1, lanes] - first
                total = jnp.where(sub == spot, share_ref[k : k + 1, lanes], total)
            tiles_ref[lanes, pl.ds(first, BLK)] = total.T.astype(jnp.bfloat16)


def build_tiles(blocks, pos, weight, columns):
    neighbours, rows = pos.shape
    return pl.pallas_call(
        tiles_kernel,
        out_shape=jax.ShapeDtypeStruct((rows, columns), jnp.bfloat16),
        in_specs=[
            pl.BlockSpec(memory_space=pltpu.SMEM),
            pl.BlockSpec(memory_space=pltpu.VMEM),
            pl.BlockSpec(memory_space=pltpu.VMEM),
        ],
        out_specs=pl.BlockSpec(memory_space=pltpu.VMEM),
        scratch_shapes=[
            pltpu.VMEM((neighbours, rows), jnp.int32),
            pltpu.VMEM((neighbours, rows), jnp.float32),
        ],
        compiler_params=pltpu.CompilerParams(vmem_limit_bytes=VMEM),
        cost_estimate=pl.CostEstimate(
            flops=2 * neighbours * rows * columns,
            bytes_accessed=rows * columns * 2,
            transcendentals=0,
        ),
        name="build_tiles",
    )(blocks, pos, weight)


def pick_kernel(asked_ref, seeds_ref, out_ref, pick_ref):
    peers, _, slots = asked_ref.shape
    rows = seeds_ref.shape[0]
    count = peers * slots

    @pl.when(pl.program_id(0) == 0)
    def _():
        spread = jnp.broadcast_to(asked_ref[...].astype(jnp.float32), (peers, slots, slots))
        spread = spread.reshape(count, slots)
        slot = lax.broadcasted_iota(jnp.int32, (count, slots), 0) % slots
        lane = lax.broadcasted_iota(jnp.int32, (count, slots), 1)
        row = jnp.sum(jnp.where(slot == lane, spread, 0.0), axis=1, keepdims=True)
        hits = lax.broadcasted_iota(jnp.int32, (count, rows), 1) == row.astype(jnp.int32)
        pick_ref[...] = hits.astype(jnp.float32).astype(jnp.bfloat16)

    out_ref[...] = jnp.dot(
        pick_ref[...], seeds_ref[...], preferred_element_type=jnp.float32
    ).astype(jnp.bfloat16)


def pick_rows(asked, seeds):
    peers, _, slots = asked.shape
    rows, width = seeds.shape
    count = peers * slots
    return pl.pallas_call(
        pick_kernel,
        grid=(width // COLS,),
        out_shape=[
            jax.ShapeDtypeStruct((count, width), jnp.bfloat16),
            jax.ShapeDtypeStruct((count, rows), jnp.bfloat16),
        ],
        in_specs=[
            pl.BlockSpec((peers, 1, slots), lambda c: (0, 0, 0)),
            pl.BlockSpec((rows, COLS), lambda c: (0, c)),
        ],
        out_specs=[
            pl.BlockSpec((count, COLS), lambda c: (0, c)),
            pl.BlockSpec((count, rows), lambda c: (0, 0)),
        ],
        compiler_params=pltpu.CompilerParams(vmem_limit_bytes=VMEM),
        name="pick_rows",
    )(asked, seeds)


def propagate(tiles_ref, current_ref, received_ref, seeds_ref):
    rows = current_ref.shape[0]
    total = jnp.dot(
        tiles_ref[:, :rows], current_ref[...], preferred_element_type=jnp.float32
    ) + jnp.dot(tiles_ref[:, rows:], received_ref[...], preferred_element_type=jnp.float32)
    return (0.85 * total + 0.15 * seeds_ref[...].astype(jnp.float32)).astype(jnp.bfloat16)


def first_kernel(tiles_ref, pick_ref, seeds_ref, received_ref, labels_ref, out_ref):
    labels = propagate(tiles_ref, seeds_ref, received_ref, seeds_ref)
    labels_ref[...] = labels
    out_ref[...] = jnp.dot(
        pick_ref[...], labels, preferred_element_type=jnp.float32
    ).astype(jnp.bfloat16)


def last_kernel(tiles_ref, seeds_ref, current_ref, received_ref, labels_ref):
    labels_ref[...] = propagate(tiles_ref, current_ref, received_ref, seeds_ref)


def first_step(tiles, pick, seeds, received):
    rows, width = seeds.shape
    count = received.shape[0]
    by_columns = lambda c: (0, c)
    whole = lambda c: (0, 0)
    return pl.pallas_call(
        first_kernel,
        grid=(width // COLS,),
        out_shape=[
            jax.ShapeDtypeStruct((rows, width), jnp.bfloat16),
            jax.ShapeDtypeStruct((count, width), jnp.bfloat16),
        ],
        in_specs=[
            pl.BlockSpec(tiles.shape, whole),
            pl.BlockSpec(pick.shape, whole),
            pl.BlockSpec((rows, COLS), by_columns),
            pl.BlockSpec((count, COLS), by_columns),
        ],
        out_specs=[
            pl.BlockSpec((rows, COLS), by_columns),
            pl.BlockSpec((count, COLS), by_columns),
        ],
        compiler_params=pltpu.CompilerParams(vmem_limit_bytes=VMEM),
        name="first_step",
    )(tiles, pick, seeds, received)


def last_step(tiles, seeds, current, received):
    rows, width = seeds.shape
    count = received.shape[0]
    by_columns = lambda c: (0, c)
    return pl.pallas_call(
        last_kernel,
        grid=(width // COLS,),
        out_shape=jax.ShapeDtypeStruct((rows, width), jnp.bfloat16),
        in_specs=[
            pl.BlockSpec(tiles.shape, lambda c: (0, 0)),
            pl.BlockSpec((rows, COLS), by_columns),
            pl.BlockSpec((rows, COLS), by_columns),
            pl.BlockSpec((count, COLS), by_columns),
        ],
        out_specs=pl.BlockSpec((rows, COLS), by_columns),
        compiler_params=pltpu.CompilerParams(vmem_limit_bytes=VMEM),
        name="last_step",
    )(tiles, seeds, current, received)


def exchange(rows_out, peers):
    count, width = rows_out.shape
    sent = rows_out.reshape(peers, count // peers, width)
    got = lax.all_to_all(sent, "rows", split_axis=0, concat_axis=0, tiled=True)
    return got.reshape(count, width)


def on_device(seeds, neighbor_pos, edge_weight, tile_blocks, wanted):
    rows, width = seeds.shape
    peers, slots = wanted.shape[1:]
    asked = lax.all_to_all(
        wanted.reshape(peers, 1, slots), "rows", split_axis=0, concat_axis=0, tiled=True
    )
    tiles = build_tiles(tile_blocks, neighbor_pos.T, edge_weight.T, rows + peers * slots)
    outgoing, pick = pick_rows(asked, seeds)
    received = exchange(outgoing, peers)
    current, outgoing = first_step(tiles, pick, seeds, received)
    received = exchange(outgoing, peers)
    return last_step(tiles, seeds, current, received)


def solution(mesh):
    in_specs = (
        P(("parts", "rows"), "cls"),
        P(("parts", "rows"), None),
        P(("parts", "rows"), None),
        P(("parts", "rows"), None),
        P(("parts", "rows"), None, None),
    )
    out_specs = P(("parts", "rows"), "cls")
    return jax.shard_map(
        on_device, mesh=mesh, in_specs=in_specs, out_specs=out_specs, check_vma=False
    )
```

time: 131 us -> 86.8 us (0.66)
  other arithmetic: 30.4 us -> 0 us
  local copies, waits for them, and re-layouts: 31.5 us -> 3.85 us
  Pallas kernels: 0 us -> 23.6 us
  matrix products: 17.6 us -> 0 us
  blocking collectives: 29.6 us -> 43.8 us
  starting transfers between devices: 9.94 us -> 2.78 us
  waiting for transfers between devices: 10.8 us -> 12.3 us
    gather x10 -> x0, local copies, waits for them, and re-layouts: 25.1 us -> none  [the longest x8 18.2 us: body_one_block(): operand = ext_blocks[block_list].reshape(tile_count * BLK, width)]
    pallas_call x0 -> x4, Pallas kernels: none -> 23.6 us  [the longest x1 13.9 us: build_tiles(): pl.pallas_call(tiles_kernel, out_shape=jax.ShapeDtypeStruct((rows, column...]
    dot_general x8 -> x0, matrix products: 17.6 us -> none  [body_one_block(): return jnp.dot(tile_row, operand, preferred_element_type=jnp.float32)]
    reduce_sum x13 -> x0, other arithmetic: 16.5 us -> none  [the longest x12 15.6 us: build_one_block(): jnp.sum(jnp.where(hits, weights[:, first:last, None], 0.0), axis=1)]
    all_to_all x1 -> x2, blocking collectives: 29.6 us -> 43.8 us  [the longest x1 29.6 us: exchange(): got = lax.all_to_all(sent, 'rows', split_axis=0, concat_axis=0, tiled=True)]
    all_to_all x2 -> x1, starting transfers between devices: 9.94 us -> 2.78 us  [exchange(): got = lax.all_to_all(sent, 'rows', split_axis=0, concat_axis=0, tiled=True)]
    mul x2 -> x0, other arithmetic: 3.61 us -> none  [on_device(): 0.85 * summed.reshape(rows_dev, width) + 0.15 * seeds_float]
    dynamic_update_slice x4 -> x0, other arithmetic: 3.55 us -> none  [build_tiles(): return lax.map(build_one_block, (pos_blocks, share_blocks))]
  transfers between devices with their start and end apart: 2 -> 1, of which waited for: 2 -> 1; matrix products, arithmetic and copies ran while one was open for 17% -> 0% of each run, Pallas kernels for 0% -> 16%
where the time goes in v1:
time: 86.8 us; the launch traced here: 86.4 us
  blocking collectives  43.8 us (50%)
  Pallas kernels  23.6 us (27%)
  waiting for transfers between devices  12.3 us (14%)
  local copies, waits for them, and re-layouts  3.85 us (4%)
  starting transfers between devices  2.78 us (3%)
    all_to_all x1, blocking collectives, exchange(): got = lax.all_to_all(sent, 'rows', split_axis=0, concat_axis=0, tiled=True)  29.6 us
    all_to_all x1, blocking collectives, on_device(): lax.all_to_all(wanted.reshape(peers, 1, slots), 'rows', split_axis=0, con...  14.2 us
    pallas_call x1, Pallas kernels, build_tiles(): pl.pallas_call(tiles_kernel, out_shape=jax.ShapeDtypeStruct((rows, column...  13.9 us
    all_to_all x1, waiting for transfers between devices, exchange(): got = lax.all_to_all(sent, 'rows', split_axis=0, concat_axis=0, tiled=True)  12.3 us
    pallas_call x1, Pallas kernels, first_step(): pl.pallas_call(first_kernel, grid=(width // COLS,), out_shape=[jax.ShapeD...  4 us
    unnamed x15, local copies, waits for them, and re-layouts  3.85 us
    pallas_call x1, Pallas kernels, last_step(): pl.pallas_call(last_kernel, grid=(width // COLS,), out_shape=jax.ShapeDty...  3.08 us
    all_to_all x1, starting transfers between devices, exchange(): got = lax.all_to_all(sent, 'rows', split_axis=0, concat_axis=0, tiled=True)  2.78 us
  transfers between devices with their start and end apart: 1, of which 1 were waited for; matrix products, arithmetic and copies ran while one was open for 0% of the time, Pallas kernels for 16%

profile of v1, /device:TPU:0, one launch (start us, length us, event | category | flops | bytes accessed | tf_op | source)
XLA Modules:
  0.0 86.4 jit_solution(7556937905350877958)
XLA Ops:
  0.0 0.8 copy.6
  0.8 14.2 %all_to_all.15.asked_ref = s32[32,1,16]{2,1,0:T(1,128)S(1)} all-to-all(s32[32,1,16]{2,1,0:T(1,128)S(1)} %bitcast.12), channel_id=1, replica_groups=mesh['parts'=1,'rows'=32,'cls'=1] {'rows'}, dimensions={0} | all-to-all | bytes 4096 | tf_op jit(solution)/shard_map/all_to_all | solution.py:192
  15.0 0.0 copy-start
  15.0 1.2 %copy-done = bf16[512,1024]{1,0:T(8,128)(2,1)S(1)} copy-done((bf16[512,1024]{1,0:T(8,128)(2,1)S(1)}, bf16[512,1024]{1,0:T(8,128)(2,1)}, u32[]{:S(2)}) %copy-start) | copy-done | bytes 1048600
  16.2 2.6 %pick_rows.1 = (bf16[512,1024]{1,0:T(8,128)(2,1)}, bf16[512,512]{1,0:T(8,128)(2,1)S(1)}) custom-call(s32[32,1,16]{2,1,0:T(1,128)S(1)} %all_to_all.15.asked_ref, bf16[512,1024]{1,0:T(8,128)(2,1)S(1)} %copy-done), custom_call_target="tpu_custom_call" | custom-call | tf_op jit(solution)/shard_map/pick_rows/pallas_call | solution.py:95
  18.9 0.0 copy-start.2
  18.9 0.8 copy-done.2
  19.7 0.0 copy-start.4
  19.7 0.0 copy-start.5
  19.7 0.0 copy-start.6
  19.7 2.8 %all-to-all-start.1 = ((bf16[32,16,1024]{2,1,0:T(8,128)(2,1)}), bf16[32,16,1024]{2,1,0:T(8,128)(2,1)S(1)}, u32[]{:S(2)}, u32[]{:S(2)}) async-start(bf16[32,16,1024]{2,1,0:T(8,128)(2,1)} %bitcast.3), calls=%async_computation.1 | async-start | bytes 2097152 | tf_op jit(solution)/shard_map/all_to_all | solution.py:185
  22.5 0.0 copy-start.1
  22.5 0.0 copy-done.4
  22.5 0.0 copy-done.5
  22.5 0.0 copy-done.6
  22.5 13.9 %build_tiles.1.tiles_ref = bf16[512,1024]{1,0:T(8,128)(2,1)S(1)} custom-call(s32[4,8]{1,0:T(4,128)S(1)} %copy-done.6, s32[50,512]{1,0:T(8,128)S(1)} %bitcast.10, s32[50,512]{1,0:T(8,128)S(1)} %bitcast.11), custom_call_target="tpu_custom_call" | custom-call | flops 52428800 | bytes 1048576 | tf_op jit(solution)/shard_map/build_tiles/pallas_call | solution.py:48
  36.4 12.3 %all-to-all-done.1 = bf16[32,16,1024]{2,1,0:T(8,128)(2,1)S(1)} async-done(((bf16[32,16,1024]{2,1,0:T(8,128)(2,1)}), bf16[32,16,1024]{2,1,0:T(8,128)(2,1)S(1)}, u32[]{:S(2)}, u32[]{:S(2)}) %all-to-all-start.1) | async-done | bytes 1048608 | tf_op jit(solution)/shard_map/all_to_all | solution.py:185
  48.7 0.0 copy-done.1
  48.7 0.0 copy-start.3
  48.7 1.0 %copy-done.3 = bf16[512,512]{1,0:T(8,128)(2,1)S(1)} copy-done((bf16[512,512]{1,0:T(8,128)(2,1)S(1)}, bf16[512,512]{1,0:T(8,128)(2,1)}, u32[]{:S(2)}) %copy-start.3) | copy-done | bytes 524312
  49.7 4.0 %first_step.1 = (bf16[512,1024]{1,0:T(8,128)(2,1)S(1)}, bf16[512,1024]{1,0:T(8,128)(2,1)S(1)}) custom-call(bf16[512,1024]{1,0:T(8,128)(2,1)S(1)} %build_tiles.1.tiles_ref, bf16[512,512]{1,0:T(8,128)(2,1)S(1)} %copy-done.3, bf16[512,1024]{1,0:T(8,128)(2,1)S(1)} %copy-done.1, bf16[512,1024]{1,0:T(8,128)(2,1)S(1)} %bitcast.7), custom_call_target="tpu_custom_call" | custom-call | tf_op jit(solution)/shard_map/first_step/pallas_call | solution.py:140
  53.7 29.6 %all_to_all.16 = bf16[32,16,1024]{2,1,0:T(8,128)(2,1)S(1)} all-to-all(bf16[32,16,1024]{2,1,0:T(8,128)(2,1)S(1)} %bitcast.9), channel_id=1, replica_groups=mesh['parts'=1,'rows'=32,'cls'=1] {'rows'}, dimensions={0} | all-to-all | bytes 2097152 | tf_op jit(solution)/shard_map/all_to_all | solution.py:185
  83.3 3.1 %last_step.1 = bf16[512,1024]{1,0:T(8,128)(2,1)} custom-call(bf16[512,1024]{1,0:T(8,128)(2,1)S(1)} %build_tiles.1.tiles_ref, bf16[512,1024]{1,0:T(8,128)(2,1)S(1)} %copy-done.1, bf16[512,1024]{1,0:T(8,128)(2,1)S(1)} %get-tuple-element.11.current_ref, bf16[512,1024]{1,0:T(8,128)(2,1)S(1)} %bitcast.8), custom_call_target="tpu_custom_call" | custom-call | tf_op jit(solution)/shard_map/last_step/pallas_call | solution.py:166
Async XLA Ops:
  15.0 1.2 %copy-start = (bf16[512,1024]{1,0:T(8,128)(2,1)S(1)}, bf16[512,1024]{1,0:T(8,128)(2,1)}, u32[]{:S(2)}) copy-start(bf16[512,1024]{1,0:T(8,128)(2,1)} %seeds_ref.5) | copy-start | bytes 3145732
  18.9 0.8 copy-start.2
  19.7 2.8 %copy-start.4 = (s32[512,50]{0,1:T(8,128)S(1)}, s32[512,50]{0,1:T(8,128)}, u32[]{:S(2)}) copy-start(s32[512,50]{0,1:T(8,128)} %param.6) | copy-start | bytes 307204
  19.7 2.8 %copy-start.5 = (s32[512,50]{0,1:T(8,128)S(1)}, s32[512,50]{0,1:T(8,128)}, u32[]{:S(2)}) copy-start(s32[512,50]{0,1:T(8,128)} %param.7) | copy-start | bytes 307204
  19.7 2.8 %copy-start.6 = (s32[4,8]{1,0:T(4,128)S(1)}, s32[4,8]{1,0:T(4,128)}, u32[]{:S(2)}) copy-start(s32[4,8]{1,0:T(4,128)} %blocks_ref.1) | copy-start | bytes 388
  19.7 29.0 %all-to-all-start.1 = ((bf16[32,16,1024]{2,1,0:T(8,128)(2,1)}), bf16[32,16,1024]{2,1,0:T(8,128)(2,1)S(1)}, u32[]{:S(2)}, u32[]{:S(2)}) async-start(bf16[32,16,1024]{2,1,0:T(8,128)(2,1)} %bitcast.3), calls=%async_computation.1 | async-start | bytes 2097152 | tf_op jit(solution)/shard_map/all_to_all | solution.py:185
  22.5 26.2 %copy-start.1 = (bf16[512,1024]{1,0:T(8,128)(2,1)S(1)}, bf16[512,1024]{1,0:T(8,128)(2,1)}, u32[]{:S(2)}) copy-start(bf16[512,1024]{1,0:T(8,128)(2,1)} %seeds_ref.5) | copy-start | bytes 3145732
  48.7 1.0 %copy-start.3 = (bf16[512,512]{1,0:T(8,128)(2,1)S(1)}, bf16[512,512]{1,0:T(8,128)(2,1)}, u32[]{:S(2)}) copy-start(bf16[512,512]{1,0:T(8,128)(2,1)} %copy-done.2) | copy-start | bytes 1572868

commit v2 on v0

v2 whole, which is shorter than its diff:
```python
import jax
import jax.numpy as jnp
from jax import lax
from jax.experimental import pallas as pl
from jax.experimental.pallas import tpu as pltpu
from jax.sharding import PartitionSpec as P

BLK = 128
COLS = 256
VMEM_LIMIT = 32 * 1024 * 1024
KEEP = 0.85
ANCHOR = 0.15

SMEM = pl.BlockSpec(memory_space=pltpu.SMEM)
VMEM = pl.BlockSpec(memory_space=pltpu.VMEM)
ANY = pl.BlockSpec(memory_space=pl.ANY)


def call(kernel, name, out_shape, in_specs, out_specs=VMEM, scratch_shapes=(), flops=0, nbytes=0):
    return pl.pallas_call(
        kernel,
        out_shape=out_shape,
        in_specs=in_specs,
        out_specs=out_specs,
        scratch_shapes=scratch_shapes,
        compiler_params=pltpu.CompilerParams(vmem_limit_bytes=VMEM_LIMIT),
        cost_estimate=pl.CostEstimate(flops=flops, bytes_accessed=nbytes, transcendentals=0),
        name=name,
    )


def dot(a, b):
    return jnp.dot(a, b, preferred_element_type=jnp.float32)


def column_loop(width, body):
    @pl.loop(0, width // COLS)
    def _(c):
        body(pl.ds(pl.multiple_of(c * COLS, COLS), COLS))


def edges_kernel(blocks_ref, pos_ref, weight_ref, column_ref, share_ref):
    block_count, tile_count = blocks_ref.shape
    weights = weight_ref[...].astype(jnp.float32)
    share = weights / jnp.sum(weights, axis=0, keepdims=True)
    share_ref[...] = share.astype(jnp.bfloat16).astype(jnp.float32)
    for block in range(block_count):
        lanes = slice(block * BLK, (block + 1) * BLK)
        pos = pos_ref[:, lanes]
        tile = pos // BLK
        base = jnp.full(pos.shape, blocks_ref[block, 0], jnp.int32)
        for j in range(1, tile_count):
            base = jnp.where(tile == j, blocks_ref[block, j], base)
        column_ref[:, lanes] = base * BLK + pos % BLK


def tiles_kernel(column_ref, share_ref, pick_ref, tiles_ref):
    del pick_ref
    neighbours = column_ref.shape[0]
    sub = lax.broadcasted_iota(jnp.int32, (BLK, BLK), 0)

    @pl.loop(0, tiles_ref.shape[0] // BLK)
    def _(block):
        lanes = pl.ds(pl.multiple_of(block * BLK, BLK), BLK)

        @pl.loop(0, tiles_ref.shape[1] // BLK)
        def _(chunk):
            first = pl.multiple_of(chunk * BLK, BLK)
            total = jnp.zeros((BLK, BLK), jnp.float32)
            for k in range(neighbours):
                spot = column_ref[k : k + 1, lanes] - first
                total = jnp.where(sub == spot, share_ref[k : k + 1, lanes], total)
            tiles_ref[lanes, pl.ds(first, BLK)] = total.T.astype(jnp.bfloat16)


def pick_kernel(asked_ref, seeds_ref, out_ref, pick_ref):
    peers, _, slots = asked_ref.shape
    rows = seeds_ref.shape[0]
    count = peers * slots
    spread = jnp.broadcast_to(asked_ref[...].astype(jnp.float32), (peers, slots, slots))
    spread = spread.reshape(count, slots)
    slot = lax.broadcasted_iota(jnp.int32, (count, slots), 0) % slots
    lane = lax.broadcasted_iota(jnp.int32, (count, slots), 1)
    row = jnp.sum(jnp.where(slot == lane, spread, 0.0), axis=1, keepdims=True)
    hits = lax.broadcasted_iota(jnp.int32, (count, rows), 1) == row.astype(jnp.int32)
    pick_ref[...] = hits.astype(jnp.float32).astype(jnp.bfloat16)

    def body(cols):
        out_ref[:, cols] = dot(pick_ref[...], seeds_ref[:, cols]).astype(jnp.bfloat16)

    column_loop(seeds_ref.shape[1], body)


def own_kernel(tiles_ref, pick_ref, seeds_ref, sent_ref, picked_ref, base_ref, sent_base_ref):
    rows, width = seeds_ref.shape

    def pick_tiles(cols):
        picked_ref[:, cols] = dot(pick_ref[...], tiles_ref[:, cols]).astype(jnp.bfloat16)

    column_loop(tiles_ref.shape[1], pick_tiles)

    def body(cols):
        seeds = seeds_ref[:, cols]
        sent_base_ref[:, cols] = KEEP * dot(picked_ref[:, :rows], seeds) + ANCHOR * sent_ref[
            :, cols
        ].astype(jnp.float32)
        base_ref[:, cols] = KEEP * dot(tiles_ref[:, :rows], seeds) + ANCHOR * seeds.astype(
            jnp.float32
        )

    column_loop(width, body)


def send_kernel(picked_ref, received_ref, sent_base_ref, out_ref):
    rows = picked_ref.shape[1] - received_ref.shape[0]

    def body(cols):
        total = KEEP * dot(picked_ref[:, rows:], received_ref[:, cols]) + sent_base_ref[:, cols]
        out_ref[:, cols] = total.astype(jnp.bfloat16)

    column_loop(received_ref.shape[1], body)


def labels_kernel(tiles_ref, received_ref, base_ref, seeds_ref, next_base_ref):
    rows, width = seeds_ref.shape

    def body(cols):
        total = KEEP * dot(tiles_ref[:, rows:], received_ref[:, cols]) + base_ref[:, cols]
        labels = total.astype(jnp.bfloat16)
        next_base_ref[:, cols] = KEEP * dot(tiles_ref[:, :rows], labels) + ANCHOR * seeds_ref[
            :, cols
        ].astype(jnp.float32)

    column_loop(width, body)


def last_kernel(tiles_ref, received_ref, base_ref, out_ref, labels_ref, sems):
    rows, width = base_ref.shape
    copies = []
    for c in range(width // COLS):
        cols = slice(c * COLS, (c + 1) * COLS)
        total = KEEP * dot(tiles_ref[:, rows:], received_ref[:, cols]) + base_ref[:, cols]
        labels_ref[:, cols] = total.astype(jnp.bfloat16)
        copies.append(
            pltpu.make_async_copy(labels_ref.at[:, cols], out_ref.at[:, cols], sems.at[c])
        )
        copies[-1].start()
    for copy in copies:
        copy.wait()


def exchange(rows_out, peers):
    count, width = rows_out.shape
    sent = rows_out.reshape(peers, count // peers, width)
    got = lax.all_to_all(sent, "rows", split_axis=0, concat_axis=0, tiled=True)
    return got.reshape(count, width)


def on_device(seeds, neighbor_pos, edge_weight, tile_blocks, wanted):
    rows, width = seeds.shape
    peers, slots = wanted.shape[1:]
    count = peers * slots
    columns = rows + count
    neighbours = neighbor_pos.shape[1]
    bf16 = lambda *shape: jax.ShapeDtypeStruct(shape, jnp.bfloat16)
    f32 = lambda *shape: jax.ShapeDtypeStruct(shape, jnp.float32)

    asked = lax.all_to_all(
        wanted.reshape(peers, 1, slots), "rows", split_axis=0, concat_axis=0, tiled=True
    )
    column, share = call(
        edges_kernel,
        "edges",
        [jax.ShapeDtypeStruct((neighbours, rows), jnp.int32), f32(neighbours, rows)],
        [SMEM, VMEM, VMEM],
        [VMEM, VMEM],
        nbytes=16 * neighbours * rows,
    )(tile_blocks, neighbor_pos.T, edge_weight.T)
    outgoing, pick = call(
        pick_kernel,
        "pick",
        [bf16(count, width), bf16(count, rows)],
        [VMEM, VMEM],
        [VMEM, VMEM],
        flops=2 * count * rows * width,
        nbytes=2 * (2 * count * width + count * rows),
    )(asked, seeds)
    received = exchange(outgoing, peers)
    tiles = call(
        tiles_kernel,
        "tiles",
        bf16(rows, columns),
        [VMEM, VMEM, ANY],
        flops=2 * neighbours * rows * columns,
        nbytes=rows * columns * 2,
    )(column, share, pick)
    picked, base, sent_base = call(
        own_kernel,
        "own",
        [bf16(count, columns), f32(rows, width), f32(count, width)],
        [VMEM] * 4,
        [VMEM] * 3,
        flops=2 * rows * (count * columns + count * width + rows * width),
        nbytes=4 * (rows + count) * width,
    )(tiles, pick, seeds, outgoing)
    outgoing = call(
        send_kernel,
        "send",
        bf16(count, width),
        [VMEM] * 3,
        flops=2 * count * count * width,
        nbytes=8 * count * width,
    )(picked, received, sent_base)
    received_next = exchange(outgoing, peers)
    next_base = call(
        labels_kernel,
        "labels",
        f32(rows, width),
        [VMEM] * 4,
        flops=2 * rows * (count + rows) * width,
        nbytes=8 * (rows + count) * width,
    )(tiles, received, base, seeds)
    return call(
        last_kernel,
        "last",
        bf16(rows, width),
        [VMEM] * 3,
        ANY,
        [pltpu.VMEM((rows, width), jnp.bfloat16), pltpu.SemaphoreType.DMA((width // COLS,))],
        flops=2 * rows * count * width,
        nbytes=8 * rows * width,
    )(tiles, received_next, next_base)


def solution(mesh):
    in_specs = (
        P(("parts", "rows"), "cls"),
        P(("parts", "rows"), None),
        P(("parts", "rows"), None),
        P(("parts", "rows"), None),
        P(("parts", "rows"), None, None),
    )
    out_specs = P(("parts", "rows"), "cls")
    return jax.shard_map(
        on_device, mesh=mesh, in_specs=in_specs, out_specs=out_specs, check_vma=False
    )
```

time: 131 us -> 86.2 us (0.66)
  other arithmetic: 30.4 us -> 0 us
  Pallas kernels: 0 us -> 26.2 us
  matrix products: 17.6 us -> 0 us
  blocking collectives: 29.6 us -> 14.2 us
  local copies, waits for them, and re-layouts: 31.5 us -> 17.4 us
  waiting for transfers between devices: 10.8 us -> 21.4 us
  starting transfers between devices: 9.94 us -> 6.18 us
    pallas_call x0 -> x7, Pallas kernels: none -> 26.2 us  [the longest x1 13 us: on_device(): call(tiles_kernel, 'tiles', bf16(rows, columns), [VMEM, VMEM, ANY], flops...]
    gather x10 -> x0, local copies, waits for them, and re-layouts: 25.1 us -> none  [the longest x8 18.2 us: body_one_block(): operand = ext_blocks[block_list].reshape(tile_count * BLK, width)]
    dot_general x8 -> x0, matrix products: 17.6 us -> none  [body_one_block(): return jnp.dot(tile_row, operand, preferred_element_type=jnp.float32)]
    reduce_sum x13 -> x0, other arithmetic: 16.5 us -> none  [the longest x12 15.6 us: build_one_block(): jnp.sum(jnp.where(hits, weights[:, first:last, None], 0.0), axis=1)]
    unnamed x5 -> x35, local copies, waits for them, and re-layouts: 1.37 us -> 17.4 us
    all_to_all x1, blocking collectives: 29.6 us -> 14.2 us  [on_device(): lax.all_to_all(wanted.reshape(peers, 1, slots), 'rows', split_axis=0, con...]
    all_to_all x2, waiting for transfers between devices: 10.8 us -> 21.4 us  [exchange(): got = lax.all_to_all(sent, 'rows', split_axis=0, concat_axis=0, tiled=True)]
    all_to_all x2, starting transfers between devices: 9.94 us -> 6.18 us  [exchange(): got = lax.all_to_all(sent, 'rows', split_axis=0, concat_axis=0, tiled=True)]
  transfers between devices with their start and end apart: 2 -> 2, of which waited for: 2 -> 2; matrix products, arithmetic and copies ran while one was open for 17% -> 0% of each run, Pallas kernels for 0% -> 25%
where the time goes in v2:
time: 86.2 us; the launch traced here: 85.5 us
  Pallas kernels  26.2 us (30%)
  waiting for transfers between devices  21.4 us (25%)
  local copies, waits for them, and re-layouts  17.4 us (20%)
  blocking collectives  14.2 us (16%)
  starting transfers between devices  6.18 us (7%)
    all_to_all x2, waiting for transfers between devices, exchange(): got = lax.all_to_all(sent, 'rows', split_axis=0, concat_axis=0, tiled=True)  21.4 us
    unnamed x35, local copies, waits for them, and re-layouts  17.4 us
    all_to_all x1, blocking collectives, on_device(): lax.all_to_all(wanted.reshape(peers, 1, slots), 'rows', split_axis=0, con...  14.2 us
    pallas_call x1, Pallas kernels, on_device(): call(tiles_kernel, 'tiles', bf16(rows, columns), [VMEM, VMEM, ANY], flops...  13 us
    all_to_all x2, starting transfers between devices, exchange(): got = lax.all_to_all(sent, 'rows', split_axis=0, concat_axis=0, tiled=True)  6.18 us
    pallas_call x1, Pallas kernels, on_device(): call(own_kernel, 'own', [bf16(count, columns), f32(rows, width), f32(coun...  4.26 us
    pallas_call x1, Pallas kernels, on_device(): call(labels_kernel, 'labels', f32(rows, width), [VMEM] * 4, flops=2 * row...  3 us
    pallas_call x1, Pallas kernels, on_device(): call(pick_kernel, 'pick', [bf16(count, width), bf16(count, rows)], [VMEM,...  2.38 us
  transfers between devices with their start and end apart: 2, of which 2 were waited for; matrix products, arithmetic and copies ran while one was open for 0% of the time, Pallas kernels for 25%

profile of v2, /device:TPU:0, one launch (start us, length us, event | category | flops | bytes accessed | tf_op | source)
XLA Modules:
  0.0 85.5 jit_solution(13099803166715290362)
XLA Ops:
  0.0 0.0 copy-start.16
  0.0 0.8 copy.6
  0.8 14.2 %all_to_all.15.asked_ref = s32[32,1,16]{2,1,0:T(1,128)S(1)} all-to-all(s32[32,1,16]{2,1,0:T(1,128)S(1)} %bitcast.13), channel_id=1, replica_groups=mesh['parts'=1,'rows'=32,'cls'=1] {'rows'}, dimensions={0} | all-to-all | bytes 4096 | tf_op jit(solution)/shard_map/all_to_all | solution.py:168
  15.0 0.0 copy-start.7
  15.0 1.2 %copy-done.7 = bf16[512,1024]{1,0:T(8,128)(2,1)S(1)} copy-done((bf16[512,1024]{1,0:T(8,128)(2,1)S(1)}, bf16[512,1024]{1,0:T(8,128)(2,1)}, u32[]{:S(2)}) %copy-start.7) | copy-done | bytes 1048600
  16.3 0.0 copy-start.14
  16.3 0.0 copy-start.15
  16.3 2.4 %pick.1 = (bf16[512,1024]{1,0:T(8,128)(2,1)}, bf16[512,512]{1,0:T(8,128)(2,1)S(1)}) custom-call(s32[32,1,16]{2,1,0:T(1,128)S(1)} %all_to_all.15.asked_ref, bf16[512,1024]{1,0:T(8,128)(2,1)S(1)} %copy-done.7), custom_call_target="tpu_custom_call" | custom-call | flops 536870912 | bytes 2621440 | tf_op jit(solution)/shard_map/pick/pallas_call | solution.py:179
  18.6 0.0 copy-start.12
  18.6 2.6 %all-to-all-start.1 = ((bf16[32,16,1024]{2,1,0:T(8,128)(2,1)}), bf16[32,16,1024]{2,1,0:T(8,128)(2,1)S(1)}, u32[]{:S(2)}, u32[]{:S(2)}) async-start(bf16[32,16,1024]{2,1,0:T(8,128)(2,1)} %bitcast.3), calls=%async_computation.1 | async-start | bytes 2097152 | tf_op jit(solution)/shard_map/all_to_all | solution.py:155
  21.3 0.0 copy-done.16
  21.3 0.0 copy-done.14
  21.3 0.0 copy-done.15
  21.3 0.7 edges.1
  22.1 0.0 copy-done.12
  22.1 13.0 %tiles.1.tiles_ref = bf16[512,1024]{1,0:T(8,128)(2,1)S(1)} custom-call(s32[50,512]{1,0:T(8,128)S(1)} %get-tuple-element.12.column_ref, f32[50,512]{1,0:T(8,128)S(1)} %get-tuple-element.13.share_ref, bf16[512,512]{1,0:T(8,128)(2,1)S(1)} %get-tuple-element.14.pick_ref), custom_call_target="tpu_custom_call" | custom-call | flops 52428800 | bytes 1048576 | tf_op jit(solution)/shard_map/tiles/pallas_call | solution.py:189
  35.1 0.0 copy-start.8
  35.1 1.2 %copy-done.8 = bf16[512,1024]{1,0:T(8,128)(2,1)S(1)} copy-done((bf16[512,1024]{1,0:T(8,128)(2,1)S(1)}, bf16[512,1024]{1,0:T(8,128)(2,1)}, u32[]{:S(2)}) %copy-start.8) | copy-done | bytes 1048600
  36.3 0.0 copy-start.13
  36.3 1.0 %copy-done.13 = bf16[512,512]{1,0:T(8,128)(2,1)S(1)} copy-done((bf16[512,512]{1,0:T(8,128)(2,1)S(1)}, bf16[512,512]{1,0:T(8,128)(2,1)}, u32[]{:S(2)}) %copy-start.13) | copy-done | bytes 524312
  37.3 4.3 %own.1 = (bf16[512,1024]{1,0:T(8,128)(2,1)S(1)}, f32[512,1024]{1,0:T(8,128)S(1)}, f32[512,1024]{1,0:T(8,128)S(1)}) custom-call(bf16[512,1024]{1,0:T(8,128)(2,1)S(1)} %tiles.1.tiles_ref, bf16[512,512]{1,0:T(8,128)(2,1)S(1)} %copy-done.13, bf16[512,1024]{1,0:T(8,128)(2,1)S(1)} %copy-done.8, bf16[512,1024]{1,0:T(8,128)(2,1)} %get-tuple-element.15.sent_ref), custom_call_target="tpu_custom_call" | custom-call | flops 1610612736 | bytes 4194304 | tf_op jit(solution)/shard_map/own/pallas_call | solution.py:197
  41.6 0.0 copy-start.3
  41.6 1.3 %copy-done.3 = f32[512,1024]{1,0:T(8,128)} copy-done((f32[512,1024]{1,0:T(8,128)}, f32[512,1024]{1,0:T(8,128)S(1)}, u32[]{:S(2)}) %copy-start.3) | copy-done | bytes 2097176
  42.9 0.0 copy-start.5
  42.9 1.3 %copy-done.5 = f32[512,1024]{1,0:T(8,128)} copy-done((f32[512,1024]{1,0:T(8,128)}, f32[512,1024]{1,0:T(8,128)S(1)}, u32[]{:S(2)}) %copy-start.5) | copy-done | bytes 2097176
  44.2 0.0 copy-start.10
  44.2 1.0 %copy-done.10 = bf16[512,1024]{1,0:T(8,128)(2,1)} copy-done((bf16[512,1024]{1,0:T(8,128)(2,1)}, bf16[512,1024]{1,0:T(8,128)(2,1)S(1)}, u32[]{:S(2)}) %copy-start.10) | copy-done | bytes 1048600
  45.2 2.3 %all-to-all-done.1 = bf16[32,16,1024]{2,1,0:T(8,128)(2,1)S(1)} async-done(((bf16[32,16,1024]{2,1,0:T(8,128)(2,1)}), bf16[32,16,1024]{2,1,0:T(8,128)(2,1)S(1)}, u32[]{:S(2)}, u32[]{:S(2)}) %all-to-all-start.1) | async-done | bytes 1048608 | tf_op jit(solution)/shard_map/all_to_all | solution.py:155
  47.5 0.0 copy-start.6
  47.5 1.6 %copy-done.6 = f32[512,1024]{1,0:T(8,128)S(1)} copy-done((f32[512,1024]{1,0:T(8,128)S(1)}, f32[512,1024]{1,0:T(8,128)}, u32[]{:S(2)}) %copy-start.6) | copy-done | bytes 2097176
  49.1 0.0 copy-start.11
  49.1 1.2 %copy-done.11 = bf16[512,1024]{1,0:T(8,128)(2,1)S(1)} copy-done((bf16[512,1024]{1,0:T(8,128)(2,1)S(1)}, bf16[512,1024]{1,0:T(8,128)(2,1)}, u32[]{:S(2)}) %copy-start.11) | copy-done | bytes 1048600
  50.3 1.2 %send.1 = bf16[512,1024]{1,0:T(8,128)(2,1)S(1)} custom-call(bf16[512,1024]{1,0:T(8,128)(2,1)S(1)} %copy-done.11, bf16[512,1024]{1,0:T(8,128)(2,1)S(1)} %bitcast.7, f32[512,1024]{1,0:T(8,128)S(1)} %copy-done.6), custom_call_target="tpu_custom_call" | custom-call | flops 536870912 | bytes 4194304 | tf_op jit(solution)/shard_map/send/pallas_call | solution.py:206
  51.6 0.0 copy-start.2
  51.6 1.0 %copy-done.2 = bf16[512,1024]{1,0:T(8,128)(2,1)} copy-done((bf16[512,1024]{1,0:T(8,128)(2,1)}, bf16[512,1024]{1,0:T(8,128)(2,1)S(1)}, u32[]{:S(2)}) %copy-start.2) | copy-done | bytes 1048600
  52.6 3.5 %all-to-all-start.2 = ((bf16[32,16,1024]{2,1,0:T(8,128)(2,1)}), bf16[32,16,1024]{2,1,0:T(8,128)(2,1)S(1)}, u32[]{:S(2)}, u32[]{:S(2)}) async-start(bf16[32,16,1024]{2,1,0:T(8,128)(2,1)} %bitcast.10), calls=%async_computation.2 | async-start | bytes 2097152 | tf_op jit(solution)/shard_map/all_to_all | solution.py:155
  56.1 0.0 copy-start.4
  56.1 1.6 %copy-done.4 = f32[512,1024]{1,0:T(8,128)S(1)} copy-done((f32[512,1024]{1,0:T(8,128)S(1)}, f32[512,1024]{1,0:T(8,128)}, u32[]{:S(2)}) %copy-start.4) | copy-done | bytes 2097176
  57.7 0.0 copy-start.9
  57.7 1.2 %copy-done.9 = bf16[512,1024]{1,0:T(8,128)(2,1)S(1)} copy-done((bf16[512,1024]{1,0:T(8,128)(2,1)S(1)}, bf16[512,1024]{1,0:T(8,128)(2,1)}, u32[]{:S(2)}) %copy-start.9) | copy-done | bytes 1048600
  58.9 3.0 %labels.1.base_ref = f32[512,1024]{1,0:T(8,128)S(1)} custom-call(bf16[512,1024]{1,0:T(8,128)(2,1)S(1)} %tiles.1.tiles_ref, bf16[512,1024]{1,0:T(8,128)(2,1)S(1)} %bitcast.8, f32[512,1024]{1,0:T(8,128)S(1)} %copy-done.4, bf16[512,1024]{1,0:T(8,128)(2,1)S(1)} %copy-done.9), custom_call_target="tpu_custom_call" | custom-call | flops 1073741824 | bytes 8388608 | tf_op jit(solution)/shard_map/labels/pallas_call | solution.py:215
  61.9 0.0 copy-start
  61.9 1.3 %copy-done = f32[512,1024]{1,0:T(8,128)} copy-done((f32[512,1024]{1,0:T(8,128)}, f32[512,1024]{1,0:T(8,128)S(1)}, u32[]{:S(2)}) %copy-start) | copy-done | bytes 2097176
  63.3 19.1 %all-to-all-done.2 = bf16[32,16,1024]{2,1,0:T(8,128)(2,1)S(1)} async-done(((bf16[32,16,1024]{2,1,0:T(8,128)(2,1)}), bf16[32,16,1024]{2,1,0:T(8,128)(2,1)S(1)}, u32[]{:S(2)}, u32[]{:S(2)}) %all-to-all-start.2) | async-done | bytes 1048608 | tf_op jit(solution)/shard_map/all_to_all | solution.py:155
  82.3 0.0 copy-start.1
  82.3 1.6 %copy-done.1 = f32[512,1024]{1,0:T(8,128)S(1)} copy-done((f32[512,1024]{1,0:T(8,128)S(1)}, f32[512,1024]{1,0:T(8,128)}, u32[]{:S(2)}) %copy-start.1) | copy-done | bytes 2097176
  83.9 1.6 %last.1 = bf16[512,1024]{1,0:T(8,128)(2,1)} custom-call(bf16[512,1024]{1,0:T(8,128)(2,1)S(1)} %tiles.1.tiles_ref, bf16[512,1024]{1,0:T(8,128)(2,1)S(1)} %bitcast.9, f32[512,1024]{1,0:T(8,128)S(1)} %copy-done.1), custom_call_target="tpu_custom_call" | custom-call | flops 536870912 | bytes 4194304 | tf_op jit(solution)/shard_map/last/pallas_call | solution.py:223
Async XLA Ops:
  0.0 21.3 %copy-start.16 = (s32[4,8]{1,0:T(4,128)S(1)}, s32[4,8]{1,0:T(4,128)}, u32[]{:S(2)}) copy-start(s32[4,8]{1,0:T(4,128)} %blocks_ref.1) | copy-start | bytes 388
  15.0 1.2 %copy-start.7 = (bf16[512,1024]{1,0:T(8,128)(2,1)S(1)}, bf16[512,1024]{1,0:T(8,128)(2,1)}, u32[]{:S(2)}) copy-start(bf16[512,1024]{1,0:T(8,128)(2,1)} %seeds_ref.5) | copy-start | bytes 3145732
  16.3 5.1 %copy-start.14 = (s32[512,50]{0,1:T(8,128)S(1)}, s32[512,50]{0,1:T(8,128)}, u32[]{:S(2)}) copy-start(s32[512,50]{0,1:T(8,128)} %param.6) | copy-start | bytes 307204
  16.3 5.1 %copy-start.15 = (s32[512,50]{0,1:T(8,128)S(1)}, s32[512,50]{0,1:T(8,128)}, u32[]{:S(2)}) copy-start(s32[512,50]{0,1:T(8,128)} %param.7) | copy-start | bytes 307204
  18.6 3.4 %copy-start.12 = (bf16[512,512]{1,0:T(8,128)(2,1)}, bf16[512,512]{1,0:T(8,128)(2,1)S(1)}, u32[]{:S(2)}) copy-start(bf16[512,512]{1,0:T(8,128)(2,1)S(1)} %get-tuple-element.14.pick_ref) | copy-start | bytes 1572868
  18.6 28.9 %all-to-all-start.1 = ((bf16[32,16,1024]{2,1,0:T(8,128)(2,1)}), bf16[32,16,1024]{2,1,0:T(8,128)(2,1)S(1)}, u32[]{:S(2)}, u32[]{:S(2)}) async-start(bf16[32,16,1024]{2,1,0:T(8,128)(2,1)} %bitcast.3), calls=%async_computation.1 | async-start | bytes 2097152 | tf_op jit(solution)/shard_map/all_to_all | solution.py:155
  35.1 1.2 %copy-start.8 = (bf16[512,1024]{1,0:T(8,128)(2,1)S(1)}, bf16[512,1024]{1,0:T(8,128)(2,1)}, u32[]{:S(2)}) copy-start(bf16[512,1024]{1,0:T(8,128)(2,1)} %seeds_ref.5) | copy-start | bytes 3145732
  36.3 1.0 %copy-start.13 = (bf16[512,512]{1,0:T(8,128)(2,1)S(1)}, bf16[512,512]{1,0:T(8,128)(2,1)}, u32[]{:S(2)}) copy-start(bf16[512,512]{1,0:T(8,128)(2,1)} %copy-done.12) | copy-start | bytes 1572868
  41.6 1.3 %copy-start.3 = (f32[512,1024]{1,0:T(8,128)}, f32[512,1024]{1,0:T(8,128)S(1)}, u32[]{:S(2)}) copy-start(f32[512,1024]{1,0:T(8,128)S(1)} %get-tuple-element.18.base_ref) | copy-start | bytes 6291460
  42.9 1.3 %copy-start.5 = (f32[512,1024]{1,0:T(8,128)}, f32[512,1024]{1,0:T(8,128)S(1)}, u32[]{:S(2)}) copy-start(f32[512,1024]{1,0:T(8,128)S(1)} %get-tuple-element.17.sent_base_ref) | copy-start | bytes 6291460
  44.2 1.0 %copy-start.10 = (bf16[512,1024]{1,0:T(8,128)(2,1)}, bf16[512,1024]{1,0:T(8,128)(2,1)S(1)}, u32[]{:S(2)}) copy-start(bf16[512,1024]{1,0:T(8,128)(2,1)S(1)} %get-tuple-element.16.picked_ref) | copy-start | bytes 3145732
  47.5 1.6 %copy-start.6 = (f32[512,1024]{1,0:T(8,128)S(1)}, f32[512,1024]{1,0:T(8,128)}, u32[]{:S(2)}) copy-start(f32[512,1024]{1,0:T(8,128)} %copy-done.5) | copy-start | bytes 6291460
  49.1 1.2 %copy-start.11 = (bf16[512,1024]{1,0:T(8,128)(2,1)S(1)}, bf16[512,1024]{1,0:T(8,128)(2,1)}, u32[]{:S(2)}) copy-start(bf16[512,1024]{1,0:T(8,128)(2,1)} %copy-done.10) | copy-start | bytes 3145732
  51.6 1.0 %copy-start.2 = (bf16[512,1024]{1,0:T(8,128)(2,1)}, bf16[512,1024]{1,0:T(8,128)(2,1)S(1)}, u32[]{:S(2)}) copy-start(bf16[512,1024]{1,0:T(8,128)(2,1)S(1)} %send.1) | copy-start | bytes 3145732
  52.6 29.8 %all-to-all-start.2 = ((bf16[32,16,1024]{2,1,0:T(8,128)(2,1)}), bf16[32,16,1024]{2,1,0:T(8,128)(2,1)S(1)}, u32[]{:S(2)}, u32[]{:S(2)}) async-start(bf16[32,16,1024]{2,1,0:T(8,128)(2,1)} %bitcast.10), calls=%async_computation.2 | async-start | bytes 2097152 | tf_op jit(solution)/shard_map/all_to_all | solution.py:155
  56.1 1.6 %copy-start.4 = (f32[512,1024]{1,0:T(8,128)S(1)}, f32[512,1024]{1,0:T(8,128)}, u32[]{:S(2)}) copy-start(f32[512,1024]{1,0:T(8,128)} %copy-done.3) | copy-start | bytes 6291460
  57.7 1.2 %copy-start.9 = (bf16[512,1024]{1,0:T(8,128)(2,1)S(1)}, bf16[512,1024]{1,0:T(8,128)(2,1)}, u32[]{:S(2)}) copy-start(bf16[512,1024]{1,0:T(8,128)(2,1)} %seeds_ref.5) | copy-start | bytes 3145732
  61.9 1.3 %copy-start = (f32[512,1024]{1,0:T(8,128)}, f32[512,1024]{1,0:T(8,128)S(1)}, u32[]{:S(2)}) copy-start(f32[512,1024]{1,0:T(8,128)S(1)} %labels.1.base_ref) | copy-start | bytes 6291460
  82.3 1.6 %copy-start.1 = (f32[512,1024]{1,0:T(8,128)S(1)}, f32[512,1024]{1,0:T(8,128)}, u32[]{:S(2)}) copy-start(f32[512,1024]{1,0:T(8,128)} %copy-done) | copy-start | bytes 6291460

commit v3 on v2

v3 whole, which is shorter than its diff:
```python
import jax
import jax.numpy as jnp
from jax import lax
from jax.experimental import pallas as pl
from jax.experimental.pallas import tpu as pltpu
from jax.sharding import PartitionSpec as P

BLK = 128
COLS = 256
VMEM_LIMIT = 32 * 1024 * 1024
KEEP = 0.85
ANCHOR = 0.15

SMEM = pl.BlockSpec(memory_space=pltpu.SMEM)
VMEM = pl.BlockSpec(memory_space=pltpu.VMEM)
HBM = pl.BlockSpec(memory_space=pltpu.HBM)


def call(kernel, name, out_shape, in_specs, out_specs=VMEM, scratch_shapes=(), flops=0, nbytes=0):
    return pl.pallas_call(
        kernel,
        out_shape=out_shape,
        in_specs=in_specs,
        out_specs=out_specs,
        scratch_shapes=scratch_shapes,
        compiler_params=pltpu.CompilerParams(vmem_limit_bytes=VMEM_LIMIT),
        cost_estimate=pl.CostEstimate(flops=flops, bytes_accessed=nbytes, transcendentals=0),
        name=name,
    )


def dot(a, b):
    return jnp.dot(a, b, preferred_element_type=jnp.float32)


def column_loop(width, body):
    @pl.loop(0, width // COLS)
    def _(c):
        body(pl.ds(pl.multiple_of(c * COLS, COLS), COLS))


def pull(source, target, sems, columns):
    copies = []
    for c in range(columns // COLS):
        cols = slice(c * COLS, (c + 1) * COLS)
        copies.append(pltpu.make_async_copy(source.at[:, cols], target.at[:, cols], sems.at[c]))
        copies[-1].start()
    return copies


def push(source, target, sems, c):
    cols = slice(c * COLS, (c + 1) * COLS)
    copy = pltpu.make_async_copy(source.at[:, cols], target.at[:, cols], sems.at[c])
    copy.start()
    return copy


def picks(asked, rows):
    peers, _, slots = asked.shape
    count = peers * slots
    spread = jnp.broadcast_to(asked.astype(jnp.float32), (peers, slots, slots))
    spread = spread.reshape(count, slots)
    slot = lax.broadcasted_iota(jnp.int32, (count, slots), 0) % slots
    lane = lax.broadcasted_iota(jnp.int32, (count, slots), 1)
    row = jnp.sum(jnp.where(slot == lane, spread, 0.0), axis=1, keepdims=True)
    hits = lax.broadcasted_iota(jnp.int32, (count, rows), 1) == row.astype(jnp.int32)
    return hits.astype(jnp.float32).astype(jnp.bfloat16)


def pick_kernel(asked_ref, seeds_hbm, out_hbm, seeds_ref, pick_ref, out_ref, in_sems, out_sems):
    rows, width = seeds_ref.shape
    copies = pull(seeds_hbm, seeds_ref, in_sems, width)
    pick_ref[...] = picks(asked_ref[...], rows)
    pushed = []
    for c, copy in enumerate(copies):
        cols = slice(c * COLS, (c + 1) * COLS)
        copy.wait()
        out_ref[:, cols] = dot(pick_ref[...], seeds_ref[:, cols]).astype(jnp.bfloat16)
        pushed.append(push(out_ref, out_hbm, out_sems, c))
    for copy in pushed:
        copy.wait()


def fill_edges(blocks_ref, pos_ref, weight_ref, column_ref, share_ref):
    block_count, tile_count = blocks_ref.shape
    weights = weight_ref[...].astype(jnp.float32)
    share = weights / jnp.sum(weights, axis=0, keepdims=True)
    share_ref[...] = share.astype(jnp.bfloat16).astype(jnp.float32)
    for block in range(block_count):
        lanes = slice(block * BLK, (block + 1) * BLK)
        pos = pos_ref[:, lanes]
        tile = pos // BLK
        base = jnp.full(pos.shape, blocks_ref[block, 0], jnp.int32)
        for j in range(1, tile_count):
            base = jnp.where(tile == j, blocks_ref[block, j], base)
        column_ref[:, lanes] = base * BLK + pos % BLK


def fill_tiles(column_ref, share_ref, tiles_ref):
    neighbours = column_ref.shape[0]
    sub = lax.broadcasted_iota(jnp.int32, (BLK, BLK), 0)

    @pl.loop(0, tiles_ref.shape[0] // BLK)
    def _(block):
        lanes = pl.ds(pl.multiple_of(block * BLK, BLK), BLK)

        @pl.loop(0, tiles_ref.shape[1] // BLK)
        def _(chunk):
            first = pl.multiple_of(chunk * BLK, BLK)
            total = jnp.zeros((BLK, BLK), jnp.float32)
            for k in range(neighbours):
                spot = column_ref[k : k + 1, lanes] - first
                total = jnp.where(sub == spot, share_ref[k : k + 1, lanes], total)
            tiles_ref[lanes, pl.ds(first, BLK)] = total.T.astype(jnp.bfloat16)


def tiles_kernel(
    blocks_ref,
    pos_ref,
    weight_ref,
    asked_ref,
    seeds_ref,
    sent_ref,
    own_ref,
    far_ref,
    picked_far_ref,
    base_ref,
    sent_base_ref,
    column_ref,
    share_ref,
    tiles_ref,
    pick_ref,
    picked_ref,
):
    rows, width = seeds_ref.shape
    fill_edges(blocks_ref, pos_ref, weight_ref, column_ref, share_ref)
    fill_tiles(column_ref, share_ref, tiles_ref)
    own_ref[...] = tiles_ref[:, :rows]
    far_ref[...] = tiles_ref[:, rows:]
    pick_ref[...] = picks(asked_ref[...], rows)

    def pick_tiles(cols):
        picked_ref[:, cols] = dot(pick_ref[...], tiles_ref[:, cols]).astype(jnp.bfloat16)

    column_loop(tiles_ref.shape[1], pick_tiles)
    picked_far_ref[...] = picked_ref[:, rows:]

    def body(cols):
        seeds = seeds_ref[:, cols]
        sent_base_ref[:, cols] = KEEP * dot(picked_ref[:, :rows], seeds) + ANCHOR * sent_ref[
            :, cols
        ].astype(jnp.float32)
        base_ref[:, cols] = KEEP * dot(tiles_ref[:, :rows], seeds) + ANCHOR * seeds.astype(
            jnp.float32
        )

    column_loop(width, body)


def step_kernel(tiles_ref, received_ref, base_hbm, out_hbm, base_ref, out_ref, in_sems, out_sems):
    copies = pull(base_hbm, base_ref, in_sems, base_ref.shape[1])
    pushed = []
    for c, copy in enumerate(copies):
        cols = slice(c * COLS, (c + 1) * COLS)
        total = KEEP * dot(tiles_ref[...], received_ref[:, cols])
        copy.wait()
        out_ref[:, cols] = (total + base_ref[:, cols]).astype(jnp.bfloat16)
        pushed.append(push(out_ref, out_hbm, out_sems, c))
    for copy in pushed:
        copy.wait()


def labels_kernel(own_ref, far_ref, received_ref, base_ref, seeds_ref, next_base_ref):
    def body(cols):
        total = KEEP * dot(far_ref[...], received_ref[:, cols]) + base_ref[:, cols]
        labels = total.astype(jnp.bfloat16)
        next_base_ref[:, cols] = KEEP * dot(own_ref[...], labels) + ANCHOR * seeds_ref[
            :, cols
        ].astype(jnp.float32)

    column_loop(seeds_ref.shape[1], body)


def step(tiles, received, base, name):
    rows, width = base.shape
    pieces = pltpu.SemaphoreType.DMA((width // COLS,))
    return call(
        step_kernel,
        name,
        jax.ShapeDtypeStruct((rows, width), jnp.bfloat16),
        [VMEM, VMEM, HBM],
        HBM,
        [
            pltpu.VMEM((rows, width), jnp.float32),
            pltpu.VMEM((rows, width), jnp.bfloat16),
            pieces,
            pieces,
        ],
        flops=2 * rows * received.shape[0] * width,
        nbytes=8 * rows * width,
    )(tiles, received, base)


def exchange(rows_out, peers):
    count, width = rows_out.shape
    sent = rows_out.reshape(peers, count // peers, width)
    got = lax.all_to_all(sent, "rows", split_axis=0, concat_axis=0, tiled=True)
    return got.reshape(count, width)


def on_device(seeds, neighbor_pos, edge_weight, tile_blocks, wanted):
    rows, width = seeds.shape
    peers, slots = wanted.shape[1:]
    count = peers * slots
    columns = rows + count
    neighbours = neighbor_pos.shape[1]
    bf16 = lambda *shape: jax.ShapeDtypeStruct(shape, jnp.bfloat16)
    f32 = lambda *shape: jax.ShapeDtypeStruct(shape, jnp.float32)

    pieces = pltpu.SemaphoreType.DMA((width // COLS,))

    asked = lax.all_to_all(
        wanted.reshape(peers, 1, slots), "rows", split_axis=0, concat_axis=0, tiled=True
    )
    outgoing = call(
        pick_kernel,
        "pick",
        bf16(count, width),
        [VMEM, HBM],
        HBM,
        [
            pltpu.VMEM((rows, width), jnp.bfloat16),
            pltpu.VMEM((count, rows), jnp.bfloat16),
            pltpu.VMEM((count, width), jnp.bfloat16),
            pieces,
            pieces,
        ],
        flops=2 * count * rows * width,
        nbytes=2 * (rows + count) * width,
    )(asked, seeds)
    received = exchange(outgoing, peers)
    own, far, picked_far, base, sent_base = call(
        tiles_kernel,
        "tiles",
        [
            bf16(rows, rows),
            bf16(rows, count),
            bf16(count, count),
            f32(rows, width),
            f32(count, width),
        ],
        [SMEM, VMEM, VMEM, VMEM, VMEM, VMEM],
        [VMEM] * 5,
        [
            pltpu.VMEM((neighbours, rows), jnp.int32),
            pltpu.VMEM((neighbours, rows), jnp.float32),
            pltpu.VMEM((rows, columns), jnp.bfloat16),
            pltpu.VMEM((count, rows), jnp.bfloat16),
            pltpu.VMEM((count, columns), jnp.bfloat16),
        ],
        flops=2 * neighbours * rows * columns,
        nbytes=4 * (rows + count) * width,
    )(tile_blocks, neighbor_pos.T, edge_weight.T, asked, seeds, outgoing)
    outgoing = step(picked_far, received, sent_base, "send")
    received_next = exchange(outgoing, peers)
    next_base = call(
        labels_kernel,
        "labels",
        f32(rows, width),
        [VMEM] * 5,
        flops=2 * rows * (count + rows) * width,
        nbytes=8 * (rows + count) * width,
    )(own, far, received, base, seeds)
    return step(far, received_next, next_base, "last")


def solution(mesh):
    in_specs = (
        P(("parts", "rows"), "cls"),
        P(("parts", "rows"), None),
        P(("parts", "rows"), None),
        P(("parts", "rows"), None),
        P(("parts", "rows"), None, None),
    )
    out_specs = P(("parts", "rows"), "cls")
    return jax.shard_map(
        on_device, mesh=mesh, in_specs=in_specs, out_specs=out_specs, check_vma=False
    )
```

time: 86.2 us -> 89.3 us (1.036)
  Pallas kernels: 26.2 us -> 29.3 us
  local copies, waits for them, and re-layouts: 17.4 us -> 16.4 us
  waiting for transfers between devices: 21.4 us -> 22.4 us
    pallas_call x7 -> x5, Pallas kernels: 26.2 us -> 29.3 us  [the longest x1 17.8 us: on_device(): call(tiles_kernel, 'tiles', [bf16(rows, rows), bf16(rows, count), bf16(co...]
    all_to_all x2, waiting for transfers between devices: 21.4 us -> 22.4 us  [exchange(): got = lax.all_to_all(sent, 'rows', split_axis=0, concat_axis=0, tiled=True)]
    unnamed x35, local copies, waits for them, and re-layouts: 17.4 us -> 16.4 us
  transfers between devices with their start and end apart: 2 -> 2, of which waited for: 2 -> 2; matrix products, arithmetic and copies ran while one was open for 0% -> 0% of each run, Pallas kernels for 25% -> 23%
where the time goes in v3:
time: 89.3 us; the launch traced here: 88.7 us
  Pallas kernels  29.3 us (33%)
  waiting for transfers between devices  22.4 us (25%)
  local copies, waits for them, and re-layouts  16.4 us (18%)
  blocking collectives  14.2 us (16%)
  starting transfers between devices  6.21 us (7%)
    all_to_all x2, waiting for transfers between devices, exchange(): got = lax.all_to_all(sent, 'rows', split_axis=0, concat_axis=0, tiled=True)  22.4 us
    pallas_call x1, Pallas kernels, on_device(): call(tiles_kernel, 'tiles', [bf16(rows, rows), bf16(rows, count), bf16(co...  17.8 us
    unnamed x35, local copies, waits for them, and re-layouts  16.4 us
    all_to_all x1, blocking collectives, on_device(): lax.all_to_all(wanted.reshape(peers, 1, slots), 'rows', split_axis=0, con...  14.2 us
    all_to_all x2, starting transfers between devices, exchange(): got = lax.all_to_all(sent, 'rows', split_axis=0, concat_axis=0, tiled=True)  6.21 us
    pallas_call x2, Pallas kernels, step(): call(step_kernel, name, jax.ShapeDtypeStruct((rows, width), jnp.bfloat16)...  5.72 us
    pallas_call x1, Pallas kernels, on_device(): call(labels_kernel, 'labels', f32(rows, width), [VMEM] * 5, flops=2 * row...  2.98 us
    pallas_call x1, Pallas kernels, on_device(): call(pick_kernel, 'pick', bf16(count, width), [VMEM, HBM], HBM, [pltpu.VM...  2.8 us
  transfers between devices with their start and end apart: 2, of which 2 were waited for; matrix products, arithmetic and copies ran while one was open for 0% of the time, Pallas kernels for 23%

profile of v3, /device:TPU:0, one launch (start us, length us, event | category | flops | bytes accessed | tf_op | source)
XLA Modules:
  0.0 88.7 jit_solution(1049114643477634406)
XLA Ops:
  0.0 0.8 copy.6
  0.8 14.2 %all_to_all.15.asked_ref = s32[32,1,16]{2,1,0:T(1,128)S(1)} all-to-all(s32[32,1,16]{2,1,0:T(1,128)S(1)} %bitcast.13), channel_id=1, replica_groups=mesh['parts'=1,'rows'=32,'cls'=1] {'rows'}, dimensions={0} | all-to-all | bytes 4096 | tf_op jit(solution)/shard_map/all_to_all | solution.py:222
  15.0 0.0 copy-start
  15.0 1.2 %copy-done = bf16[512,1024]{1,0:T(8,128)(2,1)S(1)} copy-done((bf16[512,1024]{1,0:T(8,128)(2,1)S(1)}, bf16[512,1024]{1,0:T(8,128)(2,1)}, u32[]{:S(2)}) %copy-start) | copy-done | bytes 1048600
  16.2 0.0 copy-start.1
  16.2 0.0 copy-start.14
  16.2 0.0 copy-start.15
  16.2 0.0 copy-start.16
  16.3 2.8 %pick.1.sent_ref = bf16[512,1024]{1,0:T(8,128)(2,1)} custom-call(s32[32,1,16]{2,1,0:T(1,128)S(1)} %all_to_all.15.asked_ref, bf16[512,1024]{1,0:T(8,128)(2,1)S(1)} %copy-done), custom_call_target="tpu_custom_call" | custom-call | flops 536870912 | bytes 2097152 | tf_op jit(solution)/shard_map/pick/pallas_call | solution.py:225
  19.1 2.7 %all-to-all-start.1 = ((bf16[32,16,1024]{2,1,0:T(8,128)(2,1)}), bf16[32,16,1024]{2,1,0:T(8,128)(2,1)S(1)}, u32[]{:S(2)}, u32[]{:S(2)}) async-start(bf16[32,16,1024]{2,1,0:T(8,128)(2,1)} %bitcast.3), calls=%async_computation.1 | async-start | bytes 2097152 | tf_op jit(solution)/shard_map/all_to_all | solution.py:207
  21.7 0.0 copy-done.1
  21.7 0.0 copy-done.14
  21.7 0.0 copy-done.15
  21.8 0.0 copy-done.16
  21.8 17.8 %tiles.1 = (bf16[512,512]{1,0:T(8,128)(2,1)S(1)}, bf16[512,512]{1,0:T(8,128)(2,1)S(1)}, bf16[512,512]{1,0:T(8,128)(2,1)S(1)}, f32[512,1024]{1,0:T(8,128)S(1)}, f32[512,1024]{1,0:T(8,128)S(1)}) custom-call(s32[4,8]{1,0:T(4,128)S(1)} %copy-done.16, s32[50,512]{1,0:T(8,128)S(1)} %bitcast.11, s32[50,512]{1,0:T(8,128)S(1)} %bitcast.12, ...), custom_call_target="tpu_custom_call" | custom-call | flops 52428800 | bytes 4194304 | tf_op jit(solution)/shard_map/tiles/pallas_call | solution.py:242
  39.5 0.0 copy-start.5
  39.5 0.8 copy-done.5
  40.3 0.0 copy-start.8
  40.3 1.3 %copy-done.8 = f32[512,1024]{1,0:T(8,128)} copy-done((f32[512,1024]{1,0:T(8,128)}, f32[512,1024]{1,0:T(8,128)S(1)}, u32[]{:S(2)}) %copy-start.8) | copy-done | bytes 2097176
  41.7 0.0 copy-start.10
  41.7 1.3 %copy-done.10 = f32[512,1024]{1,0:T(8,128)} copy-done((f32[512,1024]{1,0:T(8,128)}, f32[512,1024]{1,0:T(8,128)S(1)}, u32[]{:S(2)}) %copy-start.10) | copy-done | bytes 2097176
  43.0 0.0 copy-start.12
  43.0 0.8 copy-done.12
  43.8 4.2 %all-to-all-done.1 = bf16[32,16,1024]{2,1,0:T(8,128)(2,1)S(1)} async-done(((bf16[32,16,1024]{2,1,0:T(8,128)(2,1)}), bf16[32,16,1024]{2,1,0:T(8,128)(2,1)S(1)}, u32[]{:S(2)}, u32[]{:S(2)}) %all-to-all-start.1) | async-done | bytes 1048608 | tf_op jit(solution)/shard_map/all_to_all | solution.py:207
  47.9 0.0 copy-start.11
  47.9 1.6 %copy-done.11 = f32[512,1024]{1,0:T(8,128)S(1)} copy-done((f32[512,1024]{1,0:T(8,128)S(1)}, f32[512,1024]{1,0:T(8,128)}, u32[]{:S(2)}) %copy-start.11) | copy-done | bytes 2097176
  49.5 2.6 %send.1 = bf16[512,1024]{1,0:T(8,128)(2,1)S(1)} custom-call(bf16[512,512]{1,0:T(8,128)(2,1)S(1)} %get-tuple-element.11.tiles_ref, bf16[512,1024]{1,0:T(8,128)(2,1)S(1)} %bitcast.7, f32[512,1024]{1,0:T(8,128)S(1)} %copy-done.11), custom_call_target="tpu_custom_call" | custom-call | flops 536870912 | bytes 4194304 | tf_op jit(solution)/shard_map/send/pallas_call | solution.py:187
  52.2 0.0 copy-start.4
  52.2 1.0 %copy-done.4 = bf16[512,1024]{1,0:T(8,128)(2,1)} copy-done((bf16[512,1024]{1,0:T(8,128)(2,1)}, bf16[512,1024]{1,0:T(8,128)(2,1)S(1)}, u32[]{:S(2)}) %copy-start.4) | copy-done | bytes 1048600
  53.1 3.5 %all-to-all-start.2 = ((bf16[32,16,1024]{2,1,0:T(8,128)(2,1)}), bf16[32,16,1024]{2,1,0:T(8,128)(2,1)S(1)}, u32[]{:S(2)}, u32[]{:S(2)}) async-start(bf16[32,16,1024]{2,1,0:T(8,128)(2,1)} %bitcast.10), calls=%async_computation.2 | async-start | bytes 2097152 | tf_op jit(solution)/shard_map/all_to_all | solution.py:207
  56.7 0.0 copy-start.6
  56.7 1.0 %copy-done.6 = bf16[512,512]{1,0:T(8,128)(2,1)S(1)} copy-done((bf16[512,512]{1,0:T(8,128)(2,1)S(1)}, bf16[512,512]{1,0:T(8,128)(2,1)}, u32[]{:S(2)}) %copy-start.6) | copy-done | bytes 524312
  57.7 0.0 copy-start.9
  57.7 1.6 %copy-done.9 = f32[512,1024]{1,0:T(8,128)S(1)} copy-done((f32[512,1024]{1,0:T(8,128)S(1)}, f32[512,1024]{1,0:T(8,128)}, u32[]{:S(2)}) %copy-start.9) | copy-done | bytes 2097176
  59.3 0.0 copy-start.13
  59.3 1.0 %copy-done.13 = bf16[512,512]{1,0:T(8,128)(2,1)S(1)} copy-done((bf16[512,512]{1,0:T(8,128)(2,1)S(1)}, bf16[512,512]{1,0:T(8,128)(2,1)}, u32[]{:S(2)}) %copy-start.13) | copy-done | bytes 524312
  60.4 3.0 %labels.1.base_hbm = f32[512,1024]{1,0:T(8,128)S(1)} custom-call(bf16[512,512]{1,0:T(8,128)(2,1)S(1)} %copy-done.13, bf16[512,512]{1,0:T(8,128)(2,1)S(1)} %copy-done.6, bf16[512,1024]{1,0:T(8,128)(2,1)S(1)} %bitcast.8, f32[512,1024]{1,0:T(8,128)S(1)} %copy-done.9, bf16[512,1024]{1,0:T(8,128)(2,1)S(1)} %copy-done.1), custom_call_target="tpu_custom_call" | custom-call | flops 1073741824 | bytes 8388608 | tf_op jit(solution)/shard_map/labels/pallas_call | solution.py:266
  63.4 0.0 copy-start.2
  63.4 1.3 %copy-done.2 = f32[512,1024]{1,0:T(8,128)} copy-done((f32[512,1024]{1,0:T(8,128)}, f32[512,1024]{1,0:T(8,128)S(1)}, u32[]{:S(2)}) %copy-start.2) | copy-done | bytes 2097176
  64.7 18.2 %all-to-all-done.2 = bf16[32,16,1024]{2,1,0:T(8,128)(2,1)S(1)} async-done(((bf16[32,16,1024]{2,1,0:T(8,128)(2,1)}), bf16[32,16,1024]{2,1,0:T(8,128)(2,1)S(1)}, u32[]{:S(2)}, u32[]{:S(2)}) %all-to-all-start.2) | async-done | bytes 1048608 | tf_op jit(solution)/shard_map/all_to_all | solution.py:207
  82.9 0.0 copy-start.3
  82.9 1.6 %copy-done.3 = f32[512,1024]{1,0:T(8,128)S(1)} copy-done((f32[512,1024]{1,0:T(8,128)S(1)}, f32[512,1024]{1,0:T(8,128)}, u32[]{:S(2)}) %copy-start.3) | copy-done | bytes 2097176
  84.5 0.0 copy-start.7
  84.5 1.0 %copy-done.7 = bf16[512,512]{1,0:T(8,128)(2,1)S(1)} copy-done((bf16[512,512]{1,0:T(8,128)(2,1)S(1)}, bf16[512,512]{1,0:T(8,128)(2,1)}, u32[]{:S(2)}) %copy-start.7) | copy-done | bytes 524312
  85.6 3.1 %last.1 = bf16[512,1024]{1,0:T(8,128)(2,1)} custom-call(bf16[512,512]{1,0:T(8,128)(2,1)S(1)} %copy-done.7, bf16[512,1024]{1,0:T(8,128)(2,1)S(1)} %bitcast.9, f32[512,1024]{1,0:T(8,128)S(1)} %copy-done.3), custom_call_target="tpu_custom_call" | custom-call | flops 536870912 | bytes 4194304 | tf_op jit(solution)/shard_map/last/pallas_call | solution.py:187
Async XLA Ops:
  15.0 1.2 %copy-start = (bf16[512,1024]{1,0:T(8,128)(2,1)S(1)}, bf16[512,1024]{1,0:T(8,128)(2,1)}, u32[]{:S(2)}) copy-start(bf16[512,1024]{1,0:T(8,128)(2,1)} %seeds_ref.3) | copy-start | bytes 3145732
  16.2 5.5 %copy-start.1 = (bf16[512,1024]{1,0:T(8,128)(2,1)S(1)}, bf16[512,1024]{1,0:T(8,128)(2,1)}, u32[]{:S(2)}) copy-start(bf16[512,1024]{1,0:T(8,128)(2,1)} %seeds_ref.3) | copy-start | bytes 3145732
  16.2 5.5 %copy-start.14 = (s32[512,50]{0,1:T(8,128)S(1)}, s32[512,50]{0,1:T(8,128)}, u32[]{:S(2)}) copy-start(s32[512,50]{0,1:T(8,128)} %param.6) | copy-start | bytes 307204
  16.2 5.5 %copy-start.15 = (s32[512,50]{0,1:T(8,128)S(1)}, s32[512,50]{0,1:T(8,128)}, u32[]{:S(2)}) copy-start(s32[512,50]{0,1:T(8,128)} %param.7) | copy-start | bytes 307204
  16.2 5.5 %copy-start.16 = (s32[4,8]{1,0:T(4,128)S(1)}, s32[4,8]{1,0:T(4,128)}, u32[]{:S(2)}) copy-start(s32[4,8]{1,0:T(4,128)} %blocks_ref.1) | copy-start | bytes 388
  19.1 28.9 %all-to-all-start.1 = ((bf16[32,16,1024]{2,1,0:T(8,128)(2,1)}), bf16[32,16,1024]{2,1,0:T(8,128)(2,1)S(1)}, u32[]{:S(2)}, u32[]{:S(2)}) async-start(bf16[32,16,1024]{2,1,0:T(8,128)(2,1)} %bitcast.3), calls=%async_computation.1 | async-start | bytes 2097152 | tf_op jit(solution)/shard_map/all_to_all | solution.py:207
  39.5 0.8 copy-start.5
  40.3 1.3 %copy-start.8 = (f32[512,1024]{1,0:T(8,128)}, f32[512,1024]{1,0:T(8,128)S(1)}, u32[]{:S(2)}) copy-start(f32[512,1024]{1,0:T(8,128)S(1)} %get-tuple-element.14.base_ref) | copy-start | bytes 6291460
  41.7 1.3 %copy-start.10 = (f32[512,1024]{1,0:T(8,128)}, f32[512,1024]{1,0:T(8,128)S(1)}, u32[]{:S(2)}) copy-start(f32[512,1024]{1,0:T(8,128)S(1)} %get-tuple-element.12.base_hbm) | copy-start | bytes 6291460
  43.0 0.8 copy-start.12
  47.9 1.6 %copy-start.11 = (f32[512,1024]{1,0:T(8,128)S(1)}, f32[512,1024]{1,0:T(8,128)}, u32[]{:S(2)}) copy-start(f32[512,1024]{1,0:T(8,128)} %copy-done.10) | copy-start | bytes 6291460
  52.2 1.0 %copy-start.4 = (bf16[512,1024]{1,0:T(8,128)(2,1)}, bf16[512,1024]{1,0:T(8,128)(2,1)S(1)}, u32[]{:S(2)}) copy-start(bf16[512,1024]{1,0:T(8,128)(2,1)S(1)} %send.1) | copy-start | bytes 3145732
  53.1 29.8 %all-to-all-start.2 = ((bf16[32,16,1024]{2,1,0:T(8,128)(2,1)}), bf16[32,16,1024]{2,1,0:T(8,128)(2,1)S(1)}, u32[]{:S(2)}, u32[]{:S(2)}) async-start(bf16[32,16,1024]{2,1,0:T(8,128)(2,1)} %bitcast.10), calls=%async_computation.2 | async-start | bytes 2097152 | tf_op jit(solution)/shard_map/all_to_all | solution.py:207
  56.7 1.0 %copy-start.6 = (bf16[512,512]{1,0:T(8,128)(2,1)S(1)}, bf16[512,512]{1,0:T(8,128)(2,1)}, u32[]{:S(2)}) copy-start(bf16[512,512]{1,0:T(8,128)(2,1)} %copy-done.5) | copy-start | bytes 1572868
  57.7 1.6 %copy-start.9 = (f32[512,1024]{1,0:T(8,128)S(1)}, f32[512,1024]{1,0:T(8,128)}, u32[]{:S(2)}) copy-start(f32[512,1024]{1,0:T(8,128)} %copy-done.8) | copy-start | bytes 6291460
  59.3 1.0 %copy-start.13 = (bf16[512,512]{1,0:T(8,128)(2,1)S(1)}, bf16[512,512]{1,0:T(8,128)(2,1)}, u32[]{:S(2)}) copy-start(bf16[512,512]{1,0:T(8,128)(2,1)} %copy-done.12) | copy-start | bytes 1572868
  63.4 1.3 %copy-start.2 = (f32[512,1024]{1,0:T(8,128)}, f32[512,1024]{1,0:T(8,128)S(1)}, u32[]{:S(2)}) copy-start(f32[512,1024]{1,0:T(8,128)S(1)} %labels.1.base_hbm) | copy-start | bytes 6291460
  82.9 1.6 %copy-start.3 = (f32[512,1024]{1,0:T(8,128)S(1)}, f32[512,1024]{1,0:T(8,128)}, u32[]{:S(2)}) copy-start(f32[512,1024]{1,0:T(8,128)} %copy-done.2) | copy-start | bytes 6291460
  84.5 1.0 %copy-start.7 = (bf16[512,512]{1,0:T(8,128)(2,1)S(1)}, bf16[512,512]{1,0:T(8,128)(2,1)}, u32[]{:S(2)}) copy-start(bf16[512,512]{1,0:T(8,128)(2,1)} %copy-done.5) | copy-start | bytes 1572868

commit v4 on v3

--- a/solution.py
+++ b/solution.py
@@ -1,3 +1,5 @@
+import math
+
 import jax
 import jax.numpy as jnp
 from jax import lax
@@ -8,6 +10,7 @@
 BLK = 128
 COLS = 256
 VMEM_LIMIT = 32 * 1024 * 1024
+NEAR_BYTES = 1024 * 1024
 KEEP = 0.85
 ANCHOR = 0.15
 
@@ -16,13 +19,27 @@
 HBM = pl.BlockSpec(memory_space=pltpu.HBM)
 
 
-def call(kernel, name, out_shape, in_specs, out_specs=VMEM, scratch_shapes=(), flops=0, nbytes=0):
+def far_out(shape, dtype):
+    return pltpu.HBM(shape, dtype)
+
+
+def far_in(x):
+    return pltpu.with_memory_space_constraint(x, pltpu.HBM)
+
+
+def near_out(shape, dtype):
+    small = math.prod(shape) * jnp.dtype(dtype).itemsize <= NEAR_BYTES
+    return pltpu.VMEM(shape, dtype) if small else jax.ShapeDtypeStruct(shape, dtype)
+
+
+def call(kernel, name, out_shape, in_specs, out_specs=VMEM, scratch_shapes=(), flops=0, nbytes=0, aliases=None):
     return pl.pallas_call(
         kernel,
         out_shape=out_shape,
         in_specs=in_specs,
         out_specs=out_specs,
         scratch_shapes=scratch_shapes,
+        input_output_aliases=aliases or {},
         compiler_params=pltpu.CompilerParams(vmem_limit_bytes=VMEM_LIMIT),
         cost_estimate=pl.CostEstimate(flops=flops, bytes_accessed=nbytes, transcendentals=0),
         name=name,
@@ -37,15 +54,6 @@
     @pl.loop(0, width // COLS)
     def _(c):
         body(pl.ds(pl.multiple_of(c * COLS, COLS), COLS))
-
-
-def pull(source, target, sems, columns):
-    copies = []
-    for c in range(columns // COLS):
-        cols = slice(c * COLS, (c + 1) * COLS)
-        copies.append(pltpu.make_async_copy(source.at[:, cols], target.at[:, cols], sems.at[c]))
-        copies[-1].start()
-    return copies
 
 
 def push(source, target, sems, c):
@@ -67,14 +75,18 @@
     return hits.astype(jnp.float32).astype(jnp.bfloat16)
 
 
-def pick_kernel(asked_ref, seeds_hbm, out_hbm, seeds_ref, pick_ref, out_ref, in_sems, out_sems):
+def stage_kernel(seeds_hbm, seeds_ref, sem):
+    copy = pltpu.make_async_copy(seeds_hbm, seeds_ref, sem)
+    copy.start()
+    copy.wait()
+
+
+def pick_kernel(asked_ref, seeds_ref, out_hbm, pick_ref, out_ref, out_sems):
     rows, width = seeds_ref.shape
-    copies = pull(seeds_hbm, seeds_ref, in_sems, width)
     pick_ref[...] = picks(asked_ref[...], rows)
     pushed = []
-    for c, copy in enumerate(copies):
+    for c in range(width // COLS):
         cols = slice(c * COLS, (c + 1) * COLS)
-        copy.wait()
         out_ref[:, cols] = dot(pick_ref[...], seeds_ref[:, cols]).astype(jnp.bfloat16)
         pushed.append(push(out_ref, out_hbm, out_sems, c))
     for copy in pushed:
@@ -147,9 +159,9 @@
 
     def body(cols):
         seeds = seeds_ref[:, cols]
-        sent_base_ref[:, cols] = KEEP * dot(picked_ref[:, :rows], seeds) + ANCHOR * sent_ref[
-            :, cols
-        ].astype(jnp.float32)
+        sent = ANCHOR * sent_ref[:, cols].astype(jnp.float32)
+        sent_base = KEEP * dot(picked_ref[:, :rows], seeds) + sent
+        sent_base_ref[:, cols] = sent_base.astype(jnp.bfloat16)
         base_ref[:, cols] = KEEP * dot(tiles_ref[:, :rows], seeds) + ANCHOR * seeds.astype(
             jnp.float32
         )
@@ -157,14 +169,12 @@
     column_loop(width, body)
 
 
-def step_kernel(tiles_ref, received_ref, base_hbm, out_hbm, base_ref, out_ref, in_sems, out_sems):
-    copies = pull(base_hbm, base_ref, in_sems, base_ref.shape[1])
+def step_kernel(tiles_ref, received_ref, base_ref, out_hbm, out_ref, out_sems):
     pushed = []
-    for c, copy in enumerate(copies):
+    for c in range(base_ref.shape[1] // COLS):
         cols = slice(c * COLS, (c + 1) * COLS)
         total = KEEP * dot(tiles_ref[...], received_ref[:, cols])
-        copy.wait()
-        out_ref[:, cols] = (total + base_ref[:, cols]).astype(jnp.bfloat16)
+        out_ref[:, cols] = (total + base_ref[:, cols].astype(jnp.float32)).astype(jnp.bfloat16)
         pushed.append(push(out_ref, out_hbm, out_sems, c))
     for copy in pushed:
         copy.wait()
@@ -174,9 +184,8 @@
     def body(cols):
         total = KEEP * dot(far_ref[...], received_ref[:, cols]) + base_ref[:, cols]
         labels = total.astype(jnp.bfloat16)
-        next_base_ref[:, cols] = KEEP * dot(own_ref[...], labels) + ANCHOR * seeds_ref[
-            :, cols
-        ].astype(jnp.float32)
+        seeds = ANCHOR * seeds_ref[:, cols].astype(jnp.float32)
+        next_base_ref[:, cols] = (KEEP * dot(own_ref[...], labels) + seeds).astype(jnp.bfloat16)
 
     column_loop(seeds_ref.shape[1], body)
 
@@ -187,15 +196,10 @@
     return call(
         step_kernel,
         name,
-        jax.ShapeDtypeStruct((rows, width), jnp.bfloat16),
-        [VMEM, VMEM, HBM],
+        far_out((rows, width), jnp.bfloat16),
+        [VMEM, VMEM, VMEM],
         HBM,
-        [
-            pltpu.VMEM((rows, width), jnp.float32),
-            pltpu.VMEM((rows, width), jnp.bfloat16),
-            pieces,
-            pieces,
-        ],
+        [pltpu.VMEM((rows, width), jnp.bfloat16), pieces],
         flops=2 * rows * received.shape[0] * width,
         nbytes=8 * rows * width,
     )(tiles, received, base)
@@ -214,40 +218,45 @@
     count = peers * slots
     columns = rows + count
     neighbours = neighbor_pos.shape[1]
-    bf16 = lambda *shape: jax.ShapeDtypeStruct(shape, jnp.bfloat16)
-    f32 = lambda *shape: jax.ShapeDtypeStruct(shape, jnp.float32)
 
     pieces = pltpu.SemaphoreType.DMA((width // COLS,))
 
     asked = lax.all_to_all(
         wanted.reshape(peers, 1, slots), "rows", split_axis=0, concat_axis=0, tiled=True
     )
+    staged = call(
+        stage_kernel,
+        "stage",
+        near_out((rows, width), jnp.bfloat16),
+        [HBM],
+        VMEM,
+        [pltpu.SemaphoreType.DMA],
+        nbytes=4 * rows * width,
+    )(far_in(seeds))
     outgoing = call(
         pick_kernel,
         "pick",
-        bf16(count, width),
-        [VMEM, HBM],
+        far_out((count, width), jnp.bfloat16),
+        [VMEM, VMEM],
         HBM,
         [
-            pltpu.VMEM((rows, width), jnp.bfloat16),
             pltpu.VMEM((count, rows), jnp.bfloat16),
             pltpu.VMEM((count, width), jnp.bfloat16),
-            pieces,
             pieces,
         ],
         flops=2 * count * rows * width,
         nbytes=2 * (rows + count) * width,
-    )(asked, seeds)
+    )(asked, staged)
     received = exchange(outgoing, peers)
     own, far, picked_far, base, sent_base = call(
         tiles_kernel,
         "tiles",
         [
-            bf16(rows, rows),
-            bf16(rows, count),
-            bf16(count, count),
-            f32(rows, width),
-            f32(count, width),
+            far_out((rows, rows), jnp.bfloat16),
+            near_out((rows, count), jnp.bfloat16),
+            near_out((count, count), jnp.bfloat16),
+            far_out((rows, width), jnp.float32),
+            near_out((count, width), jnp.bfloat16),
         ],
         [SMEM, VMEM, VMEM, VMEM, VMEM, VMEM],
         [VMEM] * 5,
@@ -260,17 +269,18 @@
         ],
         flops=2 * neighbours * rows * columns,
         nbytes=4 * (rows + count) * width,
-    )(tile_blocks, neighbor_pos.T, edge_weight.T, asked, seeds, outgoing)
+    )(tile_blocks, neighbor_pos.T, edge_weight.T, asked, far_in(seeds), far_in(outgoing))
     outgoing = step(picked_far, received, sent_base, "send")
     received_next = exchange(outgoing, peers)
     next_base = call(
         labels_kernel,
         "labels",
-        f32(rows, width),
+        near_out((rows, width), jnp.bfloat16),
         [VMEM] * 5,
         flops=2 * rows * (count + rows) * width,
         nbytes=8 * (rows + count) * width,
-    )(own, far, received, base, seeds)
+        aliases={2: 0} if count == rows else None,
+    )(far_in(own), far, received, far_in(base), far_in(seeds))
     return step(far, received_next, next_base, "last")
 
 

time: 89.3 us -> 79.7 us (0.89)
  local copies, waits for them, and re-layouts: 16.4 us -> 1.39 us
  blocking collectives: 14.2 us -> 0 us
  waiting for transfers between devices: 22.4 us -> 33.8 us
  starting transfers between devices: 6.21 us -> 13.5 us
  Pallas kernels: 29.3 us -> 30.5 us
    unnamed x35 -> x7, local copies, waits for them, and re-layouts: 16.4 us -> 1.39 us
    all_to_all x1 -> x0, blocking collectives: 14.2 us -> none  [on_device(): lax.all_to_all(wanted.reshape(peers, 1, slots), 'rows', split_axis=0, con...]
    all_to_all x0 -> x1, starting transfers between devices: none -> 7.3 us  [on_device(): lax.all_to_all(wanted.reshape(peers, 1, slots), 'rows', split_axis=0, con...]
    all_to_all x0 -> x1, waiting for transfers between devices: none -> 5.79 us  [on_device(): lax.all_to_all(wanted.reshape(peers, 1, slots), 'rows', split_axis=0, con...]
    all_to_all x2, waiting for transfers between devices: 22.4 us -> 28 us  [exchange(): got = lax.all_to_all(sent, 'rows', split_axis=0, concat_axis=0, tiled=True)]
    pallas_call x5 -> x6, Pallas kernels: 29.3 us -> 30.5 us  [the longest x1 19.4 us: on_device(): call(tiles_kernel, 'tiles', [far_out((rows, rows), jnp.bfloat16), near_ou...]
  transfers between devices with their start and end apart: 2 -> 3, of which waited for: 2 -> 3; matrix products, arithmetic and copies ran while one was open for 0% -> 0% of each run, Pallas kernels for 23% -> 32%
where the time goes in v4:
time: 79.7 us; the launch traced here: 79.3 us
  waiting for transfers between devices  33.8 us (42%)
  Pallas kernels  30.5 us (38%)
  starting transfers between devices  13.5 us (17%)
  local copies, waits for them, and re-layouts  1.39 us (2%)
    all_to_all x2, waiting for transfers between devices, exchange(): got = lax.all_to_all(sent, 'rows', split_axis=0, concat_axis=0, tiled=True)  28 us
    pallas_call x1, Pallas kernels, on_device(): call(tiles_kernel, 'tiles', [far_out((rows, rows), jnp.bfloat16), near_ou...  19.4 us
    all_to_all x1, starting transfers between devices, on_device(): lax.all_to_all(wanted.reshape(peers, 1, slots), 'rows', split_axis=0, con...  7.3 us
    all_to_all x2, starting transfers between devices, exchange(): got = lax.all_to_all(sent, 'rows', split_axis=0, concat_axis=0, tiled=True)  6.21 us
    all_to_all x1, waiting for transfers between devices, on_device(): lax.all_to_all(wanted.reshape(peers, 1, slots), 'rows', split_axis=0, con...  5.79 us
    pallas_call x1, Pallas kernels, on_device(): call(labels_kernel, 'labels', near_out((rows, width), jnp.bfloat16), [VME...  5 us
    pallas_call x2, Pallas kernels, step(): call(step_kernel, name, far_out((rows, width), jnp.bfloat16), [VMEM, VMEM...  3.17 us
    pallas_call x1, Pallas kernels, on_device(): call(pick_kernel, 'pick', far_out((count, width), jnp.bfloat16), [VMEM, V...  1.65 us
  transfers between devices with their start and end apart: 3, of which 3 were waited for; matrix products, arithmetic and copies ran while one was open for 0% of the time, Pallas kernels for 32%

profile of v4, /device:TPU:0, one launch (start us, length us, event | category | flops | bytes accessed | tf_op | source)
XLA Modules:
  0.0 79.3 jit_solution(17671428164336922813)
XLA Ops:
  0.0 1.4 %copy.7 = s32[1,32,16]{2,1,0:T(8,128)} copy(s32[1,32,16]{1,2,0:T(8,128)} %param.9) | data formatting | bytes 4096 | tf_op args[4]
  1.4 7.3 %all-to-all-start = ((s32[32,1,16]{2,1,0:T(1,128)}), s32[32,1,16]{2,1,0:T(1,128)S(1)}, u32[]{:S(2)}, u32[]{:S(2)}) async-start(s32[32,1,16]{2,1,0:T(1,128)} %bitcast.2), calls=%async_computation | async-start | bytes 32768 | tf_op jit(solution)/shard_map/all_to_all | solution.py:224
  8.7 1.2 %stage.1.seeds_ref = bf16[512,1024]{1,0:T(8,128)(2,1)S(1)} custom-call(bf16[512,1024]{1,0:T(8,128)(2,1)} %seeds_ref.3), custom_call_target="tpu_custom_call" | custom-call | bytes 2097152 | tf_op jit(solution)/shard_map/stage/pallas_call | solution.py:227
  9.9 0.0 copy-start
  9.9 0.0 copy-start.1
  9.9 0.0 copy-start.2
  10.0 5.8 %all-to-all-done.asked_ref = s32[32,1,16]{2,1,0:T(1,128)S(1)} async-done(((s32[32,1,16]{2,1,0:T(1,128)}), s32[32,1,16]{2,1,0:T(1,128)S(1)}, u32[]{:S(2)}, u32[]{:S(2)}) %all-to-all-start) | async-done | bytes 2080 | tf_op jit(solution)/shard_map/all_to_all | solution.py:224
  15.8 1.6 %pick.1.sent_ref = bf16[512,1024]{1,0:T(8,128)(2,1)} custom-call(s32[32,1,16]{2,1,0:T(1,128)S(1)} %all-to-all-done.asked_ref, bf16[512,1024]{1,0:T(8,128)(2,1)S(1)} %stage.1.seeds_ref), custom_call_target="tpu_custom_call" | custom-call | flops 536870912 | bytes 2097152 | tf_op jit(solution)/shard_map/pick/pallas_call | solution.py:236
  17.4 2.7 %all-to-all-start.1 = ((bf16[32,16,1024]{2,1,0:T(8,128)(2,1)}), bf16[32,16,1024]{2,1,0:T(8,128)(2,1)S(1)}, u32[]{:S(2)}, u32[]{:S(2)}) async-start(bf16[32,16,1024]{2,1,0:T(8,128)(2,1)} %bitcast.12), calls=%async_computation.1 | async-start | bytes 2097152 | tf_op jit(solution)/shard_map/all_to_all | solution.py:211
  20.1 0.0 copy-done
  20.1 0.0 copy-done.1
  20.1 0.0 copy-done.2
  20.1 19.4 %tiles.1 = (bf16[512,512]{1,0:T(8,128)(2,1)}, bf16[512,512]{1,0:T(8,128)(2,1)S(1)}, bf16[512,512]{1,0:T(8,128)(2,1)S(1)}, f32[512,1024]{1,0:T(8,128)}, bf16[512,1024]{1,0:T(8,128)(2,1)S(1)}) custom-call(s32[4,8]{1,0:T(4,128)S(1)} %copy-done.2, s32[50,512]{1,0:T(8,128)S(1)} %bitcast.10, s32[50,512]{1,0:T(8,128)S(1)} %bitcast.11, ...), custom_call_target="tpu_custom_call" | custom-call | flops 52428800 | bytes 4194304 | tf_op jit(solution)/shard_map/tiles/pallas_call | solution.py:251
  39.5 6.8 %all-to-all-done.1 = bf16[32,16,1024]{2,1,0:T(8,128)(2,1)S(1)} async-done(((bf16[32,16,1024]{2,1,0:T(8,128)(2,1)}), bf16[32,16,1024]{2,1,0:T(8,128)(2,1)S(1)}, u32[]{:S(2)}, u32[]{:S(2)}) %all-to-all-start.1) | async-done | bytes 1048608 | tf_op jit(solution)/shard_map/all_to_all | solution.py:211
  46.3 1.6 %send.1 = bf16[512,1024]{1,0:T(8,128)(2,1)} custom-call(bf16[512,512]{1,0:T(8,128)(2,1)S(1)} %get-tuple-element.11.tiles_ref, bf16[512,1024]{1,0:T(8,128)(2,1)S(1)} %bitcast.7, bf16[512,1024]{1,0:T(8,128)(2,1)S(1)} %get-tuple-element.12.base_ref), custom_call_target="tpu_custom_call" | custom-call | flops 536870912 | bytes 4194304 | tf_op jit(solution)/shard_map/send/pallas_call | solution.py:196
  47.9 3.5 %all-to-all-start.2 = ((bf16[32,16,1024]{2,1,0:T(8,128)(2,1)}), bf16[32,16,1024]{2,1,0:T(8,128)(2,1)S(1)}, u32[]{:S(2)}, u32[]{:S(2)}) async-start(bf16[32,16,1024]{2,1,0:T(8,128)(2,1)} %bitcast.13), calls=%async_computation.2 | async-start | bytes 2097152 | tf_op jit(solution)/shard_map/all_to_all | solution.py:211
  51.5 5.0 %labels.1.base_ref = bf16[512,1024]{1,0:T(8,128)(2,1)S(1)} custom-call(bf16[512,512]{1,0:T(8,128)(2,1)} %get-tuple-element.13.own_ref, bf16[512,512]{1,0:T(8,128)(2,1)S(1)} %get-tuple-element.10.far_ref.tiles_ref, bf16[512,1024]{1,0:T(8,128)(2,1)S(1)} %bitcast.8, f32[512,1024]{1,0:T(8,128)} %get-tuple-element.14.base_ref, ...), custom_call_target="tpu_custom_call", output_to_operand_aliasing={{}: (2, {})} | custom-call | flops 1073741824 | bytes 8388608 | tf_op jit(solution)/shard_map/labels/pallas_call | solution.py:275
  56.5 21.2 %all-to-all-done.2 = bf16[32,16,1024]{2,1,0:T(8,128)(2,1)S(1)} async-done(((bf16[32,16,1024]{2,1,0:T(8,128)(2,1)}), bf16[32,16,1024]{2,1,0:T(8,128)(2,1)S(1)}, u32[]{:S(2)}, u32[]{:S(2)}) %all-to-all-start.2) | async-done | bytes 1048608 | tf_op jit(solution)/shard_map/all_to_all | solution.py:211
  77.7 1.6 %last.1 = bf16[512,1024]{1,0:T(8,128)(2,1)} custom-call(bf16[512,512]{1,0:T(8,128)(2,1)S(1)} %get-tuple-element.10.far_ref.tiles_ref, bf16[512,1024]{1,0:T(8,128)(2,1)S(1)} %bitcast.9, bf16[512,1024]{1,0:T(8,128)(2,1)S(1)} %labels.1.base_ref), custom_call_target="tpu_custom_call" | custom-call | flops 536870912 | bytes 4194304 | tf_op jit(solution)/shard_map/last/pallas_call | solution.py:196
Async XLA Ops:
  1.4 14.4 %all-to-all-start = ((s32[32,1,16]{2,1,0:T(1,128)}), s32[32,1,16]{2,1,0:T(1,128)S(1)}, u32[]{:S(2)}, u32[]{:S(2)}) async-start(s32[32,1,16]{2,1,0:T(1,128)} %bitcast.2), calls=%async_computation | async-start | bytes 32768 | tf_op jit(solution)/shard_map/all_to_all | solution.py:224
  9.9 10.2 %copy-start = (s32[512,50]{0,1:T(8,128)S(1)}, s32[512,50]{0,1:T(8,128)}, u32[]{:S(2)}) copy-start(s32[512,50]{0,1:T(8,128)} %param.6) | copy-start | bytes 307204
  9.9 10.2 %copy-start.1 = (s32[512,50]{0,1:T(8,128)S(1)}, s32[512,50]{0,1:T(8,128)}, u32[]{:S(2)}) copy-start(s32[512,50]{0,1:T(8,128)} %param.7) | copy-start | bytes 307204
  9.9 10.2 %copy-start.2 = (s32[4,8]{1,0:T(4,128)S(1)}, s32[4,8]{1,0:T(4,128)}, u32[]{:S(2)}) copy-start(s32[4,8]{1,0:T(4,128)} %blocks_ref.1) | copy-start | bytes 388
  17.4 28.9 %all-to-all-start.1 = ((bf16[32,16,1024]{2,1,0:T(8,128)(2,1)}), bf16[32,16,1024]{2,1,0:T(8,128)(2,1)S(1)}, u32[]{:S(2)}, u32[]{:S(2)}) async-start(bf16[32,16,1024]{2,1,0:T(8,128)(2,1)} %bitcast.12), calls=%async_computation.1 | async-start | bytes 2097152 | tf_op jit(solution)/shard_map/all_to_all | solution.py:211
  47.9 29.8 %all-to-all-start.2 = ((bf16[32,16,1024]{2,1,0:T(8,128)(2,1)}), bf16[32,16,1024]{2,1,0:T(8,128)(2,1)S(1)}, u32[]{:S(2)}, u32[]{:S(2)}) async-start(bf16[32,16,1024]{2,1,0:T(8,128)(2,1)} %bitcast.13), calls=%async_computation.2 | async-start | bytes 2097152 | tf_op jit(solution)/shard_map/all_to_all | solution.py:211

commit v5 on v4

--- a/solution.py
+++ b/solution.py
@@ -13,6 +13,7 @@
 NEAR_BYTES = 1024 * 1024
 KEEP = 0.85
 ANCHOR = 0.15
+REST_SCALE = 4096.0
 
 SMEM = pl.BlockSpec(memory_space=pltpu.SMEM)
 VMEM = pl.BlockSpec(memory_space=pltpu.VMEM)
@@ -169,40 +170,48 @@
     column_loop(width, body)
 
 
-def step_kernel(tiles_ref, received_ref, base_ref, out_hbm, out_ref, out_sems):
+def step_kernel(tiles_ref, received_ref, base_ref, *refs):
+    *rest_ref, out_hbm, out_ref, out_sems = refs
     pushed = []
     for c in range(base_ref.shape[1] // COLS):
         cols = slice(c * COLS, (c + 1) * COLS)
         total = KEEP * dot(tiles_ref[...], received_ref[:, cols])
-        out_ref[:, cols] = (total + base_ref[:, cols].astype(jnp.float32)).astype(jnp.bfloat16)
+        total = total + base_ref[:, cols].astype(jnp.float32)
+        if rest_ref:
+            total = total + rest_ref[0][:, cols].astype(jnp.float32) * (1 / REST_SCALE)
+        out_ref[:, cols] = total.astype(jnp.bfloat16)
         pushed.append(push(out_ref, out_hbm, out_sems, c))
     for copy in pushed:
         copy.wait()
 
 
-def labels_kernel(own_ref, far_ref, received_ref, base_ref, seeds_ref, next_base_ref):
+def labels_kernel(own_ref, far_ref, received_ref, base_ref, seeds_ref, next_base_ref, rest_ref):
     def body(cols):
         total = KEEP * dot(far_ref[...], received_ref[:, cols]) + base_ref[:, cols]
         labels = total.astype(jnp.bfloat16)
         seeds = ANCHOR * seeds_ref[:, cols].astype(jnp.float32)
-        next_base_ref[:, cols] = (KEEP * dot(own_ref[...], labels) + seeds).astype(jnp.bfloat16)
+        next_base = KEEP * dot(own_ref[...], labels) + seeds
+        kept = next_base.astype(jnp.bfloat16)
+        next_base_ref[:, cols] = kept
+        rest = (next_base - kept.astype(jnp.float32)) * REST_SCALE
+        rest_ref[:, cols] = rest.astype(jnp.float8_e4m3fn)
 
     column_loop(seeds_ref.shape[1], body)
 
 
-def step(tiles, received, base, name):
+def step(name, tiles, received, base, *rest):
     rows, width = base.shape
     pieces = pltpu.SemaphoreType.DMA((width // COLS,))
     return call(
         step_kernel,
         name,
         far_out((rows, width), jnp.bfloat16),
-        [VMEM, VMEM, VMEM],
+        [VMEM] * (3 + len(rest)),
         HBM,
         [pltpu.VMEM((rows, width), jnp.bfloat16), pieces],
         flops=2 * rows * received.shape[0] * width,
         nbytes=8 * rows * width,
-    )(tiles, received, base)
+    )(tiles, received, base, *rest)
 
 
 def exchange(rows_out, peers):
@@ -270,18 +279,19 @@
         flops=2 * neighbours * rows * columns,
         nbytes=4 * (rows + count) * width,
     )(tile_blocks, neighbor_pos.T, edge_weight.T, asked, far_in(seeds), far_in(outgoing))
-    outgoing = step(picked_far, received, sent_base, "send")
+    outgoing = step("send", picked_far, received, sent_base)
     received_next = exchange(outgoing, peers)
-    next_base = call(
+    next_base, rest = call(
         labels_kernel,
         "labels",
-        near_out((rows, width), jnp.bfloat16),
+        [near_out((rows, width), jnp.bfloat16), near_out((rows, width), jnp.float8_e4m3fn)],
         [VMEM] * 5,
+        [VMEM, VMEM],
         flops=2 * rows * (count + rows) * width,
         nbytes=8 * (rows + count) * width,
         aliases={2: 0} if count == rows else None,
     )(far_in(own), far, received, far_in(base), far_in(seeds))
-    return step(far, received_next, next_base, "last")
+    return step("last", far, received_next, next_base, rest)
 
 
 def solution(mesh):

time: 79.7 us -> 79.8 us (level)
  no operation moved by 1% of the time
where the time goes in v5:
time: 79.8 us; the launch traced here: 79.4 us
  waiting for transfers between devices  33.8 us (42%)
  Pallas kernels  30.6 us (38%)
  starting transfers between devices  13.5 us (17%)
  local copies, waits for them, and re-layouts  1.39 us (2%)
    all_to_all x2, waiting for transfers between devices, exchange(): got = lax.all_to_all(sent, 'rows', split_axis=0, concat_axis=0, tiled=True)  28 us
    pallas_call x1, Pallas kernels, on_device(): call(tiles_kernel, 'tiles', [far_out((rows, rows), jnp.bfloat16), near_ou...  19.4 us
    all_to_all x1, starting transfers between devices, on_device(): lax.all_to_all(wanted.reshape(peers, 1, slots), 'rows', split_axis=0, con...  7.3 us
    all_to_all x2, starting transfers between devices, exchange(): got = lax.all_to_all(sent, 'rows', split_axis=0, concat_axis=0, tiled=True)  6.21 us
    all_to_all x1, waiting for transfers between devices, on_device(): lax.all_to_all(wanted.reshape(peers, 1, slots), 'rows', split_axis=0, con...  5.79 us
    pallas_call x1, Pallas kernels, on_device(): call(labels_kernel, 'labels', [near_out((rows, width), jnp.bfloat16), nea...  5.02 us
    pallas_call x2, Pallas kernels, step(): call(step_kernel, name, far_out((rows, width), jnp.bfloat16), [VMEM] * (3...  3.27 us
    pallas_call x1, Pallas kernels, on_device(): call(pick_kernel, 'pick', far_out((count, width), jnp.bfloat16), [VMEM, V...  1.65 us
  transfers between devices with their start and end apart: 3, of which 3 were waited for; matrix products, arithmetic and copies ran while one was open for 0% of the time, Pallas kernels for 32%

profile of v5, /device:TPU:0, one launch (start us, length us, event | category | flops | bytes accessed | tf_op | source)
XLA Modules:
  0.0 79.4 jit_solution(8659808155260398844)
XLA Ops:
  0.0 1.4 %copy.7 = s32[1,32,16]{2,1,0:T(8,128)} copy(s32[1,32,16]{1,2,0:T(8,128)} %param.9) | data formatting | bytes 4096 | tf_op args[4]
  1.4 7.3 %all-to-all-start = ((s32[32,1,16]{2,1,0:T(1,128)}), s32[32,1,16]{2,1,0:T(1,128)S(1)}, u32[]{:S(2)}, u32[]{:S(2)}) async-start(s32[32,1,16]{2,1,0:T(1,128)} %bitcast.2), calls=%async_computation | async-start | bytes 32768 | tf_op jit(solution)/shard_map/all_to_all | solution.py:233
  8.7 1.2 %stage.1.seeds_ref = bf16[512,1024]{1,0:T(8,128)(2,1)S(1)} custom-call(bf16[512,1024]{1,0:T(8,128)(2,1)} %seeds_ref.3), custom_call_target="tpu_custom_call" | custom-call | bytes 2097152 | tf_op jit(solution)/shard_map/stage/pallas_call | solution.py:236
  9.9 0.0 copy-start
  9.9 0.0 copy-start.1
  9.9 0.0 copy-start.2
  10.0 5.8 %all-to-all-done.asked_ref = s32[32,1,16]{2,1,0:T(1,128)S(1)} async-done(((s32[32,1,16]{2,1,0:T(1,128)}), s32[32,1,16]{2,1,0:T(1,128)S(1)}, u32[]{:S(2)}, u32[]{:S(2)}) %all-to-all-start) | async-done | bytes 2080 | tf_op jit(solution)/shard_map/all_to_all | solution.py:233
  15.8 1.6 %pick.1.sent_ref = bf16[512,1024]{1,0:T(8,128)(2,1)} custom-call(s32[32,1,16]{2,1,0:T(1,128)S(1)} %all-to-all-done.asked_ref, bf16[512,1024]{1,0:T(8,128)(2,1)S(1)} %stage.1.seeds_ref), custom_call_target="tpu_custom_call" | custom-call | flops 536870912 | bytes 2097152 | tf_op jit(solution)/shard_map/pick/pallas_call | solution.py:245
  17.4 2.7 %all-to-all-start.1 = ((bf16[32,16,1024]{2,1,0:T(8,128)(2,1)}), bf16[32,16,1024]{2,1,0:T(8,128)(2,1)S(1)}, u32[]{:S(2)}, u32[]{:S(2)}) async-start(bf16[32,16,1024]{2,1,0:T(8,128)(2,1)} %bitcast.12), calls=%async_computation.1 | async-start | bytes 2097152 | tf_op jit(solution)/shard_map/all_to_all | solution.py:220
  20.1 0.0 copy-done
  20.1 0.0 copy-done.1
  20.1 0.0 copy-done.2
  20.1 19.4 %tiles.1 = (bf16[512,512]{1,0:T(8,128)(2,1)}, bf16[512,512]{1,0:T(8,128)(2,1)S(1)}, bf16[512,512]{1,0:T(8,128)(2,1)S(1)}, f32[512,1024]{1,0:T(8,128)}, bf16[512,1024]{1,0:T(8,128)(2,1)S(1)}) custom-call(s32[4,8]{1,0:T(4,128)S(1)} %copy-done.2, s32[50,512]{1,0:T(8,128)S(1)} %bitcast.10, s32[50,512]{1,0:T(8,128)S(1)} %bitcast.11, ...), custom_call_target="tpu_custom_call" | custom-call | flops 52428800 | bytes 4194304 | tf_op jit(solution)/shard_map/tiles/pallas_call | solution.py:260
  39.5 6.8 %all-to-all-done.1 = bf16[32,16,1024]{2,1,0:T(8,128)(2,1)S(1)} async-done(((bf16[32,16,1024]{2,1,0:T(8,128)(2,1)}), bf16[32,16,1024]{2,1,0:T(8,128)(2,1)S(1)}, u32[]{:S(2)}, u32[]{:S(2)}) %all-to-all-start.1) | async-done | bytes 1048608 | tf_op jit(solution)/shard_map/all_to_all | solution.py:220
  46.3 1.6 %send.1 = bf16[512,1024]{1,0:T(8,128)(2,1)} custom-call(bf16[512,512]{1,0:T(8,128)(2,1)S(1)} %get-tuple-element.13.tiles_ref, bf16[512,1024]{1,0:T(8,128)(2,1)S(1)} %bitcast.7, bf16[512,1024]{1,0:T(8,128)(2,1)S(1)} %get-tuple-element.14.base_ref), custom_call_target="tpu_custom_call" | custom-call | flops 536870912 | bytes 4194304 | tf_op jit(solution)/shard_map/send/pallas_call | solution.py:205
  47.9 3.5 %all-to-all-start.2 = ((bf16[32,16,1024]{2,1,0:T(8,128)(2,1)}), bf16[32,16,1024]{2,1,0:T(8,128)(2,1)S(1)}, u32[]{:S(2)}, u32[]{:S(2)}) async-start(bf16[32,16,1024]{2,1,0:T(8,128)(2,1)} %bitcast.13), calls=%async_computation.2 | async-start | bytes 2097152 | tf_op jit(solution)/shard_map/all_to_all | solution.py:220
  51.5 5.0 %labels.1 = (bf16[512,1024]{1,0:T(8,128)(2,1)S(1)}, f8e4m3fn[512,1024]{1,0:T(32,128)(4,1)S(1)}) custom-call(bf16[512,512]{1,0:T(8,128)(2,1)} %get-tuple-element.15.own_ref, bf16[512,512]{1,0:T(8,128)(2,1)S(1)} %get-tuple-element.12.far_ref.tiles_ref, bf16[512,1024]{1,0:T(8,128)(2,1)S(1)} %bitcast.8, ...), custom_call_target="tpu_custom_call", output_to_operand_aliasing={{0}: (2, {})} | custom-call | flops 1073741824 | bytes 8388608 | tf_op jit(solution)/shard_map/labels/pallas_call | solution.py:284
  56.5 21.2 %all-to-all-done.2 = bf16[32,16,1024]{2,1,0:T(8,128)(2,1)S(1)} async-done(((bf16[32,16,1024]{2,1,0:T(8,128)(2,1)}), bf16[32,16,1024]{2,1,0:T(8,128)(2,1)S(1)}, u32[]{:S(2)}, u32[]{:S(2)}) %all-to-all-start.2) | async-done | bytes 1048608 | tf_op jit(solution)/shard_map/all_to_all | solution.py:220
  77.7 1.7 %last.1 = bf16[512,1024]{1,0:T(8,128)(2,1)} custom-call(bf16[512,512]{1,0:T(8,128)(2,1)S(1)} %get-tuple-element.12.far_ref.tiles_ref, bf16[512,1024]{1,0:T(8,128)(2,1)S(1)} %bitcast.9, bf16[512,1024]{1,0:T(8,128)(2,1)S(1)} %get-tuple-element.17.base_ref, f8e4m3fn[512,1024]{1,0:T(32,128)(4,1)S(1)} %get-tuple-element.18.refs_0_), custom_call_target="tpu_custom_call" | custom-call | flops 536870912 | bytes 4194304 | tf_op jit(solution)/shard_map/last/pallas_call | solution.py:205
Async XLA Ops:
  1.4 14.4 %all-to-all-start = ((s32[32,1,16]{2,1,0:T(1,128)}), s32[32,1,16]{2,1,0:T(1,128)S(1)}, u32[]{:S(2)}, u32[]{:S(2)}) async-start(s32[32,1,16]{2,1,0:T(1,128)} %bitcast.2), calls=%async_computation | async-start | bytes 32768 | tf_op jit(solution)/shard_map/all_to_all | solution.py:233
  9.9 10.2 %copy-start = (s32[512,50]{0,1:T(8,128)S(1)}, s32[512,50]{0,1:T(8,128)}, u32[]{:S(2)}) copy-start(s32[512,50]{0,1:T(8,128)} %param.6) | copy-start | bytes 307204
  9.9 10.2 %copy-start.1 = (s32[512,50]{0,1:T(8,128)S(1)}, s32[512,50]{0,1:T(8,128)}, u32[]{:S(2)}) copy-start(s32[512,50]{0,1:T(8,128)} %param.7) | copy-start | bytes 307204
  9.9 10.2 %copy-start.2 = (s32[4,8]{1,0:T(4,128)S(1)}, s32[4,8]{1,0:T(4,128)}, u32[]{:S(2)}) copy-start(s32[4,8]{1,0:T(4,128)} %blocks_ref.1) | copy-start | bytes 388
  17.4 28.9 %all-to-all-start.1 = ((bf16[32,16,1024]{2,1,0:T(8,128)(2,1)}), bf16[32,16,1024]{2,1,0:T(8,128)(2,1)S(1)}, u32[]{:S(2)}, u32[]{:S(2)}) async-start(bf16[32,16,1024]{2,1,0:T(8,128)(2,1)} %bitcast.12), calls=%async_computation.1 | async-start | bytes 2097152 | tf_op jit(solution)/shard_map/all_to_all | solution.py:220
  47.9 29.8 %all-to-all-start.2 = ((bf16[32,16,1024]{2,1,0:T(8,128)(2,1)}), bf16[32,16,1024]{2,1,0:T(8,128)(2,1)S(1)}, u32[]{:S(2)}, u32[]{:S(2)}) async-start(bf16[32,16,1024]{2,1,0:T(8,128)(2,1)} %bitcast.13), calls=%async_computation.2 | async-start | bytes 2097152 | tf_op jit(solution)/shard_map/all_to_all | solution.py:220

commit v6 on v0

v6 whole, which is shorter than its diff:
```python
import functools
import math

import jax
import jax.numpy as jnp
from jax import lax
from jax.experimental import pallas as pl
from jax.experimental.pallas import tpu as pltpu
from jax.sharding import PartitionSpec as P

BLK = 128
COLS = 256
GROUP = 8
PACK = 16
VMEM_LIMIT = 32 * 1024 * 1024
NEAR_BYTES = 1024 * 1024
KEEP = 0.85
ANCHOR = 0.15
REST_SCALE = 4096.0
LONG = 10**12

SMEM = pl.BlockSpec(memory_space=pltpu.SMEM)
VMEM = pl.BlockSpec(memory_space=pltpu.VMEM)
HBM = pl.BlockSpec(memory_space=pltpu.HBM)
ANY = pl.BlockSpec(memory_space=pl.ANY)


def far_out(shape, dtype=jnp.bfloat16):
    return pltpu.HBM(shape, dtype)


def far_in(x):
    return pltpu.with_memory_space_constraint(x, pltpu.HBM)


def near_out(shape, dtype=jnp.bfloat16):
    small = math.prod(shape) * jnp.dtype(dtype).itemsize <= NEAR_BYTES
    return pltpu.VMEM(shape, dtype) if small else jax.ShapeDtypeStruct(shape, dtype)


def call(kernel, name, out_shape, in_specs, out_specs, scratch_shapes=(), flops=0, aliases=None):
    return pl.pallas_call(
        kernel,
        out_shape=out_shape,
        in_specs=in_specs,
        out_specs=out_specs,
        scratch_shapes=scratch_shapes,
        input_output_aliases=aliases or {},
        compiler_params=pltpu.CompilerParams(vmem_limit_bytes=VMEM_LIMIT),
        cost_estimate=pl.CostEstimate(flops=flops, bytes_accessed=0, transcendentals=0),
        name=name,
    )


def dot(a, b):
    return jnp.dot(a, b, preferred_element_type=jnp.float32)


def pieces_of(first, last):
    return [slice(c, min(c + COLS, last)) for c in range(first, last, COLS)]


def moved(cols, by):
    return slice(cols.start + by, cols.stop + by)


def push(source, target, sem):
    copy = pltpu.make_async_copy(source, target, sem)
    copy.start()
    return copy


def picks(asked, rows):
    peers, _, slots = asked.shape
    count = peers * slots
    spread = jnp.broadcast_to(asked.astype(jnp.float32), (peers, slots, slots))
    spread = spread.reshape(count, slots)
    slot = lax.broadcasted_iota(jnp.int32, (count, slots), 0) % slots
    lane = lax.broadcasted_iota(jnp.int32, (count, slots), 1)
    row = jnp.sum(jnp.where(slot == lane, spread, 0.0), axis=1, keepdims=True)
    hits = lax.broadcasted_iota(jnp.int32, (count, rows), 1) == row.astype(jnp.int32)
    return hits.astype(jnp.float32).astype(jnp.bfloat16)


def block(peer, slots):
    return pl.ds(pl.multiple_of(peer * slots, slots), slots)


def to_planes(me, rows_ref, plane_refs, slots):
    for z, plane_ref in enumerate(plane_refs):
        for s in range(2):
            for q in range(GROUP // 2):
                peer = me ^ (GROUP * z + 2 * q + s)
                at = (s * (GROUP // 2) + q) * slots
                plane_ref[at : at + slots, :] = rows_ref[block(peer, slots), :]


def from_pairs(me, pair_refs, rows_ref, slots):
    planes = pair_refs[0].shape[0] // (2 * slots)
    for q, pair_ref in enumerate(pair_refs):
        for s in range(2):
            for z in range(planes):
                peer = me ^ (GROUP * z + 2 * q + s)
                at = (s * planes + z) * slots
                rows_ref[block(peer, slots), :] = pair_ref[at : at + slots, :]


def fill_edges(blocks_ref, pos_ref, weight_ref, column_ref, share_ref):
    block_count, tile_count = blocks_ref.shape
    weights = weight_ref[...].astype(jnp.float32)
    share = weights / jnp.sum(weights, axis=0, keepdims=True)
    share_ref[...] = share.astype(jnp.bfloat16).astype(jnp.float32)
    for b in range(block_count):
        lanes = slice(b * BLK, (b + 1) * BLK)
        pos = pos_ref[:, lanes]
        tile = pos // BLK
        base = jnp.full(pos.shape, blocks_ref[b, 0], jnp.int32)
        for j in range(1, tile_count):
            base = jnp.where(tile == j, blocks_ref[b, j], base)
        column_ref[:, lanes] = base * BLK + pos % BLK


def fill_tiles(column_ref, share_ref, tiles_ref, spot_ref, start, chunks):
    neighbours, rows = column_ref.shape
    sub = lax.broadcasted_iota(jnp.int32, (BLK, BLK), 0).astype(jnp.float32).astype(jnp.bfloat16)
    sub = sub.reshape(BLK // PACK, PACK, BLK)

    @pl.loop(*chunks)
    def _(chunk):
        first = pl.multiple_of(chunk * BLK, BLK)
        spot = column_ref[...] - (start + first)
        spot_ref[...] = jnp.where((spot >= 0) & (spot < BLK), spot, -1).astype(jnp.float32)

        @pl.loop(0, rows // BLK)
        def _(b):
            lanes = pl.ds(pl.multiple_of(b * BLK, BLK), BLK)
            row = lambda ref, k: jnp.broadcast_to(ref[k : k + 1, lanes], (PACK, BLK))
            total = jnp.zeros(sub.shape, jnp.bfloat16)
            for k in range(neighbours):
                spot = row(spot_ref, k).astype(jnp.bfloat16)
                share = row(share_ref, k).astype(jnp.bfloat16)
                total = jnp.where(sub == spot[None], share[None], total)
            tiles_ref[lanes, pl.ds(first, BLK)] = total.reshape(BLK, BLK).T


def own_tiles_kernel(
    blocks_ref, pos_ref, weight_ref, seeds_hbm, own_ref, column_ref, share_ref, near_ref, spot_ref, sem
):
    copy = push(seeds_hbm, near_ref, sem)
    fill_edges(blocks_ref, pos_ref, weight_ref, column_ref, share_ref)
    fill_tiles(column_ref, share_ref, own_ref, spot_ref, 0, (0, own_ref.shape[1] // BLK))
    copy.wait()


def pick_kernel(me_ref, asked_ref, seeds_ref, after_ref, out_a, out_b, *refs):
    *plane_refs, pick_ref, a_ref, b_ref, sems = refs
    del after_ref
    slots = asked_ref.shape[2]
    rows, width = seeds_ref.shape
    wide = a_ref.shape[1]
    pick_ref[...] = picks(asked_ref[...], rows)
    for cols in pieces_of(0, wide):
        a_ref[:, cols] = dot(pick_ref[...], seeds_ref[:, cols]).astype(jnp.bfloat16)
    copies = [push(a_ref, out_a, sems.at[0])]
    to_planes(me_ref[0], a_ref, plane_refs, slots)
    for i, cols in enumerate(pieces_of(wide, width)):
        here = moved(cols, -wide)
        b_ref[:, here] = dot(pick_ref[...], seeds_ref[:, cols]).astype(jnp.bfloat16)
        copies.append(push(b_ref.at[:, here], out_b.at[:, here], sems.at[1 + i]))
    for copy in copies:
        copy.wait()


def far_kernel(
    asked_ref,
    own_ref,
    column_ref,
    share_ref,
    seeds_ref,
    sent_a_ref,
    sent_b_ref,
    after_ref,
    far_ref,
    picked_far_ref,
    sent_base_ref,
    pick_ref,
    picked_ref,
    spot_ref,
):
    del after_ref
    rows, width = seeds_ref.shape
    wide = sent_a_ref.shape[1]
    fill_tiles(column_ref, share_ref, far_ref, spot_ref, rows, (0, far_ref.shape[1] // BLK))
    pick_ref[...] = picks(asked_ref[...], rows)
    for cols in pieces_of(0, far_ref.shape[1]):
        picked_far_ref[:, cols] = dot(pick_ref[...], far_ref[:, cols]).astype(jnp.bfloat16)
    for cols in pieces_of(0, rows):
        picked_ref[:, cols] = dot(pick_ref[...], own_ref[:, cols]).astype(jnp.bfloat16)
    for cols in pieces_of(0, wide) + pieces_of(wide, width):
        sent = sent_a_ref[:, cols] if cols.stop <= wide else sent_b_ref[:, moved(cols, -wide)]
        sent_base = KEEP * dot(picked_ref[...], seeds_ref[:, cols])
        sent_base = sent_base + ANCHOR * sent.astype(jnp.float32)
        sent_base_ref[:, cols] = sent_base.astype(jnp.bfloat16)


def gather_kernel(*refs):
    *plane_refs, out_ref = refs
    half = plane_refs[0].shape[0] // 2
    for z, plane_ref in enumerate(plane_refs):
        out_ref[z * half : (z + 1) * half, :] = plane_ref[half:, :]


def pair_kernel(slots, *refs):
    count = GROUP // 2
    *plane_refs, other_ref = refs[:-count]
    planes = len(plane_refs)
    for q, out_ref in enumerate(refs[-count:]):
        for z, plane_ref in enumerate(plane_refs):
            here = slice(z * slots, (z + 1) * slots)
            there = slice((planes + z) * slots, (planes + z + 1) * slots)
            other = (z * count + q) * slots
            out_ref[here, :] = plane_ref[q * slots : (q + 1) * slots, :]
            out_ref[there, :] = other_ref[other : other + slots, :]


def send_a_kernel(me_ref, tiles_ref, base_ref, *refs, slots):
    pair_refs = refs[: GROUP // 2]
    out_hbm, *plane_refs, received_ref, out_ref, sem = refs[GROUP // 2 :]
    me = me_ref[0]
    from_pairs(me, pair_refs, received_ref, slots)
    copy = push(received_ref, out_hbm, sem)
    for cols in pieces_of(0, received_ref.shape[1]):
        total = KEEP * dot(tiles_ref[...], received_ref[:, cols])
        out_ref[:, cols] = (total + base_ref[:, cols].astype(jnp.float32)).astype(jnp.bfloat16)
    to_planes(me, out_ref, plane_refs, slots)
    copy.wait()


def send_b_kernel(tiles_ref, base_ref, received_ref, after_ref, out_hbm, kept_hbm, out_ref, sems):
    del after_ref
    wide = base_ref.shape[1] - received_ref.shape[1]
    copies = [push(received_ref, kept_hbm, sems.at[0])]
    for i, cols in enumerate(pieces_of(0, received_ref.shape[1])):
        total = KEEP * dot(tiles_ref[...], received_ref[:, cols])
        total = total + base_ref[:, moved(cols, wide)].astype(jnp.float32)
        out_ref[:, cols] = total.astype(jnp.bfloat16)
        copies.append(push(out_ref.at[:, cols], out_hbm.at[:, cols], sems.at[1 + i]))
    for copy in copies:
        copy.wait()


def labels_kernel(
    own_ref,
    far_ref,
    seeds_ref,
    received_a_ref,
    received_b_ref,
    after_ref,
    next_ref,
    rest_ref,
    near_ref,
):
    del after_ref
    near_ref[...] = far_ref[...]
    wide = received_a_ref.shape[1]
    width = seeds_ref.shape[1]
    for cols in pieces_of(0, wide) + pieces_of(wide, width):
        first = cols.stop <= wide
        received = received_a_ref[:, cols] if first else received_b_ref[:, moved(cols, -wide)]
        seeds = ANCHOR * seeds_ref[:, cols].astype(jnp.float32)
        total = dot(own_ref[...], seeds_ref[:, cols]) + dot(far_ref[...], received)
        labels = (KEEP * total + seeds).astype(jnp.bfloat16)
        base = KEEP * dot(own_ref[...], labels) + seeds
        kept = base.astype(jnp.bfloat16)
        next_ref[:, cols] = kept
        rest = (base - kept.astype(jnp.float32)) * REST_SCALE
        rest_ref[:, cols] = rest.astype(jnp.float8_e4m3fn)


def last_kernel(me_ref, tiles_ref, base_ref, rest_ref, received_b_ref, *refs, slots):
    pair_refs = refs[: GROUP // 2]
    out_hbm, received_a_ref, out_ref, sems = refs[GROUP // 2 :]
    wide = received_a_ref.shape[1]
    width = rest_ref.shape[1]
    from_pairs(me_ref[0], pair_refs, received_a_ref, slots)
    copies = []
    for i, cols in enumerate(pieces_of(wide, width) + pieces_of(0, wide)):
        first = cols.stop <= wide
        received = received_a_ref[:, cols] if first else received_b_ref[:, moved(cols, -wide)]
        total = KEEP * dot(tiles_ref[...], received) + base_ref[:, cols].astype(jnp.float32)
        total = total + rest_ref[:, cols].astype(jnp.float32) * (1 / REST_SCALE)
        out_ref[:, cols] = total.astype(jnp.bfloat16)
        copies.append(push(out_ref.at[:, cols], out_hbm.at[:, cols], sems.at[i]))
    for copy in copies:
        copy.wait()


def swap(x, peers, distance):
    return lax.ppermute(x, "rows", [(i, i ^ distance) for i in range(peers)])


def exchange(rows_out, peers):
    count, width = rows_out.shape
    sent = rows_out.reshape(peers, count // peers, width)
    got = lax.all_to_all(sent, "rows", split_axis=0, concat_axis=0, tiled=True)
    return got.reshape(count, width)


def across(planes, peers):
    return [planes[0]] + [swap(x, peers, GROUP * z) for z, x in enumerate(planes) if z]


def within(planes, peers, slots):
    depth, wide = planes[0].shape
    n = len(planes)
    other = call(
        gather_kernel,
        "gather",
        jax.ShapeDtypeStruct((n * depth // 2, wide), jnp.bfloat16),
        [VMEM] * n,
        VMEM,
        flops=LONG,
    )(*planes)
    other = swap(other, peers, 1)
    pairs = call(
        functools.partial(pair_kernel, slots),
        "pair",
        [jax.ShapeDtypeStruct((2 * n * slots, wide), jnp.bfloat16)] * (GROUP // 2),
        [VMEM] * (n + 1),
        [VMEM] * (GROUP // 2),
    )(*planes, other)
    return [pairs[0]] + [swap(x, peers, 2 * q) for q, x in enumerate(pairs) if q]


def on_device(seeds, neighbor_pos, edge_weight, tile_blocks, wanted):
    rows, width = seeds.shape
    peers, slots = wanted.shape[1:]
    count = peers * slots
    neighbours = neighbor_pos.shape[1]
    planes = peers // GROUP
    wide = max(3 * width // 8 // BLK, 1) * BLK
    assert peers & (peers - 1) == 0 and peers >= GROUP
    me = lax.axis_index("rows").astype(jnp.int32).reshape(1)
    sems = pltpu.SemaphoreType.DMA
    bf16 = jnp.bfloat16
    plane_shape = jax.ShapeDtypeStruct((GROUP * slots, wide), bf16)
    n_b = len(pieces_of(wide, width))
    n_all = n_b + len(pieces_of(0, wide))

    asked = lax.all_to_all(
        wanted.reshape(peers, 1, slots), "rows", split_axis=0, concat_axis=0, tiled=True
    )
    own, column, share, near_seeds = call(
        own_tiles_kernel,
        "own_tiles",
        [
            far_out((rows, rows)),
            far_out((neighbours, rows), jnp.int32),
            far_out((neighbours, rows), jnp.float32),
            near_out((rows, width)),
        ],
        [SMEM, VMEM, VMEM, HBM],
        [VMEM] * 4,
        [pltpu.VMEM((neighbours, rows), jnp.float32), sems],
        flops=neighbours * rows * rows,
    )(far_in(tile_blocks), far_in(neighbor_pos.T), far_in(edge_weight.T), far_in(seeds))
    sent_a, sent_b, *sent_planes = call(
        pick_kernel,
        "pick",
        [far_out((count, wide)), far_out((count, width - wide))] + [plane_shape] * planes,
        [SMEM, VMEM, VMEM, HBM],
        [HBM, HBM] + [VMEM] * planes,
        [
            pltpu.VMEM((count, rows), bf16),
            pltpu.VMEM((count, wide), bf16),
            pltpu.VMEM((count, width - wide), bf16),
            sems((1 + n_b,)),
        ],
        flops=2 * count * rows * width,
    )(me, asked, near_seeds, far_in(own))
    got_planes = across(sent_planes, peers)
    received_b = exchange(sent_b, peers)
    got_pairs = within(got_planes, peers, slots)
    far, picked_far, sent_base = call(
        far_kernel,
        "far",
        [far_out((rows, count)), near_out((count, count)), near_out((count, width))],
        [VMEM] * 7 + [ANY],
        [VMEM] * 3,
        [
            pltpu.VMEM((count, rows), bf16),
            pltpu.VMEM((count, rows), bf16),
            pltpu.VMEM((neighbours, rows), jnp.float32),
        ],
        flops=2 * rows * count * (count + rows + width) + neighbours * rows * count,
    )(
        asked,
        far_in(own),
        far_in(column),
        far_in(share),
        far_in(seeds),
        far_in(sent_a),
        far_in(sent_b),
        got_pairs[0],
    )
    received_a, *sent_planes = call(
        functools.partial(send_a_kernel, slots=slots),
        "send_a",
        [far_out((count, wide))] + [plane_shape] * planes,
        [SMEM] + [VMEM] * (2 + GROUP // 2),
        [HBM] + [VMEM] * planes,
        [pltpu.VMEM((count, wide), bf16), pltpu.VMEM((count, wide), bf16), sems],
        flops=2 * count * count * wide,
    )(me, picked_far, sent_base, *got_pairs)
    got_planes = across(sent_planes, peers)
    sent_b, received_b = call(
        send_b_kernel,
        "send_b",
        [far_out((count, width - wide)), far_out((count, width - wide))],
        [VMEM] * 3 + [ANY],
        [HBM, HBM],
        [pltpu.VMEM((count, width - wide), bf16), sems((1 + n_b,))],
        flops=2 * count * count * (width - wide),
    )(picked_far, sent_base, received_b, sent_planes[0])
    last_b = exchange(sent_b, peers)
    got_pairs = within(got_planes, peers, slots)
    next_base, rest, near_far = call(
        labels_kernel,
        "labels",
        [
            near_out((rows, width)),
            near_out((rows, width), jnp.float8_e4m3fn),
            near_out((rows, count)),
        ],
        [VMEM] * 5 + [ANY],
        [VMEM] * 3,
        flops=2 * rows * (count + 2 * rows) * width,
    )(
        far_in(own),
        far_in(far),
        far_in(seeds),
        far_in(received_a),
        far_in(received_b),
        got_pairs[0],
    )
    return call(
        functools.partial(last_kernel, slots=slots),
        "last",
        far_out((rows, width)),
        [SMEM] + [VMEM] * (4 + GROUP // 2),
        HBM,
        [pltpu.VMEM((count, wide), bf16), pltpu.VMEM((rows, width), bf16), sems((n_all,))],
        flops=2 * rows * count * width,
    )(me, near_far, next_base, rest, last_b, *got_pairs)


def solution(mesh):
    in_specs = (
        P(("parts", "rows"), "cls"),
        P(("parts", "rows"), None),
        P(("parts", "rows"), None),
        P(("parts", "rows"), None),
        P(("parts", "rows"), None, None),
    )
    out_specs = P(("parts", "rows"), "cls")
    return jax.shard_map(
        on_device, mesh=mesh, in_specs=in_specs, out_specs=out_specs, check_vma=False
    )
```

time: 131 us -> 75.5 us (0.58)
  other arithmetic: 30.4 us -> 0 us
  local copies, waits for them, and re-layouts: 31.5 us -> 1.38 us
  blocking collectives: 29.6 us -> 0 us
  Pallas kernels: 0 us -> 25.5 us
  starting transfers between devices: 9.94 us -> 33.7 us
  matrix products: 17.6 us -> 0 us
  waiting for transfers between devices: 10.8 us -> 14.3 us
    all_to_all x1 -> x0, blocking collectives: 29.6 us -> none  [on_device(): lax.all_to_all(outgoing, 'rows', split_axis=0, concat_axis=0, tiled=True)]
    pallas_call x0 -> x11, Pallas kernels: none -> 25.5 us  [the longest x1 6.38 us: on_device(): call(far_kernel, 'far', [far_out((rows, count)), near_out((count, count))...]
    gather x10 -> x0, local copies, waits for them, and re-layouts: 25.1 us -> none  [the longest x8 18.2 us: body_one_block(): operand = ext_blocks[block_list].reshape(tile_count * BLK, width)]
    ppermute x0 -> x14, starting transfers between devices: none -> 18.2 us  [swap(): return lax.ppermute(x, 'rows', [(i, i ^ distance) for i in range(peers)])]
    dot_general x8 -> x0, matrix products: 17.6 us -> none  [body_one_block(): return jnp.dot(tile_row, operand, preferred_element_type=jnp.float32)]
    reduce_sum x13 -> x0, other arithmetic: 16.5 us -> none  [the longest x12 15.6 us: build_one_block(): jnp.sum(jnp.where(hits, weights[:, first:last, None], 0.0), axis=1)]
    ppermute x0 -> x14, waiting for transfers between devices: none -> 8.09 us  [swap(): return lax.ppermute(x, 'rows', [(i, i ^ distance) for i in range(peers)])]
    all_to_all x2 -> x3, starting transfers between devices: 9.94 us -> 15.6 us  [the longest x2 8.28 us: exchange(): got = lax.all_to_all(sent, 'rows', split_axis=0, concat_axis=0, tiled=True)]
  transfers between devices with their start and end apart: 2 -> 17, of which waited for: 2 -> 7; matrix products, arithmetic and copies ran while one was open for 17% -> 0% of each run, Pallas kernels for 0% -> 28%
where the time goes in v6:
time: 75.5 us; the launch traced here: 75 us
  starting transfers between devices  33.7 us (45%)
  Pallas kernels  25.5 us (34%)
  waiting for transfers between devices  14.3 us (19%)
  local copies, waits for them, and re-layouts  1.38 us (2%)
    ppermute x14, starting transfers between devices, swap(): return lax.ppermute(x, 'rows', [(i, i ^ distance) for i in range(peers)])  18.2 us
    all_to_all x2, starting transfers between devices, exchange(): got = lax.all_to_all(sent, 'rows', split_axis=0, concat_axis=0, tiled=True)  8.28 us
    ppermute x14, waiting for transfers between devices, swap(): return lax.ppermute(x, 'rows', [(i, i ^ distance) for i in range(peers)])  8.09 us
    all_to_all x1, starting transfers between devices, on_device(): lax.all_to_all(wanted.reshape(peers, 1, slots), 'rows', split_axis=0, con...  7.3 us
    pallas_call x1, Pallas kernels, on_device(): call(far_kernel, 'far', [far_out((rows, count)), near_out((count, count))...  6.38 us
    pallas_call x1, Pallas kernels, on_device(): call(labels_kernel, 'labels', [near_out((rows, width)), near_out((rows, w...  6.21 us
    pallas_call x1, Pallas kernels, on_device(): call(own_tiles_kernel, 'own_tiles', [far_out((rows, rows)), far_out((neig...  5.04 us
    all_to_all x2, waiting for transfers between devices, exchange(): got = lax.all_to_all(sent, 'rows', split_axis=0, concat_axis=0, tiled=True)  4.15 us
  transfers between devices with their start and end apart: 17, of which 7 were waited for; matrix products, arithmetic and copies ran while one was open for 0% of the time, Pallas kernels for 28%

profile of v6, /device:TPU:0, one launch (start us, length us, event | category | flops | bytes accessed | tf_op | source)
XLA Modules:
  0.0 75.0 jit_solution(14890503580602496804)
XLA Ops:
  0.0 1.4 %copy.6 = s32[1,32,16]{2,1,0:T(8,128)} copy(s32[1,32,16]{1,2,0:T(8,128)} %param.9) | data formatting | bytes 4096 | tf_op args[4]
  1.4 7.3 %all-to-all-start = ((s32[32,1,16]{2,1,0:T(1,128)}), s32[32,1,16]{2,1,0:T(1,128)S(1)}, u32[]{:S(2)}, u32[]{:S(2)}) async-start(s32[32,1,16]{2,1,0:T(1,128)} %bitcast.3), calls=%async_computation | async-start | bytes 32768 | tf_op jit(solution)/shard_map/all_to_all | solution.py:350
  8.7 5.0 %own_tiles.1 = (bf16[512,512]{1,0:T(8,128)(2,1)}, s32[50,512]{1,0:T(8,128)}, f32[50,512]{1,0:T(8,128)}, bf16[512,1024]{1,0:T(8,128)(2,1)S(1)}) custom-call(s32[4,8]{1,0:T(4,128)} %blocks_ref.1, s32[50,512]{1,0:T(8,128)} %bitcast.10, s32[50,512]{1,0:T(8,128)} %bitcast.11, bf16[512,1024]{1,0:T(8,128)(2,1)} %seeds_ref.3), custom_call_target="tpu_custom_call" | custom-call | flops 13107200 | tf_op jit(solution)/shard_map/own_tiles/pallas_call | solution.py:353
  13.7 2.0 %all-to-all-done.asked_ref = s32[32,1,16]{2,1,0:T(1,128)S(1)} async-done(((s32[32,1,16]{2,1,0:T(1,128)}), s32[32,1,16]{2,1,0:T(1,128)S(1)}, u32[]{:S(2)}, u32[]{:S(2)}) %all-to-all-start) | async-done | bytes 2080 | tf_op jit(solution)/shard_map/all_to_all | solution.py:350
  15.8 0.0 copy-start
  15.8 1.7 %pick.1 = (bf16[512,384]{1,0:T(8,128)(2,1)}, bf16[512,640]{1,0:T(8,128)(2,1)}, bf16[128,384]{1,0:T(8,128)(2,1)S(1)}, bf16[128,384]{1,0:T(8,128)(2,1)S(1)}, bf16[...) custom-call(s32[1]{0:T(128)} %bitcast.me_ref, s32[32,1,16]{2,1,0:T(1,128)S(1)} %all-to-all-done.asked_ref, ...), custom_call_target="tpu_custom_call" | custom-call | flops 536870912 | tf_op jit(solution)/shard_map/pick/pallas_call | solution.py:367
  17.5 0.0 copy-done
  17.5 0.6 collective-permute-start
  18.1 1.6 %collective-permute-start.1 = (bf16[128,384]{1,0:T(8,128)(2,1)S(1)}, bf16[128,384]{1,0:T(8,128)(2,1)S(1)}, u32[]{:S(2)}, u32[]{:S(2)}) collective-permute-start(bf16[128,384]{1,0:T(8,128)(2,1)S(1)} %get-tuple-element.44), channel_id=1, source_target_pairs={{0,16},{1,17},{2,18},{3,19},{4,20},{5,21},{6,22},{7,23},{8,24},{9,... | collective-permute-start | bytes 294920 | tf_op jit(solution)/shard_map/ppermute | solution.py:299
  19.7 2.2 %collective-permute-start.2 = (bf16[128,384]{1,0:T(8,128)(2,1)S(1)}, bf16[128,384]{1,0:T(8,128)(2,1)S(1)}, u32[]{:S(2)}, u32[]{:S(2)}) collective-permute-start(bf16[128,384]{1,0:T(8,128)(2,1)S(1)} %get-tuple-element.45), channel_id=1, source_target_pairs={{0,24},{1,25},{2,26},{3,27},{4,28},{5,29},{6,30},{7,31},{8,16},{9,... | collective-permute-start | bytes 294920 | tf_op jit(solution)/shard_map/ppermute | solution.py:299
  21.9 3.9 %all-to-all-start.1 = ((bf16[32,16,640]{2,1,0:T(8,128)(2,1)}), bf16[32,16,640]{2,1,0:T(8,128)(2,1)}, u32[]{:S(2)}, u32[]{:S(2)}) async-start(bf16[32,16,640]{2,1,0:T(8,128)(2,1)} %bitcast.8), calls=%async_computation.1 | async-start | bytes 1310720 | tf_op jit(solution)/shard_map/all_to_all | solution.py:305
  25.9 0.0 collective-permute-done.refs_1_
  25.9 2.5 %collective-permute-done.1.refs_2_ = bf16[128,384]{1,0:T(8,128)(2,1)S(1)} collective-permute-done((bf16[128,384]{1,0:T(8,128)(2,1)S(1)}, bf16[128,384]{1,0:T(8,128)(2,1)S(1)}, u32[]{:S(2)}, u32[]{:S(2)}) %collective-permute-start.1) | collective-permute-done | bytes 98336 | tf_op jit(solution)/shard_map/ppermute | solution.py:299
  28.4 0.0 collective-permute-done.2.refs_3_
  28.5 0.0 copy-start.1
  28.5 0.1 collective-permute-start.3
  28.5 1.4 %collective-permute-done.3.refs_4_ = bf16[256,384]{1,0:T(8,128)(2,1)S(1)} collective-permute-done((bf16[256,384]{1,0:T(8,128)(2,1)S(1)}, bf16[256,384]{1,0:T(8,128)(2,1)S(1)}, u32[]{:S(2)}, u32[]{:S(2)}) %collective-permute-start.3) | collective-permute-done | bytes 196640 | tf_op jit(solution)/shard_map/ppermute | solution.py:299
  30.0 1.2 %collective-permute-start.4 = (bf16[128,384]{1,0:T(8,128)(2,1)S(1)}, bf16[128,384]{1,0:T(8,128)(2,1)S(1)}, u32[]{:S(2)}, u32[]{:S(2)}) collective-permute-start(bf16[128,384]{1,0:T(8,128)(2,1)S(1)} %get-tuple-element.50), channel_id=1, source_target_pairs={{0,2},{1,3},{2,0},{3,1},{4,6},{5,7},{6,4},{7,5},{8,10},{9,11},{10,... | collective-permute-start | bytes 294920 | tf_op jit(solution)/shard_map/ppermute | solution.py:299
  31.2 1.4 %collective-permute-start.5 = (bf16[128,384]{1,0:T(8,128)(2,1)S(1)}, bf16[128,384]{1,0:T(8,128)(2,1)S(1)}, u32[]{:S(2)}, u32[]{:S(2)}) collective-permute-start(bf16[128,384]{1,0:T(8,128)(2,1)S(1)} %get-tuple-element.51), channel_id=1, source_target_pairs={{0,4},{1,5},{2,6},{3,7},{4,0},{5,1},{6,2},{7,3},{8,12},{9,13},{10,... | collective-permute-start | bytes 294920 | tf_op jit(solution)/shard_map/ppermute | solution.py:299
  32.6 1.0 %collective-permute-start.6 = (bf16[128,384]{1,0:T(8,128)(2,1)S(1)}, bf16[128,384]{1,0:T(8,128)(2,1)S(1)}, u32[]{:S(2)}, u32[]{:S(2)}) collective-permute-start(bf16[128,384]{1,0:T(8,128)(2,1)S(1)} %get-tuple-element.52), channel_id=1, source_target_pairs={{0,6},{1,7},{2,4},{3,5},{4,2},{5,3},{6,0},{7,1},{8,14},{9,15},{10,... | collective-permute-start | bytes 294920 | tf_op jit(solution)/shard_map/ppermute | solution.py:299
  33.6 0.0 copy-done.1
  33.6 6.4 %far.1 = (bf16[512,512]{1,0:T(8,128)(2,1)}, bf16[512,512]{1,0:T(8,128)(2,1)S(1)}, bf16[512,1024]{1,0:T(8,128)(2,1)S(1)}) custom-call(s32[32,1,16]{2,1,0:T(1,128)S(1)} %copy-done.1, bf16[512,512]{1,0:T(8,128)(2,1)} %get-tuple-element.36.after_ref.own_ref, s32[50,512]{1,0:T(8,128)} %get-tuple-element.37.column_ref, f32[50,512]{1,0:T(8,128)} %get-tuple-element.38.share_ref, ...), custom_call_target="tpu_custom_call" | custom-call | flops 1086849024 | tf_op jit(solution)/shard_map/far/pallas_call | solution.py:384
  40.0 0.0 collective-permute-done.4.refs_1_
  40.0 0.5 collective-permute-done.5.refs_2_
  40.4 0.0 collective-permute-done.6.refs_3_
  40.4 0.8 %send_a.1 = (bf16[512,384]{1,0:T(8,128)(2,1)}, bf16[128,384]{1,0:T(8,128)(2,1)S(1)}, bf16[128,384]{1,0:T(8,128)(2,1)S(1)}, bf16[128,384]{1,0:T(8,128)(2,1)S(1)}, bf16[128,384]{1,0:T(8,128)(2,1)S(1)}) custom-call(s32[1]{0:T(128)} %bitcast.me_ref, bf16[512,512]{1,0:T(8,128)(2,1)S(1)} %get-tuple-element.48.tiles_ref, ...), custom_call_target="tpu_custom_call" | custom-call | flops 201326592 | tf_op jit(solution)/shard_map/send_a/pallas_call | solution.py:406
  41.3 2.2 %collective-permute-start.7 = (bf16[128,384]{1,0:T(8,128)(2,1)S(1)}, bf16[128,384]{1,0:T(8,128)(2,1)S(1)}, u32[]{:S(2)}, u32[]{:S(2)}) collective-permute-start(bf16[128,384]{1,0:T(8,128)(2,1)S(1)} %get-tuple-element.56), channel_id=1, source_target_pairs={{0,8},{1,9},{2,10},{3,11},{4,12},{5,13},{6,14},{7,15},{8,0},{9,1},... | collective-permute-start | bytes 294920 | tf_op jit(solution)/shard_map/ppermute | solution.py:299
  43.4 2.7 %collective-permute-start.8 = (bf16[128,384]{1,0:T(8,128)(2,1)S(1)}, bf16[128,384]{1,0:T(8,128)(2,1)S(1)}, u32[]{:S(2)}, u32[]{:S(2)}) collective-permute-start(bf16[128,384]{1,0:T(8,128)(2,1)S(1)} %get-tuple-element.57), channel_id=1, source_target_pairs={{0,16},{1,17},{2,18},{3,19},{4,20},{5,21},{6,22},{7,23},{8,24},{9,... | collective-permute-start | bytes 294920 | tf_op jit(solution)/shard_map/ppermute | solution.py:299
  46.2 1.4 %collective-permute-start.9 = (bf16[128,384]{1,0:T(8,128)(2,1)S(1)}, bf16[128,384]{1,0:T(8,128)(2,1)S(1)}, u32[]{:S(2)}, u32[]{:S(2)}) collective-permute-start(bf16[128,384]{1,0:T(8,128)(2,1)S(1)} %get-tuple-element.58), channel_id=1, source_target_pairs={{0,24},{1,25},{2,26},{3,27},{4,28},{5,29},{6,30},{7,31},{8,16},{9,... | collective-permute-start | bytes 294920 | tf_op jit(solution)/shard_map/ppermute | solution.py:299
  47.5 0.0 all-to-all-done.1
  47.5 2.4 %send_b.1 = (bf16[512,640]{1,0:T(8,128)(2,1)}, bf16[512,640]{1,0:T(8,128)(2,1)}) custom-call(bf16[512,512]{1,0:T(8,128)(2,1)S(1)} %get-tuple-element.48.tiles_ref, bf16[512,1024]{1,0:T(8,128)(2,1)S(1)} %get-tuple-element.49.base_ref, bf16[512,640]{1,0:T(8,128)(2,1)} %bitcast.5.received_ref, bf16[128,384]{1,0:T(8,128)(2,1)S(1)} %get-tuple-element.54.after_ref.refs_0_), custom_call_target="tpu_custom_call" | custom-call | flops 335544320 | tf_op jit(solution)/shard_map/send_b/pallas_call | solution.py:416
  50.0 4.3 %all-to-all-start.2 = ((bf16[32,16,640]{2,1,0:T(8,128)(2,1)}), bf16[32,16,640]{2,1,0:T(8,128)(2,1)}, u32[]{:S(2)}, u32[]{:S(2)}) async-start(bf16[32,16,640]{2,1,0:T(8,128)(2,1)} %bitcast.9), calls=%async_computation.2 | async-start | bytes 1310720 | tf_op jit(solution)/shard_map/all_to_all | solution.py:305
  54.3 0.0 collective-permute-done.7.refs_1_
  54.4 0.0 collective-permute-done.8.refs_2_
  54.4 0.0 collective-permute-done.9.refs_3_
  54.4 0.3 collective-permute-start.10
  54.7 1.3 %collective-permute-done.10.refs_4_ = bf16[256,384]{1,0:T(8,128)(2,1)S(1)} collective-permute-done((bf16[256,384]{1,0:T(8,128)(2,1)S(1)}, bf16[256,384]{1,0:T(8,128)(2,1)S(1)}, u32[]{:S(2)}, u32[]{:S(2)}) %collective-permute-start.10) | collective-permute-done | bytes 196640 | tf_op jit(solution)/shard_map/ppermute | solution.py:299
  55.9 1.8 %collective-permute-start.11 = (bf16[128,384]{1,0:T(8,128)(2,1)S(1)}, bf16[128,384]{1,0:T(8,128)(2,1)S(1)}, u32[]{:S(2)}, u32[]{:S(2)}) collective-permute-start(bf16[128,384]{1,0:T(8,128)(2,1)S(1)} %get-tuple-element.64), channel_id=1, source_target_pairs={{0,2},{1,3},{2,0},{3,1},{4,6},{5,7},{6,4},{7,5},{8,10},{9,11},{10,... | collective-permute-start | bytes 294920 | tf_op jit(solution)/shard_map/ppermute | solution.py:299
  57.7 1.5 %collective-permute-start.12 = (bf16[128,384]{1,0:T(8,128)(2,1)S(1)}, bf16[128,384]{1,0:T(8,128)(2,1)S(1)}, u32[]{:S(2)}, u32[]{:S(2)}) collective-permute-start(bf16[128,384]{1,0:T(8,128)(2,1)S(1)} %get-tuple-element.65), channel_id=1, source_target_pairs={{0,4},{1,5},{2,6},{3,7},{4,0},{5,1},{6,2},{7,3},{8,12},{9,13},{10,... | collective-permute-start | bytes 294920 | tf_op jit(solution)/shard_map/ppermute | solution.py:299
  59.2 0.3 collective-permute-start.13
  59.5 6.2 %labels.1 = (bf16[512,1024]{1,0:T(8,128)(2,1)S(1)}, f8e4m3fn[512,1024]{1,0:T(32,128)(4,1)S(1)}, bf16[512,512]{1,0:T(8,128)(2,1)S(1)}) custom-call(bf16[512,512]{1,0:T(8,128)(2,1)} %get-tuple-element.36.after_ref.own_ref, bf16[512,512]{1,0:T(8,128)(2,1)} %get-tuple-element.47.far_ref, bf16[512,1024]{1,0:T(8,128)(2,1)} %seeds_ref.3, ...), custom_call_target="tpu_custom_call" | custom-call | flops 1610612736 | tf_op jit(solution)/shard_map/labels/pallas_call | solution.py:427
  65.7 0.0 collective-permute-done.11.refs_1_
  65.7 0.0 collective-permute-done.12.refs_2_
  65.7 2.4 %collective-permute-done.13.refs_3_ = bf16[128,384]{1,0:T(8,128)(2,1)S(1)} collective-permute-done((bf16[128,384]{1,0:T(8,128)(2,1)S(1)}, bf16[128,384]{1,0:T(8,128)(2,1)S(1)}, u32[]{:S(2)}, u32[]{:S(2)}) %collective-permute-start.13) | collective-permute-done | bytes 98336 | tf_op jit(solution)/shard_map/ppermute | solution.py:299
  68.1 4.1 %all-to-all-done.2 = bf16[32,16,640]{2,1,0:T(8,128)(2,1)} async-done(((bf16[32,16,640]{2,1,0:T(8,128)(2,1)}), bf16[32,16,640]{2,1,0:T(8,128)(2,1)}, u32[]{:S(2)}, u32[]{:S(2)}) %all-to-all-start.2) | async-done | bytes 655392 | tf_op jit(solution)/shard_map/all_to_all | solution.py:305
  72.3 2.8 %last.1 = bf16[512,1024]{1,0:T(8,128)(2,1)} custom-call(s32[1]{0:T(128)} %bitcast.me_ref, bf16[512,512]{1,0:T(8,128)(2,1)S(1)} %get-tuple-element.60.tiles_ref, bf16[512,1024]{1,0:T(8,128)(2,1)S(1)} %get-tuple-element.61.base_ref, f8e4m3fn[512,1024]{1,0:T(32,128)(4,1)S(1)} %get-tuple-element.62.rest_ref, bf16[512,640]{1,0:T(8,128)(2,1)} %bitcast.7.received_b_ref, ...), custom_call_target="tpu_custom_call" | custom-call | flops 536870912 | tf_op jit(solution)/shard_map/last/pallas_call | solution.py:446
  (4 shorter events, 0.1 us)
Async XLA Ops:
  1.4 14.4 %all-to-all-start = ((s32[32,1,16]{2,1,0:T(1,128)}), s32[32,1,16]{2,1,0:T(1,128)S(1)}, u32[]{:S(2)}, u32[]{:S(2)}) async-start(s32[32,1,16]{2,1,0:T(1,128)} %bitcast.3), calls=%async_computation | async-start | bytes 32768 | tf_op jit(solution)/shard_map/all_to_all | solution.py:350
  15.8 1.7 %copy-start = (s32[32,1,16]{2,1,0:T(1,128)}, s32[32,1,16]{2,1,0:T(1,128)S(1)}, u32[]{:S(2)}) copy-start(s32[32,1,16]{2,1,0:T(1,128)S(1)} %all-to-all-done.asked_ref) | copy-start | bytes 6148
  17.5 8.4 %collective-permute-start = (bf16[128,384]{1,0:T(8,128)(2,1)S(1)}, bf16[128,384]{1,0:T(8,128)(2,1)S(1)}, u32[]{:S(2)}, u32[]{:S(2)}) collective-permute-start(bf16[128,384]{1,0:T(8,128)(2,1)S(1)} %get-tuple-element.43), channel_id=1, source_target_pairs={{0,8},{1,9},{2,10},{3,11},{4,12},{5,13},{6,14},{7,15},{8,0},{9,1},... | collective-permute-start | bytes 294920 | tf_op jit(solution)/shard_map/ppermute | solution.py:299
  18.1 10.3 %collective-permute-start.1 = (bf16[128,384]{1,0:T(8,128)(2,1)S(1)}, bf16[128,384]{1,0:T(8,128)(2,1)S(1)}, u32[]{:S(2)}, u32[]{:S(2)}) collective-permute-start(bf16[128,384]{1,0:T(8,128)(2,1)S(1)} %get-tuple-element.44), channel_id=1, source_target_pairs={{0,16},{1,17},{2,18},{3,19},{4,20},{5,21},{6,22},{7,23},{8,24},{9,... | collective-permute-start | bytes 294920 | tf_op jit(solution)/shard_map/ppermute | solution.py:299
  19.7 8.7 %collective-permute-start.2 = (bf16[128,384]{1,0:T(8,128)(2,1)S(1)}, bf16[128,384]{1,0:T(8,128)(2,1)S(1)}, u32[]{:S(2)}, u32[]{:S(2)}) collective-permute-start(bf16[128,384]{1,0:T(8,128)(2,1)S(1)} %get-tuple-element.45), channel_id=1, source_target_pairs={{0,24},{1,25},{2,26},{3,27},{4,28},{5,29},{6,30},{7,31},{8,16},{9,... | collective-permute-start | bytes 294920 | tf_op jit(solution)/shard_map/ppermute | solution.py:299
  21.9 25.6 %all-to-all-start.1 = ((bf16[32,16,640]{2,1,0:T(8,128)(2,1)}), bf16[32,16,640]{2,1,0:T(8,128)(2,1)}, u32[]{:S(2)}, u32[]{:S(2)}) async-start(bf16[32,16,640]{2,1,0:T(8,128)(2,1)} %bitcast.8), calls=%async_computation.1 | async-start | bytes 1310720 | tf_op jit(solution)/shard_map/all_to_all | solution.py:305
  28.5 5.1 %copy-start.1 = (s32[32,1,16]{2,1,0:T(1,128)S(1)}, s32[32,1,16]{2,1,0:T(1,128)}, u32[]{:S(2)}) copy-start(s32[32,1,16]{2,1,0:T(1,128)} %copy-done) | copy-start | bytes 6148
  28.5 1.5 %collective-permute-start.3 = (bf16[256,384]{1,0:T(8,128)(2,1)S(1)}, bf16[256,384]{1,0:T(8,128)(2,1)S(1)}, u32[]{:S(2)}, u32[]{:S(2)}) collective-permute-start(bf16[256,384]{1,0:T(8,128)(2,1)S(1)} %gather.2), channel_id=1, source_target_pairs={{0,1},{1,0},{2,3},{3,2},{4,5},{5,4},{6,7},{7,6},{8,9},{9,8},{10,11... | collective-permute-start | bytes 589832 | tf_op jit(solution)/shard_map/ppermute | solution.py:299
  30.0 9.9 %collective-permute-start.4 = (bf16[128,384]{1,0:T(8,128)(2,1)S(1)}, bf16[128,384]{1,0:T(8,128)(2,1)S(1)}, u32[]{:S(2)}, u32[]{:S(2)}) collective-permute-start(bf16[128,384]{1,0:T(8,128)(2,1)S(1)} %get-tuple-element.50), channel_id=1, source_target_pairs={{0,2},{1,3},{2,0},{3,1},{4,6},{5,7},{6,4},{7,5},{8,10},{9,11},{10,... | collective-permute-start | bytes 294920 | tf_op jit(solution)/shard_map/ppermute | solution.py:299
  31.2 9.3 %collective-permute-start.5 = (bf16[128,384]{1,0:T(8,128)(2,1)S(1)}, bf16[128,384]{1,0:T(8,128)(2,1)S(1)}, u32[]{:S(2)}, u32[]{:S(2)}) collective-permute-start(bf16[128,384]{1,0:T(8,128)(2,1)S(1)} %get-tuple-element.51), channel_id=1, source_target_pairs={{0,4},{1,5},{2,6},{3,7},{4,0},{5,1},{6,2},{7,3},{8,12},{9,13},{10,... | collective-permute-start | bytes 294920 | tf_op jit(solution)/shard_map/ppermute | solution.py:299
  32.6 7.9 %collective-permute-start.6 = (bf16[128,384]{1,0:T(8,128)(2,1)S(1)}, bf16[128,384]{1,0:T(8,128)(2,1)S(1)}, u32[]{:S(2)}, u32[]{:S(2)}) collective-permute-start(bf16[128,384]{1,0:T(8,128)(2,1)S(1)} %get-tuple-element.52), channel_id=1, source_target_pairs={{0,6},{1,7},{2,4},{3,5},{4,2},{5,3},{6,0},{7,1},{8,14},{9,15},{10,... | collective-permute-start | bytes 294920 | tf_op jit(solution)/shard_map/ppermute | solution.py:299
  41.3 13.1 %collective-permute-start.7 = (bf16[128,384]{1,0:T(8,128)(2,1)S(1)}, bf16[128,384]{1,0:T(8,128)(2,1)S(1)}, u32[]{:S(2)}, u32[]{:S(2)}) collective-permute-start(bf16[128,384]{1,0:T(8,128)(2,1)S(1)} %get-tuple-element.56), channel_id=1, source_target_pairs={{0,8},{1,9},{2,10},{3,11},{4,12},{5,13},{6,14},{7,15},{8,0},{9,1},... | collective-permute-start | bytes 294920 | tf_op jit(solution)/shard_map/ppermute | solution.py:299
  43.4 10.9 %collective-permute-start.8 = (bf16[128,384]{1,0:T(8,128)(2,1)S(1)}, bf16[128,384]{1,0:T(8,128)(2,1)S(1)}, u32[]{:S(2)}, u32[]{:S(2)}) collective-permute-start(bf16[128,384]{1,0:T(8,128)(2,1)S(1)} %get-tuple-element.57), channel_id=1, source_target_pairs={{0,16},{1,17},{2,18},{3,19},{4,20},{5,21},{6,22},{7,23},{8,24},{9,... | collective-permute-start | bytes 294920 | tf_op jit(solution)/shard_map/ppermute | solution.py:299
  46.2 8.2 %collective-permute-start.9 = (bf16[128,384]{1,0:T(8,128)(2,1)S(1)}, bf16[128,384]{1,0:T(8,128)(2,1)S(1)}, u32[]{:S(2)}, u32[]{:S(2)}) collective-permute-start(bf16[128,384]{1,0:T(8,128)(2,1)S(1)} %get-tuple-element.58), channel_id=1, source_target_pairs={{0,24},{1,25},{2,26},{3,27},{4,28},{5,29},{6,30},{7,31},{8,16},{9,... | collective-permute-start | bytes 294920 | tf_op jit(solution)/shard_map/ppermute | solution.py:299
  50.0 22.2 %all-to-all-start.2 = ((bf16[32,16,640]{2,1,0:T(8,128)(2,1)}), bf16[32,16,640]{2,1,0:T(8,128)(2,1)}, u32[]{:S(2)}, u32[]{:S(2)}) async-start(bf16[32,16,640]{2,1,0:T(8,128)(2,1)} %bitcast.9), calls=%async_computation.2 | async-start | bytes 1310720 | tf_op jit(solution)/shard_map/all_to_all | solution.py:305
  54.4 1.5 %collective-permute-start.10 = (bf16[256,384]{1,0:T(8,128)(2,1)S(1)}, bf16[256,384]{1,0:T(8,128)(2,1)S(1)}, u32[]{:S(2)}, u32[]{:S(2)}) collective-permute-start(bf16[256,384]{1,0:T(8,128)(2,1)S(1)} %gather.3), channel_id=1, source_target_pairs={{0,1},{1,0},{2,3},{3,2},{4,5},{5,4},{6,7},{7,6},{8,9},{9,8},{10,11... | collective-permute-start | bytes 589832 | tf_op jit(solution)/shard_map/ppermute | solution.py:299
  55.9 9.8 %collective-permute-start.11 = (bf16[128,384]{1,0:T(8,128)(2,1)S(1)}, bf16[128,384]{1,0:T(8,128)(2,1)S(1)}, u32[]{:S(2)}, u32[]{:S(2)}) collective-permute-start(bf16[128,384]{1,0:T(8,128)(2,1)S(1)} %get-tuple-element.64), channel_id=1, source_target_pairs={{0,2},{1,3},{2,0},{3,1},{4,6},{5,7},{6,4},{7,5},{8,10},{9,11},{10,... | collective-permute-start | bytes 294920 | tf_op jit(solution)/shard_map/ppermute | solution.py:299
  57.7 8.0 %collective-permute-start.12 = (bf16[128,384]{1,0:T(8,128)(2,1)S(1)}, bf16[128,384]{1,0:T(8,128)(2,1)S(1)}, u32[]{:S(2)}, u32[]{:S(2)}) collective-permute-start(bf16[128,384]{1,0:T(8,128)(2,1)S(1)} %get-tuple-element.65), channel_id=1, source_target_pairs={{0,4},{1,5},{2,6},{3,7},{4,0},{5,1},{6,2},{7,3},{8,12},{9,13},{10,... | collective-permute-start | bytes 294920 | tf_op jit(solution)/shard_map/ppermute | solution.py:299
  59.2 8.9 %collective-permute-start.13 = (bf16[128,384]{1,0:T(8,128)(2,1)S(1)}, bf16[128,384]{1,0:T(8,128)(2,1)S(1)}, u32[]{:S(2)}, u32[]{:S(2)}) collective-permute-start(bf16[128,384]{1,0:T(8,128)(2,1)S(1)} %get-tuple-element.66), channel_id=1, source_target_pairs={{0,6},{1,7},{2,4},{3,5},{4,2},{5,3},{6,0},{7,1},{8,14},{9,15},{10,... | collective-permute-start | bytes 294920 | tf_op jit(solution)/shard_map/ppermute | solution.py:299

commit v7 on v6

--- a/solution.py
+++ b/solution.py
@@ -17,7 +17,7 @@
 KEEP = 0.85
 ANCHOR = 0.15
 REST_SCALE = 4096.0
-LONG = 10**12
+LONG = 4 * 10**10
 
 SMEM = pl.BlockSpec(memory_space=pltpu.SMEM)
 VMEM = pl.BlockSpec(memory_space=pltpu.VMEM)
@@ -38,16 +38,15 @@
     return pltpu.VMEM(shape, dtype) if small else jax.ShapeDtypeStruct(shape, dtype)
 
 
-def call(kernel, name, out_shape, in_specs, out_specs, scratch_shapes=(), flops=0, aliases=None):
+def call(kernel, name, out_shape, in_specs, out_specs, scratch_shapes=(), flops=0, nbytes=0):
     return pl.pallas_call(
         kernel,
         out_shape=out_shape,
         in_specs=in_specs,
         out_specs=out_specs,
         scratch_shapes=scratch_shapes,
-        input_output_aliases=aliases or {},
         compiler_params=pltpu.CompilerParams(vmem_limit_bytes=VMEM_LIMIT),
-        cost_estimate=pl.CostEstimate(flops=flops, bytes_accessed=0, transcendentals=0),
+        cost_estimate=pl.CostEstimate(flops=flops, bytes_accessed=nbytes, transcendentals=0),
         name=name,
     )
 
@@ -144,12 +143,30 @@
 
 
 def own_tiles_kernel(
-    blocks_ref, pos_ref, weight_ref, seeds_hbm, own_ref, column_ref, share_ref, near_ref, spot_ref, sem
+    blocks_ref,
+    pos_ref,
+    weight_ref,
+    seeds_hbm,
+    own_hbm,
+    column_hbm,
+    share_hbm,
+    near_ref,
+    own_ref,
+    column_ref,
+    share_ref,
+    spot_ref,
+    sems,
 ):
-    copy = push(seeds_hbm, near_ref, sem)
+    copies = [push(seeds_hbm, near_ref, sems.at[0])]
     fill_edges(blocks_ref, pos_ref, weight_ref, column_ref, share_ref)
-    fill_tiles(column_ref, share_ref, own_ref, spot_ref, 0, (0, own_ref.shape[1] // BLK))
-    copy.wait()
+    copies.append(push(column_ref, column_hbm, sems.at[1]))
+    copies.append(push(share_ref, share_hbm, sems.at[2]))
+    for i in range(own_ref.shape[1] // BLK):
+        cols = slice(i * BLK, (i + 1) * BLK)
+        fill_tiles(column_ref, share_ref, own_ref, spot_ref, 0, (i, i + 1))
+        copies.append(push(own_ref.at[:, cols], own_hbm.at[:, cols], sems.at[3 + i]))
+    for copy in copies:
+        copy.wait()
 
 
 def pick_kernel(me_ref, asked_ref, seeds_ref, after_ref, out_a, out_b, *refs):
@@ -360,8 +377,14 @@
             near_out((rows, width)),
         ],
         [SMEM, VMEM, VMEM, HBM],
-        [VMEM] * 4,
-        [pltpu.VMEM((neighbours, rows), jnp.float32), sems],
+        [HBM, HBM, HBM, VMEM],
+        [
+            pltpu.VMEM((rows, rows), bf16),
+            pltpu.VMEM((neighbours, rows), jnp.int32),
+            pltpu.VMEM((neighbours, rows), jnp.float32),
+            pltpu.VMEM((neighbours, rows), jnp.float32),
+            sems((3 + rows // BLK,)),
+        ],
         flops=neighbours * rows * rows,
     )(far_in(tile_blocks), far_in(neighbor_pos.T), far_in(edge_weight.T), far_in(seeds))
     sent_a, sent_b, *sent_planes = call(
@@ -421,6 +444,7 @@
         [HBM, HBM],
         [pltpu.VMEM((count, width - wide), bf16), sems((1 + n_b,))],
         flops=2 * count * count * (width - wide),
+        nbytes=2 * count * (3 * (width - wide) + count + width),
     )(picked_far, sent_base, received_b, sent_planes[0])
     last_b = exchange(sent_b, peers)
     got_pairs = within(got_planes, peers, slots)
@@ -451,6 +475,7 @@
         HBM,
         [pltpu.VMEM((count, wide), bf16), pltpu.VMEM((rows, width), bf16), sems((n_all,))],
         flops=2 * rows * count * width,
+        nbytes=2 * rows * count + 5 * rows * width + 2 * count * width,
     )(me, near_far, next_base, rest, last_b, *got_pairs)
 
 

time: 75.5 us -> 72.9 us (0.966)
  Pallas kernels: 25.5 us -> 23.1 us
    pallas_call x1, Pallas kernels: 2.45 us -> 1.36 us  [on_device(): call(send_b_kernel, 'send_b', [far_out((count, width - wide)), far_out((c...]
    pallas_call x1, Pallas kernels: 2.78 us -> 1.7 us  [on_device(): call(functools.partial(last_kernel, slots=slots), 'last', far_out((rows,...]
  transfers between devices with their start and end apart: 17 -> 17, of which waited for: 7 -> 8; matrix products, arithmetic and copies ran while one was open for 0% -> 0% of each run, Pallas kernels for 28% -> 27%
where the time goes in v7:
time: 72.9 us; the launch traced here: 72.5 us
  starting transfers between devices  33.1 us (45%)
  Pallas kernels  23.1 us (32%)
  waiting for transfers between devices  14.7 us (20%)
  local copies, waits for them, and re-layouts  1.38 us (2%)
    ppermute x14, starting transfers between devices, swap(): return lax.ppermute(x, 'rows', [(i, i ^ distance) for i in range(peers)])  18 us
    ppermute x14, waiting for transfers between devices, swap(): return lax.ppermute(x, 'rows', [(i, i ^ distance) for i in range(peers)])  8.56 us
    all_to_all x2, starting transfers between devices, exchange(): got = lax.all_to_all(sent, 'rows', split_axis=0, concat_axis=0, tiled=True)  7.88 us
    all_to_all x1, starting transfers between devices, on_device(): lax.all_to_all(wanted.reshape(peers, 1, slots), 'rows', split_axis=0, con...  7.3 us
    pallas_call x1, Pallas kernels, on_device(): call(far_kernel, 'far', [far_out((rows, count)), near_out((count, count))...  6.38 us
    pallas_call x1, Pallas kernels, on_device(): call(labels_kernel, 'labels', [near_out((rows, width)), near_out((rows, w...  6.21 us
    pallas_call x1, Pallas kernels, on_device(): call(own_tiles_kernel, 'own_tiles', [far_out((rows, rows)), far_out((neig...  4.88 us
    all_to_all x2, waiting for transfers between devices, exchange(): got = lax.all_to_all(sent, 'rows', split_axis=0, concat_axis=0, tiled=True)  4 us
  transfers between devices with their start and end apart: 17, of which 8 were waited for; matrix products, arithmetic and copies ran while one was open for 0% of the time, Pallas kernels for 27%

profile of v7, /device:TPU:0, one launch (start us, length us, event | category | flops | bytes accessed | tf_op | source)
XLA Modules:
  0.0 72.5 jit_solution(4381419435566121818)
XLA Ops:
  0.0 1.4 %copy.6 = s32[1,32,16]{2,1,0:T(8,128)} copy(s32[1,32,16]{1,2,0:T(8,128)} %param.9) | data formatting | bytes 4096 | tf_op args[4]
  1.4 7.3 %all-to-all-start = ((s32[32,1,16]{2,1,0:T(1,128)}), s32[32,1,16]{2,1,0:T(1,128)S(1)}, u32[]{:S(2)}, u32[]{:S(2)}) async-start(s32[32,1,16]{2,1,0:T(1,128)} %bitcast.3), calls=%async_computation | async-start | bytes 32768 | tf_op jit(solution)/shard_map/all_to_all | solution.py:367
  8.7 4.9 %own_tiles.1 = (bf16[512,512]{1,0:T(8,128)(2,1)}, s32[50,512]{1,0:T(8,128)}, f32[50,512]{1,0:T(8,128)}, bf16[512,1024]{1,0:T(8,128)(2,1)S(1)}) custom-call(s32[4,8]{1,0:T(4,128)} %blocks_ref.1, s32[50,512]{1,0:T(8,128)} %bitcast.12, s32[50,512]{1,0:T(8,128)} %bitcast.13, bf16[512,1024]{1,0:T(8,128)(2,1)} %seeds_ref.3), custom_call_target="tpu_custom_call" | custom-call | flops 13107200 | tf_op jit(solution)/shard_map/own_tiles/pallas_call | solution.py:370
  13.6 2.2 %all-to-all-done.asked_ref = s32[32,1,16]{2,1,0:T(1,128)S(1)} async-done(((s32[32,1,16]{2,1,0:T(1,128)}), s32[32,1,16]{2,1,0:T(1,128)S(1)}, u32[]{:S(2)}, u32[]{:S(2)}) %all-to-all-start) | async-done | bytes 2080 | tf_op jit(solution)/shard_map/all_to_all | solution.py:367
  15.8 1.7 %pick.1 = (bf16[512,384]{1,0:T(8,128)(2,1)}, bf16[512,640]{1,0:T(8,128)(2,1)}, bf16[128,384]{1,0:T(8,128)(2,1)S(1)}, bf16[128,384]{1,0:T(8,128)(2,1)S(1)}, bf16[...) custom-call(s32[1]{0:T(128)} %bitcast.me_ref, s32[32,1,16]{2,1,0:T(1,128)S(1)} %all-to-all-done.asked_ref, ...), custom_call_target="tpu_custom_call" | custom-call | flops 536870912 | tf_op jit(solution)/shard_map/pick/pallas_call | solution.py:390
  17.5 0.6 collective-permute-start
  18.1 1.4 %collective-permute-start.1 = (bf16[128,384]{1,0:T(8,128)(2,1)S(1)}, bf16[128,384]{1,0:T(8,128)(2,1)S(1)}, u32[]{:S(2)}, u32[]{:S(2)}) collective-permute-start(bf16[128,384]{1,0:T(8,128)(2,1)S(1)} %get-tuple-element.44), channel_id=1, source_target_pairs={{0,16},{1,17},{2,18},{3,19},{4,20},{5,21},{6,22},{7,23},{8,24},{9,... | collective-permute-start | bytes 294920 | tf_op jit(solution)/shard_map/ppermute | solution.py:316
  19.5 2.4 %collective-permute-start.2 = (bf16[128,384]{1,0:T(8,128)(2,1)S(1)}, bf16[128,384]{1,0:T(8,128)(2,1)S(1)}, u32[]{:S(2)}, u32[]{:S(2)}) collective-permute-start(bf16[128,384]{1,0:T(8,128)(2,1)S(1)} %get-tuple-element.45), channel_id=1, source_target_pairs={{0,24},{1,25},{2,26},{3,27},{4,28},{5,29},{6,30},{7,31},{8,16},{9,... | collective-permute-start | bytes 294920 | tf_op jit(solution)/shard_map/ppermute | solution.py:316
  21.9 3.7 %all-to-all-start.1 = ((bf16[32,16,640]{2,1,0:T(8,128)(2,1)}), bf16[32,16,640]{2,1,0:T(8,128)(2,1)S(1)}, u32[]{:S(2)}, u32[]{:S(2)}) async-start(bf16[32,16,640]{2,1,0:T(8,128)(2,1)} %bitcast.10), calls=%async_computation.1 | async-start | bytes 1310720 | tf_op jit(solution)/shard_map/all_to_all | solution.py:322
  25.6 0.0 collective-permute-done.refs_1_
  25.6 2.8 %collective-permute-done.1.refs_2_ = bf16[128,384]{1,0:T(8,128)(2,1)S(1)} collective-permute-done((bf16[128,384]{1,0:T(8,128)(2,1)S(1)}, bf16[128,384]{1,0:T(8,128)(2,1)S(1)}, u32[]{:S(2)}, u32[]{:S(2)}) %collective-permute-start.1) | collective-permute-done | bytes 98336 | tf_op jit(solution)/shard_map/ppermute | solution.py:316
  28.4 0.0 collective-permute-done.2.refs_3_
  28.4 0.1 collective-permute-start.3
  28.5 1.4 %collective-permute-done.3.refs_4_ = bf16[256,384]{1,0:T(8,128)(2,1)S(1)} collective-permute-done((bf16[256,384]{1,0:T(8,128)(2,1)S(1)}, bf16[256,384]{1,0:T(8,128)(2,1)S(1)}, u32[]{:S(2)}, u32[]{:S(2)}) %collective-permute-start.3) | collective-permute-done | bytes 196640 | tf_op jit(solution)/shard_map/ppermute | solution.py:316
  30.0 1.0 %collective-permute-start.4 = (bf16[128,384]{1,0:T(8,128)(2,1)S(1)}, bf16[128,384]{1,0:T(8,128)(2,1)S(1)}, u32[]{:S(2)}, u32[]{:S(2)}) collective-permute-start(bf16[128,384]{1,0:T(8,128)(2,1)S(1)} %get-tuple-element.50), channel_id=1, source_target_pairs={{0,2},{1,3},{2,0},{3,1},{4,6},{5,7},{6,4},{7,5},{8,10},{9,11},{10,... | collective-permute-start | bytes 294920 | tf_op jit(solution)/shard_map/ppermute | solution.py:316
  31.0 1.4 %collective-permute-start.5 = (bf16[128,384]{1,0:T(8,128)(2,1)S(1)}, bf16[128,384]{1,0:T(8,128)(2,1)S(1)}, u32[]{:S(2)}, u32[]{:S(2)}) collective-permute-start(bf16[128,384]{1,0:T(8,128)(2,1)S(1)} %get-tuple-element.51), channel_id=1, source_target_pairs={{0,4},{1,5},{2,6},{3,7},{4,0},{5,1},{6,2},{7,3},{8,12},{9,13},{10,... | collective-permute-start | bytes 294920 | tf_op jit(solution)/shard_map/ppermute | solution.py:316
  32.4 1.1 %collective-permute-start.6 = (bf16[128,384]{1,0:T(8,128)(2,1)S(1)}, bf16[128,384]{1,0:T(8,128)(2,1)S(1)}, u32[]{:S(2)}, u32[]{:S(2)}) collective-permute-start(bf16[128,384]{1,0:T(8,128)(2,1)S(1)} %get-tuple-element.52), channel_id=1, source_target_pairs={{0,6},{1,7},{2,4},{3,5},{4,2},{5,3},{6,0},{7,1},{8,14},{9,15},{10,... | collective-permute-start | bytes 294920 | tf_op jit(solution)/shard_map/ppermute | solution.py:316
  33.5 6.4 %far.1 = (bf16[512,512]{1,0:T(8,128)(2,1)}, bf16[512,512]{1,0:T(8,128)(2,1)S(1)}, bf16[512,1024]{1,0:T(8,128)(2,1)S(1)}) custom-call(s32[32,1,16]{2,1,0:T(1,128)S(1)} %all-to-all-done.asked_ref, bf16[512,512]{1,0:T(8,128)(2,1)} %get-tuple-element.36.after_ref.own_ref, s32[50,512]{1,0:T(8,128)} %get-tuple-element.37.column_ref, ...), custom_call_target="tpu_custom_call" | custom-call | flops 1086849024 | tf_op jit(solution)/shard_map/far/pallas_call | solution.py:407
  39.9 0.0 collective-permute-done.4.refs_1_
  39.9 0.3 collective-permute-done.5.refs_2_
  40.3 0.0 collective-permute-done.6.refs_3_
  40.3 0.8 %send_a.1 = (bf16[512,384]{1,0:T(8,128)(2,1)}, bf16[128,384]{1,0:T(8,128)(2,1)S(1)}, bf16[128,384]{1,0:T(8,128)(2,1)S(1)}, bf16[128,384]{1,0:T(8,128)(2,1)S(1)}, bf16[128,384]{1,0:T(8,128)(2,1)S(1)}) custom-call(s32[1]{0:T(128)} %bitcast.me_ref, bf16[512,512]{1,0:T(8,128)(2,1)S(1)} %get-tuple-element.48.tiles_ref, ...), custom_call_target="tpu_custom_call" | custom-call | flops 201326592 | tf_op jit(solution)/shard_map/send_a/pallas_call | solution.py:429
  41.1 2.2 %collective-permute-start.7 = (bf16[128,384]{1,0:T(8,128)(2,1)S(1)}, bf16[128,384]{1,0:T(8,128)(2,1)S(1)}, u32[]{:S(2)}, u32[]{:S(2)}) collective-permute-start(bf16[128,384]{1,0:T(8,128)(2,1)S(1)} %get-tuple-element.56), channel_id=1, source_target_pairs={{0,8},{1,9},{2,10},{3,11},{4,12},{5,13},{6,14},{7,15},{8,0},{9,1},... | collective-permute-start | bytes 294920 | tf_op jit(solution)/shard_map/ppermute | solution.py:316
  43.2 2.7 %collective-permute-start.8 = (bf16[128,384]{1,0:T(8,128)(2,1)S(1)}, bf16[128,384]{1,0:T(8,128)(2,1)S(1)}, u32[]{:S(2)}, u32[]{:S(2)}) collective-permute-start(bf16[128,384]{1,0:T(8,128)(2,1)S(1)} %get-tuple-element.57), channel_id=1, source_target_pairs={{0,16},{1,17},{2,18},{3,19},{4,20},{5,21},{6,22},{7,23},{8,24},{9,... | collective-permute-start | bytes 294920 | tf_op jit(solution)/shard_map/ppermute | solution.py:316
  46.0 1.4 %collective-permute-start.9 = (bf16[128,384]{1,0:T(8,128)(2,1)S(1)}, bf16[128,384]{1,0:T(8,128)(2,1)S(1)}, u32[]{:S(2)}, u32[]{:S(2)}) collective-permute-start(bf16[128,384]{1,0:T(8,128)(2,1)S(1)} %get-tuple-element.58), channel_id=1, source_target_pairs={{0,24},{1,25},{2,26},{3,27},{4,28},{5,29},{6,30},{7,31},{8,16},{9,... | collective-permute-start | bytes 294920 | tf_op jit(solution)/shard_map/ppermute | solution.py:316
  47.3 0.0 all-to-all-done.1
  47.3 1.4 %send_b.1 = (bf16[512,640]{1,0:T(8,128)(2,1)}, bf16[512,640]{1,0:T(8,128)(2,1)}) custom-call(bf16[512,512]{1,0:T(8,128)(2,1)S(1)} %get-tuple-element.48.tiles_ref, bf16[512,1024]{1,0:T(8,128)(2,1)S(1)} %get-tuple-element.49.base_ref, bf16[512,640]{1,0:T(8,128)(2,1)S(1)} %bitcast.9, bf16[128,384]{1,0:T(8,128)(2,1)S(1)} %get-tuple-element.54.after_ref.refs_0_), custom_call_target="tpu_custom_call" | custom-call | flops 335544320 | bytes 3538944 | tf_op jit(solution)/shard_map/send_b/pallas_call | solution.py:439
  48.7 4.2 %all-to-all-start.2 = ((bf16[32,16,640]{2,1,0:T(8,128)(2,1)}), bf16[32,16,640]{2,1,0:T(8,128)(2,1)S(1)}, u32[]{:S(2)}, u32[]{:S(2)}) async-start(bf16[32,16,640]{2,1,0:T(8,128)(2,1)} %bitcast.11), calls=%async_computation.2 | async-start | bytes 1310720 | tf_op jit(solution)/shard_map/all_to_all | solution.py:322
  52.9 0.0 collective-permute-done.7.refs_1_
  52.9 0.0 collective-permute-done.8.refs_2_
  52.9 0.9 %collective-permute-done.9.refs_3_ = bf16[128,384]{1,0:T(8,128)(2,1)S(1)} collective-permute-done((bf16[128,384]{1,0:T(8,128)(2,1)S(1)}, bf16[128,384]{1,0:T(8,128)(2,1)S(1)}, u32[]{:S(2)}, u32[]{:S(2)}) %collective-permute-start.9) | collective-permute-done | bytes 98336 | tf_op jit(solution)/shard_map/ppermute | solution.py:316
  53.9 0.1 collective-permute-start.10
  53.9 1.4 %collective-permute-done.10.refs_4_ = bf16[256,384]{1,0:T(8,128)(2,1)S(1)} collective-permute-done((bf16[256,384]{1,0:T(8,128)(2,1)S(1)}, bf16[256,384]{1,0:T(8,128)(2,1)S(1)}, u32[]{:S(2)}, u32[]{:S(2)}) %collective-permute-start.10) | collective-permute-done | bytes 196640 | tf_op jit(solution)/shard_map/ppermute | solution.py:316
  55.4 1.2 %collective-permute-start.11 = (bf16[128,384]{1,0:T(8,128)(2,1)S(1)}, bf16[128,384]{1,0:T(8,128)(2,1)S(1)}, u32[]{:S(2)}, u32[]{:S(2)}) collective-permute-start(bf16[128,384]{1,0:T(8,128)(2,1)S(1)} %get-tuple-element.64), channel_id=1, source_target_pairs={{0,2},{1,3},{2,0},{3,1},{4,6},{5,7},{6,4},{7,5},{8,10},{9,11},{10,... | collective-permute-start | bytes 294920 | tf_op jit(solution)/shard_map/ppermute | solution.py:316
  56.6 1.3 %collective-permute-start.12 = (bf16[128,384]{1,0:T(8,128)(2,1)S(1)}, bf16[128,384]{1,0:T(8,128)(2,1)S(1)}, u32[]{:S(2)}, u32[]{:S(2)}) collective-permute-start(bf16[128,384]{1,0:T(8,128)(2,1)S(1)} %get-tuple-element.65), channel_id=1, source_target_pairs={{0,4},{1,5},{2,6},{3,7},{4,0},{5,1},{6,2},{7,3},{8,12},{9,13},{10,... | collective-permute-start | bytes 294920 | tf_op jit(solution)/shard_map/ppermute | solution.py:316
  57.8 1.1 %collective-permute-start.13 = (bf16[128,384]{1,0:T(8,128)(2,1)S(1)}, bf16[128,384]{1,0:T(8,128)(2,1)S(1)}, u32[]{:S(2)}, u32[]{:S(2)}) collective-permute-start(bf16[128,384]{1,0:T(8,128)(2,1)S(1)} %get-tuple-element.66), channel_id=1, source_target_pairs={{0,6},{1,7},{2,4},{3,5},{4,2},{5,3},{6,0},{7,1},{8,14},{9,15},{10,... | collective-permute-start | bytes 294920 | tf_op jit(solution)/shard_map/ppermute | solution.py:316
  59.0 6.2 %labels.1 = (bf16[512,1024]{1,0:T(8,128)(2,1)S(1)}, f8e4m3fn[512,1024]{1,0:T(32,128)(4,1)S(1)}, bf16[512,512]{1,0:T(8,128)(2,1)S(1)}) custom-call(bf16[512,512]{1,0:T(8,128)(2,1)} %get-tuple-element.36.after_ref.own_ref, bf16[512,512]{1,0:T(8,128)(2,1)} %get-tuple-element.47.far_ref, bf16[512,1024]{1,0:T(8,128)(2,1)} %seeds_ref.3, ...), custom_call_target="tpu_custom_call" | custom-call | flops 1610612736 | tf_op jit(solution)/shard_map/labels/pallas_call | solution.py:451
  65.2 0.0 collective-permute-done.11.refs_1_
  65.2 0.0 collective-permute-done.12.refs_2_
  65.2 1.7 %collective-permute-done.13.refs_3_ = bf16[128,384]{1,0:T(8,128)(2,1)S(1)} collective-permute-done((bf16[128,384]{1,0:T(8,128)(2,1)S(1)}, bf16[128,384]{1,0:T(8,128)(2,1)S(1)}, u32[]{:S(2)}, u32[]{:S(2)}) %collective-permute-start.13) | collective-permute-done | bytes 98336 | tf_op jit(solution)/shard_map/ppermute | solution.py:316
  66.8 4.0 %all-to-all-done.2 = bf16[32,16,640]{2,1,0:T(8,128)(2,1)S(1)} async-done(((bf16[32,16,640]{2,1,0:T(8,128)(2,1)}), bf16[32,16,640]{2,1,0:T(8,128)(2,1)S(1)}, u32[]{:S(2)}, u32[]{:S(2)}) %all-to-all-start.2) | async-done | bytes 655392 | tf_op jit(solution)/shard_map/all_to_all | solution.py:322
  70.8 1.7 %last.1 = bf16[512,1024]{1,0:T(8,128)(2,1)} custom-call(s32[1]{0:T(128)} %bitcast.me_ref, bf16[512,512]{1,0:T(8,128)(2,1)S(1)} %get-tuple-element.60.tiles_ref, bf16[512,1024]{1,0:T(8,128)(2,1)S(1)} %get-tuple-element.61.base_ref, f8e4m3fn[512,1024]{1,0:T(32,128)(4,1)S(1)} %get-tuple-element.62.rest_ref, bf16[512,640]{1,0:T(8,128)(2,1)S(1)} %bitcast.8, ...), custom_call_target="tpu_custom_call" | custom-call | flops 536870912 | bytes 4194304 | tf_op jit(solution)/shard_map/last/pallas_call | solution.py:470
  (4 shorter events, 0.1 us)
Async XLA Ops:
  1.4 14.4 %all-to-all-start = ((s32[32,1,16]{2,1,0:T(1,128)}), s32[32,1,16]{2,1,0:T(1,128)S(1)}, u32[]{:S(2)}, u32[]{:S(2)}) async-start(s32[32,1,16]{2,1,0:T(1,128)} %bitcast.3), calls=%async_computation | async-start | bytes 32768 | tf_op jit(solution)/shard_map/all_to_all | solution.py:367
  17.5 8.1 %collective-permute-start = (bf16[128,384]{1,0:T(8,128)(2,1)S(1)}, bf16[128,384]{1,0:T(8,128)(2,1)S(1)}, u32[]{:S(2)}, u32[]{:S(2)}) collective-permute-start(bf16[128,384]{1,0:T(8,128)(2,1)S(1)} %get-tuple-element.43), channel_id=1, source_target_pairs={{0,8},{1,9},{2,10},{3,11},{4,12},{5,13},{6,14},{7,15},{8,0},{9,1},... | collective-permute-start | bytes 294920 | tf_op jit(solution)/shard_map/ppermute | solution.py:316
  18.1 10.3 %collective-permute-start.1 = (bf16[128,384]{1,0:T(8,128)(2,1)S(1)}, bf16[128,384]{1,0:T(8,128)(2,1)S(1)}, u32[]{:S(2)}, u32[]{:S(2)}) collective-permute-start(bf16[128,384]{1,0:T(8,128)(2,1)S(1)} %get-tuple-element.44), channel_id=1, source_target_pairs={{0,16},{1,17},{2,18},{3,19},{4,20},{5,21},{6,22},{7,23},{8,24},{9,... | collective-permute-start | bytes 294920 | tf_op jit(solution)/shard_map/ppermute | solution.py:316
  19.5 8.9 %collective-permute-start.2 = (bf16[128,384]{1,0:T(8,128)(2,1)S(1)}, bf16[128,384]{1,0:T(8,128)(2,1)S(1)}, u32[]{:S(2)}, u32[]{:S(2)}) collective-permute-start(bf16[128,384]{1,0:T(8,128)(2,1)S(1)} %get-tuple-element.45), channel_id=1, source_target_pairs={{0,24},{1,25},{2,26},{3,27},{4,28},{5,29},{6,30},{7,31},{8,16},{9,... | collective-permute-start | bytes 294920 | tf_op jit(solution)/shard_map/ppermute | solution.py:316
  21.9 25.4 %all-to-all-start.1 = ((bf16[32,16,640]{2,1,0:T(8,128)(2,1)}), bf16[32,16,640]{2,1,0:T(8,128)(2,1)S(1)}, u32[]{:S(2)}, u32[]{:S(2)}) async-start(bf16[32,16,640]{2,1,0:T(8,128)(2,1)} %bitcast.10), calls=%async_computation.1 | async-start | bytes 1310720 | tf_op jit(solution)/shard_map/all_to_all | solution.py:322
  28.4 1.5 %collective-permute-start.3 = (bf16[256,384]{1,0:T(8,128)(2,1)S(1)}, bf16[256,384]{1,0:T(8,128)(2,1)S(1)}, u32[]{:S(2)}, u32[]{:S(2)}) collective-permute-start(bf16[256,384]{1,0:T(8,128)(2,1)S(1)} %gather.2), channel_id=1, source_target_pairs={{0,1},{1,0},{2,3},{3,2},{4,5},{5,4},{6,7},{7,6},{8,9},{9,8},{10,11... | collective-permute-start | bytes 589832 | tf_op jit(solution)/shard_map/ppermute | solution.py:316
  30.0 9.9 %collective-permute-start.4 = (bf16[128,384]{1,0:T(8,128)(2,1)S(1)}, bf16[128,384]{1,0:T(8,128)(2,1)S(1)}, u32[]{:S(2)}, u32[]{:S(2)}) collective-permute-start(bf16[128,384]{1,0:T(8,128)(2,1)S(1)} %get-tuple-element.50), channel_id=1, source_target_pairs={{0,2},{1,3},{2,0},{3,1},{4,6},{5,7},{6,4},{7,5},{8,10},{9,11},{10,... | collective-permute-start | bytes 294920 | tf_op jit(solution)/shard_map/ppermute | solution.py:316
  31.0 9.3 %collective-permute-start.5 = (bf16[128,384]{1,0:T(8,128)(2,1)S(1)}, bf16[128,384]{1,0:T(8,128)(2,1)S(1)}, u32[]{:S(2)}, u32[]{:S(2)}) collective-permute-start(bf16[128,384]{1,0:T(8,128)(2,1)S(1)} %get-tuple-element.51), channel_id=1, source_target_pairs={{0,4},{1,5},{2,6},{3,7},{4,0},{5,1},{6,2},{7,3},{8,12},{9,13},{10,... | collective-permute-start | bytes 294920 | tf_op jit(solution)/shard_map/ppermute | solution.py:316
  32.4 7.9 %collective-permute-start.6 = (bf16[128,384]{1,0:T(8,128)(2,1)S(1)}, bf16[128,384]{1,0:T(8,128)(2,1)S(1)}, u32[]{:S(2)}, u32[]{:S(2)}) collective-permute-start(bf16[128,384]{1,0:T(8,128)(2,1)S(1)} %get-tuple-element.52), channel_id=1, source_target_pairs={{0,6},{1,7},{2,4},{3,5},{4,2},{5,3},{6,0},{7,1},{8,14},{9,15},{10,... | collective-permute-start | bytes 294920 | tf_op jit(solution)/shard_map/ppermute | solution.py:316
  41.1 11.9 %collective-permute-start.7 = (bf16[128,384]{1,0:T(8,128)(2,1)S(1)}, bf16[128,384]{1,0:T(8,128)(2,1)S(1)}, u32[]{:S(2)}, u32[]{:S(2)}) collective-permute-start(bf16[128,384]{1,0:T(8,128)(2,1)S(1)} %get-tuple-element.56), channel_id=1, source_target_pairs={{0,8},{1,9},{2,10},{3,11},{4,12},{5,13},{6,14},{7,15},{8,0},{9,1},... | collective-permute-start | bytes 294920 | tf_op jit(solution)/shard_map/ppermute | solution.py:316
  43.2 9.7 %collective-permute-start.8 = (bf16[128,384]{1,0:T(8,128)(2,1)S(1)}, bf16[128,384]{1,0:T(8,128)(2,1)S(1)}, u32[]{:S(2)}, u32[]{:S(2)}) collective-permute-start(bf16[128,384]{1,0:T(8,128)(2,1)S(1)} %get-tuple-element.57), channel_id=1, source_target_pairs={{0,16},{1,17},{2,18},{3,19},{4,20},{5,21},{6,22},{7,23},{8,24},{9,... | collective-permute-start | bytes 294920 | tf_op jit(solution)/shard_map/ppermute | solution.py:316
  46.0 7.9 %collective-permute-start.9 = (bf16[128,384]{1,0:T(8,128)(2,1)S(1)}, bf16[128,384]{1,0:T(8,128)(2,1)S(1)}, u32[]{:S(2)}, u32[]{:S(2)}) collective-permute-start(bf16[128,384]{1,0:T(8,128)(2,1)S(1)} %get-tuple-element.58), channel_id=1, source_target_pairs={{0,24},{1,25},{2,26},{3,27},{4,28},{5,29},{6,30},{7,31},{8,16},{9,... | collective-permute-start | bytes 294920 | tf_op jit(solution)/shard_map/ppermute | solution.py:316
  48.7 22.1 %all-to-all-start.2 = ((bf16[32,16,640]{2,1,0:T(8,128)(2,1)}), bf16[32,16,640]{2,1,0:T(8,128)(2,1)S(1)}, u32[]{:S(2)}, u32[]{:S(2)}) async-start(bf16[32,16,640]{2,1,0:T(8,128)(2,1)} %bitcast.11), calls=%async_computation.2 | async-start | bytes 1310720 | tf_op jit(solution)/shard_map/all_to_all | solution.py:322
  53.9 1.5 %collective-permute-start.10 = (bf16[256,384]{1,0:T(8,128)(2,1)S(1)}, bf16[256,384]{1,0:T(8,128)(2,1)S(1)}, u32[]{:S(2)}, u32[]{:S(2)}) collective-permute-start(bf16[256,384]{1,0:T(8,128)(2,1)S(1)} %gather.3), channel_id=1, source_target_pairs={{0,1},{1,0},{2,3},{3,2},{4,5},{5,4},{6,7},{7,6},{8,9},{9,8},{10,11... | collective-permute-start | bytes 589832 | tf_op jit(solution)/shard_map/ppermute | solution.py:316
  55.4 9.8 %collective-permute-start.11 = (bf16[128,384]{1,0:T(8,128)(2,1)S(1)}, bf16[128,384]{1,0:T(8,128)(2,1)S(1)}, u32[]{:S(2)}, u32[]{:S(2)}) collective-permute-start(bf16[128,384]{1,0:T(8,128)(2,1)S(1)} %get-tuple-element.64), channel_id=1, source_target_pairs={{0,2},{1,3},{2,0},{3,1},{4,6},{5,7},{6,4},{7,5},{8,10},{9,11},{10,... | collective-permute-start | bytes 294920 | tf_op jit(solution)/shard_map/ppermute | solution.py:316
  56.6 8.6 %collective-permute-start.12 = (bf16[128,384]{1,0:T(8,128)(2,1)S(1)}, bf16[128,384]{1,0:T(8,128)(2,1)S(1)}, u32[]{:S(2)}, u32[]{:S(2)}) collective-permute-start(bf16[128,384]{1,0:T(8,128)(2,1)S(1)} %get-tuple-element.65), channel_id=1, source_target_pairs={{0,4},{1,5},{2,6},{3,7},{4,0},{5,1},{6,2},{7,3},{8,12},{9,13},{10,... | collective-permute-start | bytes 294920 | tf_op jit(solution)/shard_map/ppermute | solution.py:316
  57.8 9.0 %collective-permute-start.13 = (bf16[128,384]{1,0:T(8,128)(2,1)S(1)}, bf16[128,384]{1,0:T(8,128)(2,1)S(1)}, u32[]{:S(2)}, u32[]{:S(2)}) collective-permute-start(bf16[128,384]{1,0:T(8,128)(2,1)S(1)} %get-tuple-element.66), channel_id=1, source_target_pairs={{0,6},{1,7},{2,4},{3,5},{4,2},{5,3},{6,0},{7,1},{8,14},{9,15},{10,... | collective-permute-start | bytes 294920 | tf_op jit(solution)/shard_map/ppermute | solution.py:316

commit v8 on v7

--- a/solution.py
+++ b/solution.py
@@ -18,6 +18,7 @@
 ANCHOR = 0.15
 REST_SCALE = 4096.0
 LONG = 4 * 10**10
+EARLY = 2
 
 SMEM = pl.BlockSpec(memory_space=pltpu.SMEM)
 VMEM = pl.BlockSpec(memory_space=pltpu.VMEM)
@@ -38,13 +39,14 @@
     return pltpu.VMEM(shape, dtype) if small else jax.ShapeDtypeStruct(shape, dtype)
 
 
-def call(kernel, name, out_shape, in_specs, out_specs, scratch_shapes=(), flops=0, nbytes=0):
+def call(kernel, name, out_shape, in_specs, out_specs, scratch_shapes=(), flops=0, nbytes=0, aliases=None):
     return pl.pallas_call(
         kernel,
         out_shape=out_shape,
         in_specs=in_specs,
         out_specs=out_specs,
         scratch_shapes=scratch_shapes,
+        input_output_aliases=aliases or {},
         compiler_params=pltpu.CompilerParams(vmem_limit_bytes=VMEM_LIMIT),
         cost_estimate=pl.CostEstimate(flops=flops, bytes_accessed=nbytes, transcendentals=0),
         name=name,
@@ -148,48 +150,49 @@
     weight_ref,
     seeds_hbm,
     own_hbm,
-    column_hbm,
-    share_hbm,
+    column_ref,
+    share_ref,
     near_ref,
     own_ref,
-    column_ref,
-    share_ref,
     spot_ref,
     sems,
 ):
     copies = [push(seeds_hbm, near_ref, sems.at[0])]
     fill_edges(blocks_ref, pos_ref, weight_ref, column_ref, share_ref)
-    copies.append(push(column_ref, column_hbm, sems.at[1]))
-    copies.append(push(share_ref, share_hbm, sems.at[2]))
     for i in range(own_ref.shape[1] // BLK):
         cols = slice(i * BLK, (i + 1) * BLK)
         fill_tiles(column_ref, share_ref, own_ref, spot_ref, 0, (i, i + 1))
-        copies.append(push(own_ref.at[:, cols], own_hbm.at[:, cols], sems.at[3 + i]))
+        copies.append(push(own_ref.at[:, cols], own_hbm.at[:, cols], sems.at[1 + i]))
     for copy in copies:
         copy.wait()
 
 
-def pick_kernel(me_ref, asked_ref, seeds_ref, after_ref, out_a, out_b, *refs):
-    *plane_refs, pick_ref, a_ref, b_ref, sems = refs
+def pick_a_kernel(me_ref, asked_ref, seeds_ref, after_ref, pick_ref, a_ref, *plane_refs):
     del after_ref
-    slots = asked_ref.shape[2]
+    pick_ref[...] = picks(asked_ref[...], seeds_ref.shape[0])
+    for cols in pieces_of(0, a_ref.shape[1]):
+        a_ref[:, cols] = dot(pick_ref[...], seeds_ref[:, cols]).astype(jnp.bfloat16)
+    to_planes(me_ref[0], a_ref, plane_refs, asked_ref.shape[2])
+
+
+def pick_b_kernel(
+    pick_ref, seeds_ref, a_ref, column_ref, share_ref, out_a, out_b, early_ref, b_ref, spot_ref, sems
+):
     rows, width = seeds_ref.shape
     wide = a_ref.shape[1]
-    pick_ref[...] = picks(asked_ref[...], rows)
-    for cols in pieces_of(0, wide):
-        a_ref[:, cols] = dot(pick_ref[...], seeds_ref[:, cols]).astype(jnp.bfloat16)
     copies = [push(a_ref, out_a, sems.at[0])]
-    to_planes(me_ref[0], a_ref, plane_refs, slots)
     for i, cols in enumerate(pieces_of(wide, width)):
         here = moved(cols, -wide)
         b_ref[:, here] = dot(pick_ref[...], seeds_ref[:, cols]).astype(jnp.bfloat16)
         copies.append(push(b_ref.at[:, here], out_b.at[:, here], sems.at[1 + i]))
+    fill_tiles(column_ref, share_ref, early_ref, spot_ref, rows, (0, early_ref.shape[1] // BLK))
     for copy in copies:
         copy.wait()
 
 
 def far_kernel(
     asked_ref,
+    early_ref,
     own_ref,
     column_ref,
     share_ref,
@@ -207,7 +210,9 @@
     del after_ref
     rows, width = seeds_ref.shape
     wide = sent_a_ref.shape[1]
-    fill_tiles(column_ref, share_ref, far_ref, spot_ref, rows, (0, far_ref.shape[1] // BLK))
+    done = early_ref.shape[1]
+    far_ref[:, :done] = early_ref[...]
+    fill_tiles(column_ref, share_ref, far_ref, spot_ref, rows, (done // BLK, far_ref.shape[1] // BLK))
     pick_ref[...] = picks(asked_ref[...], rows)
     for cols in pieces_of(0, far_ref.shape[1]):
         picked_far_ref[:, cols] = dot(pick_ref[...], far_ref[:, cols]).astype(jnp.bfloat16)
@@ -294,20 +299,33 @@
         rest_ref[:, cols] = rest.astype(jnp.float8_e4m3fn)
 
 
-def last_kernel(me_ref, tiles_ref, base_ref, rest_ref, received_b_ref, *refs, slots):
+def result(tiles_ref, received, base_ref, rest_ref, cols):
+    total = KEEP * dot(tiles_ref[...], received) + base_ref[:, cols].astype(jnp.float32)
+    total = total + rest_ref[:, cols].astype(jnp.float32) * (1 / REST_SCALE)
+    return total.astype(jnp.bfloat16)
+
+
+def last_a_kernel(me_ref, tiles_ref, base_ref, rest_ref, *refs, slots):
     pair_refs = refs[: GROUP // 2]
-    out_hbm, received_a_ref, out_ref, sems = refs[GROUP // 2 :]
-    wide = received_a_ref.shape[1]
-    width = rest_ref.shape[1]
-    from_pairs(me_ref[0], pair_refs, received_a_ref, slots)
+    out_hbm, received_ref, out_ref, sems = refs[GROUP // 2 :]
+    from_pairs(me_ref[0], pair_refs, received_ref, slots)
     copies = []
-    for i, cols in enumerate(pieces_of(wide, width) + pieces_of(0, wide)):
-        first = cols.stop <= wide
-        received = received_a_ref[:, cols] if first else received_b_ref[:, moved(cols, -wide)]
-        total = KEEP * dot(tiles_ref[...], received) + base_ref[:, cols].astype(jnp.float32)
-        total = total + rest_ref[:, cols].astype(jnp.float32) * (1 / REST_SCALE)
-        out_ref[:, cols] = total.astype(jnp.bfloat16)
+    for i, cols in enumerate(pieces_of(0, received_ref.shape[1])):
+        out_ref[:, cols] = result(tiles_ref, received_ref[:, cols], base_ref, rest_ref, cols)
         copies.append(push(out_ref.at[:, cols], out_hbm.at[:, cols], sems.at[i]))
+    for copy in copies:
+        copy.wait()
+
+
+def last_b_kernel(tiles_ref, base_ref, rest_ref, received_ref, same_ref, out_hbm, out_ref, sems):
+    del same_ref
+    width = base_ref.shape[1]
+    wide = width - received_ref.shape[1]
+    copies = []
+    for i, cols in enumerate(pieces_of(wide, width)):
+        here = moved(cols, -wide)
+        out_ref[:, here] = result(tiles_ref, received_ref[:, here], base_ref, rest_ref, cols)
+        copies.append(push(out_ref.at[:, here], out_hbm.at[:, cols], sems.at[i]))
     for copy in copies:
         copy.wait()
 
@@ -372,43 +390,52 @@
         "own_tiles",
         [
             far_out((rows, rows)),
-            far_out((neighbours, rows), jnp.int32),
-            far_out((neighbours, rows), jnp.float32),
+            near_out((neighbours, rows), jnp.int32),
+            near_out((neighbours, rows), jnp.float32),
             near_out((rows, width)),
         ],
         [SMEM, VMEM, VMEM, HBM],
-        [HBM, HBM, HBM, VMEM],
+        [HBM, VMEM, VMEM, VMEM],
         [
             pltpu.VMEM((rows, rows), bf16),
-            pltpu.VMEM((neighbours, rows), jnp.int32),
             pltpu.VMEM((neighbours, rows), jnp.float32),
-            pltpu.VMEM((neighbours, rows), jnp.float32),
-            sems((3 + rows // BLK,)),
+            sems((1 + rows // BLK,)),
         ],
         flops=neighbours * rows * rows,
     )(far_in(tile_blocks), far_in(neighbor_pos.T), far_in(edge_weight.T), far_in(seeds))
-    sent_a, sent_b, *sent_planes = call(
-        pick_kernel,
-        "pick",
-        [far_out((count, wide)), far_out((count, width - wide))] + [plane_shape] * planes,
+    pick, near_a, *sent_planes = call(
+        pick_a_kernel,
+        "pick_a",
+        [near_out((count, rows)), near_out((count, wide))] + [plane_shape] * planes,
         [SMEM, VMEM, VMEM, HBM],
-        [HBM, HBM] + [VMEM] * planes,
+        [VMEM] * (2 + planes),
+        flops=2 * count * rows * wide,
+    )(me, asked, near_seeds, far_in(own))
+    got_planes = across(sent_planes, peers)
+    sent_a, sent_b, early = call(
+        pick_b_kernel,
+        "pick_b",
         [
-            pltpu.VMEM((count, rows), bf16),
-            pltpu.VMEM((count, wide), bf16),
+            far_out((count, wide)),
+            far_out((count, width - wide)),
+            near_out((rows, count // BLK * EARLY // 8 * BLK)),
+        ],
+        [VMEM] * 5,
+        [HBM, HBM, VMEM],
+        [
             pltpu.VMEM((count, width - wide), bf16),
+            pltpu.VMEM((neighbours, rows), jnp.float32),
             sems((1 + n_b,)),
         ],
-        flops=2 * count * rows * width,
-    )(me, asked, near_seeds, far_in(own))
-    got_planes = across(sent_planes, peers)
+        flops=2 * count * rows * (width - wide),
+    )(pick, near_seeds, near_a, column, share)
     received_b = exchange(sent_b, peers)
     got_pairs = within(got_planes, peers, slots)
     far, picked_far, sent_base = call(
         far_kernel,
         "far",
         [far_out((rows, count)), near_out((count, count)), near_out((count, width))],
-        [VMEM] * 7 + [ANY],
+        [VMEM] * 8 + [ANY],
         [VMEM] * 3,
         [
             pltpu.VMEM((count, rows), bf16),
@@ -418,9 +445,10 @@
         flops=2 * rows * count * (count + rows + width) + neighbours * rows * count,
     )(
         asked,
+        early,
         far_in(own),
-        far_in(column),
-        far_in(share),
+        column,
+        share,
         far_in(seeds),
         far_in(sent_a),
         far_in(sent_b),
@@ -467,16 +495,26 @@
         far_in(received_b),
         got_pairs[0],
     )
+    first = call(
+        functools.partial(last_a_kernel, slots=slots),
+        "last_a",
+        far_out((rows, width)),
+        [SMEM] + [VMEM] * (3 + GROUP // 2),
+        HBM,
+        [pltpu.VMEM((count, wide), bf16), pltpu.VMEM((rows, wide), bf16), sems((n_all - n_b,))],
+        flops=2 * rows * count * wide,
+    )(me, near_far, next_base, rest, *got_pairs)
     return call(
-        functools.partial(last_kernel, slots=slots),
-        "last",
+        last_b_kernel,
+        "last_b",
         far_out((rows, width)),
-        [SMEM] + [VMEM] * (4 + GROUP // 2),
+        [VMEM] * 4 + [HBM],
         HBM,
-        [pltpu.VMEM((count, wide), bf16), pltpu.VMEM((rows, width), bf16), sems((n_all,))],
-        flops=2 * rows * count * width,
+        [pltpu.VMEM((rows, width - wide), bf16), sems((n_b,))],
+        flops=2 * rows * count * (width - wide),
         nbytes=2 * rows * count + 5 * rows * width + 2 * count * width,
-    )(me, near_far, next_base, rest, last_b, *got_pairs)
+        aliases={4: 0},
+    )(near_far, next_base, rest, last_b, far_in(first))
 
 
 def solution(mesh):

time: 72.9 us -> 70.3 us (0.964)
  starting transfers between devices: 33.1 us -> 31.3 us
  waiting for transfers between devices: 14.7 us -> 13.6 us
    ppermute x14, starting transfers between devices: 18 us -> 16.2 us  [swap(): return lax.ppermute(x, 'rows', [(i, i ^ distance) for i in range(peers)])]
    all_to_all x2, waiting for transfers between devices: 4 us -> 2.56 us  [exchange(): got = lax.all_to_all(sent, 'rows', split_axis=0, concat_axis=0, tiled=True)]
    pallas_call x3 -> x5, Pallas kernels: 8.27 us -> 9.39 us  [the longest x1 4.84 us: on_device(): call(own_tiles_kernel, 'own_tiles', [far_out((rows, rows)), near_out((nei...]
    pallas_call x1, Pallas kernels: 6.38 us -> 5.54 us  [on_device(): call(far_kernel, 'far', [far_out((rows, count)), near_out((count, count))...]
  transfers between devices with their start and end apart: 17 -> 17, of which waited for: 8 -> 8; matrix products, arithmetic and copies ran while one was open for 0% -> 0% of each run, Pallas kernels for 27% -> 31%
where the time goes in v8:
time: 70.3 us; the launch traced here: 69.9 us
  starting transfers between devices  31.3 us (45%)
  Pallas kernels  23.4 us (33%)
  waiting for transfers between devices  13.6 us (19%)
  local copies, waits for them, and re-layouts  1.38 us (2%)
    ppermute x14, starting transfers between devices, swap(): return lax.ppermute(x, 'rows', [(i, i ^ distance) for i in range(peers)])  16.2 us
    ppermute x14, waiting for transfers between devices, swap(): return lax.ppermute(x, 'rows', [(i, i ^ distance) for i in range(peers)])  8.82 us
    all_to_all x2, starting transfers between devices, exchange(): got = lax.all_to_all(sent, 'rows', split_axis=0, concat_axis=0, tiled=True)  7.89 us
    all_to_all x1, starting transfers between devices, on_device(): lax.all_to_all(wanted.reshape(peers, 1, slots), 'rows', split_axis=0, con...  7.3 us
    pallas_call x1, Pallas kernels, on_device(): call(labels_kernel, 'labels', [near_out((rows, width)), near_out((rows, w...  6.21 us
    pallas_call x1, Pallas kernels, on_device(): call(far_kernel, 'far', [far_out((rows, count)), near_out((count, count))...  5.54 us
    pallas_call x1, Pallas kernels, on_device(): call(own_tiles_kernel, 'own_tiles', [far_out((rows, rows)), near_out((nei...  4.84 us
    all_to_all x2, waiting for transfers between devices, exchange(): got = lax.all_to_all(sent, 'rows', split_axis=0, concat_axis=0, tiled=True)  2.56 us
  transfers between devices with their start and end apart: 17, of which 8 were waited for; matrix products, arithmetic and copies ran while one was open for 0% of the time, Pallas kernels for 31%

profile of v8, /device:TPU:0, one launch (start us, length us, event | category | flops | bytes accessed | tf_op | source)
XLA Modules:
  0.0 69.9 jit_solution(16019734572816978627)
XLA Ops:
  0.0 1.4 %copy.7 = s32[1,32,16]{2,1,0:T(8,128)} copy(s32[1,32,16]{1,2,0:T(8,128)} %param.9) | data formatting | bytes 4096 | tf_op args[4]
  1.4 7.3 %all-to-all-start = ((s32[32,1,16]{2,1,0:T(1,128)}), s32[32,1,16]{2,1,0:T(1,128)S(1)}, u32[]{:S(2)}, u32[]{:S(2)}) async-start(s32[32,1,16]{2,1,0:T(1,128)} %bitcast.2), calls=%async_computation | async-start | bytes 32768 | tf_op jit(solution)/shard_map/all_to_all | solution.py:385
  8.7 4.8 %own_tiles.1 = (bf16[512,512]{1,0:T(8,128)(2,1)}, s32[50,512]{1,0:T(8,128)S(1)}, f32[50,512]{1,0:T(8,128)S(1)}, bf16[512,1024]{1,0:T(8,128)(2,1)S(1)}) custom-call(s32[4,8]{1,0:T(4,128)} %blocks_ref.1, s32[50,512]{1,0:T(8,128)} %bitcast.12, s32[50,512]{1,0:T(8,128)} %bitcast.13, bf16[512,1024]{1,0:T(8,128)(2,1)} %seeds_ref.3), custom_call_target="tpu_custom_call" | custom-call | flops 13107200 | tf_op jit(solution)/shard_map/own_tiles/pallas_call | solution.py:388
  13.5 2.2 %all-to-all-done.asked_ref = s32[32,1,16]{2,1,0:T(1,128)S(1)} async-done(((s32[32,1,16]{2,1,0:T(1,128)}), s32[32,1,16]{2,1,0:T(1,128)S(1)}, u32[]{:S(2)}, u32[]{:S(2)}) %all-to-all-start) | async-done | bytes 2080 | tf_op jit(solution)/shard_map/all_to_all | solution.py:385
  15.8 0.6 pick_a.1
  16.3 0.6 collective-permute-start
  17.0 1.4 %collective-permute-start.1 = (bf16[128,384]{1,0:T(8,128)(2,1)S(1)}, bf16[128,384]{1,0:T(8,128)(2,1)S(1)}, u32[]{:S(2)}, u32[]{:S(2)}) collective-permute-start(bf16[128,384]{1,0:T(8,128)(2,1)S(1)} %get-tuple-element.50), channel_id=1, source_target_pairs={{0,16},{1,17},{2,18},{3,19},{4,20},{5,21},{6,22},{7,23},{8,24},{9,... | collective-permute-start | bytes 294920 | tf_op jit(solution)/shard_map/ppermute | solution.py:334
  18.4 2.4 %collective-permute-start.2 = (bf16[128,384]{1,0:T(8,128)(2,1)S(1)}, bf16[128,384]{1,0:T(8,128)(2,1)S(1)}, u32[]{:S(2)}, u32[]{:S(2)}) collective-permute-start(bf16[128,384]{1,0:T(8,128)(2,1)S(1)} %get-tuple-element.51), channel_id=1, source_target_pairs={{0,24},{1,25},{2,26},{3,27},{4,28},{5,29},{6,30},{7,31},{8,16},{9,... | collective-permute-start | bytes 294920 | tf_op jit(solution)/shard_map/ppermute | solution.py:334
  20.8 1.4 %pick_b.1 = (bf16[512,384]{1,0:T(8,128)(2,1)}, bf16[512,640]{1,0:T(8,128)(2,1)}, bf16[512,128]{1,0:T(8,128)(2,1)S(1)}) custom-call(bf16[512,512]{1,0:T(8,128)(2,1)S(1)} %get-tuple-element.41.pick_ref, bf16[512,1024]{1,0:T(8,128)(2,1)S(1)} %get-tuple-element.40.seeds_ref, bf16[512,384]{1,0:T(8,128)(2,1)S(1)} %get-tuple-element.42.a_ref, ...), custom_call_target="tpu_custom_call" | custom-call | flops 335544320 | tf_op jit(solution)/shard_map/pick_b/pallas_call | solution.py:415
  22.2 3.6 %all-to-all-start.1 = ((bf16[32,16,640]{2,1,0:T(8,128)(2,1)}), bf16[32,16,640]{2,1,0:T(8,128)(2,1)S(1)}, u32[]{:S(2)}, u32[]{:S(2)}) async-start(bf16[32,16,640]{2,1,0:T(8,128)(2,1)} %bitcast.10), calls=%async_computation.1 | async-start | bytes 1310720 | tf_op jit(solution)/shard_map/all_to_all | solution.py:340
  25.8 0.0 collective-permute-done.refs_1_
  25.8 1.5 %collective-permute-done.1.refs_2_ = bf16[128,384]{1,0:T(8,128)(2,1)S(1)} collective-permute-done((bf16[128,384]{1,0:T(8,128)(2,1)S(1)}, bf16[128,384]{1,0:T(8,128)(2,1)S(1)}, u32[]{:S(2)}, u32[]{:S(2)}) %collective-permute-start.1) | collective-permute-done | bytes 98336 | tf_op jit(solution)/shard_map/ppermute | solution.py:334
  27.3 0.0 collective-permute-done.2.refs_3_
  27.3 0.1 collective-permute-start.3
  27.4 1.4 %collective-permute-done.3.refs_4_ = bf16[256,384]{1,0:T(8,128)(2,1)S(1)} collective-permute-done((bf16[256,384]{1,0:T(8,128)(2,1)S(1)}, bf16[256,384]{1,0:T(8,128)(2,1)S(1)}, u32[]{:S(2)}, u32[]{:S(2)}) %collective-permute-start.3) | collective-permute-done | bytes 196640 | tf_op jit(solution)/shard_map/ppermute | solution.py:334
  28.9 1.0 %collective-permute-start.4 = (bf16[128,384]{1,0:T(8,128)(2,1)S(1)}, bf16[128,384]{1,0:T(8,128)(2,1)S(1)}, u32[]{:S(2)}, u32[]{:S(2)}) collective-permute-start(bf16[128,384]{1,0:T(8,128)(2,1)S(1)} %get-tuple-element.56), channel_id=1, source_target_pairs={{0,2},{1,3},{2,0},{3,1},{4,6},{5,7},{6,4},{7,5},{8,10},{9,11},{10,... | collective-permute-start | bytes 294920 | tf_op jit(solution)/shard_map/ppermute | solution.py:334
  29.8 1.4 %collective-permute-start.5 = (bf16[128,384]{1,0:T(8,128)(2,1)S(1)}, bf16[128,384]{1,0:T(8,128)(2,1)S(1)}, u32[]{:S(2)}, u32[]{:S(2)}) collective-permute-start(bf16[128,384]{1,0:T(8,128)(2,1)S(1)} %get-tuple-element.57), channel_id=1, source_target_pairs={{0,4},{1,5},{2,6},{3,7},{4,0},{5,1},{6,2},{7,3},{8,12},{9,13},{10,... | collective-permute-start | bytes 294920 | tf_op jit(solution)/shard_map/ppermute | solution.py:334
  31.2 1.2 %collective-permute-start.6 = (bf16[128,384]{1,0:T(8,128)(2,1)S(1)}, bf16[128,384]{1,0:T(8,128)(2,1)S(1)}, u32[]{:S(2)}, u32[]{:S(2)}) collective-permute-start(bf16[128,384]{1,0:T(8,128)(2,1)S(1)} %get-tuple-element.58), channel_id=1, source_target_pairs={{0,6},{1,7},{2,4},{3,5},{4,2},{5,3},{6,0},{7,1},{8,14},{9,15},{10,... | collective-permute-start | bytes 294920 | tf_op jit(solution)/shard_map/ppermute | solution.py:334
  32.4 5.5 %far.1 = (bf16[512,512]{1,0:T(8,128)(2,1)}, bf16[512,512]{1,0:T(8,128)(2,1)S(1)}, bf16[512,1024]{1,0:T(8,128)(2,1)S(1)}) custom-call(s32[32,1,16]{2,1,0:T(1,128)S(1)} %all-to-all-done.asked_ref, bf16[512,128]{1,0:T(8,128)(2,1)S(1)} %get-tuple-element.45.early_ref, bf16[512,512]{1,0:T(8,128)(2,1)} %get-tuple-element.39.after_ref.own_ref, ...), custom_call_target="tpu_custom_call" | custom-call | flops 1086849024 | tf_op jit(solution)/shard_map/far/pallas_call | solution.py:434
  38.0 0.0 collective-permute-done.4.refs_1_
  38.0 0.0 collective-permute-done.5.refs_2_
  38.0 1.7 %collective-permute-done.6.refs_3_ = bf16[128,384]{1,0:T(8,128)(2,1)S(1)} collective-permute-done((bf16[128,384]{1,0:T(8,128)(2,1)S(1)}, bf16[128,384]{1,0:T(8,128)(2,1)S(1)}, u32[]{:S(2)}, u32[]{:S(2)}) %collective-permute-start.6) | collective-permute-done | bytes 98336 | tf_op jit(solution)/shard_map/ppermute | solution.py:334
  39.7 0.8 %send_a.1 = (bf16[512,384]{1,0:T(8,128)(2,1)}, bf16[128,384]{1,0:T(8,128)(2,1)S(1)}, bf16[128,384]{1,0:T(8,128)(2,1)S(1)}, bf16[128,384]{1,0:T(8,128)(2,1)S(1)}, bf16[128,384]{1,0:T(8,128)(2,1)S(1)}) custom-call(s32[1]{0:T(128)} %bitcast.3.me_ref, bf16[512,512]{1,0:T(8,128)(2,1)S(1)} %get-tuple-element.54.tiles_ref, ...), custom_call_target="tpu_custom_call" | custom-call | flops 201326592 | tf_op jit(solution)/shard_map/send_a/pallas_call | solution.py:457
  40.5 1.6 %collective-permute-start.7 = (bf16[128,384]{1,0:T(8,128)(2,1)S(1)}, bf16[128,384]{1,0:T(8,128)(2,1)S(1)}, u32[]{:S(2)}, u32[]{:S(2)}) collective-permute-start(bf16[128,384]{1,0:T(8,128)(2,1)S(1)} %get-tuple-element.62), channel_id=1, source_target_pairs={{0,8},{1,9},{2,10},{3,11},{4,12},{5,13},{6,14},{7,15},{8,0},{9,1},... | collective-permute-start | bytes 294920 | tf_op jit(solution)/shard_map/ppermute | solution.py:334
  42.1 2.8 %collective-permute-start.8 = (bf16[128,384]{1,0:T(8,128)(2,1)S(1)}, bf16[128,384]{1,0:T(8,128)(2,1)S(1)}, u32[]{:S(2)}, u32[]{:S(2)}) collective-permute-start(bf16[128,384]{1,0:T(8,128)(2,1)S(1)} %get-tuple-element.63), channel_id=1, source_target_pairs={{0,16},{1,17},{2,18},{3,19},{4,20},{5,21},{6,22},{7,23},{8,24},{9,... | collective-permute-start | bytes 294920 | tf_op jit(solution)/shard_map/ppermute | solution.py:334
  44.9 0.0 collective-permute-start.9
  45.0 0.0 all-to-all-done.1
  45.0 1.4 %send_b.1 = (bf16[512,640]{1,0:T(8,128)(2,1)}, bf16[512,640]{1,0:T(8,128)(2,1)}) custom-call(bf16[512,512]{1,0:T(8,128)(2,1)S(1)} %get-tuple-element.54.tiles_ref, bf16[512,1024]{1,0:T(8,128)(2,1)S(1)} %get-tuple-element.55.base_ref, bf16[512,640]{1,0:T(8,128)(2,1)S(1)} %bitcast.9, bf16[128,384]{1,0:T(8,128)(2,1)S(1)} %get-tuple-element.60.after_ref.refs_0_), custom_call_target="tpu_custom_call" | custom-call | flops 335544320 | bytes 3538944 | tf_op jit(solution)/shard_map/send_b/pallas_call | solution.py:467
  46.4 4.3 %all-to-all-start.2 = ((bf16[32,16,640]{2,1,0:T(8,128)(2,1)}), bf16[32,16,640]{2,1,0:T(8,128)(2,1)S(1)}, u32[]{:S(2)}, u32[]{:S(2)}) async-start(bf16[32,16,640]{2,1,0:T(8,128)(2,1)} %bitcast.11), calls=%async_computation.2 | async-start | bytes 1310720 | tf_op jit(solution)/shard_map/all_to_all | solution.py:340
  50.6 0.0 collective-permute-done.7.refs_1_
  50.6 1.7 %collective-permute-done.8.refs_2_ = bf16[128,384]{1,0:T(8,128)(2,1)S(1)} collective-permute-done((bf16[128,384]{1,0:T(8,128)(2,1)S(1)}, bf16[128,384]{1,0:T(8,128)(2,1)S(1)}, u32[]{:S(2)}, u32[]{:S(2)}) %collective-permute-start.8) | collective-permute-done | bytes 98336 | tf_op jit(solution)/shard_map/ppermute | solution.py:334
  52.4 0.0 collective-permute-done.9.refs_3_
  52.4 0.1 collective-permute-start.10
  52.5 1.4 %collective-permute-done.10.refs_4_ = bf16[256,384]{1,0:T(8,128)(2,1)S(1)} collective-permute-done((bf16[256,384]{1,0:T(8,128)(2,1)S(1)}, bf16[256,384]{1,0:T(8,128)(2,1)S(1)}, u32[]{:S(2)}, u32[]{:S(2)}) %collective-permute-start.10) | collective-permute-done | bytes 196640 | tf_op jit(solution)/shard_map/ppermute | solution.py:334
  54.0 1.1 %collective-permute-start.11 = (bf16[128,384]{1,0:T(8,128)(2,1)S(1)}, bf16[128,384]{1,0:T(8,128)(2,1)S(1)}, u32[]{:S(2)}, u32[]{:S(2)}) collective-permute-start(bf16[128,384]{1,0:T(8,128)(2,1)S(1)} %get-tuple-element.70), channel_id=1, source_target_pairs={{0,2},{1,3},{2,0},{3,1},{4,6},{5,7},{6,4},{7,5},{8,10},{9,11},{10,... | collective-permute-start | bytes 294920 | tf_op jit(solution)/shard_map/ppermute | solution.py:334
  55.0 0.5 collective-permute-start.12
  55.5 2.0 %collective-permute-start.13 = (bf16[128,384]{1,0:T(8,128)(2,1)S(1)}, bf16[128,384]{1,0:T(8,128)(2,1)S(1)}, u32[]{:S(2)}, u32[]{:S(2)}) collective-permute-start(bf16[128,384]{1,0:T(8,128)(2,1)S(1)} %get-tuple-element.72), channel_id=1, source_target_pairs={{0,6},{1,7},{2,4},{3,5},{4,2},{5,3},{6,0},{7,1},{8,14},{9,15},{10,... | collective-permute-start | bytes 294920 | tf_op jit(solution)/shard_map/ppermute | solution.py:334
  57.5 6.2 %labels.1 = (bf16[512,1024]{1,0:T(8,128)(2,1)S(1)}, f8e4m3fn[512,1024]{1,0:T(32,128)(4,1)S(1)}, bf16[512,512]{1,0:T(8,128)(2,1)S(1)}) custom-call(bf16[512,512]{1,0:T(8,128)(2,1)} %get-tuple-element.39.after_ref.own_ref, bf16[512,512]{1,0:T(8,128)(2,1)} %get-tuple-element.53.far_ref, bf16[512,1024]{1,0:T(8,128)(2,1)} %seeds_ref.3, ...), custom_call_target="tpu_custom_call" | custom-call | flops 1610612736 | tf_op jit(solution)/shard_map/labels/pallas_call | solution.py:479
  63.7 0.0 collective-permute-done.11.refs_1_
  63.7 0.0 collective-permute-done.12.refs_2_
  63.8 1.0 %collective-permute-done.13.refs_3_ = bf16[128,384]{1,0:T(8,128)(2,1)S(1)} collective-permute-done((bf16[128,384]{1,0:T(8,128)(2,1)S(1)}, bf16[128,384]{1,0:T(8,128)(2,1)S(1)}, u32[]{:S(2)}, u32[]{:S(2)}) %collective-permute-start.13) | collective-permute-done | bytes 98336 | tf_op jit(solution)/shard_map/ppermute | solution.py:334
  64.7 1.3 %last_a.1.same_ref = bf16[512,1024]{1,0:T(8,128)(2,1)} custom-call(s32[1]{0:T(128)} %bitcast.3.me_ref, bf16[512,512]{1,0:T(8,128)(2,1)S(1)} %get-tuple-element.66.tiles_ref, bf16[512,1024]{1,0:T(8,128)(2,1)S(1)} %get-tuple-element.67.base_ref, f8e4m3fn[512,1024]{1,0:T(32,128)(4,1)S(1)} %get-tuple-element.68.rest_ref, ...), custom_call_target="tpu_custom_call" | custom-call | flops 201326592 | tf_op jit(solution)/shard_map/last_a/pallas_call | solution.py:498
  66.0 2.6 %all-to-all-done.2 = bf16[32,16,640]{2,1,0:T(8,128)(2,1)S(1)} async-done(((bf16[32,16,640]{2,1,0:T(8,128)(2,1)}), bf16[32,16,640]{2,1,0:T(8,128)(2,1)S(1)}, u32[]{:S(2)}, u32[]{:S(2)}) %all-to-all-start.2) | async-done | bytes 655392 | tf_op jit(solution)/shard_map/all_to_all | solution.py:340
  68.6 1.4 %last_b.1 = bf16[512,1024]{1,0:T(8,128)(2,1)} custom-call(bf16[512,512]{1,0:T(8,128)(2,1)S(1)} %get-tuple-element.66.tiles_ref, bf16[512,1024]{1,0:T(8,128)(2,1)S(1)} %get-tuple-element.67.base_ref, f8e4m3fn[512,1024]{1,0:T(32,128)(4,1)S(1)} %get-tuple-element.68.rest_ref, bf16[512,640]{1,0:T(8,128)(2,1)S(1)} %bitcast.8, ...), custom_call_target="tpu_custom_call", output_to_operand_aliasing={{}: (4, {})} | custom-call | flops 335544320 | bytes 4194304 | tf_op jit(solution)/shard_map/last_b/pallas_call | solution.py:507
  (4 shorter events, 0.1 us)
Async XLA Ops:
  1.4 14.4 %all-to-all-start = ((s32[32,1,16]{2,1,0:T(1,128)}), s32[32,1,16]{2,1,0:T(1,128)S(1)}, u32[]{:S(2)}, u32[]{:S(2)}) async-start(s32[32,1,16]{2,1,0:T(1,128)} %bitcast.2), calls=%async_computation | async-start | bytes 32768 | tf_op jit(solution)/shard_map/all_to_all | solution.py:385
  16.3 9.5 %collective-permute-start = (bf16[128,384]{1,0:T(8,128)(2,1)S(1)}, bf16[128,384]{1,0:T(8,128)(2,1)S(1)}, u32[]{:S(2)}, u32[]{:S(2)}) collective-permute-start(bf16[128,384]{1,0:T(8,128)(2,1)S(1)} %get-tuple-element.49), channel_id=1, source_target_pairs={{0,8},{1,9},{2,10},{3,11},{4,12},{5,13},{6,14},{7,15},{8,0},{9,1},... | collective-permute-start | bytes 294920 | tf_op jit(solution)/shard_map/ppermute | solution.py:334
  17.0 10.3 %collective-permute-start.1 = (bf16[128,384]{1,0:T(8,128)(2,1)S(1)}, bf16[128,384]{1,0:T(8,128)(2,1)S(1)}, u32[]{:S(2)}, u32[]{:S(2)}) collective-permute-start(bf16[128,384]{1,0:T(8,128)(2,1)S(1)} %get-tuple-element.50), channel_id=1, source_target_pairs={{0,16},{1,17},{2,18},{3,19},{4,20},{5,21},{6,22},{7,23},{8,24},{9,... | collective-permute-start | bytes 294920 | tf_op jit(solution)/shard_map/ppermute | solution.py:334
  18.4 8.9 %collective-permute-start.2 = (bf16[128,384]{1,0:T(8,128)(2,1)S(1)}, bf16[128,384]{1,0:T(8,128)(2,1)S(1)}, u32[]{:S(2)}, u32[]{:S(2)}) collective-permute-start(bf16[128,384]{1,0:T(8,128)(2,1)S(1)} %get-tuple-element.51), channel_id=1, source_target_pairs={{0,24},{1,25},{2,26},{3,27},{4,28},{5,29},{6,30},{7,31},{8,16},{9,... | collective-permute-start | bytes 294920 | tf_op jit(solution)/shard_map/ppermute | solution.py:334
  22.2 22.8 %all-to-all-start.1 = ((bf16[32,16,640]{2,1,0:T(8,128)(2,1)}), bf16[32,16,640]{2,1,0:T(8,128)(2,1)S(1)}, u32[]{:S(2)}, u32[]{:S(2)}) async-start(bf16[32,16,640]{2,1,0:T(8,128)(2,1)} %bitcast.10), calls=%async_computation.1 | async-start | bytes 1310720 | tf_op jit(solution)/shard_map/all_to_all | solution.py:340
  27.3 1.5 %collective-permute-start.3 = (bf16[256,384]{1,0:T(8,128)(2,1)S(1)}, bf16[256,384]{1,0:T(8,128)(2,1)S(1)}, u32[]{:S(2)}, u32[]{:S(2)}) collective-permute-start(bf16[256,384]{1,0:T(8,128)(2,1)S(1)} %gather.2), channel_id=1, source_target_pairs={{0,1},{1,0},{2,3},{3,2},{4,5},{5,4},{6,7},{7,6},{8,9},{9,8},{10,11... | collective-permute-start | bytes 589832 | tf_op jit(solution)/shard_map/ppermute | solution.py:334
  28.9 9.1 %collective-permute-start.4 = (bf16[128,384]{1,0:T(8,128)(2,1)S(1)}, bf16[128,384]{1,0:T(8,128)(2,1)S(1)}, u32[]{:S(2)}, u32[]{:S(2)}) collective-permute-start(bf16[128,384]{1,0:T(8,128)(2,1)S(1)} %get-tuple-element.56), channel_id=1, source_target_pairs={{0,2},{1,3},{2,0},{3,1},{4,6},{5,7},{6,4},{7,5},{8,10},{9,11},{10,... | collective-permute-start | bytes 294920 | tf_op jit(solution)/shard_map/ppermute | solution.py:334
  29.8 8.1 %collective-permute-start.5 = (bf16[128,384]{1,0:T(8,128)(2,1)S(1)}, bf16[128,384]{1,0:T(8,128)(2,1)S(1)}, u32[]{:S(2)}, u32[]{:S(2)}) collective-permute-start(bf16[128,384]{1,0:T(8,128)(2,1)S(1)} %get-tuple-element.57), channel_id=1, source_target_pairs={{0,4},{1,5},{2,6},{3,7},{4,0},{5,1},{6,2},{7,3},{8,12},{9,13},{10,... | collective-permute-start | bytes 294920 | tf_op jit(solution)/shard_map/ppermute | solution.py:334
  31.2 8.5 %collective-permute-start.6 = (bf16[128,384]{1,0:T(8,128)(2,1)S(1)}, bf16[128,384]{1,0:T(8,128)(2,1)S(1)}, u32[]{:S(2)}, u32[]{:S(2)}) collective-permute-start(bf16[128,384]{1,0:T(8,128)(2,1)S(1)} %get-tuple-element.58), channel_id=1, source_target_pairs={{0,6},{1,7},{2,4},{3,5},{4,2},{5,3},{6,0},{7,1},{8,14},{9,15},{10,... | collective-permute-start | bytes 294920 | tf_op jit(solution)/shard_map/ppermute | solution.py:334
  40.5 10.1 %collective-permute-start.7 = (bf16[128,384]{1,0:T(8,128)(2,1)S(1)}, bf16[128,384]{1,0:T(8,128)(2,1)S(1)}, u32[]{:S(2)}, u32[]{:S(2)}) collective-permute-start(bf16[128,384]{1,0:T(8,128)(2,1)S(1)} %get-tuple-element.62), channel_id=1, source_target_pairs={{0,8},{1,9},{2,10},{3,11},{4,12},{5,13},{6,14},{7,15},{8,0},{9,1},... | collective-permute-start | bytes 294920 | tf_op jit(solution)/shard_map/ppermute | solution.py:334
  42.1 10.2 %collective-permute-start.8 = (bf16[128,384]{1,0:T(8,128)(2,1)S(1)}, bf16[128,384]{1,0:T(8,128)(2,1)S(1)}, u32[]{:S(2)}, u32[]{:S(2)}) collective-permute-start(bf16[128,384]{1,0:T(8,128)(2,1)S(1)} %get-tuple-element.63), channel_id=1, source_target_pairs={{0,16},{1,17},{2,18},{3,19},{4,20},{5,21},{6,22},{7,23},{8,24},{9,... | collective-permute-start | bytes 294920 | tf_op jit(solution)/shard_map/ppermute | solution.py:334
  44.9 7.5 %collective-permute-start.9 = (bf16[128,384]{1,0:T(8,128)(2,1)S(1)}, bf16[128,384]{1,0:T(8,128)(2,1)S(1)}, u32[]{:S(2)}, u32[]{:S(2)}) collective-permute-start(bf16[128,384]{1,0:T(8,128)(2,1)S(1)} %get-tuple-element.64), channel_id=1, source_target_pairs={{0,24},{1,25},{2,26},{3,27},{4,28},{5,29},{6,30},{7,31},{8,16},{9,... | collective-permute-start | bytes 294920 | tf_op jit(solution)/shard_map/ppermute | solution.py:334
  46.4 22.2 %all-to-all-start.2 = ((bf16[32,16,640]{2,1,0:T(8,128)(2,1)}), bf16[32,16,640]{2,1,0:T(8,128)(2,1)S(1)}, u32[]{:S(2)}, u32[]{:S(2)}) async-start(bf16[32,16,640]{2,1,0:T(8,128)(2,1)} %bitcast.11), calls=%async_computation.2 | async-start | bytes 1310720 | tf_op jit(solution)/shard_map/all_to_all | solution.py:340
  52.4 1.5 %collective-permute-start.10 = (bf16[256,384]{1,0:T(8,128)(2,1)S(1)}, bf16[256,384]{1,0:T(8,128)(2,1)S(1)}, u32[]{:S(2)}, u32[]{:S(2)}) collective-permute-start(bf16[256,384]{1,0:T(8,128)(2,1)S(1)} %gather.3), channel_id=1, source_target_pairs={{0,1},{1,0},{2,3},{3,2},{4,5},{5,4},{6,7},{7,6},{8,9},{9,8},{10,11... | collective-permute-start | bytes 589832 | tf_op jit(solution)/shard_map/ppermute | solution.py:334
  54.0 9.8 %collective-permute-start.11 = (bf16[128,384]{1,0:T(8,128)(2,1)S(1)}, bf16[128,384]{1,0:T(8,128)(2,1)S(1)}, u32[]{:S(2)}, u32[]{:S(2)}) collective-permute-start(bf16[128,384]{1,0:T(8,128)(2,1)S(1)} %get-tuple-element.70), channel_id=1, source_target_pairs={{0,2},{1,3},{2,0},{3,1},{4,6},{5,7},{6,4},{7,5},{8,10},{9,11},{10,... | collective-permute-start | bytes 294920 | tf_op jit(solution)/shard_map/ppermute | solution.py:334
  55.0 8.7 %collective-permute-start.12 = (bf16[128,384]{1,0:T(8,128)(2,1)S(1)}, bf16[128,384]{1,0:T(8,128)(2,1)S(1)}, u32[]{:S(2)}, u32[]{:S(2)}) collective-permute-start(bf16[128,384]{1,0:T(8,128)(2,1)S(1)} %get-tuple-element.71), channel_id=1, source_target_pairs={{0,4},{1,5},{2,6},{3,7},{4,0},{5,1},{6,2},{7,3},{8,12},{9,13},{10,... | collective-permute-start | bytes 294920 | tf_op jit(solution)/shard_map/ppermute | solution.py:334
  55.5 9.2 %collective-permute-start.13 = (bf16[128,384]{1,0:T(8,128)(2,1)S(1)}, bf16[128,384]{1,0:T(8,128)(2,1)S(1)}, u32[]{:S(2)}, u32[]{:S(2)}) collective-permute-start(bf16[128,384]{1,0:T(8,128)(2,1)S(1)} %get-tuple-element.72), channel_id=1, source_target_pairs={{0,6},{1,7},{2,4},{3,5},{4,2},{5,3},{6,0},{7,1},{8,14},{9,15},{10,... | collective-permute-start | bytes 294920 | tf_op jit(solution)/shard_map/ppermute | solution.py:334

commit v9 on v8

--- a/solution.py
+++ b/solution.py
@@ -61,6 +61,10 @@
     return [slice(c, min(c + COLS, last)) for c in range(first, last, COLS)]
 
 
+def strips_of(count):
+    return [slice(r, r + BLK) for r in range(0, count, BLK)]
+
+
 def moved(cols, by):
     return slice(cols.start + by, cols.stop + by)
 
@@ -87,8 +91,16 @@
     return pl.ds(pl.multiple_of(peer * slots, slots), slots)
 
 
+def pair_order(pairs):
+    return [0] + list(range(pairs - 1, 0, -1))
+
+
+def plane_order(planes):
+    return [0] + list(range(2, planes)) + [1]
+
+
 def to_planes(me, rows_ref, plane_refs, slots):
-    for z, plane_ref in enumerate(plane_refs):
+    for z, plane_ref in zip(plane_order(len(plane_refs)), plane_refs):
         for s in range(2):
             for q in range(GROUP // 2):
                 peer = me ^ (GROUP * z + 2 * q + s)
@@ -98,11 +110,11 @@
 
 def from_pairs(me, pair_refs, rows_ref, slots):
     planes = pair_refs[0].shape[0] // (2 * slots)
-    for q, pair_ref in enumerate(pair_refs):
+    for q, pair_ref in zip(pair_order(len(pair_refs)), pair_refs):
         for s in range(2):
-            for z in range(planes):
+            for i, z in enumerate(plane_order(planes)):
                 peer = me ^ (GROUP * z + 2 * q + s)
-                at = (s * planes + z) * slots
+                at = (s * planes + i) * slots
                 rows_ref[block(peer, slots), :] = pair_ref[at : at + slots, :]
 
 
@@ -178,13 +190,12 @@
 def pick_b_kernel(
     pick_ref, seeds_ref, a_ref, column_ref, share_ref, out_a, out_b, early_ref, b_ref, spot_ref, sems
 ):
-    rows, width = seeds_ref.shape
+    rows = seeds_ref.shape[0]
     wide = a_ref.shape[1]
     copies = [push(a_ref, out_a, sems.at[0])]
-    for i, cols in enumerate(pieces_of(wide, width)):
-        here = moved(cols, -wide)
-        b_ref[:, here] = dot(pick_ref[...], seeds_ref[:, cols]).astype(jnp.bfloat16)
-        copies.append(push(b_ref.at[:, here], out_b.at[:, here], sems.at[1 + i]))
+    for i, rows_here in enumerate(strips_of(pick_ref.shape[0])):
+        b_ref[rows_here, :] = dot(pick_ref[rows_here, :], seeds_ref[:, wide:]).astype(jnp.bfloat16)
+        copies.append(push(b_ref.at[rows_here], out_b.at[rows_here], sems.at[1 + i]))
     fill_tiles(column_ref, share_ref, early_ref, spot_ref, rows, (0, early_ref.shape[1] // BLK))
     for copy in copies:
         copy.wait()
@@ -236,7 +247,7 @@
     count = GROUP // 2
     *plane_refs, other_ref = refs[:-count]
     planes = len(plane_refs)
-    for q, out_ref in enumerate(refs[-count:]):
+    for q, out_ref in zip(pair_order(count), refs[-count:]):
         for z, plane_ref in enumerate(plane_refs):
             here = slice(z * slots, (z + 1) * slots)
             there = slice((planes + z) * slots, (planes + z + 1) * slots)
@@ -262,11 +273,11 @@
     del after_ref
     wide = base_ref.shape[1] - received_ref.shape[1]
     copies = [push(received_ref, kept_hbm, sems.at[0])]
-    for i, cols in enumerate(pieces_of(0, received_ref.shape[1])):
-        total = KEEP * dot(tiles_ref[...], received_ref[:, cols])
-        total = total + base_ref[:, moved(cols, wide)].astype(jnp.float32)
-        out_ref[:, cols] = total.astype(jnp.bfloat16)
-        copies.append(push(out_ref.at[:, cols], out_hbm.at[:, cols], sems.at[1 + i]))
+    for i, rows in enumerate(strips_of(out_ref.shape[0])):
+        total = KEEP * dot(tiles_ref[rows, :], received_ref[...])
+        total = total + base_ref[rows, wide:].astype(jnp.float32)
+        out_ref[rows, :] = total.astype(jnp.bfloat16)
+        copies.append(push(out_ref.at[rows], out_hbm.at[rows], sems.at[1 + i]))
     for copy in copies:
         copy.wait()
 
@@ -299,9 +310,9 @@
         rest_ref[:, cols] = rest.astype(jnp.float8_e4m3fn)
 
 
-def result(tiles_ref, received, base_ref, rest_ref, cols):
-    total = KEEP * dot(tiles_ref[...], received) + base_ref[:, cols].astype(jnp.float32)
-    total = total + rest_ref[:, cols].astype(jnp.float32) * (1 / REST_SCALE)
+def result(tiles_ref, received, base_ref, rest_ref, rows, cols):
+    total = KEEP * dot(tiles_ref[rows, :], received) + base_ref[rows, cols].astype(jnp.float32)
+    total = total + rest_ref[rows, cols].astype(jnp.float32) * (1 / REST_SCALE)
     return total.astype(jnp.bfloat16)
 
 
@@ -311,7 +322,8 @@
     from_pairs(me_ref[0], pair_refs, received_ref, slots)
     copies = []
     for i, cols in enumerate(pieces_of(0, received_ref.shape[1])):
-        out_ref[:, cols] = result(tiles_ref, received_ref[:, cols], base_ref, rest_ref, cols)
+        received = received_ref[:, cols]
+        out_ref[:, cols] = result(tiles_ref, received, base_ref, rest_ref, slice(None), cols)
         copies.append(push(out_ref.at[:, cols], out_hbm.at[:, cols], sems.at[i]))
     for copy in copies:
         copy.wait()
@@ -322,10 +334,10 @@
     width = base_ref.shape[1]
     wide = width - received_ref.shape[1]
     copies = []
-    for i, cols in enumerate(pieces_of(wide, width)):
-        here = moved(cols, -wide)
-        out_ref[:, here] = result(tiles_ref, received_ref[:, here], base_ref, rest_ref, cols)
-        copies.append(push(out_ref.at[:, here], out_hbm.at[:, cols], sems.at[i]))
+    cols = slice(wide, width)
+    for i, rows in enumerate(strips_of(out_ref.shape[0])):
+        out_ref[rows, :] = result(tiles_ref, received_ref[...], base_ref, rest_ref, rows, cols)
+        copies.append(push(out_ref.at[rows], out_hbm.at[rows, cols], sems.at[i]))
     for copy in copies:
         copy.wait()
 
@@ -342,7 +354,8 @@
 
 
 def across(planes, peers):
-    return [planes[0]] + [swap(x, peers, GROUP * z) for z, x in enumerate(planes) if z]
+    order = plane_order(len(planes))
+    return [swap(x, peers, GROUP * z) if z else x for z, x in zip(order, planes)]
 
 
 def within(planes, peers, slots):
@@ -364,7 +377,7 @@
         [VMEM] * (n + 1),
         [VMEM] * (GROUP // 2),
     )(*planes, other)
-    return [pairs[0]] + [swap(x, peers, 2 * q) for q, x in enumerate(pairs) if q]
+    return [swap(x, peers, 2 * q) if q else x for q, x in zip(pair_order(len(pairs)), pairs)]
 
 
 def on_device(seeds, neighbor_pos, edge_weight, tile_blocks, wanted):
@@ -379,8 +392,7 @@
     sems = pltpu.SemaphoreType.DMA
     bf16 = jnp.bfloat16
     plane_shape = jax.ShapeDtypeStruct((GROUP * slots, wide), bf16)
-    n_b = len(pieces_of(wide, width))
-    n_all = n_b + len(pieces_of(0, wide))
+    n_a, n_out, n_sent = len(pieces_of(0, wide)), len(strips_of(rows)), len(strips_of(count))
 
     asked = lax.all_to_all(
         wanted.reshape(peers, 1, slots), "rows", split_axis=0, concat_axis=0, tiled=True
@@ -425,7 +437,7 @@
         [
             pltpu.VMEM((count, width - wide), bf16),
             pltpu.VMEM((neighbours, rows), jnp.float32),
-            sems((1 + n_b,)),
+            sems((1 + n_sent,)),
         ],
         flops=2 * count * rows * (width - wide),
     )(pick, near_seeds, near_a, column, share)
@@ -470,7 +482,7 @@
         [far_out((count, width - wide)), far_out((count, width - wide))],
         [VMEM] * 3 + [ANY],
         [HBM, HBM],
-        [pltpu.VMEM((count, width - wide), bf16), sems((1 + n_b,))],
+        [pltpu.VMEM((count, width - wide), bf16), sems((1 + n_sent,))],
         flops=2 * count * count * (width - wide),
         nbytes=2 * count * (3 * (width - wide) + count + width),
     )(picked_far, sent_base, received_b, sent_planes[0])
@@ -501,7 +513,7 @@
         far_out((rows, width)),
         [SMEM] + [VMEM] * (3 + GROUP // 2),
         HBM,
-        [pltpu.VMEM((count, wide), bf16), pltpu.VMEM((rows, wide), bf16), sems((n_all - n_b,))],
+        [pltpu.VMEM((count, wide), bf16), pltpu.VMEM((rows, wide), bf16), sems((n_a,))],
         flops=2 * rows * count * wide,
     )(me, near_far, next_base, rest, *got_pairs)
     return call(
@@ -510,7 +522,7 @@
         far_out((rows, width)),
         [VMEM] * 4 + [HBM],
         HBM,
-        [pltpu.VMEM((rows, width - wide), bf16), sems((n_b,))],
+        [pltpu.VMEM((rows, width - wide), bf16), sems((n_out,))],
         flops=2 * rows * count * (width - wide),
         nbytes=2 * rows * count + 5 * rows * width + 2 * count * width,
         aliases={4: 0},

time: 70.3 us -> 69.1 us (0.983)
  starting transfers between devices: 31.3 us -> 29.8 us
    ppermute x14, starting transfers between devices: 16.2 us -> 14.8 us  [swap(): return lax.ppermute(x, 'rows', [(i, i ^ distance) for i in range(peers)])]
  transfers between devices with their start and end apart: 17 -> 17, of which waited for: 8 -> 10; matrix products, arithmetic and copies ran while one was open for 0% -> 0% of each run, Pallas kernels for 31% -> 31%
where the time goes in v9:
time: 69.1 us; the launch traced here: 68.7 us
  starting transfers between devices  29.8 us (43%)
  Pallas kernels  23.3 us (34%)
  waiting for transfers between devices  14.1 us (20%)
  local copies, waits for them, and re-layouts  1.38 us (2%)
    ppermute x14, starting transfers between devices, swap(): return lax.ppermute(x, 'rows', [(i, i ^ distance) for i in range(peers)])  14.8 us
    ppermute x14, waiting for transfers between devices, swap(): return lax.ppermute(x, 'rows', [(i, i ^ distance) for i in range(peers)])  9.43 us
    all_to_all x2, starting transfers between devices, exchange(): got = lax.all_to_all(sent, 'rows', split_axis=0, concat_axis=0, tiled=True)  7.63 us
    all_to_all x1, starting transfers between devices, on_device(): lax.all_to_all(wanted.reshape(peers, 1, slots), 'rows', split_axis=0, con...  7.3 us
    pallas_call x1, Pallas kernels, on_device(): call(labels_kernel, 'labels', [near_out((rows, width)), near_out((rows, w...  6.21 us
    pallas_call x1, Pallas kernels, on_device(): call(far_kernel, 'far', [far_out((rows, count)), near_out((count, count))...  5.54 us
    pallas_call x1, Pallas kernels, on_device(): call(own_tiles_kernel, 'own_tiles', [far_out((rows, rows)), near_out((nei...  4.84 us
    all_to_all x2, waiting for transfers between devices, exchange(): got = lax.all_to_all(sent, 'rows', split_axis=0, concat_axis=0, tiled=True)  2.46 us
  transfers between devices with their start and end apart: 17, of which 10 were waited for; matrix products, arithmetic and copies ran while one was open for 0% of the time, Pallas kernels for 31%

profile of v9, /device:TPU:0, one launch (start us, length us, event | category | flops | bytes accessed | tf_op | source)
XLA Modules:
  0.0 68.7 jit_solution(15704302994227324514)
XLA Ops:
  0.0 1.4 %copy.7 = s32[1,32,16]{2,1,0:T(8,128)} copy(s32[1,32,16]{1,2,0:T(8,128)} %param.9) | data formatting | bytes 4096 | tf_op args[4]
  1.4 7.3 %all-to-all-start = ((s32[32,1,16]{2,1,0:T(1,128)}), s32[32,1,16]{2,1,0:T(1,128)S(1)}, u32[]{:S(2)}, u32[]{:S(2)}) async-start(s32[32,1,16]{2,1,0:T(1,128)} %bitcast.2), calls=%async_computation | async-start | bytes 32768 | tf_op jit(solution)/shard_map/all_to_all | solution.py:397
  8.7 4.8 %own_tiles.1 = (bf16[512,512]{1,0:T(8,128)(2,1)}, s32[50,512]{1,0:T(8,128)S(1)}, f32[50,512]{1,0:T(8,128)S(1)}, bf16[512,1024]{1,0:T(8,128)(2,1)S(1)}) custom-call(s32[4,8]{1,0:T(4,128)} %blocks_ref.1, s32[50,512]{1,0:T(8,128)} %bitcast.12, s32[50,512]{1,0:T(8,128)} %bitcast.13, bf16[512,1024]{1,0:T(8,128)(2,1)} %seeds_ref.3), custom_call_target="tpu_custom_call" | custom-call | flops 13107200 | tf_op jit(solution)/shard_map/own_tiles/pallas_call | solution.py:400
  13.5 2.2 %all-to-all-done.asked_ref = s32[32,1,16]{2,1,0:T(1,128)S(1)} async-done(((s32[32,1,16]{2,1,0:T(1,128)}), s32[32,1,16]{2,1,0:T(1,128)S(1)}, u32[]{:S(2)}, u32[]{:S(2)}) %all-to-all-start) | async-done | bytes 2080 | tf_op jit(solution)/shard_map/all_to_all | solution.py:397
  15.8 0.6 pick_a.1
  16.3 0.7 collective-permute-start
  17.0 2.3 %collective-permute-start.1 = (bf16[128,384]{1,0:T(8,128)(2,1)S(1)}, bf16[128,384]{1,0:T(8,128)(2,1)S(1)}, u32[]{:S(2)}, u32[]{:S(2)}) collective-permute-start(bf16[128,384]{1,0:T(8,128)(2,1)S(1)} %get-tuple-element.50), channel_id=1, source_target_pairs={{0,24},{1,25},{2,26},{3,27},{4,28},{5,29},{6,30},{7,31},{8,16},{9,... | collective-permute-start | bytes 294920 | tf_op jit(solution)/shard_map/ppermute | solution.py:346
  19.3 0.6 collective-permute-start.2
  19.9 1.4 %pick_b.1 = (bf16[512,384]{1,0:T(8,128)(2,1)}, bf16[512,640]{1,0:T(8,128)(2,1)}, bf16[512,128]{1,0:T(8,128)(2,1)S(1)}) custom-call(bf16[512,512]{1,0:T(8,128)(2,1)S(1)} %get-tuple-element.41.pick_ref, bf16[512,1024]{1,0:T(8,128)(2,1)S(1)} %get-tuple-element.40.seeds_ref, bf16[512,384]{1,0:T(8,128)(2,1)S(1)} %get-tuple-element.42.a_ref, ...), custom_call_target="tpu_custom_call" | custom-call | flops 335544320 | tf_op jit(solution)/shard_map/pick_b/pallas_call | solution.py:427
  21.3 3.6 %all-to-all-start.1 = ((bf16[32,16,640]{2,1,0:T(8,128)(2,1)}), bf16[32,16,640]{2,1,0:T(8,128)(2,1)S(1)}, u32[]{:S(2)}, u32[]{:S(2)}) async-start(bf16[32,16,640]{2,1,0:T(8,128)(2,1)} %bitcast.10), calls=%async_computation.1 | async-start | bytes 1310720 | tf_op jit(solution)/shard_map/all_to_all | solution.py:352
  24.9 1.2 %collective-permute-done.refs_1_ = bf16[128,384]{1,0:T(8,128)(2,1)S(1)} collective-permute-done((bf16[128,384]{1,0:T(8,128)(2,1)S(1)}, bf16[128,384]{1,0:T(8,128)(2,1)S(1)}, u32[]{:S(2)}, u32[]{:S(2)}) %collective-permute-start) | collective-permute-done | bytes 98336 | tf_op jit(solution)/shard_map/ppermute | solution.py:346
  26.1 0.0 collective-permute-done.1.refs_2_
  26.2 1.1 %collective-permute-done.2.refs_3_ = bf16[128,384]{1,0:T(8,128)(2,1)S(1)} collective-permute-done((bf16[128,384]{1,0:T(8,128)(2,1)S(1)}, bf16[128,384]{1,0:T(8,128)(2,1)S(1)}, u32[]{:S(2)}, u32[]{:S(2)}) %collective-permute-start.2) | collective-permute-done | bytes 98336 | tf_op jit(solution)/shard_map/ppermute | solution.py:346
  27.2 0.1 collective-permute-start.3
  27.3 1.4 %collective-permute-done.3.refs_4_ = bf16[256,384]{1,0:T(8,128)(2,1)S(1)} collective-permute-done((bf16[256,384]{1,0:T(8,128)(2,1)S(1)}, bf16[256,384]{1,0:T(8,128)(2,1)S(1)}, u32[]{:S(2)}, u32[]{:S(2)}) %collective-permute-start.3) | collective-permute-done | bytes 196640 | tf_op jit(solution)/shard_map/ppermute | solution.py:346
  28.8 1.0 %collective-permute-start.4 = (bf16[128,384]{1,0:T(8,128)(2,1)S(1)}, bf16[128,384]{1,0:T(8,128)(2,1)S(1)}, u32[]{:S(2)}, u32[]{:S(2)}) collective-permute-start(bf16[128,384]{1,0:T(8,128)(2,1)S(1)} %get-tuple-element.56), channel_id=1, source_target_pairs={{0,6},{1,7},{2,4},{3,5},{4,2},{5,3},{6,0},{7,1},{8,14},{9,15},{10,... | collective-permute-start | bytes 294920 | tf_op jit(solution)/shard_map/ppermute | solution.py:346
  29.8 1.3 %collective-permute-start.5 = (bf16[128,384]{1,0:T(8,128)(2,1)S(1)}, bf16[128,384]{1,0:T(8,128)(2,1)S(1)}, u32[]{:S(2)}, u32[]{:S(2)}) collective-permute-start(bf16[128,384]{1,0:T(8,128)(2,1)S(1)} %get-tuple-element.57), channel_id=1, source_target_pairs={{0,4},{1,5},{2,6},{3,7},{4,0},{5,1},{6,2},{7,3},{8,12},{9,13},{10,... | collective-permute-start | bytes 294920 | tf_op jit(solution)/shard_map/ppermute | solution.py:346
  31.1 1.3 %collective-permute-start.6 = (bf16[128,384]{1,0:T(8,128)(2,1)S(1)}, bf16[128,384]{1,0:T(8,128)(2,1)S(1)}, u32[]{:S(2)}, u32[]{:S(2)}) collective-permute-start(bf16[128,384]{1,0:T(8,128)(2,1)S(1)} %get-tuple-element.58), channel_id=1, source_target_pairs={{0,2},{1,3},{2,0},{3,1},{4,6},{5,7},{6,4},{7,5},{8,10},{9,11},{10,... | collective-permute-start | bytes 294920 | tf_op jit(solution)/shard_map/ppermute | solution.py:346
  32.4 5.5 %far.1 = (bf16[512,512]{1,0:T(8,128)(2,1)}, bf16[512,512]{1,0:T(8,128)(2,1)S(1)}, bf16[512,1024]{1,0:T(8,128)(2,1)S(1)}) custom-call(s32[32,1,16]{2,1,0:T(1,128)S(1)} %all-to-all-done.asked_ref, bf16[512,128]{1,0:T(8,128)(2,1)S(1)} %get-tuple-element.45.early_ref, bf16[512,512]{1,0:T(8,128)(2,1)} %get-tuple-element.39.after_ref.own_ref, ...), custom_call_target="tpu_custom_call" | custom-call | flops 1086849024 | tf_op jit(solution)/shard_map/far/pallas_call | solution.py:446
  37.9 0.0 collective-permute-done.4.refs_1_
  37.9 1.4 %collective-permute-done.5.refs_2_ = bf16[128,384]{1,0:T(8,128)(2,1)S(1)} collective-permute-done((bf16[128,384]{1,0:T(8,128)(2,1)S(1)}, bf16[128,384]{1,0:T(8,128)(2,1)S(1)}, u32[]{:S(2)}, u32[]{:S(2)}) %collective-permute-start.5) | collective-permute-done | bytes 98336 | tf_op jit(solution)/shard_map/ppermute | solution.py:346
  39.3 0.0 collective-permute-done.6.refs_3_
  39.3 0.8 %send_a.1 = (bf16[512,384]{1,0:T(8,128)(2,1)}, bf16[128,384]{1,0:T(8,128)(2,1)S(1)}, bf16[128,384]{1,0:T(8,128)(2,1)S(1)}, bf16[128,384]{1,0:T(8,128)(2,1)S(1)}, bf16[128,384]{1,0:T(8,128)(2,1)S(1)}) custom-call(s32[1]{0:T(128)} %bitcast.3.me_ref, bf16[512,512]{1,0:T(8,128)(2,1)S(1)} %get-tuple-element.54.tiles_ref, ...), custom_call_target="tpu_custom_call" | custom-call | flops 201326592 | tf_op jit(solution)/shard_map/send_a/pallas_call | solution.py:469
  40.1 2.4 %collective-permute-start.7 = (bf16[128,384]{1,0:T(8,128)(2,1)S(1)}, bf16[128,384]{1,0:T(8,128)(2,1)S(1)}, u32[]{:S(2)}, u32[]{:S(2)}) collective-permute-start(bf16[128,384]{1,0:T(8,128)(2,1)S(1)} %get-tuple-element.62), channel_id=1, source_target_pairs={{0,16},{1,17},{2,18},{3,19},{4,20},{5,21},{6,22},{7,23},{8,24},{9,... | collective-permute-start | bytes 294920 | tf_op jit(solution)/shard_map/ppermute | solution.py:346
  42.5 1.6 %collective-permute-start.8 = (bf16[128,384]{1,0:T(8,128)(2,1)S(1)}, bf16[128,384]{1,0:T(8,128)(2,1)S(1)}, u32[]{:S(2)}, u32[]{:S(2)}) collective-permute-start(bf16[128,384]{1,0:T(8,128)(2,1)S(1)} %get-tuple-element.63), channel_id=1, source_target_pairs={{0,24},{1,25},{2,26},{3,27},{4,28},{5,29},{6,30},{7,31},{8,16},{9,... | collective-permute-start | bytes 294920 | tf_op jit(solution)/shard_map/ppermute | solution.py:346
  44.2 0.0 collective-permute-start.9
  44.2 0.0 all-to-all-done.1
  44.2 1.3 %send_b.1 = (bf16[512,640]{1,0:T(8,128)(2,1)}, bf16[512,640]{1,0:T(8,128)(2,1)}) custom-call(bf16[512,512]{1,0:T(8,128)(2,1)S(1)} %get-tuple-element.54.tiles_ref, bf16[512,1024]{1,0:T(8,128)(2,1)S(1)} %get-tuple-element.55.base_ref, bf16[512,640]{1,0:T(8,128)(2,1)S(1)} %bitcast.9, bf16[128,384]{1,0:T(8,128)(2,1)S(1)} %get-tuple-element.60.after_ref.refs_0_), custom_call_target="tpu_custom_call" | custom-call | flops 335544320 | bytes 3538944 | tf_op jit(solution)/shard_map/send_b/pallas_call | solution.py:479
  45.5 4.0 %all-to-all-start.2 = ((bf16[32,16,640]{2,1,0:T(8,128)(2,1)}), bf16[32,16,640]{2,1,0:T(8,128)(2,1)S(1)}, u32[]{:S(2)}, u32[]{:S(2)}) async-start(bf16[32,16,640]{2,1,0:T(8,128)(2,1)} %bitcast.11), calls=%async_computation.2 | async-start | bytes 1310720 | tf_op jit(solution)/shard_map/all_to_all | solution.py:352
  49.5 1.0 %collective-permute-done.7.refs_1_ = bf16[128,384]{1,0:T(8,128)(2,1)S(1)} collective-permute-done((bf16[128,384]{1,0:T(8,128)(2,1)S(1)}, bf16[128,384]{1,0:T(8,128)(2,1)S(1)}, u32[]{:S(2)}, u32[]{:S(2)}) %collective-permute-start.7) | collective-permute-done | bytes 98336 | tf_op jit(solution)/shard_map/ppermute | solution.py:346
  50.5 0.0 collective-permute-done.8.refs_2_
  50.5 0.4 collective-permute-done.9.refs_3_
  50.9 0.1 collective-permute-start.10
  51.0 1.4 %collective-permute-done.10.refs_4_ = bf16[256,384]{1,0:T(8,128)(2,1)S(1)} collective-permute-done((bf16[256,384]{1,0:T(8,128)(2,1)S(1)}, bf16[256,384]{1,0:T(8,128)(2,1)S(1)}, u32[]{:S(2)}, u32[]{:S(2)}) %collective-permute-start.10) | collective-permute-done | bytes 196640 | tf_op jit(solution)/shard_map/ppermute | solution.py:346
  52.4 2.0 %collective-permute-start.11 = (bf16[128,384]{1,0:T(8,128)(2,1)S(1)}, bf16[128,384]{1,0:T(8,128)(2,1)S(1)}, u32[]{:S(2)}, u32[]{:S(2)}) collective-permute-start(bf16[128,384]{1,0:T(8,128)(2,1)S(1)} %get-tuple-element.70), channel_id=1, source_target_pairs={{0,6},{1,7},{2,4},{3,5},{4,2},{5,3},{6,0},{7,1},{8,14},{9,15},{10,... | collective-permute-start | bytes 294920 | tf_op jit(solution)/shard_map/ppermute | solution.py:346
  54.4 1.0 %collective-permute-start.12 = (bf16[128,384]{1,0:T(8,128)(2,1)S(1)}, bf16[128,384]{1,0:T(8,128)(2,1)S(1)}, u32[]{:S(2)}, u32[]{:S(2)}) collective-permute-start(bf16[128,384]{1,0:T(8,128)(2,1)S(1)} %get-tuple-element.71), channel_id=1, source_target_pairs={{0,4},{1,5},{2,6},{3,7},{4,0},{5,1},{6,2},{7,3},{8,12},{9,13},{10,... | collective-permute-start | bytes 294920 | tf_op jit(solution)/shard_map/ppermute | solution.py:346
  55.4 0.5 collective-permute-start.13
  56.0 6.2 %labels.1 = (bf16[512,1024]{1,0:T(8,128)(2,1)S(1)}, f8e4m3fn[512,1024]{1,0:T(32,128)(4,1)S(1)}, bf16[512,512]{1,0:T(8,128)(2,1)S(1)}) custom-call(bf16[512,512]{1,0:T(8,128)(2,1)} %get-tuple-element.39.after_ref.own_ref, bf16[512,512]{1,0:T(8,128)(2,1)} %get-tuple-element.53.far_ref, bf16[512,1024]{1,0:T(8,128)(2,1)} %seeds_ref.3, ...), custom_call_target="tpu_custom_call" | custom-call | flops 1610612736 | tf_op jit(solution)/shard_map/labels/pallas_call | solution.py:491
  62.2 0.0 collective-permute-done.11.refs_1_
  62.2 1.4 %collective-permute-done.12.refs_2_ = bf16[128,384]{1,0:T(8,128)(2,1)S(1)} collective-permute-done((bf16[128,384]{1,0:T(8,128)(2,1)S(1)}, bf16[128,384]{1,0:T(8,128)(2,1)S(1)}, u32[]{:S(2)}, u32[]{:S(2)}) %collective-permute-start.12) | collective-permute-done | bytes 98336 | tf_op jit(solution)/shard_map/ppermute | solution.py:346
  63.7 0.0 collective-permute-done.13.refs_3_
  63.7 1.3 %last_a.1.same_ref = bf16[512,1024]{1,0:T(8,128)(2,1)} custom-call(s32[1]{0:T(128)} %bitcast.3.me_ref, bf16[512,512]{1,0:T(8,128)(2,1)S(1)} %get-tuple-element.66.tiles_ref, bf16[512,1024]{1,0:T(8,128)(2,1)S(1)} %get-tuple-element.67.base_ref, f8e4m3fn[512,1024]{1,0:T(32,128)(4,1)S(1)} %get-tuple-element.68.rest_ref, ...), custom_call_target="tpu_custom_call" | custom-call | flops 201326592 | tf_op jit(solution)/shard_map/last_a/pallas_call | solution.py:510
  64.9 2.5 %all-to-all-done.2 = bf16[32,16,640]{2,1,0:T(8,128)(2,1)S(1)} async-done(((bf16[32,16,640]{2,1,0:T(8,128)(2,1)}), bf16[32,16,640]{2,1,0:T(8,128)(2,1)S(1)}, u32[]{:S(2)}, u32[]{:S(2)}) %all-to-all-start.2) | async-done | bytes 655392 | tf_op jit(solution)/shard_map/all_to_all | solution.py:352
  67.4 1.3 %last_b.1 = bf16[512,1024]{1,0:T(8,128)(2,1)} custom-call(bf16[512,512]{1,0:T(8,128)(2,1)S(1)} %get-tuple-element.66.tiles_ref, bf16[512,1024]{1,0:T(8,128)(2,1)S(1)} %get-tuple-element.67.base_ref, f8e4m3fn[512,1024]{1,0:T(32,128)(4,1)S(1)} %get-tuple-element.68.rest_ref, bf16[512,640]{1,0:T(8,128)(2,1)S(1)} %bitcast.8, ...), custom_call_target="tpu_custom_call", output_to_operand_aliasing={{}: (4, {})} | custom-call | flops 335544320 | bytes 4194304 | tf_op jit(solution)/shard_map/last_b/pallas_call | solution.py:519
  (4 shorter events, 0.1 us)
Async XLA Ops:
  1.4 14.4 %all-to-all-start = ((s32[32,1,16]{2,1,0:T(1,128)}), s32[32,1,16]{2,1,0:T(1,128)S(1)}, u32[]{:S(2)}, u32[]{:S(2)}) async-start(s32[32,1,16]{2,1,0:T(1,128)} %bitcast.2), calls=%async_computation | async-start | bytes 32768 | tf_op jit(solution)/shard_map/all_to_all | solution.py:397
  16.3 9.8 %collective-permute-start = (bf16[128,384]{1,0:T(8,128)(2,1)S(1)}, bf16[128,384]{1,0:T(8,128)(2,1)S(1)}, u32[]{:S(2)}, u32[]{:S(2)}) collective-permute-start(bf16[128,384]{1,0:T(8,128)(2,1)S(1)} %get-tuple-element.49), channel_id=1, source_target_pairs={{0,16},{1,17},{2,18},{3,19},{4,20},{5,21},{6,22},{7,23},{8,24},{9,... | collective-permute-start | bytes 294920 | tf_op jit(solution)/shard_map/ppermute | solution.py:346
  17.0 9.2 %collective-permute-start.1 = (bf16[128,384]{1,0:T(8,128)(2,1)S(1)}, bf16[128,384]{1,0:T(8,128)(2,1)S(1)}, u32[]{:S(2)}, u32[]{:S(2)}) collective-permute-start(bf16[128,384]{1,0:T(8,128)(2,1)S(1)} %get-tuple-element.50), channel_id=1, source_target_pairs={{0,24},{1,25},{2,26},{3,27},{4,28},{5,29},{6,30},{7,31},{8,16},{9,... | collective-permute-start | bytes 294920 | tf_op jit(solution)/shard_map/ppermute | solution.py:346
  19.3 7.9 %collective-permute-start.2 = (bf16[128,384]{1,0:T(8,128)(2,1)S(1)}, bf16[128,384]{1,0:T(8,128)(2,1)S(1)}, u32[]{:S(2)}, u32[]{:S(2)}) collective-permute-start(bf16[128,384]{1,0:T(8,128)(2,1)S(1)} %get-tuple-element.51), channel_id=1, source_target_pairs={{0,8},{1,9},{2,10},{3,11},{4,12},{5,13},{6,14},{7,15},{8,0},{9,1},... | collective-permute-start | bytes 294920 | tf_op jit(solution)/shard_map/ppermute | solution.py:346
  21.3 22.9 %all-to-all-start.1 = ((bf16[32,16,640]{2,1,0:T(8,128)(2,1)}), bf16[32,16,640]{2,1,0:T(8,128)(2,1)S(1)}, u32[]{:S(2)}, u32[]{:S(2)}) async-start(bf16[32,16,640]{2,1,0:T(8,128)(2,1)} %bitcast.10), calls=%async_computation.1 | async-start | bytes 1310720 | tf_op jit(solution)/shard_map/all_to_all | solution.py:352
  27.2 1.5 %collective-permute-start.3 = (bf16[256,384]{1,0:T(8,128)(2,1)S(1)}, bf16[256,384]{1,0:T(8,128)(2,1)S(1)}, u32[]{:S(2)}, u32[]{:S(2)}) collective-permute-start(bf16[256,384]{1,0:T(8,128)(2,1)S(1)} %gather.2), channel_id=1, source_target_pairs={{0,1},{1,0},{2,3},{3,2},{4,5},{5,4},{6,7},{7,6},{8,9},{9,8},{10,11... | collective-permute-start | bytes 589832 | tf_op jit(solution)/shard_map/ppermute | solution.py:346
  28.8 9.1 %collective-permute-start.4 = (bf16[128,384]{1,0:T(8,128)(2,1)S(1)}, bf16[128,384]{1,0:T(8,128)(2,1)S(1)}, u32[]{:S(2)}, u32[]{:S(2)}) collective-permute-start(bf16[128,384]{1,0:T(8,128)(2,1)S(1)} %get-tuple-element.56), channel_id=1, source_target_pairs={{0,6},{1,7},{2,4},{3,5},{4,2},{5,3},{6,0},{7,1},{8,14},{9,15},{10,... | collective-permute-start | bytes 294920 | tf_op jit(solution)/shard_map/ppermute | solution.py:346
  29.8 9.5 %collective-permute-start.5 = (bf16[128,384]{1,0:T(8,128)(2,1)S(1)}, bf16[128,384]{1,0:T(8,128)(2,1)S(1)}, u32[]{:S(2)}, u32[]{:S(2)}) collective-permute-start(bf16[128,384]{1,0:T(8,128)(2,1)S(1)} %get-tuple-element.57), channel_id=1, source_target_pairs={{0,4},{1,5},{2,6},{3,7},{4,0},{5,1},{6,2},{7,3},{8,12},{9,13},{10,... | collective-permute-start | bytes 294920 | tf_op jit(solution)/shard_map/ppermute | solution.py:346
  31.1 8.3 %collective-permute-start.6 = (bf16[128,384]{1,0:T(8,128)(2,1)S(1)}, bf16[128,384]{1,0:T(8,128)(2,1)S(1)}, u32[]{:S(2)}, u32[]{:S(2)}) collective-permute-start(bf16[128,384]{1,0:T(8,128)(2,1)S(1)} %get-tuple-element.58), channel_id=1, source_target_pairs={{0,2},{1,3},{2,0},{3,1},{4,6},{5,7},{6,4},{7,5},{8,10},{9,11},{10,... | collective-permute-start | bytes 294920 | tf_op jit(solution)/shard_map/ppermute | solution.py:346
  40.1 10.4 %collective-permute-start.7 = (bf16[128,384]{1,0:T(8,128)(2,1)S(1)}, bf16[128,384]{1,0:T(8,128)(2,1)S(1)}, u32[]{:S(2)}, u32[]{:S(2)}) collective-permute-start(bf16[128,384]{1,0:T(8,128)(2,1)S(1)} %get-tuple-element.62), channel_id=1, source_target_pairs={{0,16},{1,17},{2,18},{3,19},{4,20},{5,21},{6,22},{7,23},{8,24},{9,... | collective-permute-start | bytes 294920 | tf_op jit(solution)/shard_map/ppermute | solution.py:346
  42.5 8.0 %collective-permute-start.8 = (bf16[128,384]{1,0:T(8,128)(2,1)S(1)}, bf16[128,384]{1,0:T(8,128)(2,1)S(1)}, u32[]{:S(2)}, u32[]{:S(2)}) collective-permute-start(bf16[128,384]{1,0:T(8,128)(2,1)S(1)} %get-tuple-element.63), channel_id=1, source_target_pairs={{0,24},{1,25},{2,26},{3,27},{4,28},{5,29},{6,30},{7,31},{8,16},{9,... | collective-permute-start | bytes 294920 | tf_op jit(solution)/shard_map/ppermute | solution.py:346
  44.2 6.7 %collective-permute-start.9 = (bf16[128,384]{1,0:T(8,128)(2,1)S(1)}, bf16[128,384]{1,0:T(8,128)(2,1)S(1)}, u32[]{:S(2)}, u32[]{:S(2)}) collective-permute-start(bf16[128,384]{1,0:T(8,128)(2,1)S(1)} %get-tuple-element.64), channel_id=1, source_target_pairs={{0,8},{1,9},{2,10},{3,11},{4,12},{5,13},{6,14},{7,15},{8,0},{9,1},... | collective-permute-start | bytes 294920 | tf_op jit(solution)/shard_map/ppermute | solution.py:346
  45.5 21.9 %all-to-all-start.2 = ((bf16[32,16,640]{2,1,0:T(8,128)(2,1)}), bf16[32,16,640]{2,1,0:T(8,128)(2,1)S(1)}, u32[]{:S(2)}, u32[]{:S(2)}) async-start(bf16[32,16,640]{2,1,0:T(8,128)(2,1)} %bitcast.11), calls=%async_computation.2 | async-start | bytes 1310720 | tf_op jit(solution)/shard_map/all_to_all | solution.py:352
  50.9 1.5 %collective-permute-start.10 = (bf16[256,384]{1,0:T(8,128)(2,1)S(1)}, bf16[256,384]{1,0:T(8,128)(2,1)S(1)}, u32[]{:S(2)}, u32[]{:S(2)}) collective-permute-start(bf16[256,384]{1,0:T(8,128)(2,1)S(1)} %gather.3), channel_id=1, source_target_pairs={{0,1},{1,0},{2,3},{3,2},{4,5},{5,4},{6,7},{7,6},{8,9},{9,8},{10,11... | collective-permute-start | bytes 589832 | tf_op jit(solution)/shard_map/ppermute | solution.py:346
  52.4 9.8 %collective-permute-start.11 = (bf16[128,384]{1,0:T(8,128)(2,1)S(1)}, bf16[128,384]{1,0:T(8,128)(2,1)S(1)}, u32[]{:S(2)}, u32[]{:S(2)}) collective-permute-start(bf16[128,384]{1,0:T(8,128)(2,1)S(1)} %get-tuple-element.70), channel_id=1, source_target_pairs={{0,6},{1,7},{2,4},{3,5},{4,2},{5,3},{6,0},{7,1},{8,14},{9,15},{10,... | collective-permute-start | bytes 294920 | tf_op jit(solution)/shard_map/ppermute | solution.py:346
  54.4 9.2 %collective-permute-start.12 = (bf16[128,384]{1,0:T(8,128)(2,1)S(1)}, bf16[128,384]{1,0:T(8,128)(2,1)S(1)}, u32[]{:S(2)}, u32[]{:S(2)}) collective-permute-start(bf16[128,384]{1,0:T(8,128)(2,1)S(1)} %get-tuple-element.71), channel_id=1, source_target_pairs={{0,4},{1,5},{2,6},{3,7},{4,0},{5,1},{6,2},{7,3},{8,12},{9,13},{10,... | collective-permute-start | bytes 294920 | tf_op jit(solution)/shard_map/ppermute | solution.py:346
  55.4 8.2 %collective-permute-start.13 = (bf16[128,384]{1,0:T(8,128)(2,1)S(1)}, bf16[128,384]{1,0:T(8,128)(2,1)S(1)}, u32[]{:S(2)}, u32[]{:S(2)}) collective-permute-start(bf16[128,384]{1,0:T(8,128)(2,1)S(1)} %get-tuple-element.72), channel_id=1, source_target_pairs={{0,2},{1,3},{2,0},{3,1},{4,6},{5,7},{6,4},{7,5},{8,10},{9,11},{10,... | collective-permute-start | bytes 294920 | tf_op jit(solution)/shard_map/ppermute | solution.py:346

commit v10 on v9

--- a/solution.py
+++ b/solution.py
@@ -120,9 +120,12 @@
 
 def fill_edges(blocks_ref, pos_ref, weight_ref, column_ref, share_ref):
     block_count, tile_count = blocks_ref.shape
+    neighbours = pos_ref.shape[0]
+    column_ref[...] = jnp.full(column_ref.shape, -1, jnp.int32)
+    share_ref[...] = jnp.zeros(share_ref.shape, jnp.float32)
     weights = weight_ref[...].astype(jnp.float32)
     share = weights / jnp.sum(weights, axis=0, keepdims=True)
-    share_ref[...] = share.astype(jnp.bfloat16).astype(jnp.float32)
+    share_ref[:neighbours, :] = share.astype(jnp.bfloat16).astype(jnp.float32)
     for b in range(block_count):
         lanes = slice(b * BLK, (b + 1) * BLK)
         pos = pos_ref[:, lanes]
@@ -130,11 +133,11 @@
         base = jnp.full(pos.shape, blocks_ref[b, 0], jnp.int32)
         for j in range(1, tile_count):
             base = jnp.where(tile == j, blocks_ref[b, j], base)
-        column_ref[:, lanes] = base * BLK + pos % BLK
-
-
-def fill_tiles(column_ref, share_ref, tiles_ref, spot_ref, start, chunks):
-    neighbours, rows = column_ref.shape
+        column_ref[:neighbours, lanes] = base * BLK + pos % BLK
+
+
+def fill_tiles(neighbours, column_ref, share_ref, tiles_ref, spot_ref, start, chunks):
+    rows = column_ref.shape[1]
     sub = lax.broadcasted_iota(jnp.int32, (BLK, BLK), 0).astype(jnp.float32).astype(jnp.bfloat16)
     sub = sub.reshape(BLK // PACK, PACK, BLK)
 
@@ -173,7 +176,7 @@
     fill_edges(blocks_ref, pos_ref, weight_ref, column_ref, share_ref)
     for i in range(own_ref.shape[1] // BLK):
         cols = slice(i * BLK, (i + 1) * BLK)
-        fill_tiles(column_ref, share_ref, own_ref, spot_ref, 0, (i, i + 1))
+        fill_tiles(pos_ref.shape[0], column_ref, share_ref, own_ref, spot_ref, 0, (i, i + 1))
         copies.append(push(own_ref.at[:, cols], own_hbm.at[:, cols], sems.at[1 + i]))
     for copy in copies:
         copy.wait()
@@ -188,7 +191,19 @@
 
 
 def pick_b_kernel(
-    pick_ref, seeds_ref, a_ref, column_ref, share_ref, out_a, out_b, early_ref, b_ref, spot_ref, sems
+    pick_ref,
+    seeds_ref,
+    a_ref,
+    column_ref,
+    share_ref,
+    out_a,
+    out_b,
+    early_ref,
+    b_ref,
+    spot_ref,
+    sems,
+    *,
+    neighbours,
 ):
     rows = seeds_ref.shape[0]
     wide = a_ref.shape[1]
@@ -196,7 +211,8 @@
     for i, rows_here in enumerate(strips_of(pick_ref.shape[0])):
         b_ref[rows_here, :] = dot(pick_ref[rows_here, :], seeds_ref[:, wide:]).astype(jnp.bfloat16)
         copies.append(push(b_ref.at[rows_here], out_b.at[rows_here], sems.at[1 + i]))
-    fill_tiles(column_ref, share_ref, early_ref, spot_ref, rows, (0, early_ref.shape[1] // BLK))
+    chunks = (0, early_ref.shape[1] // BLK)
+    fill_tiles(neighbours, column_ref, share_ref, early_ref, spot_ref, rows, chunks)
     for copy in copies:
         copy.wait()
 
@@ -217,13 +233,16 @@
     pick_ref,
     picked_ref,
     spot_ref,
+    *,
+    neighbours,
 ):
     del after_ref
     rows, width = seeds_ref.shape
     wide = sent_a_ref.shape[1]
     done = early_ref.shape[1]
     far_ref[:, :done] = early_ref[...]
-    fill_tiles(column_ref, share_ref, far_ref, spot_ref, rows, (done // BLK, far_ref.shape[1] // BLK))
+    chunks = (done // BLK, far_ref.shape[1] // BLK)
+    fill_tiles(neighbours, column_ref, share_ref, far_ref, spot_ref, rows, chunks)
     pick_ref[...] = picks(asked_ref[...], rows)
     for cols in pieces_of(0, far_ref.shape[1]):
         picked_far_ref[:, cols] = dot(pick_ref[...], far_ref[:, cols]).astype(jnp.bfloat16)
@@ -385,6 +404,7 @@
     peers, slots = wanted.shape[1:]
     count = peers * slots
     neighbours = neighbor_pos.shape[1]
+    depth = -(-neighbours // PACK) * PACK
     planes = peers // GROUP
     wide = max(3 * width // 8 // BLK, 1) * BLK
     assert peers & (peers - 1) == 0 and peers >= GROUP
@@ -402,15 +422,15 @@
         "own_tiles",
         [
             far_out((rows, rows)),
-            near_out((neighbours, rows), jnp.int32),
-            near_out((neighbours, rows), jnp.float32),
+            near_out((depth, rows), jnp.int32),
+            near_out((depth, rows), jnp.float32),
             near_out((rows, width)),
         ],
         [SMEM, VMEM, VMEM, HBM],
         [HBM, VMEM, VMEM, VMEM],
         [
             pltpu.VMEM((rows, rows), bf16),
-            pltpu.VMEM((neighbours, rows), jnp.float32),
+            pltpu.VMEM((depth, rows), jnp.float32),
             sems((1 + rows // BLK,)),
         ],
         flops=neighbours * rows * rows,
@@ -425,7 +445,7 @@
     )(me, asked, near_seeds, far_in(own))
     got_planes = across(sent_planes, peers)
     sent_a, sent_b, early = call(
-        pick_b_kernel,
+        functools.partial(pick_b_kernel, neighbours=neighbours),
         "pick_b",
         [
             far_out((count, wide)),
@@ -436,7 +456,7 @@
         [HBM, HBM, VMEM],
         [
             pltpu.VMEM((count, width - wide), bf16),
-            pltpu.VMEM((neighbours, rows), jnp.float32),
+            pltpu.VMEM((depth, rows), jnp.float32),
             sems((1 + n_sent,)),
         ],
         flops=2 * count * rows * (width - wide),
@@ -444,7 +464,7 @@
     received_b = exchange(sent_b, peers)
     got_pairs = within(got_planes, peers, slots)
     far, picked_far, sent_base = call(
-        far_kernel,
+        functools.partial(far_kernel, neighbours=neighbours),
         "far",
         [far_out((rows, count)), near_out((count, count)), near_out((count, width))],
         [VMEM] * 8 + [ANY],
@@ -452,7 +472,7 @@
         [
             pltpu.VMEM((count, rows), bf16),
             pltpu.VMEM((count, rows), bf16),
-            pltpu.VMEM((neighbours, rows), jnp.float32),
+            pltpu.VMEM((depth, rows), jnp.float32),
         ],
         flops=2 * rows * count * (count + rows + width) + neighbours * rows * count,
     )(

time: 69.1 us -> 69.1 us (level)
  no operation moved by 1% of the time
where the time goes in v10:
time: 69.1 us; the launch traced here: 68.7 us
  starting transfers between devices  29.8 us (43%)
  Pallas kernels  23.3 us (34%)
  waiting for transfers between devices  14.1 us (20%)
  local copies, waits for them, and re-layouts  1.38 us (2%)
    ppermute x14, starting transfers between devices, swap(): return lax.ppermute(x, 'rows', [(i, i ^ distance) for i in range(peers)])  14.8 us
    ppermute x14, waiting for transfers between devices, swap(): return lax.ppermute(x, 'rows', [(i, i ^ distance) for i in range(peers)])  9.42 us
    all_to_all x2, starting transfers between devices, exchange(): got = lax.all_to_all(sent, 'rows', split_axis=0, concat_axis=0, tiled=True)  7.64 us
    all_to_all x1, starting transfers between devices, on_device(): lax.all_to_all(wanted.reshape(peers, 1, slots), 'rows', split_axis=0, con...  7.3 us
    pallas_call x1, Pallas kernels, on_device(): call(labels_kernel, 'labels', [near_out((rows, width)), near_out((rows, w...  6.21 us
    pallas_call x1, Pallas kernels, on_device(): call(functools.partial(far_kernel, neighbours=neighbours), 'far', [far_ou...  5.55 us
    pallas_call x1, Pallas kernels, on_device(): call(own_tiles_kernel, 'own_tiles', [far_out((rows, rows)), near_out((dep...  4.85 us
    all_to_all x2, waiting for transfers between devices, exchange(): got = lax.all_to_all(sent, 'rows', split_axis=0, concat_axis=0, tiled=True)  2.46 us
  transfers between devices with their start and end apart: 17, of which 10 were waited for; matrix products, arithmetic and copies ran while one was open for 0% of the time, Pallas kernels for 31%

profile of v10, /device:TPU:0, one launch (start us, length us, event | category | flops | bytes accessed | tf_op | source)
XLA Modules:
  0.0 68.7 jit_solution(10588094204791314301)
XLA Ops:
  0.0 1.4 %copy.7 = s32[1,32,16]{2,1,0:T(8,128)} copy(s32[1,32,16]{1,2,0:T(8,128)} %param.9) | data formatting | bytes 4096 | tf_op args[4]
  1.4 7.3 %all-to-all-start = ((s32[32,1,16]{2,1,0:T(1,128)}), s32[32,1,16]{2,1,0:T(1,128)S(1)}, u32[]{:S(2)}, u32[]{:S(2)}) async-start(s32[32,1,16]{2,1,0:T(1,128)} %bitcast.2), calls=%async_computation | async-start | bytes 32768 | tf_op jit(solution)/shard_map/all_to_all | solution.py:417
  8.7 4.9 %own_tiles.1 = (bf16[512,512]{1,0:T(8,128)(2,1)}, s32[64,512]{1,0:T(8,128)S(1)}, f32[64,512]{1,0:T(8,128)S(1)}, bf16[512,1024]{1,0:T(8,128)(2,1)S(1)}) custom-call(s32[4,8]{1,0:T(4,128)} %blocks_ref.1, s32[50,512]{1,0:T(8,128)} %bitcast.12, s32[50,512]{1,0:T(8,128)} %bitcast.13, bf16[512,1024]{1,0:T(8,128)(2,1)} %seeds_ref.3), custom_call_target="tpu_custom_call" | custom-call | flops 13107200 | tf_op jit(solution)/shard_map/own_tiles/pallas_call | solution.py:420
  13.5 2.2 %all-to-all-done.asked_ref = s32[32,1,16]{2,1,0:T(1,128)S(1)} async-done(((s32[32,1,16]{2,1,0:T(1,128)}), s32[32,1,16]{2,1,0:T(1,128)S(1)}, u32[]{:S(2)}, u32[]{:S(2)}) %all-to-all-start) | async-done | bytes 2080 | tf_op jit(solution)/shard_map/all_to_all | solution.py:417
  15.8 0.6 pick_a.1
  16.3 0.7 collective-permute-start
  17.0 2.3 %collective-permute-start.1 = (bf16[128,384]{1,0:T(8,128)(2,1)S(1)}, bf16[128,384]{1,0:T(8,128)(2,1)S(1)}, u32[]{:S(2)}, u32[]{:S(2)}) collective-permute-start(bf16[128,384]{1,0:T(8,128)(2,1)S(1)} %get-tuple-element.50), channel_id=1, source_target_pairs={{0,24},{1,25},{2,26},{3,27},{4,28},{5,29},{6,30},{7,31},{8,16},{9,... | collective-permute-start | bytes 294920 | tf_op jit(solution)/shard_map/ppermute | solution.py:365
  19.3 0.6 collective-permute-start.2
  19.9 1.4 %pick_b.1 = (bf16[512,384]{1,0:T(8,128)(2,1)}, bf16[512,640]{1,0:T(8,128)(2,1)}, bf16[512,128]{1,0:T(8,128)(2,1)S(1)}) custom-call(bf16[512,512]{1,0:T(8,128)(2,1)S(1)} %get-tuple-element.41.pick_ref, bf16[512,1024]{1,0:T(8,128)(2,1)S(1)} %get-tuple-element.40.seeds_ref, bf16[512,384]{1,0:T(8,128)(2,1)S(1)} %get-tuple-element.42.a_ref, ...), custom_call_target="tpu_custom_call" | custom-call | flops 335544320 | tf_op jit(solution)/shard_map/pick_b/pallas_call | solution.py:447
  21.3 3.6 %all-to-all-start.1 = ((bf16[32,16,640]{2,1,0:T(8,128)(2,1)}), bf16[32,16,640]{2,1,0:T(8,128)(2,1)S(1)}, u32[]{:S(2)}, u32[]{:S(2)}) async-start(bf16[32,16,640]{2,1,0:T(8,128)(2,1)} %bitcast.10), calls=%async_computation.1 | async-start | bytes 1310720 | tf_op jit(solution)/shard_map/all_to_all | solution.py:371
  24.9 1.2 %collective-permute-done.refs_1_ = bf16[128,384]{1,0:T(8,128)(2,1)S(1)} collective-permute-done((bf16[128,384]{1,0:T(8,128)(2,1)S(1)}, bf16[128,384]{1,0:T(8,128)(2,1)S(1)}, u32[]{:S(2)}, u32[]{:S(2)}) %collective-permute-start) | collective-permute-done | bytes 98336 | tf_op jit(solution)/shard_map/ppermute | solution.py:365
  26.1 0.0 collective-permute-done.1.refs_2_
  26.2 1.1 %collective-permute-done.2.refs_3_ = bf16[128,384]{1,0:T(8,128)(2,1)S(1)} collective-permute-done((bf16[128,384]{1,0:T(8,128)(2,1)S(1)}, bf16[128,384]{1,0:T(8,128)(2,1)S(1)}, u32[]{:S(2)}, u32[]{:S(2)}) %collective-permute-start.2) | collective-permute-done | bytes 98336 | tf_op jit(solution)/shard_map/ppermute | solution.py:365
  27.2 0.1 collective-permute-start.3
  27.3 1.4 %collective-permute-done.3.refs_4_ = bf16[256,384]{1,0:T(8,128)(2,1)S(1)} collective-permute-done((bf16[256,384]{1,0:T(8,128)(2,1)S(1)}, bf16[256,384]{1,0:T(8,128)(2,1)S(1)}, u32[]{:S(2)}, u32[]{:S(2)}) %collective-permute-start.3) | collective-permute-done | bytes 196640 | tf_op jit(solution)/shard_map/ppermute | solution.py:365
  28.8 1.0 %collective-permute-start.4 = (bf16[128,384]{1,0:T(8,128)(2,1)S(1)}, bf16[128,384]{1,0:T(8,128)(2,1)S(1)}, u32[]{:S(2)}, u32[]{:S(2)}) collective-permute-start(bf16[128,384]{1,0:T(8,128)(2,1)S(1)} %get-tuple-element.56), channel_id=1, source_target_pairs={{0,6},{1,7},{2,4},{3,5},{4,2},{5,3},{6,0},{7,1},{8,14},{9,15},{10,... | collective-permute-start | bytes 294920 | tf_op jit(solution)/shard_map/ppermute | solution.py:365
  29.8 1.2 %collective-permute-start.5 = (bf16[128,384]{1,0:T(8,128)(2,1)S(1)}, bf16[128,384]{1,0:T(8,128)(2,1)S(1)}, u32[]{:S(2)}, u32[]{:S(2)}) collective-permute-start(bf16[128,384]{1,0:T(8,128)(2,1)S(1)} %get-tuple-element.57), channel_id=1, source_target_pairs={{0,4},{1,5},{2,6},{3,7},{4,0},{5,1},{6,2},{7,3},{8,12},{9,13},{10,... | collective-permute-start | bytes 294920 | tf_op jit(solution)/shard_map/ppermute | solution.py:365
  31.1 1.3 %collective-permute-start.6 = (bf16[128,384]{1,0:T(8,128)(2,1)S(1)}, bf16[128,384]{1,0:T(8,128)(2,1)S(1)}, u32[]{:S(2)}, u32[]{:S(2)}) collective-permute-start(bf16[128,384]{1,0:T(8,128)(2,1)S(1)} %get-tuple-element.58), channel_id=1, source_target_pairs={{0,2},{1,3},{2,0},{3,1},{4,6},{5,7},{6,4},{7,5},{8,10},{9,11},{10,... | collective-permute-start | bytes 294920 | tf_op jit(solution)/shard_map/ppermute | solution.py:365
  32.4 5.5 %far.1 = (bf16[512,512]{1,0:T(8,128)(2,1)}, bf16[512,512]{1,0:T(8,128)(2,1)S(1)}, bf16[512,1024]{1,0:T(8,128)(2,1)S(1)}) custom-call(s32[32,1,16]{2,1,0:T(1,128)S(1)} %all-to-all-done.asked_ref, bf16[512,128]{1,0:T(8,128)(2,1)S(1)} %get-tuple-element.45.early_ref, bf16[512,512]{1,0:T(8,128)(2,1)} %get-tuple-element.39.after_ref.own_ref, ...), custom_call_target="tpu_custom_call" | custom-call | flops 1086849024 | tf_op jit(solution)/shard_map/far/pallas_call | solution.py:466
  37.9 0.0 collective-permute-done.4.refs_1_
  37.9 1.4 %collective-permute-done.5.refs_2_ = bf16[128,384]{1,0:T(8,128)(2,1)S(1)} collective-permute-done((bf16[128,384]{1,0:T(8,128)(2,1)S(1)}, bf16[128,384]{1,0:T(8,128)(2,1)S(1)}, u32[]{:S(2)}, u32[]{:S(2)}) %collective-permute-start.5) | collective-permute-done | bytes 98336 | tf_op jit(solution)/shard_map/ppermute | solution.py:365
  39.3 0.0 collective-permute-done.6.refs_3_
  39.3 0.8 %send_a.1 = (bf16[512,384]{1,0:T(8,128)(2,1)}, bf16[128,384]{1,0:T(8,128)(2,1)S(1)}, bf16[128,384]{1,0:T(8,128)(2,1)S(1)}, bf16[128,384]{1,0:T(8,128)(2,1)S(1)}, bf16[128,384]{1,0:T(8,128)(2,1)S(1)}) custom-call(s32[1]{0:T(128)} %bitcast.3.me_ref, bf16[512,512]{1,0:T(8,128)(2,1)S(1)} %get-tuple-element.54.tiles_ref, ...), custom_call_target="tpu_custom_call" | custom-call | flops 201326592 | tf_op jit(solution)/shard_map/send_a/pallas_call | solution.py:489
  40.1 2.4 %collective-permute-start.7 = (bf16[128,384]{1,0:T(8,128)(2,1)S(1)}, bf16[128,384]{1,0:T(8,128)(2,1)S(1)}, u32[]{:S(2)}, u32[]{:S(2)}) collective-permute-start(bf16[128,384]{1,0:T(8,128)(2,1)S(1)} %get-tuple-element.62), channel_id=1, source_target_pairs={{0,16},{1,17},{2,18},{3,19},{4,20},{5,21},{6,22},{7,23},{8,24},{9,... | collective-permute-start | bytes 294920 | tf_op jit(solution)/shard_map/ppermute | solution.py:365
  42.5 1.6 %collective-permute-start.8 = (bf16[128,384]{1,0:T(8,128)(2,1)S(1)}, bf16[128,384]{1,0:T(8,128)(2,1)S(1)}, u32[]{:S(2)}, u32[]{:S(2)}) collective-permute-start(bf16[128,384]{1,0:T(8,128)(2,1)S(1)} %get-tuple-element.63), channel_id=1, source_target_pairs={{0,24},{1,25},{2,26},{3,27},{4,28},{5,29},{6,30},{7,31},{8,16},{9,... | collective-permute-start | bytes 294920 | tf_op jit(solution)/shard_map/ppermute | solution.py:365
  44.2 0.0 collective-permute-start.9
  44.2 0.0 all-to-all-done.1
  44.2 1.3 %send_b.1 = (bf16[512,640]{1,0:T(8,128)(2,1)}, bf16[512,640]{1,0:T(8,128)(2,1)}) custom-call(bf16[512,512]{1,0:T(8,128)(2,1)S(1)} %get-tuple-element.54.tiles_ref, bf16[512,1024]{1,0:T(8,128)(2,1)S(1)} %get-tuple-element.55.base_ref, bf16[512,640]{1,0:T(8,128)(2,1)S(1)} %bitcast.9, bf16[128,384]{1,0:T(8,128)(2,1)S(1)} %get-tuple-element.60.after_ref.refs_0_), custom_call_target="tpu_custom_call" | custom-call | flops 335544320 | bytes 3538944 | tf_op jit(solution)/shard_map/send_b/pallas_call | solution.py:499
  45.5 4.0 %all-to-all-start.2 = ((bf16[32,16,640]{2,1,0:T(8,128)(2,1)}), bf16[32,16,640]{2,1,0:T(8,128)(2,1)S(1)}, u32[]{:S(2)}, u32[]{:S(2)}) async-start(bf16[32,16,640]{2,1,0:T(8,128)(2,1)} %bitcast.11), calls=%async_computation.2 | async-start | bytes 1310720 | tf_op jit(solution)/shard_map/all_to_all | solution.py:371
  49.5 1.0 %collective-permute-done.7.refs_1_ = bf16[128,384]{1,0:T(8,128)(2,1)S(1)} collective-permute-done((bf16[128,384]{1,0:T(8,128)(2,1)S(1)}, bf16[128,384]{1,0:T(8,128)(2,1)S(1)}, u32[]{:S(2)}, u32[]{:S(2)}) %collective-permute-start.7) | collective-permute-done | bytes 98336 | tf_op jit(solution)/shard_map/ppermute | solution.py:365
  50.5 0.0 collective-permute-done.8.refs_2_
  50.5 0.3 collective-permute-done.9.refs_3_
  50.9 0.1 collective-permute-start.10
  51.0 1.4 %collective-permute-done.10.refs_4_ = bf16[256,384]{1,0:T(8,128)(2,1)S(1)} collective-permute-done((bf16[256,384]{1,0:T(8,128)(2,1)S(1)}, bf16[256,384]{1,0:T(8,128)(2,1)S(1)}, u32[]{:S(2)}, u32[]{:S(2)}) %collective-permute-start.10) | collective-permute-done | bytes 196640 | tf_op jit(solution)/shard_map/ppermute | solution.py:365
  52.4 2.0 %collective-permute-start.11 = (bf16[128,384]{1,0:T(8,128)(2,1)S(1)}, bf16[128,384]{1,0:T(8,128)(2,1)S(1)}, u32[]{:S(2)}, u32[]{:S(2)}) collective-permute-start(bf16[128,384]{1,0:T(8,128)(2,1)S(1)} %get-tuple-element.70), channel_id=1, source_target_pairs={{0,6},{1,7},{2,4},{3,5},{4,2},{5,3},{6,0},{7,1},{8,14},{9,15},{10,... | collective-permute-start | bytes 294920 | tf_op jit(solution)/shard_map/ppermute | solution.py:365
  54.5 1.0 %collective-permute-start.12 = (bf16[128,384]{1,0:T(8,128)(2,1)S(1)}, bf16[128,384]{1,0:T(8,128)(2,1)S(1)}, u32[]{:S(2)}, u32[]{:S(2)}) collective-permute-start(bf16[128,384]{1,0:T(8,128)(2,1)S(1)} %get-tuple-element.71), channel_id=1, source_target_pairs={{0,4},{1,5},{2,6},{3,7},{4,0},{5,1},{6,2},{7,3},{8,12},{9,13},{10,... | collective-permute-start | bytes 294920 | tf_op jit(solution)/shard_map/ppermute | solution.py:365
  55.5 0.5 collective-permute-start.13
  56.0 6.2 %labels.1 = (bf16[512,1024]{1,0:T(8,128)(2,1)S(1)}, f8e4m3fn[512,1024]{1,0:T(32,128)(4,1)S(1)}, bf16[512,512]{1,0:T(8,128)(2,1)S(1)}) custom-call(bf16[512,512]{1,0:T(8,128)(2,1)} %get-tuple-element.39.after_ref.own_ref, bf16[512,512]{1,0:T(8,128)(2,1)} %get-tuple-element.53.far_ref, bf16[512,1024]{1,0:T(8,128)(2,1)} %seeds_ref.3, ...), custom_call_target="tpu_custom_call" | custom-call | flops 1610612736 | tf_op jit(solution)/shard_map/labels/pallas_call | solution.py:511
  62.2 0.0 collective-permute-done.11.refs_1_
  62.2 1.4 %collective-permute-done.12.refs_2_ = bf16[128,384]{1,0:T(8,128)(2,1)S(1)} collective-permute-done((bf16[128,384]{1,0:T(8,128)(2,1)S(1)}, bf16[128,384]{1,0:T(8,128)(2,1)S(1)}, u32[]{:S(2)}, u32[]{:S(2)}) %collective-permute-start.12) | collective-permute-done | bytes 98336 | tf_op jit(solution)/shard_map/ppermute | solution.py:365
  63.7 0.0 collective-permute-done.13.refs_3_
  63.7 1.3 %last_a.1.same_ref = bf16[512,1024]{1,0:T(8,128)(2,1)} custom-call(s32[1]{0:T(128)} %bitcast.3.me_ref, bf16[512,512]{1,0:T(8,128)(2,1)S(1)} %get-tuple-element.66.tiles_ref, bf16[512,1024]{1,0:T(8,128)(2,1)S(1)} %get-tuple-element.67.base_ref, f8e4m3fn[512,1024]{1,0:T(32,128)(4,1)S(1)} %get-tuple-element.68.rest_ref, ...), custom_call_target="tpu_custom_call" | custom-call | flops 201326592 | tf_op jit(solution)/shard_map/last_a/pallas_call | solution.py:530
  64.9 2.5 %all-to-all-done.2 = bf16[32,16,640]{2,1,0:T(8,128)(2,1)S(1)} async-done(((bf16[32,16,640]{2,1,0:T(8,128)(2,1)}), bf16[32,16,640]{2,1,0:T(8,128)(2,1)S(1)}, u32[]{:S(2)}, u32[]{:S(2)}) %all-to-all-start.2) | async-done | bytes 655392 | tf_op jit(solution)/shard_map/all_to_all | solution.py:371
  67.4 1.3 %last_b.1 = bf16[512,1024]{1,0:T(8,128)(2,1)} custom-call(bf16[512,512]{1,0:T(8,128)(2,1)S(1)} %get-tuple-element.66.tiles_ref, bf16[512,1024]{1,0:T(8,128)(2,1)S(1)} %get-tuple-element.67.base_ref, f8e4m3fn[512,1024]{1,0:T(32,128)(4,1)S(1)} %get-tuple-element.68.rest_ref, bf16[512,640]{1,0:T(8,128)(2,1)S(1)} %bitcast.8, ...), custom_call_target="tpu_custom_call", output_to_operand_aliasing={{}: (4, {})} | custom-call | flops 335544320 | bytes 4194304 | tf_op jit(solution)/shard_map/last_b/pallas_call | solution.py:539
  (4 shorter events, 0.1 us)
Async XLA Ops:
  1.4 14.4 %all-to-all-start = ((s32[32,1,16]{2,1,0:T(1,128)}), s32[32,1,16]{2,1,0:T(1,128)S(1)}, u32[]{:S(2)}, u32[]{:S(2)}) async-start(s32[32,1,16]{2,1,0:T(1,128)} %bitcast.2), calls=%async_computation | async-start | bytes 32768 | tf_op jit(solution)/shard_map/all_to_all | solution.py:417
  16.3 9.8 %collective-permute-start = (bf16[128,384]{1,0:T(8,128)(2,1)S(1)}, bf16[128,384]{1,0:T(8,128)(2,1)S(1)}, u32[]{:S(2)}, u32[]{:S(2)}) collective-permute-start(bf16[128,384]{1,0:T(8,128)(2,1)S(1)} %get-tuple-element.49), channel_id=1, source_target_pairs={{0,16},{1,17},{2,18},{3,19},{4,20},{5,21},{6,22},{7,23},{8,24},{9,... | collective-permute-start | bytes 294920 | tf_op jit(solution)/shard_map/ppermute | solution.py:365
  17.0 9.2 %collective-permute-start.1 = (bf16[128,384]{1,0:T(8,128)(2,1)S(1)}, bf16[128,384]{1,0:T(8,128)(2,1)S(1)}, u32[]{:S(2)}, u32[]{:S(2)}) collective-permute-start(bf16[128,384]{1,0:T(8,128)(2,1)S(1)} %get-tuple-element.50), channel_id=1, source_target_pairs={{0,24},{1,25},{2,26},{3,27},{4,28},{5,29},{6,30},{7,31},{8,16},{9,... | collective-permute-start | bytes 294920 | tf_op jit(solution)/shard_map/ppermute | solution.py:365
  19.3 7.9 %collective-permute-start.2 = (bf16[128,384]{1,0:T(8,128)(2,1)S(1)}, bf16[128,384]{1,0:T(8,128)(2,1)S(1)}, u32[]{:S(2)}, u32[]{:S(2)}) collective-permute-start(bf16[128,384]{1,0:T(8,128)(2,1)S(1)} %get-tuple-element.51), channel_id=1, source_target_pairs={{0,8},{1,9},{2,10},{3,11},{4,12},{5,13},{6,14},{7,15},{8,0},{9,1},... | collective-permute-start | bytes 294920 | tf_op jit(solution)/shard_map/ppermute | solution.py:365
  21.3 22.9 %all-to-all-start.1 = ((bf16[32,16,640]{2,1,0:T(8,128)(2,1)}), bf16[32,16,640]{2,1,0:T(8,128)(2,1)S(1)}, u32[]{:S(2)}, u32[]{:S(2)}) async-start(bf16[32,16,640]{2,1,0:T(8,128)(2,1)} %bitcast.10), calls=%async_computation.1 | async-start | bytes 1310720 | tf_op jit(solution)/shard_map/all_to_all | solution.py:371
  27.2 1.5 %collective-permute-start.3 = (bf16[256,384]{1,0:T(8,128)(2,1)S(1)}, bf16[256,384]{1,0:T(8,128)(2,1)S(1)}, u32[]{:S(2)}, u32[]{:S(2)}) collective-permute-start(bf16[256,384]{1,0:T(8,128)(2,1)S(1)} %gather.2), channel_id=1, source_target_pairs={{0,1},{1,0},{2,3},{3,2},{4,5},{5,4},{6,7},{7,6},{8,9},{9,8},{10,11... | collective-permute-start | bytes 589832 | tf_op jit(solution)/shard_map/ppermute | solution.py:365
  28.8 9.1 %collective-permute-start.4 = (bf16[128,384]{1,0:T(8,128)(2,1)S(1)}, bf16[128,384]{1,0:T(8,128)(2,1)S(1)}, u32[]{:S(2)}, u32[]{:S(2)}) collective-permute-start(bf16[128,384]{1,0:T(8,128)(2,1)S(1)} %get-tuple-element.56), channel_id=1, source_target_pairs={{0,6},{1,7},{2,4},{3,5},{4,2},{5,3},{6,0},{7,1},{8,14},{9,15},{10,... | collective-permute-start | bytes 294920 | tf_op jit(solution)/shard_map/ppermute | solution.py:365
  29.8 9.5 %collective-permute-start.5 = (bf16[128,384]{1,0:T(8,128)(2,1)S(1)}, bf16[128,384]{1,0:T(8,128)(2,1)S(1)}, u32[]{:S(2)}, u32[]{:S(2)}) collective-permute-start(bf16[128,384]{1,0:T(8,128)(2,1)S(1)} %get-tuple-element.57), channel_id=1, source_target_pairs={{0,4},{1,5},{2,6},{3,7},{4,0},{5,1},{6,2},{7,3},{8,12},{9,13},{10,... | collective-permute-start | bytes 294920 | tf_op jit(solution)/shard_map/ppermute | solution.py:365
  31.1 8.3 %collective-permute-start.6 = (bf16[128,384]{1,0:T(8,128)(2,1)S(1)}, bf16[128,384]{1,0:T(8,128)(2,1)S(1)}, u32[]{:S(2)}, u32[]{:S(2)}) collective-permute-start(bf16[128,384]{1,0:T(8,128)(2,1)S(1)} %get-tuple-element.58), channel_id=1, source_target_pairs={{0,2},{1,3},{2,0},{3,1},{4,6},{5,7},{6,4},{7,5},{8,10},{9,11},{10,... | collective-permute-start | bytes 294920 | tf_op jit(solution)/shard_map/ppermute | solution.py:365
  40.1 10.4 %collective-permute-start.7 = (bf16[128,384]{1,0:T(8,128)(2,1)S(1)}, bf16[128,384]{1,0:T(8,128)(2,1)S(1)}, u32[]{:S(2)}, u32[]{:S(2)}) collective-permute-start(bf16[128,384]{1,0:T(8,128)(2,1)S(1)} %get-tuple-element.62), channel_id=1, source_target_pairs={{0,16},{1,17},{2,18},{3,19},{4,20},{5,21},{6,22},{7,23},{8,24},{9,... | collective-permute-start | bytes 294920 | tf_op jit(solution)/shard_map/ppermute | solution.py:365
  42.5 8.0 %collective-permute-start.8 = (bf16[128,384]{1,0:T(8,128)(2,1)S(1)}, bf16[128,384]{1,0:T(8,128)(2,1)S(1)}, u32[]{:S(2)}, u32[]{:S(2)}) collective-permute-start(bf16[128,384]{1,0:T(8,128)(2,1)S(1)} %get-tuple-element.63), channel_id=1, source_target_pairs={{0,24},{1,25},{2,26},{3,27},{4,28},{5,29},{6,30},{7,31},{8,16},{9,... | collective-permute-start | bytes 294920 | tf_op jit(solution)/shard_map/ppermute | solution.py:365
  44.2 6.7 %collective-permute-start.9 = (bf16[128,384]{1,0:T(8,128)(2,1)S(1)}, bf16[128,384]{1,0:T(8,128)(2,1)S(1)}, u32[]{:S(2)}, u32[]{:S(2)}) collective-permute-start(bf16[128,384]{1,0:T(8,128)(2,1)S(1)} %get-tuple-element.64), channel_id=1, source_target_pairs={{0,8},{1,9},{2,10},{3,11},{4,12},{5,13},{6,14},{7,15},{8,0},{9,1},... | collective-permute-start | bytes 294920 | tf_op jit(solution)/shard_map/ppermute | solution.py:365
  45.5 21.9 %all-to-all-start.2 = ((bf16[32,16,640]{2,1,0:T(8,128)(2,1)}), bf16[32,16,640]{2,1,0:T(8,128)(2,1)S(1)}, u32[]{:S(2)}, u32[]{:S(2)}) async-start(bf16[32,16,640]{2,1,0:T(8,128)(2,1)} %bitcast.11), calls=%async_computation.2 | async-start | bytes 1310720 | tf_op jit(solution)/shard_map/all_to_all | solution.py:371
  50.9 1.5 %collective-permute-start.10 = (bf16[256,384]{1,0:T(8,128)(2,1)S(1)}, bf16[256,384]{1,0:T(8,128)(2,1)S(1)}, u32[]{:S(2)}, u32[]{:S(2)}) collective-permute-start(bf16[256,384]{1,0:T(8,128)(2,1)S(1)} %gather.3), channel_id=1, source_target_pairs={{0,1},{1,0},{2,3},{3,2},{4,5},{5,4},{6,7},{7,6},{8,9},{9,8},{10,11... | collective-permute-start | bytes 589832 | tf_op jit(solution)/shard_map/ppermute | solution.py:365
  52.4 9.8 %collective-permute-start.11 = (bf16[128,384]{1,0:T(8,128)(2,1)S(1)}, bf16[128,384]{1,0:T(8,128)(2,1)S(1)}, u32[]{:S(2)}, u32[]{:S(2)}) collective-permute-start(bf16[128,384]{1,0:T(8,128)(2,1)S(1)} %get-tuple-element.70), channel_id=1, source_target_pairs={{0,6},{1,7},{2,4},{3,5},{4,2},{5,3},{6,0},{7,1},{8,14},{9,15},{10,... | collective-permute-start | bytes 294920 | tf_op jit(solution)/shard_map/ppermute | solution.py:365
  54.5 9.2 %collective-permute-start.12 = (bf16[128,384]{1,0:T(8,128)(2,1)S(1)}, bf16[128,384]{1,0:T(8,128)(2,1)S(1)}, u32[]{:S(2)}, u32[]{:S(2)}) collective-permute-start(bf16[128,384]{1,0:T(8,128)(2,1)S(1)} %get-tuple-element.71), channel_id=1, source_target_pairs={{0,4},{1,5},{2,6},{3,7},{4,0},{5,1},{6,2},{7,3},{8,12},{9,13},{10,... | collective-permute-start | bytes 294920 | tf_op jit(solution)/shard_map/ppermute | solution.py:365
  55.5 8.2 %collective-permute-start.13 = (bf16[128,384]{1,0:T(8,128)(2,1)S(1)}, bf16[128,384]{1,0:T(8,128)(2,1)S(1)}, u32[]{:S(2)}, u32[]{:S(2)}) collective-permute-start(bf16[128,384]{1,0:T(8,128)(2,1)S(1)} %get-tuple-element.72), channel_id=1, source_target_pairs={{0,2},{1,3},{2,0},{3,1},{4,6},{5,7},{6,4},{7,5},{8,10},{9,11},{10,... | collective-permute-start | bytes 294920 | tf_op jit(solution)/shard_map/ppermute | solution.py:365

commit v11 on v10

--- a/solution.py
+++ b/solution.py
@@ -230,6 +230,7 @@
     far_ref,
     picked_far_ref,
     sent_base_ref,
+    whole_ref,
     pick_ref,
     picked_ref,
     spot_ref,
@@ -238,6 +239,10 @@
 ):
     del after_ref
     rows, width = seeds_ref.shape
+    head = own_ref.shape[1]
+    whole_ref[:, :head] = own_ref[...]
+    chunks = (head // BLK, rows // BLK)
+    fill_tiles(neighbours, column_ref, share_ref, whole_ref, spot_ref, 0, chunks)
     wide = sent_a_ref.shape[1]
     done = early_ref.shape[1]
     far_ref[:, :done] = early_ref[...]
@@ -247,7 +252,7 @@
     for cols in pieces_of(0, far_ref.shape[1]):
         picked_far_ref[:, cols] = dot(pick_ref[...], far_ref[:, cols]).astype(jnp.bfloat16)
     for cols in pieces_of(0, rows):
-        picked_ref[:, cols] = dot(pick_ref[...], own_ref[:, cols]).astype(jnp.bfloat16)
+        picked_ref[:, cols] = dot(pick_ref[...], whole_ref[:, cols]).astype(jnp.bfloat16)
     for cols in pieces_of(0, wide) + pieces_of(wide, width):
         sent = sent_a_ref[:, cols] if cols.stop <= wide else sent_b_ref[:, moved(cols, -wide)]
         sent_base = KEEP * dot(picked_ref[...], seeds_ref[:, cols])
@@ -408,6 +413,7 @@
     planes = peers // GROUP
     wide = max(3 * width // 8 // BLK, 1) * BLK
     assert peers & (peers - 1) == 0 and peers >= GROUP
+    head = rows - BLK
     me = lax.axis_index("rows").astype(jnp.int32).reshape(1)
     sems = pltpu.SemaphoreType.DMA
     bf16 = jnp.bfloat16
@@ -421,7 +427,7 @@
         own_tiles_kernel,
         "own_tiles",
         [
-            far_out((rows, rows)),
+            far_out((rows, head)),
             near_out((depth, rows), jnp.int32),
             near_out((depth, rows), jnp.float32),
             near_out((rows, width)),
@@ -429,9 +435,9 @@
         [SMEM, VMEM, VMEM, HBM],
         [HBM, VMEM, VMEM, VMEM],
         [
-            pltpu.VMEM((rows, rows), bf16),
+            pltpu.VMEM((rows, head), bf16),
             pltpu.VMEM((depth, rows), jnp.float32),
-            sems((1 + rows // BLK,)),
+            sems((1 + head // BLK,)),
         ],
         flops=neighbours * rows * rows,
     )(far_in(tile_blocks), far_in(neighbor_pos.T), far_in(edge_weight.T), far_in(seeds))
@@ -463,12 +469,17 @@
     )(pick, near_seeds, near_a, column, share)
     received_b = exchange(sent_b, peers)
     got_pairs = within(got_planes, peers, slots)
-    far, picked_far, sent_base = call(
+    far, picked_far, sent_base, own = call(
         functools.partial(far_kernel, neighbours=neighbours),
         "far",
-        [far_out((rows, count)), near_out((count, count)), near_out((count, width))],
+        [
+            far_out((rows, count)),
+            near_out((count, count)),
+            near_out((count, width)),
+            far_out((rows, rows)),
+        ],
         [VMEM] * 8 + [ANY],
-        [VMEM] * 3,
+        [VMEM] * 4,
         [
             pltpu.VMEM((count, rows), bf16),
             pltpu.VMEM((count, rows), bf16),

time: 69.1 us -> 68.3 us (0.988)
  starting transfers between devices: 29.8 us -> 28.7 us
    all_to_all x2, starting transfers between devices: 7.64 us -> 6.35 us  [exchange(): got = lax.all_to_all(sent, 'rows', split_axis=0, concat_axis=0, tiled=True)]
    all_to_all x1, waiting for transfers between devices: 2.21 us -> 2.97 us  [on_device(): lax.all_to_all(wanted.reshape(peers, 1, slots), 'rows', split_axis=0, con...]
    pallas_call x1, Pallas kernels: 4.85 us -> 4.09 us  [on_device(): call(own_tiles_kernel, 'own_tiles', [far_out((rows, head)), near_out((dep...]
    pallas_call x1, Pallas kernels: 5.55 us -> 6.28 us  [on_device(): call(functools.partial(far_kernel, neighbours=neighbours), 'far', [far_ou...]
  transfers between devices with their start and end apart: 17 -> 17, of which waited for: 10 -> 10; matrix products, arithmetic and copies ran while one was open for 0% -> 0% of each run, Pallas kernels for 31% -> 32%
where the time goes in v11:
time: 68.3 us; the launch traced here: 67.9 us
  starting transfers between devices  28.7 us (42%)
  Pallas kernels  23.3 us (34%)
  waiting for transfers between devices  14.4 us (21%)
  local copies, waits for them, and re-layouts  1.38 us (2%)
    ppermute x14, starting transfers between devices, swap(): return lax.ppermute(x, 'rows', [(i, i ^ distance) for i in range(peers)])  15.1 us
    ppermute x14, waiting for transfers between devices, swap(): return lax.ppermute(x, 'rows', [(i, i ^ distance) for i in range(peers)])  9.2 us
    all_to_all x1, starting transfers between devices, on_device(): lax.all_to_all(wanted.reshape(peers, 1, slots), 'rows', split_axis=0, con...  7.3 us
    all_to_all x2, starting transfers between devices, exchange(): got = lax.all_to_all(sent, 'rows', split_axis=0, concat_axis=0, tiled=True)  6.35 us
    pallas_call x1, Pallas kernels, on_device(): call(functools.partial(far_kernel, neighbours=neighbours), 'far', [far_ou...  6.28 us
    pallas_call x1, Pallas kernels, on_device(): call(labels_kernel, 'labels', [near_out((rows, width)), near_out((rows, w...  6.21 us
    pallas_call x1, Pallas kernels, on_device(): call(own_tiles_kernel, 'own_tiles', [far_out((rows, head)), near_out((dep...  4.09 us
    all_to_all x1, waiting for transfers between devices, on_device(): lax.all_to_all(wanted.reshape(peers, 1, slots), 'rows', split_axis=0, con...  2.97 us
  transfers between devices with their start and end apart: 17, of which 10 were waited for; matrix products, arithmetic and copies ran while one was open for 0% of the time, Pallas kernels for 32%

profile of v11, /device:TPU:0, one launch (start us, length us, event | category | flops | bytes accessed | tf_op | source)
XLA Modules:
  0.0 67.9 jit_solution(10294948292822064724)
XLA Ops:
  0.0 1.4 %copy.7 = s32[1,32,16]{2,1,0:T(8,128)} copy(s32[1,32,16]{1,2,0:T(8,128)} %param.9) | data formatting | bytes 4096 | tf_op args[4]
  1.4 7.3 %all-to-all-start = ((s32[32,1,16]{2,1,0:T(1,128)}), s32[32,1,16]{2,1,0:T(1,128)S(1)}, u32[]{:S(2)}, u32[]{:S(2)}) async-start(s32[32,1,16]{2,1,0:T(1,128)} %bitcast), calls=%async_computation | async-start | bytes 32768 | tf_op jit(solution)/shard_map/all_to_all | solution.py:423
  8.7 4.1 %own_tiles.1 = (bf16[512,384]{1,0:T(8,128)(2,1)}, s32[64,512]{1,0:T(8,128)S(1)}, f32[64,512]{1,0:T(8,128)S(1)}, bf16[512,1024]{1,0:T(8,128)(2,1)S(1)}) custom-call(s32[4,8]{1,0:T(4,128)} %blocks_ref.1, s32[50,512]{1,0:T(8,128)} %bitcast.12, s32[50,512]{1,0:T(8,128)} %bitcast.13, bf16[512,1024]{1,0:T(8,128)(2,1)} %seeds_ref.3), custom_call_target="tpu_custom_call" | custom-call | flops 13107200 | tf_op jit(solution)/shard_map/own_tiles/pallas_call | solution.py:426
  12.8 3.0 %all-to-all-done.asked_ref = s32[32,1,16]{2,1,0:T(1,128)S(1)} async-done(((s32[32,1,16]{2,1,0:T(1,128)}), s32[32,1,16]{2,1,0:T(1,128)S(1)}, u32[]{:S(2)}, u32[]{:S(2)}) %all-to-all-start) | async-done | bytes 2080 | tf_op jit(solution)/shard_map/all_to_all | solution.py:423
  15.8 0.6 pick_a.1
  16.3 0.7 collective-permute-start
  17.0 2.3 %collective-permute-start.1 = (bf16[128,384]{1,0:T(8,128)(2,1)S(1)}, bf16[128,384]{1,0:T(8,128)(2,1)S(1)}, u32[]{:S(2)}, u32[]{:S(2)}) collective-permute-start(bf16[128,384]{1,0:T(8,128)(2,1)S(1)} %get-tuple-element.51), channel_id=1, source_target_pairs={{0,24},{1,25},{2,26},{3,27},{4,28},{5,29},{6,30},{7,31},{8,16},{9,... | collective-permute-start | bytes 294920 | tf_op jit(solution)/shard_map/ppermute | solution.py:370
  19.3 0.6 collective-permute-start.2
  19.9 1.4 %pick_b.1 = (bf16[512,384]{1,0:T(8,128)(2,1)}, bf16[512,640]{1,0:T(8,128)(2,1)}, bf16[512,128]{1,0:T(8,128)(2,1)S(1)}) custom-call(bf16[512,512]{1,0:T(8,128)(2,1)S(1)} %get-tuple-element.42.pick_ref, bf16[512,1024]{1,0:T(8,128)(2,1)S(1)} %get-tuple-element.40.seeds_ref, bf16[512,384]{1,0:T(8,128)(2,1)S(1)} %get-tuple-element.43.a_ref, ...), custom_call_target="tpu_custom_call" | custom-call | flops 335544320 | tf_op jit(solution)/shard_map/pick_b/pallas_call | solution.py:453
  21.3 2.9 %all-to-all-start.1 = ((bf16[32,16,640]{2,1,0:T(8,128)(2,1)}), bf16[32,16,640]{2,1,0:T(8,128)(2,1)S(1)}, u32[]{:S(2)}, u32[]{:S(2)}) async-start(bf16[32,16,640]{2,1,0:T(8,128)(2,1)} %bitcast.10), calls=%async_computation.1 | async-start | bytes 1310720 | tf_op jit(solution)/shard_map/all_to_all | solution.py:376
  24.2 2.0 %collective-permute-done.refs_1_ = bf16[128,384]{1,0:T(8,128)(2,1)S(1)} collective-permute-done((bf16[128,384]{1,0:T(8,128)(2,1)S(1)}, bf16[128,384]{1,0:T(8,128)(2,1)S(1)}, u32[]{:S(2)}, u32[]{:S(2)}) %collective-permute-start) | collective-permute-done | bytes 98336 | tf_op jit(solution)/shard_map/ppermute | solution.py:370
  26.1 0.0 collective-permute-done.1.refs_2_
  26.1 1.0 %collective-permute-done.2.refs_3_ = bf16[128,384]{1,0:T(8,128)(2,1)S(1)} collective-permute-done((bf16[128,384]{1,0:T(8,128)(2,1)S(1)}, bf16[128,384]{1,0:T(8,128)(2,1)S(1)}, u32[]{:S(2)}, u32[]{:S(2)}) %collective-permute-start.2) | collective-permute-done | bytes 98336 | tf_op jit(solution)/shard_map/ppermute | solution.py:370
  27.1 0.1 collective-permute-start.3
  27.2 1.4 %collective-permute-done.3.refs_4_ = bf16[256,384]{1,0:T(8,128)(2,1)S(1)} collective-permute-done((bf16[256,384]{1,0:T(8,128)(2,1)S(1)}, bf16[256,384]{1,0:T(8,128)(2,1)S(1)}, u32[]{:S(2)}, u32[]{:S(2)}) %collective-permute-start.3) | collective-permute-done | bytes 196640 | tf_op jit(solution)/shard_map/ppermute | solution.py:370
  28.7 0.9 %collective-permute-start.4 = (bf16[128,384]{1,0:T(8,128)(2,1)S(1)}, bf16[128,384]{1,0:T(8,128)(2,1)S(1)}, u32[]{:S(2)}, u32[]{:S(2)}) collective-permute-start(bf16[128,384]{1,0:T(8,128)(2,1)S(1)} %get-tuple-element.58), channel_id=1, source_target_pairs={{0,6},{1,7},{2,4},{3,5},{4,2},{5,3},{6,0},{7,1},{8,14},{9,15},{10,... | collective-permute-start | bytes 294920 | tf_op jit(solution)/shard_map/ppermute | solution.py:370
  29.6 1.5 %collective-permute-start.5 = (bf16[128,384]{1,0:T(8,128)(2,1)S(1)}, bf16[128,384]{1,0:T(8,128)(2,1)S(1)}, u32[]{:S(2)}, u32[]{:S(2)}) collective-permute-start(bf16[128,384]{1,0:T(8,128)(2,1)S(1)} %get-tuple-element.59), channel_id=1, source_target_pairs={{0,4},{1,5},{2,6},{3,7},{4,0},{5,1},{6,2},{7,3},{8,12},{9,13},{10,... | collective-permute-start | bytes 294920 | tf_op jit(solution)/shard_map/ppermute | solution.py:370
  31.1 1.2 %collective-permute-start.6 = (bf16[128,384]{1,0:T(8,128)(2,1)S(1)}, bf16[128,384]{1,0:T(8,128)(2,1)S(1)}, u32[]{:S(2)}, u32[]{:S(2)}) collective-permute-start(bf16[128,384]{1,0:T(8,128)(2,1)S(1)} %get-tuple-element.60), channel_id=1, source_target_pairs={{0,2},{1,3},{2,0},{3,1},{4,6},{5,7},{6,4},{7,5},{8,10},{9,11},{10,... | collective-permute-start | bytes 294920 | tf_op jit(solution)/shard_map/ppermute | solution.py:370
  32.2 6.3 %far.1 = (bf16[512,512]{1,0:T(8,128)(2,1)}, bf16[512,512]{1,0:T(8,128)(2,1)S(1)}, bf16[512,1024]{1,0:T(8,128)(2,1)S(1)}, bf16[512,512]{1,0:T(8,128)(2,1)}) custom-call(s32[32,1,16]{2,1,0:T(1,128)S(1)} %all-to-all-done.asked_ref, bf16[512,128]{1,0:T(8,128)(2,1)S(1)} %get-tuple-element.46.early_ref, bf16[512,384]{1,0:T(8,128)(2,1)} %get-tuple-element.41.after_ref.own_ref, ...), custom_call_target="tpu_custom_call" | custom-call | flops 1086849024 | tf_op jit(solution)/shard_map/far/pallas_call | solution.py:472
  38.5 0.0 collective-permute-done.4.refs_1_
  38.5 0.3 collective-permute-done.5.refs_2_
  38.9 0.0 collective-permute-done.6.refs_3_
  38.9 0.8 %send_a.1 = (bf16[512,384]{1,0:T(8,128)(2,1)}, bf16[128,384]{1,0:T(8,128)(2,1)S(1)}, bf16[128,384]{1,0:T(8,128)(2,1)S(1)}, bf16[128,384]{1,0:T(8,128)(2,1)S(1)}, bf16[128,384]{1,0:T(8,128)(2,1)S(1)}) custom-call(s32[1]{0:T(128)} %bitcast.1.me_ref, bf16[512,512]{1,0:T(8,128)(2,1)S(1)} %get-tuple-element.56.tiles_ref, ...), custom_call_target="tpu_custom_call" | custom-call | flops 201326592 | tf_op jit(solution)/shard_map/send_a/pallas_call | solution.py:500
  39.7 2.1 %collective-permute-start.7 = (bf16[128,384]{1,0:T(8,128)(2,1)S(1)}, bf16[128,384]{1,0:T(8,128)(2,1)S(1)}, u32[]{:S(2)}, u32[]{:S(2)}) collective-permute-start(bf16[128,384]{1,0:T(8,128)(2,1)S(1)} %get-tuple-element.64), channel_id=1, source_target_pairs={{0,16},{1,17},{2,18},{3,19},{4,20},{5,21},{6,22},{7,23},{8,24},{9,... | collective-permute-start | bytes 294920 | tf_op jit(solution)/shard_map/ppermute | solution.py:370
  41.8 2.1 %collective-permute-start.8 = (bf16[128,384]{1,0:T(8,128)(2,1)S(1)}, bf16[128,384]{1,0:T(8,128)(2,1)S(1)}, u32[]{:S(2)}, u32[]{:S(2)}) collective-permute-start(bf16[128,384]{1,0:T(8,128)(2,1)S(1)} %get-tuple-element.65), channel_id=1, source_target_pairs={{0,24},{1,25},{2,26},{3,27},{4,28},{5,29},{6,30},{7,31},{8,16},{9,... | collective-permute-start | bytes 294920 | tf_op jit(solution)/shard_map/ppermute | solution.py:370
  43.9 0.0 collective-permute-start.9
  43.9 0.0 all-to-all-done.1
  43.9 1.3 %send_b.1 = (bf16[512,640]{1,0:T(8,128)(2,1)}, bf16[512,640]{1,0:T(8,128)(2,1)}) custom-call(bf16[512,512]{1,0:T(8,128)(2,1)S(1)} %get-tuple-element.56.tiles_ref, bf16[512,1024]{1,0:T(8,128)(2,1)S(1)} %get-tuple-element.57.base_ref, bf16[512,640]{1,0:T(8,128)(2,1)S(1)} %bitcast.9, bf16[128,384]{1,0:T(8,128)(2,1)S(1)} %get-tuple-element.62.after_ref.refs_0_), custom_call_target="tpu_custom_call" | custom-call | flops 335544320 | bytes 3538944 | tf_op jit(solution)/shard_map/send_b/pallas_call | solution.py:510
  45.2 3.5 %all-to-all-start.2 = ((bf16[32,16,640]{2,1,0:T(8,128)(2,1)}), bf16[32,16,640]{2,1,0:T(8,128)(2,1)S(1)}, u32[]{:S(2)}, u32[]{:S(2)}) async-start(bf16[32,16,640]{2,1,0:T(8,128)(2,1)} %bitcast.11), calls=%async_computation.2 | async-start | bytes 1310720 | tf_op jit(solution)/shard_map/all_to_all | solution.py:376
  48.7 1.8 %collective-permute-done.7.refs_1_ = bf16[128,384]{1,0:T(8,128)(2,1)S(1)} collective-permute-done((bf16[128,384]{1,0:T(8,128)(2,1)S(1)}, bf16[128,384]{1,0:T(8,128)(2,1)S(1)}, u32[]{:S(2)}, u32[]{:S(2)}) %collective-permute-start.7) | collective-permute-done | bytes 98336 | tf_op jit(solution)/shard_map/ppermute | solution.py:370
  50.5 0.0 collective-permute-done.8.refs_2_
  50.5 0.2 collective-permute-done.9.refs_3_
  50.8 0.1 collective-permute-start.10
  50.8 1.4 %collective-permute-done.10.refs_4_ = bf16[256,384]{1,0:T(8,128)(2,1)S(1)} collective-permute-done((bf16[256,384]{1,0:T(8,128)(2,1)S(1)}, bf16[256,384]{1,0:T(8,128)(2,1)S(1)}, u32[]{:S(2)}, u32[]{:S(2)}) %collective-permute-start.10) | collective-permute-done | bytes 196640 | tf_op jit(solution)/shard_map/ppermute | solution.py:370
  52.3 1.4 %collective-permute-start.11 = (bf16[128,384]{1,0:T(8,128)(2,1)S(1)}, bf16[128,384]{1,0:T(8,128)(2,1)S(1)}, u32[]{:S(2)}, u32[]{:S(2)}) collective-permute-start(bf16[128,384]{1,0:T(8,128)(2,1)S(1)} %get-tuple-element.72), channel_id=1, source_target_pairs={{0,6},{1,7},{2,4},{3,5},{4,2},{5,3},{6,0},{7,1},{8,14},{9,15},{10,... | collective-permute-start | bytes 294920 | tf_op jit(solution)/shard_map/ppermute | solution.py:370
  53.7 1.0 %collective-permute-start.12 = (bf16[128,384]{1,0:T(8,128)(2,1)S(1)}, bf16[128,384]{1,0:T(8,128)(2,1)S(1)}, u32[]{:S(2)}, u32[]{:S(2)}) collective-permute-start(bf16[128,384]{1,0:T(8,128)(2,1)S(1)} %get-tuple-element.73), channel_id=1, source_target_pairs={{0,4},{1,5},{2,6},{3,7},{4,0},{5,1},{6,2},{7,3},{8,12},{9,13},{10,... | collective-permute-start | bytes 294920 | tf_op jit(solution)/shard_map/ppermute | solution.py:370
  54.7 1.1 %collective-permute-start.13 = (bf16[128,384]{1,0:T(8,128)(2,1)S(1)}, bf16[128,384]{1,0:T(8,128)(2,1)S(1)}, u32[]{:S(2)}, u32[]{:S(2)}) collective-permute-start(bf16[128,384]{1,0:T(8,128)(2,1)S(1)} %get-tuple-element.74), channel_id=1, source_target_pairs={{0,2},{1,3},{2,0},{3,1},{4,6},{5,7},{6,4},{7,5},{8,10},{9,11},{10,... | collective-permute-start | bytes 294920 | tf_op jit(solution)/shard_map/ppermute | solution.py:370
  55.9 6.2 %labels.1 = (bf16[512,1024]{1,0:T(8,128)(2,1)S(1)}, f8e4m3fn[512,1024]{1,0:T(32,128)(4,1)S(1)}, bf16[512,512]{1,0:T(8,128)(2,1)S(1)}) custom-call(bf16[512,512]{1,0:T(8,128)(2,1)} %get-tuple-element.54.own_ref, bf16[512,512]{1,0:T(8,128)(2,1)} %get-tuple-element.55.far_ref, bf16[512,1024]{1,0:T(8,128)(2,1)} %seeds_ref.3, ...), custom_call_target="tpu_custom_call" | custom-call | flops 1610612736 | tf_op jit(solution)/shard_map/labels/pallas_call | solution.py:522
  62.1 0.0 collective-permute-done.11.refs_1_
  62.1 1.0 %collective-permute-done.12.refs_2_ = bf16[128,384]{1,0:T(8,128)(2,1)S(1)} collective-permute-done((bf16[128,384]{1,0:T(8,128)(2,1)S(1)}, bf16[128,384]{1,0:T(8,128)(2,1)S(1)}, u32[]{:S(2)}, u32[]{:S(2)}) %collective-permute-start.12) | collective-permute-done | bytes 98336 | tf_op jit(solution)/shard_map/ppermute | solution.py:370
  63.1 0.0 collective-permute-done.13.refs_3_
  63.1 1.3 %last_a.1.same_ref = bf16[512,1024]{1,0:T(8,128)(2,1)} custom-call(s32[1]{0:T(128)} %bitcast.1.me_ref, bf16[512,512]{1,0:T(8,128)(2,1)S(1)} %get-tuple-element.68.tiles_ref, bf16[512,1024]{1,0:T(8,128)(2,1)S(1)} %get-tuple-element.69.base_ref, f8e4m3fn[512,1024]{1,0:T(32,128)(4,1)S(1)} %get-tuple-element.70.rest_ref, ...), custom_call_target="tpu_custom_call" | custom-call | flops 201326592 | tf_op jit(solution)/shard_map/last_a/pallas_call | solution.py:541
  64.4 2.2 %all-to-all-done.2 = bf16[32,16,640]{2,1,0:T(8,128)(2,1)S(1)} async-done(((bf16[32,16,640]{2,1,0:T(8,128)(2,1)}), bf16[32,16,640]{2,1,0:T(8,128)(2,1)S(1)}, u32[]{:S(2)}, u32[]{:S(2)}) %all-to-all-start.2) | async-done | bytes 655392 | tf_op jit(solution)/shard_map/all_to_all | solution.py:376
  66.6 1.3 %last_b.1 = bf16[512,1024]{1,0:T(8,128)(2,1)} custom-call(bf16[512,512]{1,0:T(8,128)(2,1)S(1)} %get-tuple-element.68.tiles_ref, bf16[512,1024]{1,0:T(8,128)(2,1)S(1)} %get-tuple-element.69.base_ref, f8e4m3fn[512,1024]{1,0:T(32,128)(4,1)S(1)} %get-tuple-element.70.rest_ref, bf16[512,640]{1,0:T(8,128)(2,1)S(1)} %bitcast.8, ...), custom_call_target="tpu_custom_call", output_to_operand_aliasing={{}: (4, {})} | custom-call | flops 335544320 | bytes 4194304 | tf_op jit(solution)/shard_map/last_b/pallas_call | solution.py:550
  (4 shorter events, 0.1 us)
Async XLA Ops:
  1.4 14.4 %all-to-all-start = ((s32[32,1,16]{2,1,0:T(1,128)}), s32[32,1,16]{2,1,0:T(1,128)S(1)}, u32[]{:S(2)}, u32[]{:S(2)}) async-start(s32[32,1,16]{2,1,0:T(1,128)} %bitcast), calls=%async_computation | async-start | bytes 32768 | tf_op jit(solution)/shard_map/all_to_all | solution.py:423
  16.3 9.8 %collective-permute-start = (bf16[128,384]{1,0:T(8,128)(2,1)S(1)}, bf16[128,384]{1,0:T(8,128)(2,1)S(1)}, u32[]{:S(2)}, u32[]{:S(2)}) collective-permute-start(bf16[128,384]{1,0:T(8,128)(2,1)S(1)} %get-tuple-element.50), channel_id=1, source_target_pairs={{0,16},{1,17},{2,18},{3,19},{4,20},{5,21},{6,22},{7,23},{8,24},{9,... | collective-permute-start | bytes 294920 | tf_op jit(solution)/shard_map/ppermute | solution.py:370
  17.0 9.2 %collective-permute-start.1 = (bf16[128,384]{1,0:T(8,128)(2,1)S(1)}, bf16[128,384]{1,0:T(8,128)(2,1)S(1)}, u32[]{:S(2)}, u32[]{:S(2)}) collective-permute-start(bf16[128,384]{1,0:T(8,128)(2,1)S(1)} %get-tuple-element.51), channel_id=1, source_target_pairs={{0,24},{1,25},{2,26},{3,27},{4,28},{5,29},{6,30},{7,31},{8,16},{9,... | collective-permute-start | bytes 294920 | tf_op jit(solution)/shard_map/ppermute | solution.py:370
  19.3 7.8 %collective-permute-start.2 = (bf16[128,384]{1,0:T(8,128)(2,1)S(1)}, bf16[128,384]{1,0:T(8,128)(2,1)S(1)}, u32[]{:S(2)}, u32[]{:S(2)}) collective-permute-start(bf16[128,384]{1,0:T(8,128)(2,1)S(1)} %get-tuple-element.52), channel_id=1, source_target_pairs={{0,8},{1,9},{2,10},{3,11},{4,12},{5,13},{6,14},{7,15},{8,0},{9,1},... | collective-permute-start | bytes 294920 | tf_op jit(solution)/shard_map/ppermute | solution.py:370
  21.3 22.6 %all-to-all-start.1 = ((bf16[32,16,640]{2,1,0:T(8,128)(2,1)}), bf16[32,16,640]{2,1,0:T(8,128)(2,1)S(1)}, u32[]{:S(2)}, u32[]{:S(2)}) async-start(bf16[32,16,640]{2,1,0:T(8,128)(2,1)} %bitcast.10), calls=%async_computation.1 | async-start | bytes 1310720 | tf_op jit(solution)/shard_map/all_to_all | solution.py:376
  27.1 1.5 %collective-permute-start.3 = (bf16[256,384]{1,0:T(8,128)(2,1)S(1)}, bf16[256,384]{1,0:T(8,128)(2,1)S(1)}, u32[]{:S(2)}, u32[]{:S(2)}) collective-permute-start(bf16[256,384]{1,0:T(8,128)(2,1)S(1)} %gather.2), channel_id=1, source_target_pairs={{0,1},{1,0},{2,3},{3,2},{4,5},{5,4},{6,7},{7,6},{8,9},{9,8},{10,11... | collective-permute-start | bytes 589832 | tf_op jit(solution)/shard_map/ppermute | solution.py:370
  28.7 9.8 %collective-permute-start.4 = (bf16[128,384]{1,0:T(8,128)(2,1)S(1)}, bf16[128,384]{1,0:T(8,128)(2,1)S(1)}, u32[]{:S(2)}, u32[]{:S(2)}) collective-permute-start(bf16[128,384]{1,0:T(8,128)(2,1)S(1)} %get-tuple-element.58), channel_id=1, source_target_pairs={{0,6},{1,7},{2,4},{3,5},{4,2},{5,3},{6,0},{7,1},{8,14},{9,15},{10,... | collective-permute-start | bytes 294920 | tf_op jit(solution)/shard_map/ppermute | solution.py:370
  29.6 9.3 %collective-permute-start.5 = (bf16[128,384]{1,0:T(8,128)(2,1)S(1)}, bf16[128,384]{1,0:T(8,128)(2,1)S(1)}, u32[]{:S(2)}, u32[]{:S(2)}) collective-permute-start(bf16[128,384]{1,0:T(8,128)(2,1)S(1)} %get-tuple-element.59), channel_id=1, source_target_pairs={{0,4},{1,5},{2,6},{3,7},{4,0},{5,1},{6,2},{7,3},{8,12},{9,13},{10,... | collective-permute-start | bytes 294920 | tf_op jit(solution)/shard_map/ppermute | solution.py:370
  31.1 7.8 %collective-permute-start.6 = (bf16[128,384]{1,0:T(8,128)(2,1)S(1)}, bf16[128,384]{1,0:T(8,128)(2,1)S(1)}, u32[]{:S(2)}, u32[]{:S(2)}) collective-permute-start(bf16[128,384]{1,0:T(8,128)(2,1)S(1)} %get-tuple-element.60), channel_id=1, source_target_pairs={{0,2},{1,3},{2,0},{3,1},{4,6},{5,7},{6,4},{7,5},{8,10},{9,11},{10,... | collective-permute-start | bytes 294920 | tf_op jit(solution)/shard_map/ppermute | solution.py:370
  39.7 10.8 %collective-permute-start.7 = (bf16[128,384]{1,0:T(8,128)(2,1)S(1)}, bf16[128,384]{1,0:T(8,128)(2,1)S(1)}, u32[]{:S(2)}, u32[]{:S(2)}) collective-permute-start(bf16[128,384]{1,0:T(8,128)(2,1)S(1)} %get-tuple-element.64), channel_id=1, source_target_pairs={{0,16},{1,17},{2,18},{3,19},{4,20},{5,21},{6,22},{7,23},{8,24},{9,... | collective-permute-start | bytes 294920 | tf_op jit(solution)/shard_map/ppermute | solution.py:370
  41.8 8.7 %collective-permute-start.8 = (bf16[128,384]{1,0:T(8,128)(2,1)S(1)}, bf16[128,384]{1,0:T(8,128)(2,1)S(1)}, u32[]{:S(2)}, u32[]{:S(2)}) collective-permute-start(bf16[128,384]{1,0:T(8,128)(2,1)S(1)} %get-tuple-element.65), channel_id=1, source_target_pairs={{0,24},{1,25},{2,26},{3,27},{4,28},{5,29},{6,30},{7,31},{8,16},{9,... | collective-permute-start | bytes 294920 | tf_op jit(solution)/shard_map/ppermute | solution.py:370
  43.9 6.8 %collective-permute-start.9 = (bf16[128,384]{1,0:T(8,128)(2,1)S(1)}, bf16[128,384]{1,0:T(8,128)(2,1)S(1)}, u32[]{:S(2)}, u32[]{:S(2)}) collective-permute-start(bf16[128,384]{1,0:T(8,128)(2,1)S(1)} %get-tuple-element.66), channel_id=1, source_target_pairs={{0,8},{1,9},{2,10},{3,11},{4,12},{5,13},{6,14},{7,15},{8,0},{9,1},... | collective-permute-start | bytes 294920 | tf_op jit(solution)/shard_map/ppermute | solution.py:370
  45.2 21.4 %all-to-all-start.2 = ((bf16[32,16,640]{2,1,0:T(8,128)(2,1)}), bf16[32,16,640]{2,1,0:T(8,128)(2,1)S(1)}, u32[]{:S(2)}, u32[]{:S(2)}) async-start(bf16[32,16,640]{2,1,0:T(8,128)(2,1)} %bitcast.11), calls=%async_computation.2 | async-start | bytes 1310720 | tf_op jit(solution)/shard_map/all_to_all | solution.py:376
  50.8 1.5 %collective-permute-start.10 = (bf16[256,384]{1,0:T(8,128)(2,1)S(1)}, bf16[256,384]{1,0:T(8,128)(2,1)S(1)}, u32[]{:S(2)}, u32[]{:S(2)}) collective-permute-start(bf16[256,384]{1,0:T(8,128)(2,1)S(1)} %gather.3), channel_id=1, source_target_pairs={{0,1},{1,0},{2,3},{3,2},{4,5},{5,4},{6,7},{7,6},{8,9},{9,8},{10,11... | collective-permute-start | bytes 589832 | tf_op jit(solution)/shard_map/ppermute | solution.py:370
  52.3 9.8 %collective-permute-start.11 = (bf16[128,384]{1,0:T(8,128)(2,1)S(1)}, bf16[128,384]{1,0:T(8,128)(2,1)S(1)}, u32[]{:S(2)}, u32[]{:S(2)}) collective-permute-start(bf16[128,384]{1,0:T(8,128)(2,1)S(1)} %get-tuple-element.72), channel_id=1, source_target_pairs={{0,6},{1,7},{2,4},{3,5},{4,2},{5,3},{6,0},{7,1},{8,14},{9,15},{10,... | collective-permute-start | bytes 294920 | tf_op jit(solution)/shard_map/ppermute | solution.py:370
  53.7 9.4 %collective-permute-start.12 = (bf16[128,384]{1,0:T(8,128)(2,1)S(1)}, bf16[128,384]{1,0:T(8,128)(2,1)S(1)}, u32[]{:S(2)}, u32[]{:S(2)}) collective-permute-start(bf16[128,384]{1,0:T(8,128)(2,1)S(1)} %get-tuple-element.73), channel_id=1, source_target_pairs={{0,4},{1,5},{2,6},{3,7},{4,0},{5,1},{6,2},{7,3},{8,12},{9,13},{10,... | collective-permute-start | bytes 294920 | tf_op jit(solution)/shard_map/ppermute | solution.py:370
  54.7 8.4 %collective-permute-start.13 = (bf16[128,384]{1,0:T(8,128)(2,1)S(1)}, bf16[128,384]{1,0:T(8,128)(2,1)S(1)}, u32[]{:S(2)}, u32[]{:S(2)}) collective-permute-start(bf16[128,384]{1,0:T(8,128)(2,1)S(1)} %get-tuple-element.74), channel_id=1, source_target_pairs={{0,2},{1,3},{2,0},{3,1},{4,6},{5,7},{6,4},{7,5},{8,10},{9,11},{10,... | collective-permute-start | bytes 294920 | tf_op jit(solution)/shard_map/ppermute | solution.py:370

commit v12 on v11

--- a/solution.py
+++ b/solution.py
@@ -99,11 +99,16 @@
     return [0] + list(range(2, planes)) + [1]
 
 
+def plane_of(z, planes, device):
+    other = {1: 2, 2: 3, 3: 1}.get(z, z) if planes > 3 else z
+    return z + (device & 1) * (other - z)
+
+
 def to_planes(me, rows_ref, plane_refs, slots):
     for z, plane_ref in zip(plane_order(len(plane_refs)), plane_refs):
         for s in range(2):
             for q in range(GROUP // 2):
-                peer = me ^ (GROUP * z + 2 * q + s)
+                peer = me ^ (GROUP * plane_of(z, len(plane_refs), me) + 2 * q + s)
                 at = (s * (GROUP // 2) + q) * slots
                 plane_ref[at : at + slots, :] = rows_ref[block(peer, slots), :]
 
@@ -113,7 +118,8 @@
     for q, pair_ref in zip(pair_order(len(pair_refs)), pair_refs):
         for s in range(2):
             for i, z in enumerate(plane_order(planes)):
-                peer = me ^ (GROUP * z + 2 * q + s)
+                holder = me ^ (2 * q + s)
+                peer = holder ^ (GROUP * plane_of(z, planes, holder))
                 at = (s * planes + i) * slots
                 rows_ref[block(peer, slots), :] = pair_ref[at : at + slots, :]
 
@@ -182,7 +188,8 @@
         copy.wait()
 
 
-def pick_a_kernel(me_ref, asked_ref, seeds_ref, after_ref, pick_ref, a_ref, *plane_refs):
+def pick_a_kernel(me_ref, asked_ref, seeds_ref, after_ref, pick_ref, *refs):
+    *plane_refs, a_ref = refs
     del after_ref
     pick_ref[...] = picks(asked_ref[...], seeds_ref.shape[0])
     for cols in pieces_of(0, a_ref.shape[1]):
@@ -193,10 +200,8 @@
 def pick_b_kernel(
     pick_ref,
     seeds_ref,
-    a_ref,
     column_ref,
     share_ref,
-    out_a,
     out_b,
     early_ref,
     b_ref,
@@ -205,12 +210,12 @@
     *,
     neighbours,
 ):
-    rows = seeds_ref.shape[0]
-    wide = a_ref.shape[1]
-    copies = [push(a_ref, out_a, sems.at[0])]
+    rows, width = seeds_ref.shape
+    wide = width - b_ref.shape[1]
+    copies = []
     for i, rows_here in enumerate(strips_of(pick_ref.shape[0])):
         b_ref[rows_here, :] = dot(pick_ref[rows_here, :], seeds_ref[:, wide:]).astype(jnp.bfloat16)
-        copies.append(push(b_ref.at[rows_here], out_b.at[rows_here], sems.at[1 + i]))
+        copies.append(push(b_ref.at[rows_here], out_b.at[rows_here], sems.at[i]))
     chunks = (0, early_ref.shape[1] // BLK)
     fill_tiles(neighbours, column_ref, share_ref, early_ref, spot_ref, rows, chunks)
     for copy in copies:
@@ -224,8 +229,6 @@
     column_ref,
     share_ref,
     seeds_ref,
-    sent_a_ref,
-    sent_b_ref,
     after_ref,
     far_ref,
     picked_far_ref,
@@ -243,7 +246,6 @@
     whole_ref[:, :head] = own_ref[...]
     chunks = (head // BLK, rows // BLK)
     fill_tiles(neighbours, column_ref, share_ref, whole_ref, spot_ref, 0, chunks)
-    wide = sent_a_ref.shape[1]
     done = early_ref.shape[1]
     far_ref[:, :done] = early_ref[...]
     chunks = (done // BLK, far_ref.shape[1] // BLK)
@@ -253,10 +255,9 @@
         picked_far_ref[:, cols] = dot(pick_ref[...], far_ref[:, cols]).astype(jnp.bfloat16)
     for cols in pieces_of(0, rows):
         picked_ref[:, cols] = dot(pick_ref[...], whole_ref[:, cols]).astype(jnp.bfloat16)
-    for cols in pieces_of(0, wide) + pieces_of(wide, width):
-        sent = sent_a_ref[:, cols] if cols.stop <= wide else sent_b_ref[:, moved(cols, -wide)]
-        sent_base = KEEP * dot(picked_ref[...], seeds_ref[:, cols])
-        sent_base = sent_base + ANCHOR * sent.astype(jnp.float32)
+    for cols in pieces_of(0, width):
+        seeds = seeds_ref[:, cols]
+        sent_base = KEEP * dot(picked_ref[...], seeds) + ANCHOR * dot(pick_ref[...], seeds)
         sent_base_ref[:, cols] = sent_base.astype(jnp.bfloat16)
 
 
@@ -367,7 +368,7 @@
 
 
 def swap(x, peers, distance):
-    return lax.ppermute(x, "rows", [(i, i ^ distance) for i in range(peers)])
+    return lax.ppermute(x, "rows", [(i, i ^ distance(i)) for i in range(peers)])
 
 
 def exchange(rows_out, peers):
@@ -379,7 +380,8 @@
 
 def across(planes, peers):
     order = plane_order(len(planes))
-    return [swap(x, peers, GROUP * z) if z else x for z, x in zip(order, planes)]
+    far = lambda z: lambda i: GROUP * plane_of(z, len(planes), i)
+    return [swap(x, peers, far(z)) if z else x for z, x in zip(order, planes)]
 
 
 def within(planes, peers, slots):
@@ -393,7 +395,7 @@
         VMEM,
         flops=LONG,
     )(*planes)
-    other = swap(other, peers, 1)
+    other = swap(other, peers, lambda i: 1)
     pairs = call(
         functools.partial(pair_kernel, slots),
         "pair",
@@ -401,7 +403,7 @@
         [VMEM] * (n + 1),
         [VMEM] * (GROUP // 2),
     )(*planes, other)
-    return [swap(x, peers, 2 * q) if q else x for q, x in zip(pair_order(len(pairs)), pairs)]
+    return [swap(x, peers, lambda i, q=q: 2 * q) if q else x for q, x in zip(pair_order(len(pairs)), pairs)]
 
 
 def on_device(seeds, neighbor_pos, edge_weight, tile_blocks, wanted):
@@ -441,32 +443,32 @@
         ],
         flops=neighbours * rows * rows,
     )(far_in(tile_blocks), far_in(neighbor_pos.T), far_in(edge_weight.T), far_in(seeds))
-    pick, near_a, *sent_planes = call(
+    pick, *sent_planes = call(
         pick_a_kernel,
         "pick_a",
-        [near_out((count, rows)), near_out((count, wide))] + [plane_shape] * planes,
+        [near_out((count, rows))] + [plane_shape] * planes,
         [SMEM, VMEM, VMEM, HBM],
-        [VMEM] * (2 + planes),
+        [VMEM] * (1 + planes),
+        [pltpu.VMEM((count, wide), bf16)],
         flops=2 * count * rows * wide,
     )(me, asked, near_seeds, far_in(own))
     got_planes = across(sent_planes, peers)
-    sent_a, sent_b, early = call(
+    sent_b, early = call(
         functools.partial(pick_b_kernel, neighbours=neighbours),
         "pick_b",
         [
-            far_out((count, wide)),
             far_out((count, width - wide)),
             near_out((rows, count // BLK * EARLY // 8 * BLK)),
         ],
-        [VMEM] * 5,
-        [HBM, HBM, VMEM],
+        [VMEM] * 4,
+        [HBM, VMEM],
         [
             pltpu.VMEM((count, width - wide), bf16),
             pltpu.VMEM((depth, rows), jnp.float32),
-            sems((1 + n_sent,)),
+            sems((n_sent,)),
         ],
         flops=2 * count * rows * (width - wide),
-    )(pick, near_seeds, near_a, column, share)
+    )(pick, near_seeds, column, share)
     received_b = exchange(sent_b, peers)
     got_pairs = within(got_planes, peers, slots)
     far, picked_far, sent_base, own = call(
@@ -478,7 +480,7 @@
             near_out((count, width)),
             far_out((rows, rows)),
         ],
-        [VMEM] * 8 + [ANY],
+        [VMEM] * 6 + [ANY],
         [VMEM] * 4,
         [
             pltpu.VMEM((count, rows), bf16),
@@ -493,8 +495,6 @@
         column,
         share,
         far_in(seeds),
-        far_in(sent_a),
-        far_in(sent_b),
         got_pairs[0],
     )
     received_a, *sent_planes = call(

time: 68.3 us -> 68.2 us (level)
  transfers between devices with their start and end apart: 17 -> 17, of which waited for: 10 -> 8; matrix products, arithmetic and copies ran while one was open for 0% -> 0% of each run, Pallas kernels for 32% -> 32%
where the time goes in v12:
time: 68.2 us; the launch traced here: 67.8 us
  starting transfers between devices  28.8 us (42%)
  Pallas kernels  23.3 us (34%)
  waiting for transfers between devices  14.1 us (21%)
  local copies, waits for them, and re-layouts  1.38 us (2%)
    ppermute x14, starting transfers between devices, swap(): return lax.ppermute(x, 'rows', [(i, i ^ distance(i)) for i in range(peers)])  15.1 us
    ppermute x14, waiting for transfers between devices, swap(): return lax.ppermute(x, 'rows', [(i, i ^ distance(i)) for i in range(peers)])  8.81 us
    all_to_all x1, starting transfers between devices, on_device(): lax.all_to_all(wanted.reshape(peers, 1, slots), 'rows', split_axis=0, con...  7.3 us
    all_to_all x2, starting transfers between devices, exchange(): got = lax.all_to_all(sent, 'rows', split_axis=0, concat_axis=0, tiled=True)  6.4 us
    pallas_call x1, Pallas kernels, on_device(): call(functools.partial(far_kernel, neighbours=neighbours), 'far', [far_ou...  6.28 us
    pallas_call x1, Pallas kernels, on_device(): call(labels_kernel, 'labels', [near_out((rows, width)), near_out((rows, w...  6.21 us
    pallas_call x1, Pallas kernels, on_device(): call(own_tiles_kernel, 'own_tiles', [far_out((rows, head)), near_out((dep...  4.09 us
    all_to_all x1, waiting for transfers between devices, on_device(): lax.all_to_all(wanted.reshape(peers, 1, slots), 'rows', split_axis=0, con...  2.97 us
  transfers between devices with their start and end apart: 17, of which 8 were waited for; matrix products, arithmetic and copies ran while one was open for 0% of the time, Pallas kernels for 32%

profile of v12, /device:TPU:0, one launch (start us, length us, event | category | flops | bytes accessed | tf_op | source)
XLA Modules:
  0.0 67.8 jit_solution(16271211807633343756)
XLA Ops:
  0.0 1.4 %copy.7 = s32[1,32,16]{2,1,0:T(8,128)} copy(s32[1,32,16]{1,2,0:T(8,128)} %param.9) | data formatting | bytes 4096 | tf_op args[4]
  1.4 7.3 %all-to-all-start = ((s32[32,1,16]{2,1,0:T(1,128)}), s32[32,1,16]{2,1,0:T(1,128)S(1)}, u32[]{:S(2)}, u32[]{:S(2)}) async-start(s32[32,1,16]{2,1,0:T(1,128)} %bitcast), calls=%async_computation | async-start | bytes 32768 | tf_op jit(solution)/shard_map/all_to_all | solution.py:425
  8.7 4.1 %own_tiles.1 = (bf16[512,384]{1,0:T(8,128)(2,1)}, s32[64,512]{1,0:T(8,128)S(1)}, f32[64,512]{1,0:T(8,128)S(1)}, bf16[512,1024]{1,0:T(8,128)(2,1)S(1)}) custom-call(s32[4,8]{1,0:T(4,128)} %blocks_ref.1, s32[50,512]{1,0:T(8,128)} %bitcast.12, s32[50,512]{1,0:T(8,128)} %bitcast.13, bf16[512,1024]{1,0:T(8,128)(2,1)} %seeds_ref.3), custom_call_target="tpu_custom_call" | custom-call | flops 13107200 | tf_op jit(solution)/shard_map/own_tiles/pallas_call | solution.py:428
  12.8 3.0 %all-to-all-done.asked_ref = s32[32,1,16]{2,1,0:T(1,128)S(1)} async-done(((s32[32,1,16]{2,1,0:T(1,128)}), s32[32,1,16]{2,1,0:T(1,128)S(1)}, u32[]{:S(2)}, u32[]{:S(2)}) %all-to-all-start) | async-done | bytes 2080 | tf_op jit(solution)/shard_map/all_to_all | solution.py:425
  15.8 0.5 pick_a.1
  16.3 0.7 collective-permute-start
  17.0 2.3 %collective-permute-start.1 = (bf16[128,384]{1,0:T(8,128)(2,1)S(1)}, bf16[128,384]{1,0:T(8,128)(2,1)S(1)}, u32[]{:S(2)}, u32[]{:S(2)}) collective-permute-start(bf16[128,384]{1,0:T(8,128)(2,1)S(1)} %get-tuple-element.46), channel_id=1, source_target_pairs={{0,24},{1,9},{2,26},{3,11},{4,28},{5,13},{6,30},{7,15},{8,16},{9,1... | collective-permute-start | bytes 294920 | tf_op jit(solution)/shard_map/ppermute | solution.py:371
  19.3 0.6 collective-permute-start.2
  19.9 1.4 %pick_b.1 = (bf16[512,640]{1,0:T(8,128)(2,1)}, bf16[512,128]{1,0:T(8,128)(2,1)S(1)}) custom-call(bf16[512,512]{1,0:T(8,128)(2,1)S(1)} %get-tuple-element.40.pick_ref, bf16[512,1024]{1,0:T(8,128)(2,1)S(1)} %get-tuple-element.38.seeds_ref, s32[64,512]{1,0:T(8,128)S(1)} %get-tuple-element.41.column_ref, f32[64,512]{1,0:T(8,128)S(1)} %get-tuple-element.42.share_ref), custom_call_target="tpu_custom_call" | custom-call | flops 335544320 | tf_op jit(solution)/shard_map/pick_b/pallas_call | solution.py:456
  21.3 2.9 %all-to-all-start.1 = ((bf16[32,16,640]{2,1,0:T(8,128)(2,1)}), bf16[32,16,640]{2,1,0:T(8,128)(2,1)S(1)}, u32[]{:S(2)}, u32[]{:S(2)}) async-start(bf16[32,16,640]{2,1,0:T(8,128)(2,1)} %bitcast.10), calls=%async_computation.1 | async-start | bytes 1310720 | tf_op jit(solution)/shard_map/all_to_all | solution.py:377
  24.2 2.8 %collective-permute-done.refs_1_ = bf16[128,384]{1,0:T(8,128)(2,1)S(1)} collective-permute-done((bf16[128,384]{1,0:T(8,128)(2,1)S(1)}, bf16[128,384]{1,0:T(8,128)(2,1)S(1)}, u32[]{:S(2)}, u32[]{:S(2)}) %collective-permute-start) | collective-permute-done | bytes 98336 | tf_op jit(solution)/shard_map/ppermute | solution.py:371
  27.0 0.0 collective-permute-done.1.refs_2_
  27.0 0.0 collective-permute-done.2.refs_3_
  27.0 0.2 collective-permute-start.3
  27.2 1.3 %collective-permute-done.3.refs_4_ = bf16[256,384]{1,0:T(8,128)(2,1)S(1)} collective-permute-done((bf16[256,384]{1,0:T(8,128)(2,1)S(1)}, bf16[256,384]{1,0:T(8,128)(2,1)S(1)}, u32[]{:S(2)}, u32[]{:S(2)}) %collective-permute-start.3) | collective-permute-done | bytes 196640 | tf_op jit(solution)/shard_map/ppermute | solution.py:371
  28.6 0.7 %collective-permute-start.4 = (bf16[128,384]{1,0:T(8,128)(2,1)S(1)}, bf16[128,384]{1,0:T(8,128)(2,1)S(1)}, u32[]{:S(2)}, u32[]{:S(2)}) collective-permute-start(bf16[128,384]{1,0:T(8,128)(2,1)S(1)} %get-tuple-element.53), channel_id=1, source_target_pairs={{0,6},{1,7},{2,4},{3,5},{4,2},{5,3},{6,0},{7,1},{8,14},{9,15},{10,... | collective-permute-start | bytes 294920 | tf_op jit(solution)/shard_map/ppermute | solution.py:371
  29.3 1.2 %collective-permute-start.5 = (bf16[128,384]{1,0:T(8,128)(2,1)S(1)}, bf16[128,384]{1,0:T(8,128)(2,1)S(1)}, u32[]{:S(2)}, u32[]{:S(2)}) collective-permute-start(bf16[128,384]{1,0:T(8,128)(2,1)S(1)} %get-tuple-element.54), channel_id=1, source_target_pairs={{0,4},{1,5},{2,6},{3,7},{4,0},{5,1},{6,2},{7,3},{8,12},{9,13},{10,... | collective-permute-start | bytes 294920 | tf_op jit(solution)/shard_map/ppermute | solution.py:371
  30.6 1.6 %collective-permute-start.6 = (bf16[128,384]{1,0:T(8,128)(2,1)S(1)}, bf16[128,384]{1,0:T(8,128)(2,1)S(1)}, u32[]{:S(2)}, u32[]{:S(2)}) collective-permute-start(bf16[128,384]{1,0:T(8,128)(2,1)S(1)} %get-tuple-element.55), channel_id=1, source_target_pairs={{0,2},{1,3},{2,0},{3,1},{4,6},{5,7},{6,4},{7,5},{8,10},{9,11},{10,... | collective-permute-start | bytes 294920 | tf_op jit(solution)/shard_map/ppermute | solution.py:371
  32.1 6.3 %far.1 = (bf16[512,512]{1,0:T(8,128)(2,1)}, bf16[512,512]{1,0:T(8,128)(2,1)S(1)}, bf16[512,1024]{1,0:T(8,128)(2,1)S(1)}, bf16[512,512]{1,0:T(8,128)(2,1)}) custom-call(s32[32,1,16]{2,1,0:T(1,128)S(1)} %all-to-all-done.asked_ref, bf16[512,128]{1,0:T(8,128)(2,1)S(1)} %get-tuple-element.43.early_ref, bf16[512,384]{1,0:T(8,128)(2,1)} %get-tuple-element.39.after_ref.own_ref, ...), custom_call_target="tpu_custom_call" | custom-call | flops 1086849024 | tf_op jit(solution)/shard_map/far/pallas_call | solution.py:474
  38.4 0.0 collective-permute-done.4.refs_1_
  38.4 0.4 collective-permute-done.5.refs_2_
  38.8 0.0 collective-permute-done.6.refs_3_
  38.8 0.8 %send_a.1 = (bf16[512,384]{1,0:T(8,128)(2,1)}, bf16[128,384]{1,0:T(8,128)(2,1)S(1)}, bf16[128,384]{1,0:T(8,128)(2,1)S(1)}, bf16[128,384]{1,0:T(8,128)(2,1)S(1)}, bf16[128,384]{1,0:T(8,128)(2,1)S(1)}) custom-call(s32[1]{0:T(128)} %bitcast.1.me_ref, bf16[512,512]{1,0:T(8,128)(2,1)S(1)} %get-tuple-element.51.tiles_ref, ...), custom_call_target="tpu_custom_call" | custom-call | flops 201326592 | tf_op jit(solution)/shard_map/send_a/pallas_call | solution.py:500
  39.6 2.2 %collective-permute-start.7 = (bf16[128,384]{1,0:T(8,128)(2,1)S(1)}, bf16[128,384]{1,0:T(8,128)(2,1)S(1)}, u32[]{:S(2)}, u32[]{:S(2)}) collective-permute-start(bf16[128,384]{1,0:T(8,128)(2,1)S(1)} %get-tuple-element.60), channel_id=1, source_target_pairs={{0,16},{1,25},{2,18},{3,27},{4,20},{5,29},{6,22},{7,31},{8,24},{9,... | collective-permute-start | bytes 294920 | tf_op jit(solution)/shard_map/ppermute | solution.py:371
  41.8 1.9 %collective-permute-start.8 = (bf16[128,384]{1,0:T(8,128)(2,1)S(1)}, bf16[128,384]{1,0:T(8,128)(2,1)S(1)}, u32[]{:S(2)}, u32[]{:S(2)}) collective-permute-start(bf16[128,384]{1,0:T(8,128)(2,1)S(1)} %get-tuple-element.61), channel_id=1, source_target_pairs={{0,24},{1,9},{2,26},{3,11},{4,28},{5,13},{6,30},{7,15},{8,16},{9,1... | collective-permute-start | bytes 294920 | tf_op jit(solution)/shard_map/ppermute | solution.py:371
  43.7 0.0 collective-permute-start.9
  43.7 0.0 all-to-all-done.1
  43.7 1.3 %send_b.1 = (bf16[512,640]{1,0:T(8,128)(2,1)}, bf16[512,640]{1,0:T(8,128)(2,1)}) custom-call(bf16[512,512]{1,0:T(8,128)(2,1)S(1)} %get-tuple-element.51.tiles_ref, bf16[512,1024]{1,0:T(8,128)(2,1)S(1)} %get-tuple-element.52.base_ref, bf16[512,640]{1,0:T(8,128)(2,1)S(1)} %bitcast.9, bf16[128,384]{1,0:T(8,128)(2,1)S(1)} %get-tuple-element.58.after_ref.refs_0_), custom_call_target="tpu_custom_call" | custom-call | flops 335544320 | bytes 3538944 | tf_op jit(solution)/shard_map/send_b/pallas_call | solution.py:510
  45.0 3.5 %all-to-all-start.2 = ((bf16[32,16,640]{2,1,0:T(8,128)(2,1)}), bf16[32,16,640]{2,1,0:T(8,128)(2,1)S(1)}, u32[]{:S(2)}, u32[]{:S(2)}) async-start(bf16[32,16,640]{2,1,0:T(8,128)(2,1)} %bitcast.11), calls=%async_computation.2 | async-start | bytes 1310720 | tf_op jit(solution)/shard_map/all_to_all | solution.py:377
  48.5 1.7 %collective-permute-done.7.refs_1_ = bf16[128,384]{1,0:T(8,128)(2,1)S(1)} collective-permute-done((bf16[128,384]{1,0:T(8,128)(2,1)S(1)}, bf16[128,384]{1,0:T(8,128)(2,1)S(1)}, u32[]{:S(2)}, u32[]{:S(2)}) %collective-permute-start.7) | collective-permute-done | bytes 98336 | tf_op jit(solution)/shard_map/ppermute | solution.py:371
  50.2 0.0 collective-permute-done.8.refs_2_
  50.2 0.0 collective-permute-done.9.refs_3_
  50.2 0.2 collective-permute-start.10
  50.5 1.3 %collective-permute-done.10.refs_4_ = bf16[256,384]{1,0:T(8,128)(2,1)S(1)} collective-permute-done((bf16[256,384]{1,0:T(8,128)(2,1)S(1)}, bf16[256,384]{1,0:T(8,128)(2,1)S(1)}, u32[]{:S(2)}, u32[]{:S(2)}) %collective-permute-start.10) | collective-permute-done | bytes 196640 | tf_op jit(solution)/shard_map/ppermute | solution.py:371
  51.8 1.6 %collective-permute-start.11 = (bf16[128,384]{1,0:T(8,128)(2,1)S(1)}, bf16[128,384]{1,0:T(8,128)(2,1)S(1)}, u32[]{:S(2)}, u32[]{:S(2)}) collective-permute-start(bf16[128,384]{1,0:T(8,128)(2,1)S(1)} %get-tuple-element.68), channel_id=1, source_target_pairs={{0,6},{1,7},{2,4},{3,5},{4,2},{5,3},{6,0},{7,1},{8,14},{9,15},{10,... | collective-permute-start | bytes 294920 | tf_op jit(solution)/shard_map/ppermute | solution.py:371
  53.4 0.7 collective-permute-start.12
  54.0 1.3 %collective-permute-start.13 = (bf16[128,384]{1,0:T(8,128)(2,1)S(1)}, bf16[128,384]{1,0:T(8,128)(2,1)S(1)}, u32[]{:S(2)}, u32[]{:S(2)}) collective-permute-start(bf16[128,384]{1,0:T(8,128)(2,1)S(1)} %get-tuple-element.70), channel_id=1, source_target_pairs={{0,2},{1,3},{2,0},{3,1},{4,6},{5,7},{6,4},{7,5},{8,10},{9,11},{10,... | collective-permute-start | bytes 294920 | tf_op jit(solution)/shard_map/ppermute | solution.py:371
  55.3 6.2 %labels.1 = (bf16[512,1024]{1,0:T(8,128)(2,1)S(1)}, f8e4m3fn[512,1024]{1,0:T(32,128)(4,1)S(1)}, bf16[512,512]{1,0:T(8,128)(2,1)S(1)}) custom-call(bf16[512,512]{1,0:T(8,128)(2,1)} %get-tuple-element.49.own_ref, bf16[512,512]{1,0:T(8,128)(2,1)} %get-tuple-element.50.far_ref, bf16[512,1024]{1,0:T(8,128)(2,1)} %seeds_ref.3, ...), custom_call_target="tpu_custom_call" | custom-call | flops 1610612736 | tf_op jit(solution)/shard_map/labels/pallas_call | solution.py:522
  61.5 0.0 collective-permute-done.11.refs_1_
  61.6 1.3 %collective-permute-done.12.refs_2_ = bf16[128,384]{1,0:T(8,128)(2,1)S(1)} collective-permute-done((bf16[128,384]{1,0:T(8,128)(2,1)S(1)}, bf16[128,384]{1,0:T(8,128)(2,1)S(1)}, u32[]{:S(2)}, u32[]{:S(2)}) %collective-permute-start.12) | collective-permute-done | bytes 98336 | tf_op jit(solution)/shard_map/ppermute | solution.py:371
  62.9 0.0 collective-permute-done.13.refs_3_
  62.9 1.3 %last_a.1.same_ref = bf16[512,1024]{1,0:T(8,128)(2,1)} custom-call(s32[1]{0:T(128)} %bitcast.1.me_ref, bf16[512,512]{1,0:T(8,128)(2,1)S(1)} %get-tuple-element.64.tiles_ref, bf16[512,1024]{1,0:T(8,128)(2,1)S(1)} %get-tuple-element.65.base_ref, f8e4m3fn[512,1024]{1,0:T(32,128)(4,1)S(1)} %get-tuple-element.66.rest_ref, ...), custom_call_target="tpu_custom_call" | custom-call | flops 201326592 | tf_op jit(solution)/shard_map/last_a/pallas_call | solution.py:541
  64.1 2.3 %all-to-all-done.2 = bf16[32,16,640]{2,1,0:T(8,128)(2,1)S(1)} async-done(((bf16[32,16,640]{2,1,0:T(8,128)(2,1)}), bf16[32,16,640]{2,1,0:T(8,128)(2,1)S(1)}, u32[]{:S(2)}, u32[]{:S(2)}) %all-to-all-start.2) | async-done | bytes 655392 | tf_op jit(solution)/shard_map/all_to_all | solution.py:377
  66.4 1.3 %last_b.1 = bf16[512,1024]{1,0:T(8,128)(2,1)} custom-call(bf16[512,512]{1,0:T(8,128)(2,1)S(1)} %get-tuple-element.64.tiles_ref, bf16[512,1024]{1,0:T(8,128)(2,1)S(1)} %get-tuple-element.65.base_ref, f8e4m3fn[512,1024]{1,0:T(32,128)(4,1)S(1)} %get-tuple-element.66.rest_ref, bf16[512,640]{1,0:T(8,128)(2,1)S(1)} %bitcast.8, ...), custom_call_target="tpu_custom_call", output_to_operand_aliasing={{}: (4, {})} | custom-call | flops 335544320 | bytes 4194304 | tf_op jit(solution)/shard_map/last_b/pallas_call | solution.py:550
  (4 shorter events, 0.1 us)
Async XLA Ops:
  1.4 14.4 %all-to-all-start = ((s32[32,1,16]{2,1,0:T(1,128)}), s32[32,1,16]{2,1,0:T(1,128)S(1)}, u32[]{:S(2)}, u32[]{:S(2)}) async-start(s32[32,1,16]{2,1,0:T(1,128)} %bitcast), calls=%async_computation | async-start | bytes 32768 | tf_op jit(solution)/shard_map/all_to_all | solution.py:425
  16.3 10.7 %collective-permute-start = (bf16[128,384]{1,0:T(8,128)(2,1)S(1)}, bf16[128,384]{1,0:T(8,128)(2,1)S(1)}, u32[]{:S(2)}, u32[]{:S(2)}) collective-permute-start(bf16[128,384]{1,0:T(8,128)(2,1)S(1)} %get-tuple-element.45), channel_id=1, source_target_pairs={{0,16},{1,25},{2,18},{3,27},{4,20},{5,29},{6,22},{7,31},{8,24},{9,... | collective-permute-start | bytes 294920 | tf_op jit(solution)/shard_map/ppermute | solution.py:371
  17.0 10.0 %collective-permute-start.1 = (bf16[128,384]{1,0:T(8,128)(2,1)S(1)}, bf16[128,384]{1,0:T(8,128)(2,1)S(1)}, u32[]{:S(2)}, u32[]{:S(2)}) collective-permute-start(bf16[128,384]{1,0:T(8,128)(2,1)S(1)} %get-tuple-element.46), channel_id=1, source_target_pairs={{0,24},{1,9},{2,26},{3,11},{4,28},{5,13},{6,30},{7,15},{8,16},{9,1... | collective-permute-start | bytes 294920 | tf_op jit(solution)/shard_map/ppermute | solution.py:371
  19.3 7.7 %collective-permute-start.2 = (bf16[128,384]{1,0:T(8,128)(2,1)S(1)}, bf16[128,384]{1,0:T(8,128)(2,1)S(1)}, u32[]{:S(2)}, u32[]{:S(2)}) collective-permute-start(bf16[128,384]{1,0:T(8,128)(2,1)S(1)} %get-tuple-element.47), channel_id=1, source_target_pairs={{0,8},{1,17},{2,10},{3,19},{4,12},{5,21},{6,14},{7,23},{8,0},{9,25... | collective-permute-start | bytes 294920 | tf_op jit(solution)/shard_map/ppermute | solution.py:371
  21.3 22.4 %all-to-all-start.1 = ((bf16[32,16,640]{2,1,0:T(8,128)(2,1)}), bf16[32,16,640]{2,1,0:T(8,128)(2,1)S(1)}, u32[]{:S(2)}, u32[]{:S(2)}) async-start(bf16[32,16,640]{2,1,0:T(8,128)(2,1)} %bitcast.10), calls=%async_computation.1 | async-start | bytes 1310720 | tf_op jit(solution)/shard_map/all_to_all | solution.py:377
  27.0 1.5 %collective-permute-start.3 = (bf16[256,384]{1,0:T(8,128)(2,1)S(1)}, bf16[256,384]{1,0:T(8,128)(2,1)S(1)}, u32[]{:S(2)}, u32[]{:S(2)}) collective-permute-start(bf16[256,384]{1,0:T(8,128)(2,1)S(1)} %gather.2), channel_id=1, source_target_pairs={{0,1},{1,0},{2,3},{3,2},{4,5},{5,4},{6,7},{7,6},{8,9},{9,8},{10,11... | collective-permute-start | bytes 589832 | tf_op jit(solution)/shard_map/ppermute | solution.py:371
  28.6 9.8 %collective-permute-start.4 = (bf16[128,384]{1,0:T(8,128)(2,1)S(1)}, bf16[128,384]{1,0:T(8,128)(2,1)S(1)}, u32[]{:S(2)}, u32[]{:S(2)}) collective-permute-start(bf16[128,384]{1,0:T(8,128)(2,1)S(1)} %get-tuple-element.53), channel_id=1, source_target_pairs={{0,6},{1,7},{2,4},{3,5},{4,2},{5,3},{6,0},{7,1},{8,14},{9,15},{10,... | collective-permute-start | bytes 294920 | tf_op jit(solution)/shard_map/ppermute | solution.py:371
  29.3 9.5 %collective-permute-start.5 = (bf16[128,384]{1,0:T(8,128)(2,1)S(1)}, bf16[128,384]{1,0:T(8,128)(2,1)S(1)}, u32[]{:S(2)}, u32[]{:S(2)}) collective-permute-start(bf16[128,384]{1,0:T(8,128)(2,1)S(1)} %get-tuple-element.54), channel_id=1, source_target_pairs={{0,4},{1,5},{2,6},{3,7},{4,0},{5,1},{6,2},{7,3},{8,12},{9,13},{10,... | collective-permute-start | bytes 294920 | tf_op jit(solution)/shard_map/ppermute | solution.py:371
  30.6 8.2 %collective-permute-start.6 = (bf16[128,384]{1,0:T(8,128)(2,1)S(1)}, bf16[128,384]{1,0:T(8,128)(2,1)S(1)}, u32[]{:S(2)}, u32[]{:S(2)}) collective-permute-start(bf16[128,384]{1,0:T(8,128)(2,1)S(1)} %get-tuple-element.55), channel_id=1, source_target_pairs={{0,2},{1,3},{2,0},{3,1},{4,6},{5,7},{6,4},{7,5},{8,10},{9,11},{10,... | collective-permute-start | bytes 294920 | tf_op jit(solution)/shard_map/ppermute | solution.py:371
  39.6 10.6 %collective-permute-start.7 = (bf16[128,384]{1,0:T(8,128)(2,1)S(1)}, bf16[128,384]{1,0:T(8,128)(2,1)S(1)}, u32[]{:S(2)}, u32[]{:S(2)}) collective-permute-start(bf16[128,384]{1,0:T(8,128)(2,1)S(1)} %get-tuple-element.60), channel_id=1, source_target_pairs={{0,16},{1,25},{2,18},{3,27},{4,20},{5,29},{6,22},{7,31},{8,24},{9,... | collective-permute-start | bytes 294920 | tf_op jit(solution)/shard_map/ppermute | solution.py:371
  41.8 8.4 %collective-permute-start.8 = (bf16[128,384]{1,0:T(8,128)(2,1)S(1)}, bf16[128,384]{1,0:T(8,128)(2,1)S(1)}, u32[]{:S(2)}, u32[]{:S(2)}) collective-permute-start(bf16[128,384]{1,0:T(8,128)(2,1)S(1)} %get-tuple-element.61), channel_id=1, source_target_pairs={{0,24},{1,9},{2,26},{3,11},{4,28},{5,13},{6,30},{7,15},{8,16},{9,1... | collective-permute-start | bytes 294920 | tf_op jit(solution)/shard_map/ppermute | solution.py:371
  43.7 6.5 %collective-permute-start.9 = (bf16[128,384]{1,0:T(8,128)(2,1)S(1)}, bf16[128,384]{1,0:T(8,128)(2,1)S(1)}, u32[]{:S(2)}, u32[]{:S(2)}) collective-permute-start(bf16[128,384]{1,0:T(8,128)(2,1)S(1)} %get-tuple-element.62), channel_id=1, source_target_pairs={{0,8},{1,17},{2,10},{3,19},{4,12},{5,21},{6,14},{7,23},{8,0},{9,25... | collective-permute-start | bytes 294920 | tf_op jit(solution)/shard_map/ppermute | solution.py:371
  45.0 21.4 %all-to-all-start.2 = ((bf16[32,16,640]{2,1,0:T(8,128)(2,1)}), bf16[32,16,640]{2,1,0:T(8,128)(2,1)S(1)}, u32[]{:S(2)}, u32[]{:S(2)}) async-start(bf16[32,16,640]{2,1,0:T(8,128)(2,1)} %bitcast.11), calls=%async_computation.2 | async-start | bytes 1310720 | tf_op jit(solution)/shard_map/all_to_all | solution.py:377
  50.2 1.5 %collective-permute-start.10 = (bf16[256,384]{1,0:T(8,128)(2,1)S(1)}, bf16[256,384]{1,0:T(8,128)(2,1)S(1)}, u32[]{:S(2)}, u32[]{:S(2)}) collective-permute-start(bf16[256,384]{1,0:T(8,128)(2,1)S(1)} %gather.3), channel_id=1, source_target_pairs={{0,1},{1,0},{2,3},{3,2},{4,5},{5,4},{6,7},{7,6},{8,9},{9,8},{10,11... | collective-permute-start | bytes 589832 | tf_op jit(solution)/shard_map/ppermute | solution.py:371
  51.8 9.8 %collective-permute-start.11 = (bf16[128,384]{1,0:T(8,128)(2,1)S(1)}, bf16[128,384]{1,0:T(8,128)(2,1)S(1)}, u32[]{:S(2)}, u32[]{:S(2)}) collective-permute-start(bf16[128,384]{1,0:T(8,128)(2,1)S(1)} %get-tuple-element.68), channel_id=1, source_target_pairs={{0,6},{1,7},{2,4},{3,5},{4,2},{5,3},{6,0},{7,1},{8,14},{9,15},{10,... | collective-permute-start | bytes 294920 | tf_op jit(solution)/shard_map/ppermute | solution.py:371
  53.4 9.5 %collective-permute-start.12 = (bf16[128,384]{1,0:T(8,128)(2,1)S(1)}, bf16[128,384]{1,0:T(8,128)(2,1)S(1)}, u32[]{:S(2)}, u32[]{:S(2)}) collective-permute-start(bf16[128,384]{1,0:T(8,128)(2,1)S(1)} %get-tuple-element.69), channel_id=1, source_target_pairs={{0,4},{1,5},{2,6},{3,7},{4,0},{5,1},{6,2},{7,3},{8,12},{9,13},{10,... | collective-permute-start | bytes 294920 | tf_op jit(solution)/shard_map/ppermute | solution.py:371
  54.0 8.8 %collective-permute-start.13 = (bf16[128,384]{1,0:T(8,128)(2,1)S(1)}, bf16[128,384]{1,0:T(8,128)(2,1)S(1)}, u32[]{:S(2)}, u32[]{:S(2)}) collective-permute-start(bf16[128,384]{1,0:T(8,128)(2,1)S(1)} %get-tuple-element.70), channel_id=1, source_target_pairs={{0,2},{1,3},{2,0},{3,1},{4,6},{5,7},{6,4},{7,5},{8,10},{9,11},{10,... | collective-permute-start | bytes 294920 | tf_op jit(solution)/shard_map/ppermute | solution.py:371

commit v13 on v12

--- a/solution.py
+++ b/solution.py
@@ -99,6 +99,11 @@
     return [0] + list(range(2, planes)) + [1]
 
 
+def pair_of(q, device):
+    other = {3: 2, 2: 1, 1: 3}.get(q, q)
+    return q + (device & 1) * (other - q)
+
+
 def plane_of(z, planes, device):
     other = {1: 2, 2: 3, 3: 1}.get(z, z) if planes > 3 else z
     return z + (device & 1) * (other - z)
@@ -118,7 +123,7 @@
     for q, pair_ref in zip(pair_order(len(pair_refs)), pair_refs):
         for s in range(2):
             for i, z in enumerate(plane_order(planes)):
-                holder = me ^ (2 * q + s)
+                holder = me ^ (2 * pair_of(q, me) + s)
                 peer = holder ^ (GROUP * plane_of(z, planes, holder))
                 at = (s * planes + i) * slots
                 rows_ref[block(peer, slots), :] = pair_ref[at : at + slots, :]
@@ -268,17 +273,17 @@
         out_ref[z * half : (z + 1) * half, :] = plane_ref[half:, :]
 
 
-def pair_kernel(slots, *refs):
+def pair_kernel(slots, me_ref, *refs):
     count = GROUP // 2
     *plane_refs, other_ref = refs[:-count]
     planes = len(plane_refs)
     for q, out_ref in zip(pair_order(count), refs[-count:]):
+        q = pair_of(q, me_ref[0])
         for z, plane_ref in enumerate(plane_refs):
             here = slice(z * slots, (z + 1) * slots)
             there = slice((planes + z) * slots, (planes + z + 1) * slots)
-            other = (z * count + q) * slots
-            out_ref[here, :] = plane_ref[q * slots : (q + 1) * slots, :]
-            out_ref[there, :] = other_ref[other : other + slots, :]
+            out_ref[here, :] = plane_ref[block(q, slots), :]
+            out_ref[there, :] = other_ref[block(z * count + q, slots), :]
 
 
 def send_a_kernel(me_ref, tiles_ref, base_ref, *refs, slots):
@@ -384,7 +389,7 @@
     return [swap(x, peers, far(z)) if z else x for z, x in zip(order, planes)]
 
 
-def within(planes, peers, slots):
+def within(me, planes, peers, slots):
     depth, wide = planes[0].shape
     n = len(planes)
     other = call(
@@ -400,10 +405,11 @@
         functools.partial(pair_kernel, slots),
         "pair",
         [jax.ShapeDtypeStruct((2 * n * slots, wide), jnp.bfloat16)] * (GROUP // 2),
-        [VMEM] * (n + 1),
+        [SMEM] + [VMEM] * (n + 1),
         [VMEM] * (GROUP // 2),
-    )(*planes, other)
-    return [swap(x, peers, lambda i, q=q: 2 * q) if q else x for q, x in zip(pair_order(len(pairs)), pairs)]
+    )(me, *planes, other)
+    even = lambda q: lambda i: 2 * pair_of(q, i)
+    return [swap(x, peers, even(q)) if q else x for q, x in zip(pair_order(len(pairs)), pairs)]
 
 
 def on_device(seeds, neighbor_pos, edge_weight, tile_blocks, wanted):
@@ -470,7 +476,7 @@
         flops=2 * count * rows * (width - wide),
     )(pick, near_seeds, column, share)
     received_b = exchange(sent_b, peers)
-    got_pairs = within(got_planes, peers, slots)
+    got_pairs = within(me, got_planes, peers, slots)
     far, picked_far, sent_base, own = call(
         functools.partial(far_kernel, neighbours=neighbours),
         "far",
@@ -518,7 +524,7 @@
         nbytes=2 * count * (3 * (width - wide) + count + width),
     )(picked_far, sent_base, received_b, sent_planes[0])
     last_b = exchange(sent_b, peers)
-    got_pairs = within(got_planes, peers, slots)
+    got_pairs = within(me, got_planes, peers, slots)
     next_base, rest, near_far = call(
         labels_kernel,
         "labels",

time: 68.2 us -> 68 us (level)
  waiting for transfers between devices: 14.1 us -> 12.4 us
  starting transfers between devices: 28.8 us -> 30.3 us
    ppermute x14, waiting for transfers between devices: 8.81 us -> 7.31 us  [swap(): return lax.ppermute(x, 'rows', [(i, i ^ distance(i)) for i in range(peers)])]
    ppermute x14, starting transfers between devices: 15.1 us -> 16.6 us  [swap(): return lax.ppermute(x, 'rows', [(i, i ^ distance(i)) for i in range(peers)])]
  transfers between devices with their start and end apart: 17 -> 17, of which waited for: 8 -> 7; matrix products, arithmetic and copies ran while one was open for 0% -> 0% of each run, Pallas kernels for 32% -> 32%
where the time goes in v13:
time: 68 us; the launch traced here: 67.6 us
  starting transfers between devices  30.3 us (45%)
  Pallas kernels  23.3 us (34%)
  waiting for transfers between devices  12.4 us (18%)
  local copies, waits for them, and re-layouts  1.38 us (2%)
    ppermute x14, starting transfers between devices, swap(): return lax.ppermute(x, 'rows', [(i, i ^ distance(i)) for i in range(peers)])  16.6 us
    ppermute x14, waiting for transfers between devices, swap(): return lax.ppermute(x, 'rows', [(i, i ^ distance(i)) for i in range(peers)])  7.31 us
    all_to_all x1, starting transfers between devices, on_device(): lax.all_to_all(wanted.reshape(peers, 1, slots), 'rows', split_axis=0, con...  7.3 us
    all_to_all x2, starting transfers between devices, exchange(): got = lax.all_to_all(sent, 'rows', split_axis=0, concat_axis=0, tiled=True)  6.47 us
    pallas_call x1, Pallas kernels, on_device(): call(functools.partial(far_kernel, neighbours=neighbours), 'far', [far_ou...  6.28 us
    pallas_call x1, Pallas kernels, on_device(): call(labels_kernel, 'labels', [near_out((rows, width)), near_out((rows, w...  6.21 us
    pallas_call x1, Pallas kernels, on_device(): call(own_tiles_kernel, 'own_tiles', [far_out((rows, head)), near_out((dep...  4.09 us
    all_to_all x1, waiting for transfers between devices, on_device(): lax.all_to_all(wanted.reshape(peers, 1, slots), 'rows', split_axis=0, con...  2.97 us
  transfers between devices with their start and end apart: 17, of which 7 were waited for; matrix products, arithmetic and copies ran while one was open for 0% of the time, Pallas kernels for 32%

profile of v13, /device:TPU:0, one launch (start us, length us, event | category | flops | bytes accessed | tf_op | source)
XLA Modules:
  0.0 67.6 jit_solution(4531306448054692850)
XLA Ops:
  0.0 1.4 %copy.7 = s32[1,32,16]{2,1,0:T(8,128)} copy(s32[1,32,16]{1,2,0:T(8,128)} %param.9) | data formatting | bytes 4096 | tf_op args[4]
  1.4 7.3 %all-to-all-start = ((s32[32,1,16]{2,1,0:T(1,128)}), s32[32,1,16]{2,1,0:T(1,128)S(1)}, u32[]{:S(2)}, u32[]{:S(2)}) async-start(s32[32,1,16]{2,1,0:T(1,128)} %bitcast), calls=%async_computation | async-start | bytes 32768 | tf_op jit(solution)/shard_map/all_to_all | solution.py:431
  8.7 4.1 %own_tiles.1 = (bf16[512,384]{1,0:T(8,128)(2,1)}, s32[64,512]{1,0:T(8,128)S(1)}, f32[64,512]{1,0:T(8,128)S(1)}, bf16[512,1024]{1,0:T(8,128)(2,1)S(1)}) custom-call(s32[4,8]{1,0:T(4,128)} %blocks_ref.1, s32[50,512]{1,0:T(8,128)} %bitcast.12, s32[50,512]{1,0:T(8,128)} %bitcast.13, bf16[512,1024]{1,0:T(8,128)(2,1)} %seeds_ref.3), custom_call_target="tpu_custom_call" | custom-call | flops 13107200 | tf_op jit(solution)/shard_map/own_tiles/pallas_call | solution.py:434
  12.8 3.0 %all-to-all-done.asked_ref = s32[32,1,16]{2,1,0:T(1,128)S(1)} async-done(((s32[32,1,16]{2,1,0:T(1,128)}), s32[32,1,16]{2,1,0:T(1,128)S(1)}, u32[]{:S(2)}, u32[]{:S(2)}) %all-to-all-start) | async-done | bytes 2080 | tf_op jit(solution)/shard_map/all_to_all | solution.py:431
  15.8 0.5 pick_a.1
  16.3 0.7 collective-permute-start
  17.0 2.3 %collective-permute-start.1 = (bf16[128,384]{1,0:T(8,128)(2,1)S(1)}, bf16[128,384]{1,0:T(8,128)(2,1)S(1)}, u32[]{:S(2)}, u32[]{:S(2)}) collective-permute-start(bf16[128,384]{1,0:T(8,128)(2,1)S(1)} %get-tuple-element.46), channel_id=1, source_target_pairs={{0,24},{1,9},{2,26},{3,11},{4,28},{5,13},{6,30},{7,15},{8,16},{9,1... | collective-permute-start | bytes 294920 | tf_op jit(solution)/shard_map/ppermute | solution.py:376
  19.3 0.6 collective-permute-start.2
  19.9 1.4 %pick_b.1 = (bf16[512,640]{1,0:T(8,128)(2,1)}, bf16[512,128]{1,0:T(8,128)(2,1)S(1)}) custom-call(bf16[512,512]{1,0:T(8,128)(2,1)S(1)} %get-tuple-element.40.pick_ref, bf16[512,1024]{1,0:T(8,128)(2,1)S(1)} %get-tuple-element.38.seeds_ref, s32[64,512]{1,0:T(8,128)S(1)} %get-tuple-element.41.column_ref, f32[64,512]{1,0:T(8,128)S(1)} %get-tuple-element.42.share_ref), custom_call_target="tpu_custom_call" | custom-call | flops 335544320 | tf_op jit(solution)/shard_map/pick_b/pallas_call | solution.py:462
  21.3 2.9 %all-to-all-start.1 = ((bf16[32,16,640]{2,1,0:T(8,128)(2,1)}), bf16[32,16,640]{2,1,0:T(8,128)(2,1)S(1)}, u32[]{:S(2)}, u32[]{:S(2)}) async-start(bf16[32,16,640]{2,1,0:T(8,128)(2,1)} %bitcast.10), calls=%async_computation.1 | async-start | bytes 1310720 | tf_op jit(solution)/shard_map/all_to_all | solution.py:382
  24.2 2.8 %collective-permute-done.refs_1_ = bf16[128,384]{1,0:T(8,128)(2,1)S(1)} collective-permute-done((bf16[128,384]{1,0:T(8,128)(2,1)S(1)}, bf16[128,384]{1,0:T(8,128)(2,1)S(1)}, u32[]{:S(2)}, u32[]{:S(2)}) %collective-permute-start) | collective-permute-done | bytes 98336 | tf_op jit(solution)/shard_map/ppermute | solution.py:376
  27.0 0.0 collective-permute-done.1.refs_2_
  27.0 0.0 collective-permute-done.2.refs_3_
  27.0 0.2 collective-permute-start.3
  27.2 1.3 %collective-permute-done.3.refs_4_ = bf16[256,384]{1,0:T(8,128)(2,1)S(1)} collective-permute-done((bf16[256,384]{1,0:T(8,128)(2,1)S(1)}, bf16[256,384]{1,0:T(8,128)(2,1)S(1)}, u32[]{:S(2)}, u32[]{:S(2)}) %collective-permute-start.3) | collective-permute-done | bytes 196640 | tf_op jit(solution)/shard_map/ppermute | solution.py:376
  28.6 0.7 %collective-permute-start.4 = (bf16[128,384]{1,0:T(8,128)(2,1)S(1)}, bf16[128,384]{1,0:T(8,128)(2,1)S(1)}, u32[]{:S(2)}, u32[]{:S(2)}) collective-permute-start(bf16[128,384]{1,0:T(8,128)(2,1)S(1)} %get-tuple-element.53), channel_id=1, source_target_pairs={{0,6},{1,5},{2,4},{3,7},{4,2},{5,1},{6,0},{7,3},{8,14},{9,13},{10,... | collective-permute-start | bytes 294920 | tf_op jit(solution)/shard_map/ppermute | solution.py:376
  29.3 1.2 %collective-permute-start.5 = (bf16[128,384]{1,0:T(8,128)(2,1)S(1)}, bf16[128,384]{1,0:T(8,128)(2,1)S(1)}, u32[]{:S(2)}, u32[]{:S(2)}) collective-permute-start(bf16[128,384]{1,0:T(8,128)(2,1)S(1)} %get-tuple-element.54), channel_id=1, source_target_pairs={{0,4},{1,3},{2,6},{3,1},{4,0},{5,7},{6,2},{7,5},{8,12},{9,11},{10,... | collective-permute-start | bytes 294920 | tf_op jit(solution)/shard_map/ppermute | solution.py:376
  30.6 1.6 %collective-permute-start.6 = (bf16[128,384]{1,0:T(8,128)(2,1)S(1)}, bf16[128,384]{1,0:T(8,128)(2,1)S(1)}, u32[]{:S(2)}, u32[]{:S(2)}) collective-permute-start(bf16[128,384]{1,0:T(8,128)(2,1)S(1)} %get-tuple-element.55), channel_id=1, source_target_pairs={{0,2},{1,7},{2,0},{3,5},{4,6},{5,3},{6,4},{7,1},{8,10},{9,15},{10,... | collective-permute-start | bytes 294920 | tf_op jit(solution)/shard_map/ppermute | solution.py:376
  32.1 6.3 %far.1 = (bf16[512,512]{1,0:T(8,128)(2,1)}, bf16[512,512]{1,0:T(8,128)(2,1)S(1)}, bf16[512,1024]{1,0:T(8,128)(2,1)S(1)}, bf16[512,512]{1,0:T(8,128)(2,1)}) custom-call(s32[32,1,16]{2,1,0:T(1,128)S(1)} %all-to-all-done.asked_ref, bf16[512,128]{1,0:T(8,128)(2,1)S(1)} %get-tuple-element.43.early_ref, bf16[512,384]{1,0:T(8,128)(2,1)} %get-tuple-element.39.after_ref.own_ref, ...), custom_call_target="tpu_custom_call" | custom-call | flops 1086849024 | tf_op jit(solution)/shard_map/far/pallas_call | solution.py:480
  38.4 0.0 collective-permute-done.4.refs_1_
  38.4 0.0 collective-permute-done.5.refs_2_
  38.4 0.0 collective-permute-done.6.refs_3_
  38.5 0.8 %send_a.1 = (bf16[512,384]{1,0:T(8,128)(2,1)}, bf16[128,384]{1,0:T(8,128)(2,1)S(1)}, bf16[128,384]{1,0:T(8,128)(2,1)S(1)}, bf16[128,384]{1,0:T(8,128)(2,1)S(1)}, bf16[128,384]{1,0:T(8,128)(2,1)S(1)}) custom-call(s32[1]{0:T(128)} %bitcast.1.me_ref, bf16[512,512]{1,0:T(8,128)(2,1)S(1)} %get-tuple-element.51.tiles_ref, ...), custom_call_target="tpu_custom_call" | custom-call | flops 201326592 | tf_op jit(solution)/shard_map/send_a/pallas_call | solution.py:506
  39.3 2.1 %collective-permute-start.7 = (bf16[128,384]{1,0:T(8,128)(2,1)S(1)}, bf16[128,384]{1,0:T(8,128)(2,1)S(1)}, u32[]{:S(2)}, u32[]{:S(2)}) collective-permute-start(bf16[128,384]{1,0:T(8,128)(2,1)S(1)} %get-tuple-element.60), channel_id=1, source_target_pairs={{0,16},{1,25},{2,18},{3,27},{4,20},{5,29},{6,22},{7,31},{8,24},{9,... | collective-permute-start | bytes 294920 | tf_op jit(solution)/shard_map/ppermute | solution.py:376
  41.4 2.0 %collective-permute-start.8 = (bf16[128,384]{1,0:T(8,128)(2,1)S(1)}, bf16[128,384]{1,0:T(8,128)(2,1)S(1)}, u32[]{:S(2)}, u32[]{:S(2)}) collective-permute-start(bf16[128,384]{1,0:T(8,128)(2,1)S(1)} %get-tuple-element.61), channel_id=1, source_target_pairs={{0,24},{1,9},{2,26},{3,11},{4,28},{5,13},{6,30},{7,15},{8,16},{9,1... | collective-permute-start | bytes 294920 | tf_op jit(solution)/shard_map/ppermute | solution.py:376
  43.4 0.0 collective-permute-start.9
  43.4 0.0 all-to-all-done.1
  43.4 1.3 %send_b.1 = (bf16[512,640]{1,0:T(8,128)(2,1)}, bf16[512,640]{1,0:T(8,128)(2,1)}) custom-call(bf16[512,512]{1,0:T(8,128)(2,1)S(1)} %get-tuple-element.51.tiles_ref, bf16[512,1024]{1,0:T(8,128)(2,1)S(1)} %get-tuple-element.52.base_ref, bf16[512,640]{1,0:T(8,128)(2,1)S(1)} %bitcast.9, bf16[128,384]{1,0:T(8,128)(2,1)S(1)} %get-tuple-element.58.after_ref.refs_0_), custom_call_target="tpu_custom_call" | custom-call | flops 335544320 | bytes 3538944 | tf_op jit(solution)/shard_map/send_b/pallas_call | solution.py:516
  44.7 3.6 %all-to-all-start.2 = ((bf16[32,16,640]{2,1,0:T(8,128)(2,1)}), bf16[32,16,640]{2,1,0:T(8,128)(2,1)S(1)}, u32[]{:S(2)}, u32[]{:S(2)}) async-start(bf16[32,16,640]{2,1,0:T(8,128)(2,1)} %bitcast.11), calls=%async_computation.2 | async-start | bytes 1310720 | tf_op jit(solution)/shard_map/all_to_all | solution.py:382
  48.3 1.8 %collective-permute-done.7.refs_1_ = bf16[128,384]{1,0:T(8,128)(2,1)S(1)} collective-permute-done((bf16[128,384]{1,0:T(8,128)(2,1)S(1)}, bf16[128,384]{1,0:T(8,128)(2,1)S(1)}, u32[]{:S(2)}, u32[]{:S(2)}) %collective-permute-start.7) | collective-permute-done | bytes 98336 | tf_op jit(solution)/shard_map/ppermute | solution.py:376
  50.1 0.0 collective-permute-done.8.refs_2_
  50.1 0.0 collective-permute-done.9.refs_3_
  50.1 1.6 %collective-permute-start.10 = (bf16[256,384]{1,0:T(8,128)(2,1)S(1)}, bf16[256,384]{1,0:T(8,128)(2,1)S(1)}, u32[]{:S(2)}, u32[]{:S(2)}) collective-permute-start(bf16[256,384]{1,0:T(8,128)(2,1)S(1)} %gather.3), channel_id=1, source_target_pairs={{0,1},{1,0},{2,3},{3,2},{4,5},{5,4},{6,7},{7,6},{8,9},{9,8},{10,11... | collective-permute-start | bytes 589832 | tf_op jit(solution)/shard_map/ppermute | solution.py:376
  51.7 1.1 %collective-permute-done.10.refs_4_ = bf16[256,384]{1,0:T(8,128)(2,1)S(1)} collective-permute-done((bf16[256,384]{1,0:T(8,128)(2,1)S(1)}, bf16[256,384]{1,0:T(8,128)(2,1)S(1)}, u32[]{:S(2)}, u32[]{:S(2)}) %collective-permute-start.10) | collective-permute-done | bytes 196640 | tf_op jit(solution)/shard_map/ppermute | solution.py:376
  52.8 0.8 %collective-permute-start.11 = (bf16[128,384]{1,0:T(8,128)(2,1)S(1)}, bf16[128,384]{1,0:T(8,128)(2,1)S(1)}, u32[]{:S(2)}, u32[]{:S(2)}) collective-permute-start(bf16[128,384]{1,0:T(8,128)(2,1)S(1)} %get-tuple-element.68), channel_id=1, source_target_pairs={{0,6},{1,5},{2,4},{3,7},{4,2},{5,1},{6,0},{7,3},{8,14},{9,13},{10,... | collective-permute-start | bytes 294920 | tf_op jit(solution)/shard_map/ppermute | solution.py:376
  53.6 1.3 %collective-permute-start.12 = (bf16[128,384]{1,0:T(8,128)(2,1)S(1)}, bf16[128,384]{1,0:T(8,128)(2,1)S(1)}, u32[]{:S(2)}, u32[]{:S(2)}) collective-permute-start(bf16[128,384]{1,0:T(8,128)(2,1)S(1)} %get-tuple-element.69), channel_id=1, source_target_pairs={{0,4},{1,3},{2,6},{3,1},{4,0},{5,7},{6,2},{7,5},{8,12},{9,11},{10,... | collective-permute-start | bytes 294920 | tf_op jit(solution)/shard_map/ppermute | solution.py:376
  54.9 1.5 %collective-permute-start.13 = (bf16[128,384]{1,0:T(8,128)(2,1)S(1)}, bf16[128,384]{1,0:T(8,128)(2,1)S(1)}, u32[]{:S(2)}, u32[]{:S(2)}) collective-permute-start(bf16[128,384]{1,0:T(8,128)(2,1)S(1)} %get-tuple-element.70), channel_id=1, source_target_pairs={{0,2},{1,7},{2,0},{3,5},{4,6},{5,3},{6,4},{7,1},{8,10},{9,15},{10,... | collective-permute-start | bytes 294920 | tf_op jit(solution)/shard_map/ppermute | solution.py:376
  56.4 6.2 %labels.1 = (bf16[512,1024]{1,0:T(8,128)(2,1)S(1)}, f8e4m3fn[512,1024]{1,0:T(32,128)(4,1)S(1)}, bf16[512,512]{1,0:T(8,128)(2,1)S(1)}) custom-call(bf16[512,512]{1,0:T(8,128)(2,1)} %get-tuple-element.49.own_ref, bf16[512,512]{1,0:T(8,128)(2,1)} %get-tuple-element.50.far_ref, bf16[512,1024]{1,0:T(8,128)(2,1)} %seeds_ref.3, ...), custom_call_target="tpu_custom_call" | custom-call | flops 1610612736 | tf_op jit(solution)/shard_map/labels/pallas_call | solution.py:528
  62.6 0.0 collective-permute-done.11.refs_1_
  62.6 0.3 collective-permute-done.12.refs_2_
  62.9 0.0 collective-permute-done.13.refs_3_
  62.9 1.3 %last_a.1.same_ref = bf16[512,1024]{1,0:T(8,128)(2,1)} custom-call(s32[1]{0:T(128)} %bitcast.1.me_ref, bf16[512,512]{1,0:T(8,128)(2,1)S(1)} %get-tuple-element.64.tiles_ref, bf16[512,1024]{1,0:T(8,128)(2,1)S(1)} %get-tuple-element.65.base_ref, f8e4m3fn[512,1024]{1,0:T(32,128)(4,1)S(1)} %get-tuple-element.66.rest_ref, ...), custom_call_target="tpu_custom_call" | custom-call | flops 201326592 | tf_op jit(solution)/shard_map/last_a/pallas_call | solution.py:547
  64.2 2.1 %all-to-all-done.2 = bf16[32,16,640]{2,1,0:T(8,128)(2,1)S(1)} async-done(((bf16[32,16,640]{2,1,0:T(8,128)(2,1)}), bf16[32,16,640]{2,1,0:T(8,128)(2,1)S(1)}, u32[]{:S(2)}, u32[]{:S(2)}) %all-to-all-start.2) | async-done | bytes 655392 | tf_op jit(solution)/shard_map/all_to_all | solution.py:382
  66.2 1.3 %last_b.1 = bf16[512,1024]{1,0:T(8,128)(2,1)} custom-call(bf16[512,512]{1,0:T(8,128)(2,1)S(1)} %get-tuple-element.64.tiles_ref, bf16[512,1024]{1,0:T(8,128)(2,1)S(1)} %get-tuple-element.65.base_ref, f8e4m3fn[512,1024]{1,0:T(32,128)(4,1)S(1)} %get-tuple-element.66.rest_ref, bf16[512,640]{1,0:T(8,128)(2,1)S(1)} %bitcast.8, ...), custom_call_target="tpu_custom_call", output_to_operand_aliasing={{}: (4, {})} | custom-call | flops 335544320 | bytes 4194304 | tf_op jit(solution)/shard_map/last_b/pallas_call | solution.py:556
  (4 shorter events, 0.1 us)
Async XLA Ops:
  1.4 14.4 %all-to-all-start = ((s32[32,1,16]{2,1,0:T(1,128)}), s32[32,1,16]{2,1,0:T(1,128)S(1)}, u32[]{:S(2)}, u32[]{:S(2)}) async-start(s32[32,1,16]{2,1,0:T(1,128)} %bitcast), calls=%async_computation | async-start | bytes 32768 | tf_op jit(solution)/shard_map/all_to_all | solution.py:431
  16.3 10.7 %collective-permute-start = (bf16[128,384]{1,0:T(8,128)(2,1)S(1)}, bf16[128,384]{1,0:T(8,128)(2,1)S(1)}, u32[]{:S(2)}, u32[]{:S(2)}) collective-permute-start(bf16[128,384]{1,0:T(8,128)(2,1)S(1)} %get-tuple-element.45), channel_id=1, source_target_pairs={{0,16},{1,25},{2,18},{3,27},{4,20},{5,29},{6,22},{7,31},{8,24},{9,... | collective-permute-start | bytes 294920 | tf_op jit(solution)/shard_map/ppermute | solution.py:376
  17.0 10.0 %collective-permute-start.1 = (bf16[128,384]{1,0:T(8,128)(2,1)S(1)}, bf16[128,384]{1,0:T(8,128)(2,1)S(1)}, u32[]{:S(2)}, u32[]{:S(2)}) collective-permute-start(bf16[128,384]{1,0:T(8,128)(2,1)S(1)} %get-tuple-element.46), channel_id=1, source_target_pairs={{0,24},{1,9},{2,26},{3,11},{4,28},{5,13},{6,30},{7,15},{8,16},{9,1... | collective-permute-start | bytes 294920 | tf_op jit(solution)/shard_map/ppermute | solution.py:376
  19.3 7.7 %collective-permute-start.2 = (bf16[128,384]{1,0:T(8,128)(2,1)S(1)}, bf16[128,384]{1,0:T(8,128)(2,1)S(1)}, u32[]{:S(2)}, u32[]{:S(2)}) collective-permute-start(bf16[128,384]{1,0:T(8,128)(2,1)S(1)} %get-tuple-element.47), channel_id=1, source_target_pairs={{0,8},{1,17},{2,10},{3,19},{4,12},{5,21},{6,14},{7,23},{8,0},{9,25... | collective-permute-start | bytes 294920 | tf_op jit(solution)/shard_map/ppermute | solution.py:376
  21.3 22.1 %all-to-all-start.1 = ((bf16[32,16,640]{2,1,0:T(8,128)(2,1)}), bf16[32,16,640]{2,1,0:T(8,128)(2,1)S(1)}, u32[]{:S(2)}, u32[]{:S(2)}) async-start(bf16[32,16,640]{2,1,0:T(8,128)(2,1)} %bitcast.10), calls=%async_computation.1 | async-start | bytes 1310720 | tf_op jit(solution)/shard_map/all_to_all | solution.py:382
  27.0 1.5 %collective-permute-start.3 = (bf16[256,384]{1,0:T(8,128)(2,1)S(1)}, bf16[256,384]{1,0:T(8,128)(2,1)S(1)}, u32[]{:S(2)}, u32[]{:S(2)}) collective-permute-start(bf16[256,384]{1,0:T(8,128)(2,1)S(1)} %gather.2), channel_id=1, source_target_pairs={{0,1},{1,0},{2,3},{3,2},{4,5},{5,4},{6,7},{7,6},{8,9},{9,8},{10,11... | collective-permute-start | bytes 589832 | tf_op jit(solution)/shard_map/ppermute | solution.py:376
  28.6 9.8 %collective-permute-start.4 = (bf16[128,384]{1,0:T(8,128)(2,1)S(1)}, bf16[128,384]{1,0:T(8,128)(2,1)S(1)}, u32[]{:S(2)}, u32[]{:S(2)}) collective-permute-start(bf16[128,384]{1,0:T(8,128)(2,1)S(1)} %get-tuple-element.53), channel_id=1, source_target_pairs={{0,6},{1,5},{2,4},{3,7},{4,2},{5,1},{6,0},{7,3},{8,14},{9,13},{10,... | collective-permute-start | bytes 294920 | tf_op jit(solution)/shard_map/ppermute | solution.py:376
  29.3 9.1 %collective-permute-start.5 = (bf16[128,384]{1,0:T(8,128)(2,1)S(1)}, bf16[128,384]{1,0:T(8,128)(2,1)S(1)}, u32[]{:S(2)}, u32[]{:S(2)}) collective-permute-start(bf16[128,384]{1,0:T(8,128)(2,1)S(1)} %get-tuple-element.54), channel_id=1, source_target_pairs={{0,4},{1,3},{2,6},{3,1},{4,0},{5,7},{6,2},{7,5},{8,12},{9,11},{10,... | collective-permute-start | bytes 294920 | tf_op jit(solution)/shard_map/ppermute | solution.py:376
  30.6 7.9 %collective-permute-start.6 = (bf16[128,384]{1,0:T(8,128)(2,1)S(1)}, bf16[128,384]{1,0:T(8,128)(2,1)S(1)}, u32[]{:S(2)}, u32[]{:S(2)}) collective-permute-start(bf16[128,384]{1,0:T(8,128)(2,1)S(1)} %get-tuple-element.55), channel_id=1, source_target_pairs={{0,2},{1,7},{2,0},{3,5},{4,6},{5,3},{6,4},{7,1},{8,10},{9,15},{10,... | collective-permute-start | bytes 294920 | tf_op jit(solution)/shard_map/ppermute | solution.py:376
  39.3 10.8 %collective-permute-start.7 = (bf16[128,384]{1,0:T(8,128)(2,1)S(1)}, bf16[128,384]{1,0:T(8,128)(2,1)S(1)}, u32[]{:S(2)}, u32[]{:S(2)}) collective-permute-start(bf16[128,384]{1,0:T(8,128)(2,1)S(1)} %get-tuple-element.60), channel_id=1, source_target_pairs={{0,16},{1,25},{2,18},{3,27},{4,20},{5,29},{6,22},{7,31},{8,24},{9,... | collective-permute-start | bytes 294920 | tf_op jit(solution)/shard_map/ppermute | solution.py:376
  41.4 8.7 %collective-permute-start.8 = (bf16[128,384]{1,0:T(8,128)(2,1)S(1)}, bf16[128,384]{1,0:T(8,128)(2,1)S(1)}, u32[]{:S(2)}, u32[]{:S(2)}) collective-permute-start(bf16[128,384]{1,0:T(8,128)(2,1)S(1)} %get-tuple-element.61), channel_id=1, source_target_pairs={{0,24},{1,9},{2,26},{3,11},{4,28},{5,13},{6,30},{7,15},{8,16},{9,1... | collective-permute-start | bytes 294920 | tf_op jit(solution)/shard_map/ppermute | solution.py:376
  43.4 6.7 %collective-permute-start.9 = (bf16[128,384]{1,0:T(8,128)(2,1)S(1)}, bf16[128,384]{1,0:T(8,128)(2,1)S(1)}, u32[]{:S(2)}, u32[]{:S(2)}) collective-permute-start(bf16[128,384]{1,0:T(8,128)(2,1)S(1)} %get-tuple-element.62), channel_id=1, source_target_pairs={{0,8},{1,17},{2,10},{3,19},{4,12},{5,21},{6,14},{7,23},{8,0},{9,25... | collective-permute-start | bytes 294920 | tf_op jit(solution)/shard_map/ppermute | solution.py:376
  44.7 21.5 %all-to-all-start.2 = ((bf16[32,16,640]{2,1,0:T(8,128)(2,1)}), bf16[32,16,640]{2,1,0:T(8,128)(2,1)S(1)}, u32[]{:S(2)}, u32[]{:S(2)}) async-start(bf16[32,16,640]{2,1,0:T(8,128)(2,1)} %bitcast.11), calls=%async_computation.2 | async-start | bytes 1310720 | tf_op jit(solution)/shard_map/all_to_all | solution.py:382
  50.1 2.7 %collective-permute-start.10 = (bf16[256,384]{1,0:T(8,128)(2,1)S(1)}, bf16[256,384]{1,0:T(8,128)(2,1)S(1)}, u32[]{:S(2)}, u32[]{:S(2)}) collective-permute-start(bf16[256,384]{1,0:T(8,128)(2,1)S(1)} %gather.3), channel_id=1, source_target_pairs={{0,1},{1,0},{2,3},{3,2},{4,5},{5,4},{6,7},{7,6},{8,9},{9,8},{10,11... | collective-permute-start | bytes 589832 | tf_op jit(solution)/shard_map/ppermute | solution.py:376
  52.8 9.8 %collective-permute-start.11 = (bf16[128,384]{1,0:T(8,128)(2,1)S(1)}, bf16[128,384]{1,0:T(8,128)(2,1)S(1)}, u32[]{:S(2)}, u32[]{:S(2)}) collective-permute-start(bf16[128,384]{1,0:T(8,128)(2,1)S(1)} %get-tuple-element.68), channel_id=1, source_target_pairs={{0,6},{1,5},{2,4},{3,7},{4,2},{5,1},{6,0},{7,3},{8,14},{9,13},{10,... | collective-permute-start | bytes 294920 | tf_op jit(solution)/shard_map/ppermute | solution.py:376
  53.6 9.2 %collective-permute-start.12 = (bf16[128,384]{1,0:T(8,128)(2,1)S(1)}, bf16[128,384]{1,0:T(8,128)(2,1)S(1)}, u32[]{:S(2)}, u32[]{:S(2)}) collective-permute-start(bf16[128,384]{1,0:T(8,128)(2,1)S(1)} %get-tuple-element.69), channel_id=1, source_target_pairs={{0,4},{1,3},{2,6},{3,1},{4,0},{5,7},{6,2},{7,5},{8,12},{9,11},{10,... | collective-permute-start | bytes 294920 | tf_op jit(solution)/shard_map/ppermute | solution.py:376
  54.9 7.9 %collective-permute-start.13 = (bf16[128,384]{1,0:T(8,128)(2,1)S(1)}, bf16[128,384]{1,0:T(8,128)(2,1)S(1)}, u32[]{:S(2)}, u32[]{:S(2)}) collective-permute-start(bf16[128,384]{1,0:T(8,128)(2,1)S(1)} %get-tuple-element.70), channel_id=1, source_target_pairs={{0,2},{1,7},{2,0},{3,5},{4,6},{5,3},{6,4},{7,1},{8,10},{9,15},{10,... | collective-permute-start | bytes 294920 | tf_op jit(solution)/shard_map/ppermute | solution.py:376

commit v14 on v13

--- a/solution.py
+++ b/solution.py
@@ -105,7 +105,7 @@
 
 
 def plane_of(z, planes, device):
-    other = {1: 2, 2: 3, 3: 1}.get(z, z) if planes > 3 else z
+    other = {2: 3, 3: 2}.get(z, z) if planes > 3 else z
     return z + (device & 1) * (other - z)
 
 

time: 68 us -> 67.8 us (level)
  starting transfers between devices: 30.3 us -> 29.4 us
  waiting for transfers between devices: 12.4 us -> 13.1 us
    ppermute x14, starting transfers between devices: 16.6 us -> 15.8 us  [swap(): return lax.ppermute(x, 'rows', [(i, i ^ distance(i)) for i in range(peers)])]
  transfers between devices with their start and end apart: 17 -> 17, of which waited for: 7 -> 9; matrix products, arithmetic and copies ran while one was open for 0% -> 0% of each run, Pallas kernels for 32% -> 32%
where the time goes in v14:
time: 67.8 us; the launch traced here: 67.4 us
  starting transfers between devices  29.4 us (43%)
  Pallas kernels  23.3 us (34%)
  waiting for transfers between devices  13.1 us (19%)
  local copies, waits for them, and re-layouts  1.38 us (2%)
    ppermute x14, starting transfers between devices, swap(): return lax.ppermute(x, 'rows', [(i, i ^ distance(i)) for i in range(peers)])  15.8 us
    ppermute x14, waiting for transfers between devices, swap(): return lax.ppermute(x, 'rows', [(i, i ^ distance(i)) for i in range(peers)])  7.92 us
    all_to_all x1, starting transfers between devices, on_device(): lax.all_to_all(wanted.reshape(peers, 1, slots), 'rows', split_axis=0, con...  7.3 us
    all_to_all x2, starting transfers between devices, exchange(): got = lax.all_to_all(sent, 'rows', split_axis=0, concat_axis=0, tiled=True)  6.31 us
    pallas_call x1, Pallas kernels, on_device(): call(functools.partial(far_kernel, neighbours=neighbours), 'far', [far_ou...  6.28 us
    pallas_call x1, Pallas kernels, on_device(): call(labels_kernel, 'labels', [near_out((rows, width)), near_out((rows, w...  6.21 us
    pallas_call x1, Pallas kernels, on_device(): call(own_tiles_kernel, 'own_tiles', [far_out((rows, head)), near_out((dep...  4.09 us
    all_to_all x1, waiting for transfers between devices, on_device(): lax.all_to_all(wanted.reshape(peers, 1, slots), 'rows', split_axis=0, con...  2.97 us
  transfers between devices with their start and end apart: 17, of which 9 were waited for; matrix products, arithmetic and copies ran while one was open for 0% of the time, Pallas kernels for 32%

profile of v14, /device:TPU:0, one launch (start us, length us, event | category | flops | bytes accessed | tf_op | source)
XLA Modules:
  0.0 67.4 jit_solution(18356282738275124385)
XLA Ops:
  0.0 1.4 %copy.7 = s32[1,32,16]{2,1,0:T(8,128)} copy(s32[1,32,16]{1,2,0:T(8,128)} %param.9) | data formatting | bytes 4096 | tf_op args[4]
  1.4 7.3 %all-to-all-start = ((s32[32,1,16]{2,1,0:T(1,128)}), s32[32,1,16]{2,1,0:T(1,128)S(1)}, u32[]{:S(2)}, u32[]{:S(2)}) async-start(s32[32,1,16]{2,1,0:T(1,128)} %bitcast), calls=%async_computation | async-start | bytes 32768 | tf_op jit(solution)/shard_map/all_to_all | solution.py:431
  8.7 4.1 %own_tiles.1 = (bf16[512,384]{1,0:T(8,128)(2,1)}, s32[64,512]{1,0:T(8,128)S(1)}, f32[64,512]{1,0:T(8,128)S(1)}, bf16[512,1024]{1,0:T(8,128)(2,1)S(1)}) custom-call(s32[4,8]{1,0:T(4,128)} %blocks_ref.1, s32[50,512]{1,0:T(8,128)} %bitcast.12, s32[50,512]{1,0:T(8,128)} %bitcast.13, bf16[512,1024]{1,0:T(8,128)(2,1)} %seeds_ref.3), custom_call_target="tpu_custom_call" | custom-call | flops 13107200 | tf_op jit(solution)/shard_map/own_tiles/pallas_call | solution.py:434
  12.8 3.0 %all-to-all-done.asked_ref = s32[32,1,16]{2,1,0:T(1,128)S(1)} async-done(((s32[32,1,16]{2,1,0:T(1,128)}), s32[32,1,16]{2,1,0:T(1,128)S(1)}, u32[]{:S(2)}, u32[]{:S(2)}) %all-to-all-start) | async-done | bytes 2080 | tf_op jit(solution)/shard_map/all_to_all | solution.py:431
  15.8 0.6 pick_a.1
  16.3 0.7 collective-permute-start
  17.0 2.3 %collective-permute-start.1 = (bf16[128,384]{1,0:T(8,128)(2,1)S(1)}, bf16[128,384]{1,0:T(8,128)(2,1)S(1)}, u32[]{:S(2)}, u32[]{:S(2)}) collective-permute-start(bf16[128,384]{1,0:T(8,128)(2,1)S(1)} %get-tuple-element.46), channel_id=1, source_target_pairs={{0,24},{1,17},{2,26},{3,19},{4,28},{5,21},{6,30},{7,23},{8,16},{9,... | collective-permute-start | bytes 294920 | tf_op jit(solution)/shard_map/ppermute | solution.py:376
  19.3 0.6 collective-permute-start.2
  19.9 1.4 %pick_b.1 = (bf16[512,640]{1,0:T(8,128)(2,1)}, bf16[512,128]{1,0:T(8,128)(2,1)S(1)}) custom-call(bf16[512,512]{1,0:T(8,128)(2,1)S(1)} %get-tuple-element.40.pick_ref, bf16[512,1024]{1,0:T(8,128)(2,1)S(1)} %get-tuple-element.38.seeds_ref, s32[64,512]{1,0:T(8,128)S(1)} %get-tuple-element.41.column_ref, f32[64,512]{1,0:T(8,128)S(1)} %get-tuple-element.42.share_ref), custom_call_target="tpu_custom_call" | custom-call | flops 335544320 | tf_op jit(solution)/shard_map/pick_b/pallas_call | solution.py:462
  21.3 2.9 %all-to-all-start.1 = ((bf16[32,16,640]{2,1,0:T(8,128)(2,1)}), bf16[32,16,640]{2,1,0:T(8,128)(2,1)S(1)}, u32[]{:S(2)}, u32[]{:S(2)}) async-start(bf16[32,16,640]{2,1,0:T(8,128)(2,1)} %bitcast.10), calls=%async_computation.1 | async-start | bytes 1310720 | tf_op jit(solution)/shard_map/all_to_all | solution.py:382
  24.2 2.6 %collective-permute-done.refs_1_ = bf16[128,384]{1,0:T(8,128)(2,1)S(1)} collective-permute-done((bf16[128,384]{1,0:T(8,128)(2,1)S(1)}, bf16[128,384]{1,0:T(8,128)(2,1)S(1)}, u32[]{:S(2)}, u32[]{:S(2)}) %collective-permute-start) | collective-permute-done | bytes 98336 | tf_op jit(solution)/shard_map/ppermute | solution.py:376
  26.8 0.0 collective-permute-done.1.refs_2_
  26.8 0.0 collective-permute-done.2.refs_3_
  26.8 0.1 collective-permute-start.3
  26.9 1.4 %collective-permute-done.3.refs_4_ = bf16[256,384]{1,0:T(8,128)(2,1)S(1)} collective-permute-done((bf16[256,384]{1,0:T(8,128)(2,1)S(1)}, bf16[256,384]{1,0:T(8,128)(2,1)S(1)}, u32[]{:S(2)}, u32[]{:S(2)}) %collective-permute-start.3) | collective-permute-done | bytes 196640 | tf_op jit(solution)/shard_map/ppermute | solution.py:376
  28.3 1.0 %collective-permute-start.4 = (bf16[128,384]{1,0:T(8,128)(2,1)S(1)}, bf16[128,384]{1,0:T(8,128)(2,1)S(1)}, u32[]{:S(2)}, u32[]{:S(2)}) collective-permute-start(bf16[128,384]{1,0:T(8,128)(2,1)S(1)} %get-tuple-element.53), channel_id=1, source_target_pairs={{0,6},{1,5},{2,4},{3,7},{4,2},{5,1},{6,0},{7,3},{8,14},{9,13},{10,... | collective-permute-start | bytes 294920 | tf_op jit(solution)/shard_map/ppermute | solution.py:376
  29.3 1.3 %collective-permute-start.5 = (bf16[128,384]{1,0:T(8,128)(2,1)S(1)}, bf16[128,384]{1,0:T(8,128)(2,1)S(1)}, u32[]{:S(2)}, u32[]{:S(2)}) collective-permute-start(bf16[128,384]{1,0:T(8,128)(2,1)S(1)} %get-tuple-element.54), channel_id=1, source_target_pairs={{0,4},{1,3},{2,6},{3,1},{4,0},{5,7},{6,2},{7,5},{8,12},{9,11},{10,... | collective-permute-start | bytes 294920 | tf_op jit(solution)/shard_map/ppermute | solution.py:376
  30.6 1.3 %collective-permute-start.6 = (bf16[128,384]{1,0:T(8,128)(2,1)S(1)}, bf16[128,384]{1,0:T(8,128)(2,1)S(1)}, u32[]{:S(2)}, u32[]{:S(2)}) collective-permute-start(bf16[128,384]{1,0:T(8,128)(2,1)S(1)} %get-tuple-element.55), channel_id=1, source_target_pairs={{0,2},{1,7},{2,0},{3,5},{4,6},{5,3},{6,4},{7,1},{8,10},{9,15},{10,... | collective-permute-start | bytes 294920 | tf_op jit(solution)/shard_map/ppermute | solution.py:376
  31.9 6.3 %far.1 = (bf16[512,512]{1,0:T(8,128)(2,1)}, bf16[512,512]{1,0:T(8,128)(2,1)S(1)}, bf16[512,1024]{1,0:T(8,128)(2,1)S(1)}, bf16[512,512]{1,0:T(8,128)(2,1)}) custom-call(s32[32,1,16]{2,1,0:T(1,128)S(1)} %all-to-all-done.asked_ref, bf16[512,128]{1,0:T(8,128)(2,1)S(1)} %get-tuple-element.43.early_ref, bf16[512,384]{1,0:T(8,128)(2,1)} %get-tuple-element.39.after_ref.own_ref, ...), custom_call_target="tpu_custom_call" | custom-call | flops 1086849024 | tf_op jit(solution)/shard_map/far/pallas_call | solution.py:480
  38.2 0.0 collective-permute-done.4.refs_1_
  38.2 0.0 collective-permute-done.5.refs_2_
  38.2 0.2 collective-permute-done.6.refs_3_
  38.4 0.8 %send_a.1 = (bf16[512,384]{1,0:T(8,128)(2,1)}, bf16[128,384]{1,0:T(8,128)(2,1)S(1)}, bf16[128,384]{1,0:T(8,128)(2,1)S(1)}, bf16[128,384]{1,0:T(8,128)(2,1)S(1)}, bf16[128,384]{1,0:T(8,128)(2,1)S(1)}) custom-call(s32[1]{0:T(128)} %bitcast.1.me_ref, bf16[512,512]{1,0:T(8,128)(2,1)S(1)} %get-tuple-element.51.tiles_ref, ...), custom_call_target="tpu_custom_call" | custom-call | flops 201326592 | tf_op jit(solution)/shard_map/send_a/pallas_call | solution.py:506
  39.2 2.2 %collective-permute-start.7 = (bf16[128,384]{1,0:T(8,128)(2,1)S(1)}, bf16[128,384]{1,0:T(8,128)(2,1)S(1)}, u32[]{:S(2)}, u32[]{:S(2)}) collective-permute-start(bf16[128,384]{1,0:T(8,128)(2,1)S(1)} %get-tuple-element.60), channel_id=1, source_target_pairs={{0,16},{1,25},{2,18},{3,27},{4,20},{5,29},{6,22},{7,31},{8,24},{9,... | collective-permute-start | bytes 294920 | tf_op jit(solution)/shard_map/ppermute | solution.py:376
  41.4 2.0 %collective-permute-start.8 = (bf16[128,384]{1,0:T(8,128)(2,1)S(1)}, bf16[128,384]{1,0:T(8,128)(2,1)S(1)}, u32[]{:S(2)}, u32[]{:S(2)}) collective-permute-start(bf16[128,384]{1,0:T(8,128)(2,1)S(1)} %get-tuple-element.61), channel_id=1, source_target_pairs={{0,24},{1,17},{2,26},{3,19},{4,28},{5,21},{6,30},{7,23},{8,16},{9,... | collective-permute-start | bytes 294920 | tf_op jit(solution)/shard_map/ppermute | solution.py:376
  43.4 0.0 collective-permute-start.9
  43.4 0.0 all-to-all-done.1
  43.4 1.3 %send_b.1 = (bf16[512,640]{1,0:T(8,128)(2,1)}, bf16[512,640]{1,0:T(8,128)(2,1)}) custom-call(bf16[512,512]{1,0:T(8,128)(2,1)S(1)} %get-tuple-element.51.tiles_ref, bf16[512,1024]{1,0:T(8,128)(2,1)S(1)} %get-tuple-element.52.base_ref, bf16[512,640]{1,0:T(8,128)(2,1)S(1)} %bitcast.9, bf16[128,384]{1,0:T(8,128)(2,1)S(1)} %get-tuple-element.58.after_ref.refs_0_), custom_call_target="tpu_custom_call" | custom-call | flops 335544320 | bytes 3538944 | tf_op jit(solution)/shard_map/send_b/pallas_call | solution.py:516
  44.7 3.4 %all-to-all-start.2 = ((bf16[32,16,640]{2,1,0:T(8,128)(2,1)}), bf16[32,16,640]{2,1,0:T(8,128)(2,1)S(1)}, u32[]{:S(2)}, u32[]{:S(2)}) async-start(bf16[32,16,640]{2,1,0:T(8,128)(2,1)} %bitcast.11), calls=%async_computation.2 | async-start | bytes 1310720 | tf_op jit(solution)/shard_map/all_to_all | solution.py:382
  48.2 1.9 %collective-permute-done.7.refs_1_ = bf16[128,384]{1,0:T(8,128)(2,1)S(1)} collective-permute-done((bf16[128,384]{1,0:T(8,128)(2,1)S(1)}, bf16[128,384]{1,0:T(8,128)(2,1)S(1)}, u32[]{:S(2)}, u32[]{:S(2)}) %collective-permute-start.7) | collective-permute-done | bytes 98336 | tf_op jit(solution)/shard_map/ppermute | solution.py:376
  50.1 0.0 collective-permute-done.8.refs_2_
  50.1 0.5 collective-permute-done.9.refs_3_
  50.6 0.9 %collective-permute-start.10 = (bf16[256,384]{1,0:T(8,128)(2,1)S(1)}, bf16[256,384]{1,0:T(8,128)(2,1)S(1)}, u32[]{:S(2)}, u32[]{:S(2)}) collective-permute-start(bf16[256,384]{1,0:T(8,128)(2,1)S(1)} %gather.3), channel_id=1, source_target_pairs={{0,1},{1,0},{2,3},{3,2},{4,5},{5,4},{6,7},{7,6},{8,9},{9,8},{10,11... | collective-permute-start | bytes 589832 | tf_op jit(solution)/shard_map/ppermute | solution.py:376
  51.4 1.1 %collective-permute-done.10.refs_4_ = bf16[256,384]{1,0:T(8,128)(2,1)S(1)} collective-permute-done((bf16[256,384]{1,0:T(8,128)(2,1)S(1)}, bf16[256,384]{1,0:T(8,128)(2,1)S(1)}, u32[]{:S(2)}, u32[]{:S(2)}) %collective-permute-start.10) | collective-permute-done | bytes 196640 | tf_op jit(solution)/shard_map/ppermute | solution.py:376
  52.5 1.1 %collective-permute-start.11 = (bf16[128,384]{1,0:T(8,128)(2,1)S(1)}, bf16[128,384]{1,0:T(8,128)(2,1)S(1)}, u32[]{:S(2)}, u32[]{:S(2)}) collective-permute-start(bf16[128,384]{1,0:T(8,128)(2,1)S(1)} %get-tuple-element.68), channel_id=1, source_target_pairs={{0,6},{1,5},{2,4},{3,7},{4,2},{5,1},{6,0},{7,3},{8,14},{9,13},{10,... | collective-permute-start | bytes 294920 | tf_op jit(solution)/shard_map/ppermute | solution.py:376
  53.6 1.4 %collective-permute-start.12 = (bf16[128,384]{1,0:T(8,128)(2,1)S(1)}, bf16[128,384]{1,0:T(8,128)(2,1)S(1)}, u32[]{:S(2)}, u32[]{:S(2)}) collective-permute-start(bf16[128,384]{1,0:T(8,128)(2,1)S(1)} %get-tuple-element.69), channel_id=1, source_target_pairs={{0,4},{1,3},{2,6},{3,1},{4,0},{5,7},{6,2},{7,5},{8,12},{9,11},{10,... | collective-permute-start | bytes 294920 | tf_op jit(solution)/shard_map/ppermute | solution.py:376
  55.0 1.1 %collective-permute-start.13 = (bf16[128,384]{1,0:T(8,128)(2,1)S(1)}, bf16[128,384]{1,0:T(8,128)(2,1)S(1)}, u32[]{:S(2)}, u32[]{:S(2)}) collective-permute-start(bf16[128,384]{1,0:T(8,128)(2,1)S(1)} %get-tuple-element.70), channel_id=1, source_target_pairs={{0,2},{1,7},{2,0},{3,5},{4,6},{5,3},{6,4},{7,1},{8,10},{9,15},{10,... | collective-permute-start | bytes 294920 | tf_op jit(solution)/shard_map/ppermute | solution.py:376
  56.1 6.2 %labels.1 = (bf16[512,1024]{1,0:T(8,128)(2,1)S(1)}, f8e4m3fn[512,1024]{1,0:T(32,128)(4,1)S(1)}, bf16[512,512]{1,0:T(8,128)(2,1)S(1)}) custom-call(bf16[512,512]{1,0:T(8,128)(2,1)} %get-tuple-element.49.own_ref, bf16[512,512]{1,0:T(8,128)(2,1)} %get-tuple-element.50.far_ref, bf16[512,1024]{1,0:T(8,128)(2,1)} %seeds_ref.3, ...), custom_call_target="tpu_custom_call" | custom-call | flops 1610612736 | tf_op jit(solution)/shard_map/labels/pallas_call | solution.py:528
  62.3 0.0 collective-permute-done.11.refs_1_
  62.3 0.3 collective-permute-done.12.refs_2_
  62.6 0.0 collective-permute-done.13.refs_3_
  62.6 1.3 %last_a.1.same_ref = bf16[512,1024]{1,0:T(8,128)(2,1)} custom-call(s32[1]{0:T(128)} %bitcast.1.me_ref, bf16[512,512]{1,0:T(8,128)(2,1)S(1)} %get-tuple-element.64.tiles_ref, bf16[512,1024]{1,0:T(8,128)(2,1)S(1)} %get-tuple-element.65.base_ref, f8e4m3fn[512,1024]{1,0:T(32,128)(4,1)S(1)} %get-tuple-element.66.rest_ref, ...), custom_call_target="tpu_custom_call" | custom-call | flops 201326592 | tf_op jit(solution)/shard_map/last_a/pallas_call | solution.py:547
  63.9 2.2 %all-to-all-done.2 = bf16[32,16,640]{2,1,0:T(8,128)(2,1)S(1)} async-done(((bf16[32,16,640]{2,1,0:T(8,128)(2,1)}), bf16[32,16,640]{2,1,0:T(8,128)(2,1)S(1)}, u32[]{:S(2)}, u32[]{:S(2)}) %all-to-all-start.2) | async-done | bytes 655392 | tf_op jit(solution)/shard_map/all_to_all | solution.py:382
  66.1 1.3 %last_b.1 = bf16[512,1024]{1,0:T(8,128)(2,1)} custom-call(bf16[512,512]{1,0:T(8,128)(2,1)S(1)} %get-tuple-element.64.tiles_ref, bf16[512,1024]{1,0:T(8,128)(2,1)S(1)} %get-tuple-element.65.base_ref, f8e4m3fn[512,1024]{1,0:T(32,128)(4,1)S(1)} %get-tuple-element.66.rest_ref, bf16[512,640]{1,0:T(8,128)(2,1)S(1)} %bitcast.8, ...), custom_call_target="tpu_custom_call", output_to_operand_aliasing={{}: (4, {})} | custom-call | flops 335544320 | bytes 4194304 | tf_op jit(solution)/shard_map/last_b/pallas_call | solution.py:556
  (4 shorter events, 0.1 us)
Async XLA Ops:
  1.4 14.4 %all-to-all-start = ((s32[32,1,16]{2,1,0:T(1,128)}), s32[32,1,16]{2,1,0:T(1,128)S(1)}, u32[]{:S(2)}, u32[]{:S(2)}) async-start(s32[32,1,16]{2,1,0:T(1,128)} %bitcast), calls=%async_computation | async-start | bytes 32768 | tf_op jit(solution)/shard_map/all_to_all | solution.py:431
  16.3 10.4 %collective-permute-start = (bf16[128,384]{1,0:T(8,128)(2,1)S(1)}, bf16[128,384]{1,0:T(8,128)(2,1)S(1)}, u32[]{:S(2)}, u32[]{:S(2)}) collective-permute-start(bf16[128,384]{1,0:T(8,128)(2,1)S(1)} %get-tuple-element.45), channel_id=1, source_target_pairs={{0,16},{1,25},{2,18},{3,27},{4,20},{5,29},{6,22},{7,31},{8,24},{9,... | collective-permute-start | bytes 294920 | tf_op jit(solution)/shard_map/ppermute | solution.py:376
  17.0 9.8 %collective-permute-start.1 = (bf16[128,384]{1,0:T(8,128)(2,1)S(1)}, bf16[128,384]{1,0:T(8,128)(2,1)S(1)}, u32[]{:S(2)}, u32[]{:S(2)}) collective-permute-start(bf16[128,384]{1,0:T(8,128)(2,1)S(1)} %get-tuple-element.46), channel_id=1, source_target_pairs={{0,24},{1,17},{2,26},{3,19},{4,28},{5,21},{6,30},{7,23},{8,16},{9,... | collective-permute-start | bytes 294920 | tf_op jit(solution)/shard_map/ppermute | solution.py:376
  19.3 7.4 %collective-permute-start.2 = (bf16[128,384]{1,0:T(8,128)(2,1)S(1)}, bf16[128,384]{1,0:T(8,128)(2,1)S(1)}, u32[]{:S(2)}, u32[]{:S(2)}) collective-permute-start(bf16[128,384]{1,0:T(8,128)(2,1)S(1)} %get-tuple-element.47), channel_id=1, source_target_pairs={{0,8},{1,9},{2,10},{3,11},{4,12},{5,13},{6,14},{7,15},{8,0},{9,1},... | collective-permute-start | bytes 294920 | tf_op jit(solution)/shard_map/ppermute | solution.py:376
  21.3 22.2 %all-to-all-start.1 = ((bf16[32,16,640]{2,1,0:T(8,128)(2,1)}), bf16[32,16,640]{2,1,0:T(8,128)(2,1)S(1)}, u32[]{:S(2)}, u32[]{:S(2)}) async-start(bf16[32,16,640]{2,1,0:T(8,128)(2,1)} %bitcast.10), calls=%async_computation.1 | async-start | bytes 1310720 | tf_op jit(solution)/shard_map/all_to_all | solution.py:382
  26.8 1.5 %collective-permute-start.3 = (bf16[256,384]{1,0:T(8,128)(2,1)S(1)}, bf16[256,384]{1,0:T(8,128)(2,1)S(1)}, u32[]{:S(2)}, u32[]{:S(2)}) collective-permute-start(bf16[256,384]{1,0:T(8,128)(2,1)S(1)} %gather.2), channel_id=1, source_target_pairs={{0,1},{1,0},{2,3},{3,2},{4,5},{5,4},{6,7},{7,6},{8,9},{9,8},{10,11... | collective-permute-start | bytes 589832 | tf_op jit(solution)/shard_map/ppermute | solution.py:376
  28.3 9.8 %collective-permute-start.4 = (bf16[128,384]{1,0:T(8,128)(2,1)S(1)}, bf16[128,384]{1,0:T(8,128)(2,1)S(1)}, u32[]{:S(2)}, u32[]{:S(2)}) collective-permute-start(bf16[128,384]{1,0:T(8,128)(2,1)S(1)} %get-tuple-element.53), channel_id=1, source_target_pairs={{0,6},{1,5},{2,4},{3,7},{4,2},{5,1},{6,0},{7,3},{8,14},{9,13},{10,... | collective-permute-start | bytes 294920 | tf_op jit(solution)/shard_map/ppermute | solution.py:376
  29.3 8.9 %collective-permute-start.5 = (bf16[128,384]{1,0:T(8,128)(2,1)S(1)}, bf16[128,384]{1,0:T(8,128)(2,1)S(1)}, u32[]{:S(2)}, u32[]{:S(2)}) collective-permute-start(bf16[128,384]{1,0:T(8,128)(2,1)S(1)} %get-tuple-element.54), channel_id=1, source_target_pairs={{0,4},{1,3},{2,6},{3,1},{4,0},{5,7},{6,2},{7,5},{8,12},{9,11},{10,... | collective-permute-start | bytes 294920 | tf_op jit(solution)/shard_map/ppermute | solution.py:376
  30.6 7.8 %collective-permute-start.6 = (bf16[128,384]{1,0:T(8,128)(2,1)S(1)}, bf16[128,384]{1,0:T(8,128)(2,1)S(1)}, u32[]{:S(2)}, u32[]{:S(2)}) collective-permute-start(bf16[128,384]{1,0:T(8,128)(2,1)S(1)} %get-tuple-element.55), channel_id=1, source_target_pairs={{0,2},{1,7},{2,0},{3,5},{4,6},{5,3},{6,4},{7,1},{8,10},{9,15},{10,... | collective-permute-start | bytes 294920 | tf_op jit(solution)/shard_map/ppermute | solution.py:376
  39.2 10.9 %collective-permute-start.7 = (bf16[128,384]{1,0:T(8,128)(2,1)S(1)}, bf16[128,384]{1,0:T(8,128)(2,1)S(1)}, u32[]{:S(2)}, u32[]{:S(2)}) collective-permute-start(bf16[128,384]{1,0:T(8,128)(2,1)S(1)} %get-tuple-element.60), channel_id=1, source_target_pairs={{0,16},{1,25},{2,18},{3,27},{4,20},{5,29},{6,22},{7,31},{8,24},{9,... | collective-permute-start | bytes 294920 | tf_op jit(solution)/shard_map/ppermute | solution.py:376
  41.4 8.7 %collective-permute-start.8 = (bf16[128,384]{1,0:T(8,128)(2,1)S(1)}, bf16[128,384]{1,0:T(8,128)(2,1)S(1)}, u32[]{:S(2)}, u32[]{:S(2)}) collective-permute-start(bf16[128,384]{1,0:T(8,128)(2,1)S(1)} %get-tuple-element.61), channel_id=1, source_target_pairs={{0,24},{1,17},{2,26},{3,19},{4,28},{5,21},{6,30},{7,23},{8,16},{9,... | collective-permute-start | bytes 294920 | tf_op jit(solution)/shard_map/ppermute | solution.py:376
  43.4 7.1 %collective-permute-start.9 = (bf16[128,384]{1,0:T(8,128)(2,1)S(1)}, bf16[128,384]{1,0:T(8,128)(2,1)S(1)}, u32[]{:S(2)}, u32[]{:S(2)}) collective-permute-start(bf16[128,384]{1,0:T(8,128)(2,1)S(1)} %get-tuple-element.62), channel_id=1, source_target_pairs={{0,8},{1,9},{2,10},{3,11},{4,12},{5,13},{6,14},{7,15},{8,0},{9,1},... | collective-permute-start | bytes 294920 | tf_op jit(solution)/shard_map/ppermute | solution.py:376
  44.7 21.4 %all-to-all-start.2 = ((bf16[32,16,640]{2,1,0:T(8,128)(2,1)}), bf16[32,16,640]{2,1,0:T(8,128)(2,1)S(1)}, u32[]{:S(2)}, u32[]{:S(2)}) async-start(bf16[32,16,640]{2,1,0:T(8,128)(2,1)} %bitcast.11), calls=%async_computation.2 | async-start | bytes 1310720 | tf_op jit(solution)/shard_map/all_to_all | solution.py:382
  50.6 1.9 %collective-permute-start.10 = (bf16[256,384]{1,0:T(8,128)(2,1)S(1)}, bf16[256,384]{1,0:T(8,128)(2,1)S(1)}, u32[]{:S(2)}, u32[]{:S(2)}) collective-permute-start(bf16[256,384]{1,0:T(8,128)(2,1)S(1)} %gather.3), channel_id=1, source_target_pairs={{0,1},{1,0},{2,3},{3,2},{4,5},{5,4},{6,7},{7,6},{8,9},{9,8},{10,11... | collective-permute-start | bytes 589832 | tf_op jit(solution)/shard_map/ppermute | solution.py:376
  52.5 9.8 %collective-permute-start.11 = (bf16[128,384]{1,0:T(8,128)(2,1)S(1)}, bf16[128,384]{1,0:T(8,128)(2,1)S(1)}, u32[]{:S(2)}, u32[]{:S(2)}) collective-permute-start(bf16[128,384]{1,0:T(8,128)(2,1)S(1)} %get-tuple-element.68), channel_id=1, source_target_pairs={{0,6},{1,5},{2,4},{3,7},{4,2},{5,1},{6,0},{7,3},{8,14},{9,13},{10,... | collective-permute-start | bytes 294920 | tf_op jit(solution)/shard_map/ppermute | solution.py:376
  53.6 8.9 %collective-permute-start.12 = (bf16[128,384]{1,0:T(8,128)(2,1)S(1)}, bf16[128,384]{1,0:T(8,128)(2,1)S(1)}, u32[]{:S(2)}, u32[]{:S(2)}) collective-permute-start(bf16[128,384]{1,0:T(8,128)(2,1)S(1)} %get-tuple-element.69), channel_id=1, source_target_pairs={{0,4},{1,3},{2,6},{3,1},{4,0},{5,7},{6,2},{7,5},{8,12},{9,11},{10,... | collective-permute-start | bytes 294920 | tf_op jit(solution)/shard_map/ppermute | solution.py:376
  55.0 7.6 %collective-permute-start.13 = (bf16[128,384]{1,0:T(8,128)(2,1)S(1)}, bf16[128,384]{1,0:T(8,128)(2,1)S(1)}, u32[]{:S(2)}, u32[]{:S(2)}) collective-permute-start(bf16[128,384]{1,0:T(8,128)(2,1)S(1)} %get-tuple-element.70), channel_id=1, source_target_pairs={{0,2},{1,7},{2,0},{3,5},{4,6},{5,3},{6,4},{7,1},{8,10},{9,15},{10,... | collective-permute-start | bytes 294920 | tf_op jit(solution)/shard_map/ppermute | solution.py:376

commit v15 on v14

--- a/solution.py
+++ b/solution.py
@@ -421,7 +421,7 @@
     planes = peers // GROUP
     wide = max(3 * width // 8 // BLK, 1) * BLK
     assert peers & (peers - 1) == 0 and peers >= GROUP
-    head = rows - BLK
+    head = rows - 2 * BLK
     me = lax.axis_index("rows").astype(jnp.int32).reshape(1)
     sems = pltpu.SemaphoreType.DMA
     bf16 = jnp.bfloat16

time: 67.8 us -> 67.8 us (level)
  waiting for transfers between devices: 13.1 us -> 14.1 us
  starting transfers between devices: 29.4 us -> 28.5 us
    ppermute x14, starting transfers between devices: 15.8 us -> 15 us  [swap(): return lax.ppermute(x, 'rows', [(i, i ^ distance(i)) for i in range(peers)])]
    all_to_all x1, waiting for transfers between devices: 2.97 us -> 3.73 us  [on_device(): lax.all_to_all(wanted.reshape(peers, 1, slots), 'rows', split_axis=0, con...]
    pallas_call x1, Pallas kernels: 4.09 us -> 3.33 us  [on_device(): call(own_tiles_kernel, 'own_tiles', [far_out((rows, head)), near_out((dep...]
    pallas_call x1, Pallas kernels: 6.28 us -> 7.01 us  [on_device(): call(functools.partial(far_kernel, neighbours=neighbours), 'far', [far_ou...]
where the time goes in v15:
time: 67.8 us; the launch traced here: 67.4 us
  starting transfers between devices  28.5 us (42%)
  Pallas kernels  23.3 us (34%)
  waiting for transfers between devices  14.1 us (21%)
  local copies, waits for them, and re-layouts  1.38 us (2%)
    ppermute x14, starting transfers between devices, swap(): return lax.ppermute(x, 'rows', [(i, i ^ distance(i)) for i in range(peers)])  15 us
    ppermute x14, waiting for transfers between devices, swap(): return lax.ppermute(x, 'rows', [(i, i ^ distance(i)) for i in range(peers)])  8.02 us
    all_to_all x1, starting transfers between devices, on_device(): lax.all_to_all(wanted.reshape(peers, 1, slots), 'rows', split_axis=0, con...  7.3 us
    pallas_call x1, Pallas kernels, on_device(): call(functools.partial(far_kernel, neighbours=neighbours), 'far', [far_ou...  7.01 us
    pallas_call x1, Pallas kernels, on_device(): call(labels_kernel, 'labels', [near_out((rows, width)), near_out((rows, w...  6.21 us
    all_to_all x2, starting transfers between devices, exchange(): got = lax.all_to_all(sent, 'rows', split_axis=0, concat_axis=0, tiled=True)  6.15 us
    all_to_all x1, waiting for transfers between devices, on_device(): lax.all_to_all(wanted.reshape(peers, 1, slots), 'rows', split_axis=0, con...  3.73 us
    pallas_call x1, Pallas kernels, on_device(): call(own_tiles_kernel, 'own_tiles', [far_out((rows, head)), near_out((dep...  3.33 us
  transfers between devices with their start and end apart: 17, of which 9 were waited for; matrix products, arithmetic and copies ran while one was open for 0% of the time, Pallas kernels for 32%

profile of v15, /device:TPU:0, one launch (start us, length us, event | category | flops | bytes accessed | tf_op | source)
XLA Modules:
  0.0 67.4 jit_solution(2640642957358125846)
XLA Ops:
  0.0 1.4 %copy.7 = s32[1,32,16]{2,1,0:T(8,128)} copy(s32[1,32,16]{1,2,0:T(8,128)} %param.9) | data formatting | bytes 4096 | tf_op args[4]
  1.4 7.3 %all-to-all-start = ((s32[32,1,16]{2,1,0:T(1,128)}), s32[32,1,16]{2,1,0:T(1,128)S(1)}, u32[]{:S(2)}, u32[]{:S(2)}) async-start(s32[32,1,16]{2,1,0:T(1,128)} %bitcast), calls=%async_computation | async-start | bytes 32768 | tf_op jit(solution)/shard_map/all_to_all | solution.py:431
  8.7 3.3 %own_tiles.1 = (bf16[512,256]{1,0:T(8,128)(2,1)}, s32[64,512]{1,0:T(8,128)S(1)}, f32[64,512]{1,0:T(8,128)S(1)}, bf16[512,1024]{1,0:T(8,128)(2,1)S(1)}) custom-call(s32[4,8]{1,0:T(4,128)} %blocks_ref.1, s32[50,512]{1,0:T(8,128)} %bitcast.12, s32[50,512]{1,0:T(8,128)} %bitcast.13, bf16[512,1024]{1,0:T(8,128)(2,1)} %seeds_ref.3), custom_call_target="tpu_custom_call" | custom-call | flops 13107200 | tf_op jit(solution)/shard_map/own_tiles/pallas_call | solution.py:434
  12.0 3.7 %all-to-all-done.asked_ref = s32[32,1,16]{2,1,0:T(1,128)S(1)} async-done(((s32[32,1,16]{2,1,0:T(1,128)}), s32[32,1,16]{2,1,0:T(1,128)S(1)}, u32[]{:S(2)}, u32[]{:S(2)}) %all-to-all-start) | async-done | bytes 2080 | tf_op jit(solution)/shard_map/all_to_all | solution.py:431
  15.8 0.6 pick_a.1
  16.3 0.7 collective-permute-start
  17.0 2.3 %collective-permute-start.1 = (bf16[128,384]{1,0:T(8,128)(2,1)S(1)}, bf16[128,384]{1,0:T(8,128)(2,1)S(1)}, u32[]{:S(2)}, u32[]{:S(2)}) collective-permute-start(bf16[128,384]{1,0:T(8,128)(2,1)S(1)} %get-tuple-element.46), channel_id=1, source_target_pairs={{0,24},{1,17},{2,26},{3,19},{4,28},{5,21},{6,30},{7,23},{8,16},{9,... | collective-permute-start | bytes 294920 | tf_op jit(solution)/shard_map/ppermute | solution.py:376
  19.3 0.6 collective-permute-start.2
  19.9 1.4 %pick_b.1 = (bf16[512,640]{1,0:T(8,128)(2,1)}, bf16[512,128]{1,0:T(8,128)(2,1)S(1)}) custom-call(bf16[512,512]{1,0:T(8,128)(2,1)S(1)} %get-tuple-element.40.pick_ref, bf16[512,1024]{1,0:T(8,128)(2,1)S(1)} %get-tuple-element.38.seeds_ref, s32[64,512]{1,0:T(8,128)S(1)} %get-tuple-element.41.column_ref, f32[64,512]{1,0:T(8,128)S(1)} %get-tuple-element.42.share_ref), custom_call_target="tpu_custom_call" | custom-call | flops 335544320 | tf_op jit(solution)/shard_map/pick_b/pallas_call | solution.py:462
  21.3 2.6 %all-to-all-start.1 = ((bf16[32,16,640]{2,1,0:T(8,128)(2,1)}), bf16[32,16,640]{2,1,0:T(8,128)(2,1)S(1)}, u32[]{:S(2)}, u32[]{:S(2)}) async-start(bf16[32,16,640]{2,1,0:T(8,128)(2,1)} %bitcast.10), calls=%async_computation.1 | async-start | bytes 1310720 | tf_op jit(solution)/shard_map/all_to_all | solution.py:382
  23.9 2.4 %collective-permute-done.refs_1_ = bf16[128,384]{1,0:T(8,128)(2,1)S(1)} collective-permute-done((bf16[128,384]{1,0:T(8,128)(2,1)S(1)}, bf16[128,384]{1,0:T(8,128)(2,1)S(1)}, u32[]{:S(2)}, u32[]{:S(2)}) %collective-permute-start) | collective-permute-done | bytes 98336 | tf_op jit(solution)/shard_map/ppermute | solution.py:376
  26.3 0.0 collective-permute-done.1.refs_2_
  26.3 0.0 collective-permute-done.2.refs_3_
  26.3 0.1 collective-permute-start.3
  26.4 1.4 %collective-permute-done.3.refs_4_ = bf16[256,384]{1,0:T(8,128)(2,1)S(1)} collective-permute-done((bf16[256,384]{1,0:T(8,128)(2,1)S(1)}, bf16[256,384]{1,0:T(8,128)(2,1)S(1)}, u32[]{:S(2)}, u32[]{:S(2)}) %collective-permute-start.3) | collective-permute-done | bytes 196640 | tf_op jit(solution)/shard_map/ppermute | solution.py:376
  27.9 1.4 %collective-permute-start.4 = (bf16[128,384]{1,0:T(8,128)(2,1)S(1)}, bf16[128,384]{1,0:T(8,128)(2,1)S(1)}, u32[]{:S(2)}, u32[]{:S(2)}) collective-permute-start(bf16[128,384]{1,0:T(8,128)(2,1)S(1)} %get-tuple-element.53), channel_id=1, source_target_pairs={{0,6},{1,5},{2,4},{3,7},{4,2},{5,1},{6,0},{7,3},{8,14},{9,13},{10,... | collective-permute-start | bytes 294920 | tf_op jit(solution)/shard_map/ppermute | solution.py:376
  29.2 1.3 %collective-permute-start.5 = (bf16[128,384]{1,0:T(8,128)(2,1)S(1)}, bf16[128,384]{1,0:T(8,128)(2,1)S(1)}, u32[]{:S(2)}, u32[]{:S(2)}) collective-permute-start(bf16[128,384]{1,0:T(8,128)(2,1)S(1)} %get-tuple-element.54), channel_id=1, source_target_pairs={{0,4},{1,3},{2,6},{3,1},{4,0},{5,7},{6,2},{7,5},{8,12},{9,11},{10,... | collective-permute-start | bytes 294920 | tf_op jit(solution)/shard_map/ppermute | solution.py:376
  30.6 0.8 %collective-permute-start.6 = (bf16[128,384]{1,0:T(8,128)(2,1)S(1)}, bf16[128,384]{1,0:T(8,128)(2,1)S(1)}, u32[]{:S(2)}, u32[]{:S(2)}) collective-permute-start(bf16[128,384]{1,0:T(8,128)(2,1)S(1)} %get-tuple-element.55), channel_id=1, source_target_pairs={{0,2},{1,7},{2,0},{3,5},{4,6},{5,3},{6,4},{7,1},{8,10},{9,15},{10,... | collective-permute-start | bytes 294920 | tf_op jit(solution)/shard_map/ppermute | solution.py:376
  31.4 7.0 %far.1 = (bf16[512,512]{1,0:T(8,128)(2,1)}, bf16[512,512]{1,0:T(8,128)(2,1)S(1)}, bf16[512,1024]{1,0:T(8,128)(2,1)S(1)}, bf16[512,512]{1,0:T(8,128)(2,1)}) custom-call(s32[32,1,16]{2,1,0:T(1,128)S(1)} %all-to-all-done.asked_ref, bf16[512,128]{1,0:T(8,128)(2,1)S(1)} %get-tuple-element.43.early_ref, bf16[512,256]{1,0:T(8,128)(2,1)} %get-tuple-element.39.after_ref.own_ref, ...), custom_call_target="tpu_custom_call" | custom-call | flops 1086849024 | tf_op jit(solution)/shard_map/far/pallas_call | solution.py:480
  38.4 0.0 collective-permute-done.4.refs_1_
  38.4 0.0 collective-permute-done.5.refs_2_
  38.5 0.0 collective-permute-done.6.refs_3_
  38.5 0.8 %send_a.1 = (bf16[512,384]{1,0:T(8,128)(2,1)}, bf16[128,384]{1,0:T(8,128)(2,1)S(1)}, bf16[128,384]{1,0:T(8,128)(2,1)S(1)}, bf16[128,384]{1,0:T(8,128)(2,1)S(1)}, bf16[128,384]{1,0:T(8,128)(2,1)S(1)}) custom-call(s32[1]{0:T(128)} %bitcast.1.me_ref, bf16[512,512]{1,0:T(8,128)(2,1)S(1)} %get-tuple-element.51.tiles_ref, ...), custom_call_target="tpu_custom_call" | custom-call | flops 201326592 | tf_op jit(solution)/shard_map/send_a/pallas_call | solution.py:506
  39.3 1.7 %collective-permute-start.7 = (bf16[128,384]{1,0:T(8,128)(2,1)S(1)}, bf16[128,384]{1,0:T(8,128)(2,1)S(1)}, u32[]{:S(2)}, u32[]{:S(2)}) collective-permute-start(bf16[128,384]{1,0:T(8,128)(2,1)S(1)} %get-tuple-element.60), channel_id=1, source_target_pairs={{0,16},{1,25},{2,18},{3,27},{4,20},{5,29},{6,22},{7,31},{8,24},{9,... | collective-permute-start | bytes 294920 | tf_op jit(solution)/shard_map/ppermute | solution.py:376
  40.9 2.4 %collective-permute-start.8 = (bf16[128,384]{1,0:T(8,128)(2,1)S(1)}, bf16[128,384]{1,0:T(8,128)(2,1)S(1)}, u32[]{:S(2)}, u32[]{:S(2)}) collective-permute-start(bf16[128,384]{1,0:T(8,128)(2,1)S(1)} %get-tuple-element.61), channel_id=1, source_target_pairs={{0,24},{1,17},{2,26},{3,19},{4,28},{5,21},{6,30},{7,23},{8,16},{9,... | collective-permute-start | bytes 294920 | tf_op jit(solution)/shard_map/ppermute | solution.py:376
  43.3 0.0 collective-permute-start.9
  43.3 0.0 all-to-all-done.1
  43.3 1.3 %send_b.1 = (bf16[512,640]{1,0:T(8,128)(2,1)}, bf16[512,640]{1,0:T(8,128)(2,1)}) custom-call(bf16[512,512]{1,0:T(8,128)(2,1)S(1)} %get-tuple-element.51.tiles_ref, bf16[512,1024]{1,0:T(8,128)(2,1)S(1)} %get-tuple-element.52.base_ref, bf16[512,640]{1,0:T(8,128)(2,1)S(1)} %bitcast.9, bf16[128,384]{1,0:T(8,128)(2,1)S(1)} %get-tuple-element.58.after_ref.refs_0_), custom_call_target="tpu_custom_call" | custom-call | flops 335544320 | bytes 3538944 | tf_op jit(solution)/shard_map/send_b/pallas_call | solution.py:516
  44.6 3.5 %all-to-all-start.2 = ((bf16[32,16,640]{2,1,0:T(8,128)(2,1)}), bf16[32,16,640]{2,1,0:T(8,128)(2,1)S(1)}, u32[]{:S(2)}, u32[]{:S(2)}) async-start(bf16[32,16,640]{2,1,0:T(8,128)(2,1)} %bitcast.11), calls=%async_computation.2 | async-start | bytes 1310720 | tf_op jit(solution)/shard_map/all_to_all | solution.py:382
  48.1 2.0 %collective-permute-done.7.refs_1_ = bf16[128,384]{1,0:T(8,128)(2,1)S(1)} collective-permute-done((bf16[128,384]{1,0:T(8,128)(2,1)S(1)}, bf16[128,384]{1,0:T(8,128)(2,1)S(1)}, u32[]{:S(2)}, u32[]{:S(2)}) %collective-permute-start.7) | collective-permute-done | bytes 98336 | tf_op jit(solution)/shard_map/ppermute | solution.py:376
  50.1 0.0 collective-permute-done.8.refs_2_
  50.1 0.7 %collective-permute-done.9.refs_3_ = bf16[128,384]{1,0:T(8,128)(2,1)S(1)} collective-permute-done((bf16[128,384]{1,0:T(8,128)(2,1)S(1)}, bf16[128,384]{1,0:T(8,128)(2,1)S(1)}, u32[]{:S(2)}, u32[]{:S(2)}) %collective-permute-start.9) | collective-permute-done | bytes 98336 | tf_op jit(solution)/shard_map/ppermute | solution.py:376
  50.9 0.3 collective-permute-start.10
  51.1 1.2 %collective-permute-done.10.refs_4_ = bf16[256,384]{1,0:T(8,128)(2,1)S(1)} collective-permute-done((bf16[256,384]{1,0:T(8,128)(2,1)S(1)}, bf16[256,384]{1,0:T(8,128)(2,1)S(1)}, u32[]{:S(2)}, u32[]{:S(2)}) %collective-permute-start.10) | collective-permute-done | bytes 196640 | tf_op jit(solution)/shard_map/ppermute | solution.py:376
  52.4 1.6 %collective-permute-start.11 = (bf16[128,384]{1,0:T(8,128)(2,1)S(1)}, bf16[128,384]{1,0:T(8,128)(2,1)S(1)}, u32[]{:S(2)}, u32[]{:S(2)}) collective-permute-start(bf16[128,384]{1,0:T(8,128)(2,1)S(1)} %get-tuple-element.68), channel_id=1, source_target_pairs={{0,6},{1,5},{2,4},{3,7},{4,2},{5,1},{6,0},{7,3},{8,14},{9,13},{10,... | collective-permute-start | bytes 294920 | tf_op jit(solution)/shard_map/ppermute | solution.py:376
  54.0 0.8 %collective-permute-start.12 = (bf16[128,384]{1,0:T(8,128)(2,1)S(1)}, bf16[128,384]{1,0:T(8,128)(2,1)S(1)}, u32[]{:S(2)}, u32[]{:S(2)}) collective-permute-start(bf16[128,384]{1,0:T(8,128)(2,1)S(1)} %get-tuple-element.69), channel_id=1, source_target_pairs={{0,4},{1,3},{2,6},{3,1},{4,0},{5,7},{6,2},{7,5},{8,12},{9,11},{10,... | collective-permute-start | bytes 294920 | tf_op jit(solution)/shard_map/ppermute | solution.py:376
  54.8 1.2 %collective-permute-start.13 = (bf16[128,384]{1,0:T(8,128)(2,1)S(1)}, bf16[128,384]{1,0:T(8,128)(2,1)S(1)}, u32[]{:S(2)}, u32[]{:S(2)}) collective-permute-start(bf16[128,384]{1,0:T(8,128)(2,1)S(1)} %get-tuple-element.70), channel_id=1, source_target_pairs={{0,2},{1,7},{2,0},{3,5},{4,6},{5,3},{6,4},{7,1},{8,10},{9,15},{10,... | collective-permute-start | bytes 294920 | tf_op jit(solution)/shard_map/ppermute | solution.py:376
  56.0 6.2 %labels.1 = (bf16[512,1024]{1,0:T(8,128)(2,1)S(1)}, f8e4m3fn[512,1024]{1,0:T(32,128)(4,1)S(1)}, bf16[512,512]{1,0:T(8,128)(2,1)S(1)}) custom-call(bf16[512,512]{1,0:T(8,128)(2,1)} %get-tuple-element.49.own_ref, bf16[512,512]{1,0:T(8,128)(2,1)} %get-tuple-element.50.far_ref, bf16[512,1024]{1,0:T(8,128)(2,1)} %seeds_ref.3, ...), custom_call_target="tpu_custom_call" | custom-call | flops 1610612736 | tf_op jit(solution)/shard_map/labels/pallas_call | solution.py:528
  62.2 0.0 collective-permute-done.11.refs_1_
  62.2 0.1 collective-permute-done.12.refs_2_
  62.3 0.2 collective-permute-done.13.refs_3_
  62.5 1.3 %last_a.1.same_ref = bf16[512,1024]{1,0:T(8,128)(2,1)} custom-call(s32[1]{0:T(128)} %bitcast.1.me_ref, bf16[512,512]{1,0:T(8,128)(2,1)S(1)} %get-tuple-element.64.tiles_ref, bf16[512,1024]{1,0:T(8,128)(2,1)S(1)} %get-tuple-element.65.base_ref, f8e4m3fn[512,1024]{1,0:T(32,128)(4,1)S(1)} %get-tuple-element.66.rest_ref, ...), custom_call_target="tpu_custom_call" | custom-call | flops 201326592 | tf_op jit(solution)/shard_map/last_a/pallas_call | solution.py:547
  63.7 2.3 %all-to-all-done.2 = bf16[32,16,640]{2,1,0:T(8,128)(2,1)S(1)} async-done(((bf16[32,16,640]{2,1,0:T(8,128)(2,1)}), bf16[32,16,640]{2,1,0:T(8,128)(2,1)S(1)}, u32[]{:S(2)}, u32[]{:S(2)}) %all-to-all-start.2) | async-done | bytes 655392 | tf_op jit(solution)/shard_map/all_to_all | solution.py:382
  66.1 1.3 %last_b.1 = bf16[512,1024]{1,0:T(8,128)(2,1)} custom-call(bf16[512,512]{1,0:T(8,128)(2,1)S(1)} %get-tuple-element.64.tiles_ref, bf16[512,1024]{1,0:T(8,128)(2,1)S(1)} %get-tuple-element.65.base_ref, f8e4m3fn[512,1024]{1,0:T(32,128)(4,1)S(1)} %get-tuple-element.66.rest_ref, bf16[512,640]{1,0:T(8,128)(2,1)S(1)} %bitcast.8, ...), custom_call_target="tpu_custom_call", output_to_operand_aliasing={{}: (4, {})} | custom-call | flops 335544320 | bytes 4194304 | tf_op jit(solution)/shard_map/last_b/pallas_call | solution.py:556
  (4 shorter events, 0.1 us)
Async XLA Ops:
  1.4 14.4 %all-to-all-start = ((s32[32,1,16]{2,1,0:T(1,128)}), s32[32,1,16]{2,1,0:T(1,128)S(1)}, u32[]{:S(2)}, u32[]{:S(2)}) async-start(s32[32,1,16]{2,1,0:T(1,128)} %bitcast), calls=%async_computation | async-start | bytes 32768 | tf_op jit(solution)/shard_map/all_to_all | solution.py:431
  16.3 10.0 %collective-permute-start = (bf16[128,384]{1,0:T(8,128)(2,1)S(1)}, bf16[128,384]{1,0:T(8,128)(2,1)S(1)}, u32[]{:S(2)}, u32[]{:S(2)}) collective-permute-start(bf16[128,384]{1,0:T(8,128)(2,1)S(1)} %get-tuple-element.45), channel_id=1, source_target_pairs={{0,16},{1,25},{2,18},{3,27},{4,20},{5,29},{6,22},{7,31},{8,24},{9,... | collective-permute-start | bytes 294920 | tf_op jit(solution)/shard_map/ppermute | solution.py:376
  17.0 9.3 %collective-permute-start.1 = (bf16[128,384]{1,0:T(8,128)(2,1)S(1)}, bf16[128,384]{1,0:T(8,128)(2,1)S(1)}, u32[]{:S(2)}, u32[]{:S(2)}) collective-permute-start(bf16[128,384]{1,0:T(8,128)(2,1)S(1)} %get-tuple-element.46), channel_id=1, source_target_pairs={{0,24},{1,17},{2,26},{3,19},{4,28},{5,21},{6,30},{7,23},{8,16},{9,... | collective-permute-start | bytes 294920 | tf_op jit(solution)/shard_map/ppermute | solution.py:376
  19.3 7.0 %collective-permute-start.2 = (bf16[128,384]{1,0:T(8,128)(2,1)S(1)}, bf16[128,384]{1,0:T(8,128)(2,1)S(1)}, u32[]{:S(2)}, u32[]{:S(2)}) collective-permute-start(bf16[128,384]{1,0:T(8,128)(2,1)S(1)} %get-tuple-element.47), channel_id=1, source_target_pairs={{0,8},{1,9},{2,10},{3,11},{4,12},{5,13},{6,14},{7,15},{8,0},{9,1},... | collective-permute-start | bytes 294920 | tf_op jit(solution)/shard_map/ppermute | solution.py:376
  21.3 22.0 %all-to-all-start.1 = ((bf16[32,16,640]{2,1,0:T(8,128)(2,1)}), bf16[32,16,640]{2,1,0:T(8,128)(2,1)S(1)}, u32[]{:S(2)}, u32[]{:S(2)}) async-start(bf16[32,16,640]{2,1,0:T(8,128)(2,1)} %bitcast.10), calls=%async_computation.1 | async-start | bytes 1310720 | tf_op jit(solution)/shard_map/all_to_all | solution.py:382
  26.3 1.5 %collective-permute-start.3 = (bf16[256,384]{1,0:T(8,128)(2,1)S(1)}, bf16[256,384]{1,0:T(8,128)(2,1)S(1)}, u32[]{:S(2)}, u32[]{:S(2)}) collective-permute-start(bf16[256,384]{1,0:T(8,128)(2,1)S(1)} %gather.2), channel_id=1, source_target_pairs={{0,1},{1,0},{2,3},{3,2},{4,5},{5,4},{6,7},{7,6},{8,9},{9,8},{10,11... | collective-permute-start | bytes 589832 | tf_op jit(solution)/shard_map/ppermute | solution.py:376
  27.9 10.6 %collective-permute-start.4 = (bf16[128,384]{1,0:T(8,128)(2,1)S(1)}, bf16[128,384]{1,0:T(8,128)(2,1)S(1)}, u32[]{:S(2)}, u32[]{:S(2)}) collective-permute-start(bf16[128,384]{1,0:T(8,128)(2,1)S(1)} %get-tuple-element.53), channel_id=1, source_target_pairs={{0,6},{1,5},{2,4},{3,7},{4,2},{5,1},{6,0},{7,3},{8,14},{9,13},{10,... | collective-permute-start | bytes 294920 | tf_op jit(solution)/shard_map/ppermute | solution.py:376
  29.2 9.2 %collective-permute-start.5 = (bf16[128,384]{1,0:T(8,128)(2,1)S(1)}, bf16[128,384]{1,0:T(8,128)(2,1)S(1)}, u32[]{:S(2)}, u32[]{:S(2)}) collective-permute-start(bf16[128,384]{1,0:T(8,128)(2,1)S(1)} %get-tuple-element.54), channel_id=1, source_target_pairs={{0,4},{1,3},{2,6},{3,1},{4,0},{5,7},{6,2},{7,5},{8,12},{9,11},{10,... | collective-permute-start | bytes 294920 | tf_op jit(solution)/shard_map/ppermute | solution.py:376
  30.6 7.9 %collective-permute-start.6 = (bf16[128,384]{1,0:T(8,128)(2,1)S(1)}, bf16[128,384]{1,0:T(8,128)(2,1)S(1)}, u32[]{:S(2)}, u32[]{:S(2)}) collective-permute-start(bf16[128,384]{1,0:T(8,128)(2,1)S(1)} %get-tuple-element.55), channel_id=1, source_target_pairs={{0,2},{1,7},{2,0},{3,5},{4,6},{5,3},{6,4},{7,1},{8,10},{9,15},{10,... | collective-permute-start | bytes 294920 | tf_op jit(solution)/shard_map/ppermute | solution.py:376
  39.3 10.8 %collective-permute-start.7 = (bf16[128,384]{1,0:T(8,128)(2,1)S(1)}, bf16[128,384]{1,0:T(8,128)(2,1)S(1)}, u32[]{:S(2)}, u32[]{:S(2)}) collective-permute-start(bf16[128,384]{1,0:T(8,128)(2,1)S(1)} %get-tuple-element.60), channel_id=1, source_target_pairs={{0,16},{1,25},{2,18},{3,27},{4,20},{5,29},{6,22},{7,31},{8,24},{9,... | collective-permute-start | bytes 294920 | tf_op jit(solution)/shard_map/ppermute | solution.py:376
  40.9 9.2 %collective-permute-start.8 = (bf16[128,384]{1,0:T(8,128)(2,1)S(1)}, bf16[128,384]{1,0:T(8,128)(2,1)S(1)}, u32[]{:S(2)}, u32[]{:S(2)}) collective-permute-start(bf16[128,384]{1,0:T(8,128)(2,1)S(1)} %get-tuple-element.61), channel_id=1, source_target_pairs={{0,24},{1,17},{2,26},{3,19},{4,28},{5,21},{6,30},{7,23},{8,16},{9,... | collective-permute-start | bytes 294920 | tf_op jit(solution)/shard_map/ppermute | solution.py:376
  43.3 7.5 %collective-permute-start.9 = (bf16[128,384]{1,0:T(8,128)(2,1)S(1)}, bf16[128,384]{1,0:T(8,128)(2,1)S(1)}, u32[]{:S(2)}, u32[]{:S(2)}) collective-permute-start(bf16[128,384]{1,0:T(8,128)(2,1)S(1)} %get-tuple-element.62), channel_id=1, source_target_pairs={{0,8},{1,9},{2,10},{3,11},{4,12},{5,13},{6,14},{7,15},{8,0},{9,1},... | collective-permute-start | bytes 294920 | tf_op jit(solution)/shard_map/ppermute | solution.py:376
  44.6 21.4 %all-to-all-start.2 = ((bf16[32,16,640]{2,1,0:T(8,128)(2,1)}), bf16[32,16,640]{2,1,0:T(8,128)(2,1)S(1)}, u32[]{:S(2)}, u32[]{:S(2)}) async-start(bf16[32,16,640]{2,1,0:T(8,128)(2,1)} %bitcast.11), calls=%async_computation.2 | async-start | bytes 1310720 | tf_op jit(solution)/shard_map/all_to_all | solution.py:382
  50.9 1.5 %collective-permute-start.10 = (bf16[256,384]{1,0:T(8,128)(2,1)S(1)}, bf16[256,384]{1,0:T(8,128)(2,1)S(1)}, u32[]{:S(2)}, u32[]{:S(2)}) collective-permute-start(bf16[256,384]{1,0:T(8,128)(2,1)S(1)} %gather.3), channel_id=1, source_target_pairs={{0,1},{1,0},{2,3},{3,2},{4,5},{5,4},{6,7},{7,6},{8,9},{9,8},{10,11... | collective-permute-start | bytes 589832 | tf_op jit(solution)/shard_map/ppermute | solution.py:376
  52.4 9.8 %collective-permute-start.11 = (bf16[128,384]{1,0:T(8,128)(2,1)S(1)}, bf16[128,384]{1,0:T(8,128)(2,1)S(1)}, u32[]{:S(2)}, u32[]{:S(2)}) collective-permute-start(bf16[128,384]{1,0:T(8,128)(2,1)S(1)} %get-tuple-element.68), channel_id=1, source_target_pairs={{0,6},{1,5},{2,4},{3,7},{4,2},{5,1},{6,0},{7,3},{8,14},{9,13},{10,... | collective-permute-start | bytes 294920 | tf_op jit(solution)/shard_map/ppermute | solution.py:376
  54.0 8.3 %collective-permute-start.12 = (bf16[128,384]{1,0:T(8,128)(2,1)S(1)}, bf16[128,384]{1,0:T(8,128)(2,1)S(1)}, u32[]{:S(2)}, u32[]{:S(2)}) collective-permute-start(bf16[128,384]{1,0:T(8,128)(2,1)S(1)} %get-tuple-element.69), channel_id=1, source_target_pairs={{0,4},{1,3},{2,6},{3,1},{4,0},{5,7},{6,2},{7,5},{8,12},{9,11},{10,... | collective-permute-start | bytes 294920 | tf_op jit(solution)/shard_map/ppermute | solution.py:376
  54.8 7.7 %collective-permute-start.13 = (bf16[128,384]{1,0:T(8,128)(2,1)S(1)}, bf16[128,384]{1,0:T(8,128)(2,1)S(1)}, u32[]{:S(2)}, u32[]{:S(2)}) collective-permute-start(bf16[128,384]{1,0:T(8,128)(2,1)S(1)} %get-tuple-element.70), channel_id=1, source_target_pairs={{0,2},{1,7},{2,0},{3,5},{4,6},{5,3},{6,4},{7,1},{8,10},{9,15},{10,... | collective-permute-start | bytes 294920 | tf_op jit(solution)/shard_map/ppermute | solution.py:376
